TPU v7x, 128 devices: a whole 4x4x4 slice. The times are simulated.
128 devices in a mesh: section: 2 (over x_hi), dp: 32 (over x_lo, y, z), tensor: 2 (over core).
Axes of the slice: x: 4 (x_hi: 2, x_lo: 2; x = x_hi * 2 + x_lo), y: 4, z: 4, core: 2. Of those that a mesh axis runs over, the one named last changes fastest.
Arguments:
- inputs: bfloat16 [32, 2, 128, 1536], P('dp', None, 'tensor'), may hold values from -6 to 6
- out_cotangent: bfloat16 [32, 2, 128, 1536], P('dp', None, 'tensor'), may hold values from -6 to 6
- segments: int32 [32, 2, 128], P('dp'), may hold values from 0 to 2, as said below
- norm_gains: bfloat16 [2, 2, 1536], replicated, may hold values from 0.25 to 1.75
- conv_kernel: bfloat16 [3, 1536], replicated, may hold values from -3 to 3
- qk_gains: bfloat16 [2, 64], replicated, may hold values from 0.25 to 1.75
- conv_in: bfloat16 [1536, 3, 1536], P(('section', 'dp'), None, 'tensor'), may hold values from -0.15625 to 0.15625
- attn_qkv: bfloat16 [1536, 2560], P(('section', 'dp'), 'tensor'), may hold values from -0.15625 to 0.15625
- mixer_out: bfloat16 [2, 1536, 1536], P('section', 'tensor'), may hold values from -0.3125 to 0.3125
- gate_up: bfloat16 [2, 2, 1536, 6912], P('section', None, None, 'tensor'), may hold values from -0.15625 to 0.15625
- down: bfloat16 [2, 6912, 1536], P('section', 'tensor'), may hold values from -0.078125 to 0.078125
Outputs:
- activations: bfloat16 [2, 32, 2, 128, 1536], P('section', 'dp', None, 'tensor')
- input_grads: bfloat16 [2, 32, 2, 128, 1536], P('section', 'dp', None, 'tensor')
- grad_norm_gains: float32 [2, 2, 1536], replicated
- grad_conv_kernel: float32 [3, 1536], replicated
- grad_qk_gains: float32 [2, 64], replicated
- grad_conv_in: float32 [1536, 3, 1536], P(('section', 'dp'), None, 'tensor')
- grad_attn_qkv: float32 [1536, 2560], P(('section', 'dp'), 'tensor')
- grad_mixer_out: float32 [2, 1536, 1536], P('section', 'tensor', 'dp')
- grad_gate_up: float32 [2, 2, 1536, 6912], P('section', None, 'dp', 'tensor')
- grad_down: float32 [2, 6912, 1536], P('section', 'tensor', 'dp')
Inputs may be any that keep to these rules, and one draw needn't show every extreme that they name: `segments`: segment numbers never fall along a sequence, and every document has 16 positions or more.
All inputs are finite; a program needn't handle non-finite values.
Results may differ from a plain program's by a relative error of at most 0.04.
Values may be sent and summed in bfloat16 or wider, within the bound.
No kernel may reach another device: no remote copies, remote signals or barrier semaphores. Data moves between devices by JAX's collectives and lax.ppermute only.
A program may use at most 448 MiB of HBM per device.

v0:
```python
import functools

import jax
import jax.numpy as jnp
from jax import lax
from jax.experimental import pallas as pl
from jax.experimental.pallas import tpu as pltpu
from jax.sharding import Mesh
from jax.sharding import PartitionSpec as P

HEADS = 24
KV_HEADS = 8
HEAD_DIM = 64
GROUP = HEADS // KV_HEADS

EPSILON = 1e-05
ROPE_BASE = 1000000.0
MASKED_SCORE = -1e30

F32 = jnp.float32
BF16 = jnp.bfloat16

PLANE = ("y", "z")
AXES = ("xh", "xl", "y", "z", "c")


def product(left, right):
    return jnp.dot(left, right, preferred_element_type=F32)


def product_left(left, right):
    return lax.dot_general(left, right, (((0,), (0,)), ((), ())), preferred_element_type=F32)


def product_right(left, right):
    return lax.dot_general(left, right, (((1,), (1,)), ((), ())), preferred_element_type=F32)


def swapped(shard, axis):
    return lax.ppermute(shard, axis, [(0, 1), (1, 0)])


def spread(own):
    return lax.all_gather(own, "c", tiled=True)


def joined(mine, other):
    return mine + swapped(other, "c").astype(F32)


def mean_last(values):
    return jnp.mean(values, axis=-1, keepdims=True)


def inverse_rms(values):
    return lax.rsqrt(mean_last(values * values) + EPSILON)


def normalize(values):
    return values * inverse_rms(values)


def norm_backward(grad, gain, values):
    inverse = inverse_rms(values)
    normed = values * inverse
    scaled = grad * gain
    grad_gain = jnp.sum(grad * normed, axis=0)
    return inverse * (scaled - normed * mean_last(scaled * normed)), grad_gain


def exchanged(tiles, axes):
    return lax.all_to_all(tiles, axes, 0, 0, tiled=True)


def ffn_grads(grad_active, gate, up):
    sigmoid = jax.nn.sigmoid(gate)
    grad_gate = grad_active * up * sigmoid * (1.0 + gate * (1.0 - sigmoid))
    grad_up = grad_active * gate * sigmoid
    return grad_gate.astype(BF16), grad_up.astype(BF16)


VMEM_LIMIT = 56 * 1024 * 1024


def unit_tiles(units, tile):
    short = units % tile
    tiles = [(0, short)] if short else []
    return tiles + [(at, tile) for at in range(short, units, tile)]


def streamed(tiles, copies, work):
    for copy in copies(0, 0):
        copy.start()
    for k in range(len(tiles)):
        slot = k % 2
        if k + 1 < len(tiles):
            for copy in copies(k + 1, 1 - slot):
                copy.start()
        for copy in copies(k, slot):
            copy.wait()
        work(k, slot)


def ffn_forward_kernel(
    tiles, core_ref, rows_ref, pair_ref, down_ref, gate_ref, up_ref, mine_ref, other_ref,
    pair_buf, down_buf, gate_buf, up_buf, acc_ref, sems, out_sems,
):
    def copies(k, slot):
        at, size = tiles[k]
        return [
            pltpu.make_async_copy(
                pair_ref.at[0, :, pl.ds(at, size)],
                pair_buf.at[slot, :, pl.ds(0, size)],
                sems.at[slot, 0],
            ),
            pltpu.make_async_copy(
                pair_ref.at[1, :, pl.ds(at, size)],
                pair_buf.at[slot, :, pl.ds(size, size)],
                sems.at[slot, 1],
            ),
            pltpu.make_async_copy(
                down_ref.at[pl.ds(at, size)], down_buf.at[slot, pl.ds(0, size)], sems.at[slot, 2]
            ),
        ]

    def kept(k):
        here = (slice(None), pl.ds(*tiles[k]))
        return [
            pltpu.make_async_copy(gate_buf.at[here], gate_ref.at[here], out_sems.at[k, 0]),
            pltpu.make_async_copy(up_buf.at[here], up_ref.at[here], out_sems.at[k, 1]),
        ]

    def work(k, slot):
        at, size = tiles[k]
        both = product(rows_ref[...], pair_buf[slot, :, : 2 * size])
        gate, up = both[:, :size], both[:, size:]
        gate_buf[:, at : at + size] = gate.astype(BF16)
        up_buf[:, at : at + size] = up.astype(BF16)
        for copy in kept(k):
            copy.start()
        active = (gate * jax.nn.sigmoid(gate) * up).astype(BF16)
        part = product(active, down_buf[slot, :size])
        if k == 0:
            acc_ref[...] = part
        else:
            acc_ref[...] += part

    streamed(tiles, copies, work)
    rows_out(acc_ref, core_ref[0], mine_ref, other_ref)
    for k in range(len(tiles)):
        for copy in kept(k):
            copy.wait()


def ffn_backward_kernel(
    tiles, core_ref, rows_ref, gate_ref, up_ref, pair_ref, down_ref, mine_ref, other_ref,
    pair_buf, down_buf, gate_buf, up_buf, acc_ref, sems,
):
    def copies(k, slot):
        at, size = tiles[k]
        columns, place = pl.ds(at, size), pl.ds(0, size)
        return [
            pltpu.make_async_copy(
                down_ref.at[columns], down_buf.at[slot, place], sems.at[slot, 0]
            ),
            pltpu.make_async_copy(
                gate_ref.at[:, columns], gate_buf.at[slot, :, place], sems.at[slot, 1]
            ),
            pltpu.make_async_copy(
                up_ref.at[:, columns], up_buf.at[slot, :, place], sems.at[slot, 2]
            ),
            pltpu.make_async_copy(
                pair_ref.at[0, :, columns], pair_buf.at[slot, :, place], sems.at[slot, 3]
            ),
            pltpu.make_async_copy(
                pair_ref.at[1, :, columns],
                pair_buf.at[slot, :, pl.ds(size, size)],
                sems.at[slot, 4],
            ),
        ]

    def work(k, slot):
        _, size = tiles[k]
        grad_active = product_right(rows_ref[...], down_buf[slot, :size])
        grads = ffn_grads(
            grad_active,
            gate_buf[slot, :, :size].astype(F32),
            up_buf[slot, :, :size].astype(F32),
        )
        part = product_right(jnp.concatenate(grads, axis=1), pair_buf[slot, :, : 2 * size])
        if k == 0:
            acc_ref[...] = part
        else:
            acc_ref[...] += part

    streamed(tiles, copies, work)
    rows_out(acc_ref, core_ref[0], mine_ref, other_ref)


def feed_forward_call(backward, core, rows, pair, down, saved=()):
    count, width = rows.shape
    units = down.shape[0]
    tile = 768
    tiles = unit_tiles(units, tile)
    vmem, any_space = pl.BlockSpec(memory_space=pltpu.VMEM), pl.BlockSpec(memory_space=pl.ANY)
    scalar = pl.BlockSpec(memory_space=pltpu.SMEM)
    out_shape = [
        jax.ShapeDtypeStruct((count // 2, width), F32),
        jax.ShapeDtypeStruct((count // 2, width), BF16),
    ]
    out_specs = [vmem, vmem]
    buffers = [pltpu.VMEM((2, width, 2 * tile), BF16), pltpu.VMEM((2, tile, width), BF16)]
    acc = pltpu.VMEM((count, width), F32)
    if backward:
        body = functools.partial(ffn_backward_kernel, tiles)
        in_specs = [scalar, vmem, any_space, any_space, any_space, any_space]
        buffers += [pltpu.VMEM((2, count, tile), BF16)] * 2
        scratch = [*buffers, acc, pltpu.SemaphoreType.DMA((2, 5))]
    else:
        body = functools.partial(ffn_forward_kernel, tiles)
        in_specs = [scalar, vmem, any_space, any_space]
        out_shape = [jax.ShapeDtypeStruct((count, units), BF16)] * 2 + out_shape
        out_specs = [any_space, any_space, *out_specs]
        buffers += [pltpu.VMEM((count, units), BF16)] * 2
        scratch = [*buffers, acc]
        scratch += [pltpu.SemaphoreType.DMA((2, 3)), pltpu.SemaphoreType.DMA((len(tiles), 2))]
    return pl.pallas_call(
        body,
        in_specs=in_specs,
        out_specs=out_specs,
        out_shape=out_shape,
        scratch_shapes=scratch,
        compiler_params=pltpu.CompilerParams(vmem_limit_bytes=VMEM_LIMIT),
        cost_estimate=pl.CostEstimate(
            flops=6 * count * width * units,
            bytes_accessed=6 * width * units,
            transcendentals=count * units,
        ),
    )(core, rows, *saved, pair, down)


def part_forward_kernel(rows_ref, pair_ref, kept_ref):
    both = product(rows_ref[...], pair_ref[...])
    units = both.shape[1] // 2
    gate, up = both[:, :units], both[:, units:]
    sigmoid = jax.nn.sigmoid(gate)
    silu = gate * sigmoid
    kept_ref[:, :units] = (up * (sigmoid + silu * (1.0 - sigmoid))).astype(BF16)
    kept_ref[:, units : 2 * units] = silu.astype(BF16)
    kept_ref[:, 2 * units :] = (silu * up).astype(BF16)


def part_forward_call(rows, pair):
    tokens, width = rows.shape
    units = pair.shape[1] // 2
    tile = 1024
    return pl.pallas_call(
        part_forward_kernel,
        grid=(tokens // tile,),
        in_specs=[
            pl.BlockSpec((tile, width), lambda i: (i, 0)),
            pl.BlockSpec((width, 2 * units), lambda i: (0, 0)),
        ],
        out_specs=pl.BlockSpec((tile, 3 * units), lambda i: (i, 0)),
        out_shape=jax.ShapeDtypeStruct((tokens, 3 * units), BF16),
        compiler_params=pltpu.CompilerParams(vmem_limit_bytes=VMEM_LIMIT),
        cost_estimate=pl.CostEstimate(
            flops=4 * tokens * width * units,
            bytes_accessed=2 * tokens * (width + 3 * units),
            transcendentals=tokens * units,
        ),
    )(rows, pair)


def part_grads_kernel(
    here_ref, inner_ref, grad_ref, kept_ref, down_ref, mine_ref, other_ref, acc_ref
):
    step = pl.program_id(0)
    inner, grad = inner_ref[...], grad_ref[...]
    units = down_ref.shape[0]
    grad_active = product_right(grad, down_ref[...])
    grad_gate = (grad_active * kept_ref[:, :units].astype(F32)).astype(BF16)
    grad_up = (grad_active * kept_ref[:, units : 2 * units].astype(F32)).astype(BF16)
    parts = [
        product_left(inner, jnp.concatenate([grad_gate, grad_up], axis=1)),
        product_left(grad, kept_ref[:, 2 * units :]),
    ]

    @pl.when(step == 0)
    def _():
        acc_ref[:, : 2 * units] = parts[0]
        acc_ref[:, 2 * units :] = parts[1]

    @pl.when(step > 0)
    def _():
        acc_ref[:, : 2 * units] += parts[0]
        acc_ref[:, 2 * units :] += parts[1]

    @pl.when(step == pl.num_programs(0) - 1)
    def _():
        rows = mine_ref.shape[0]
        here = here_ref[0]
        mine_ref[...] = acc_ref[pl.ds(pl.multiple_of(here * rows, rows), rows)]
        rest = acc_ref[pl.ds(pl.multiple_of((1 - here) * rows, rows), rows)]
        other_ref[...] = rest.astype(BF16)


def part_grads_call(here, inner, grad, both, down):
    tokens, width = inner.shape
    units = down.shape[0]
    tile = 1024
    rows = pl.BlockSpec((tile, width), lambda i, c: (i, 0))
    out = pl.BlockSpec((width // 2, 3 * units), lambda i, c: (0, 0))
    return pl.pallas_call(
        part_grads_kernel,
        grid_spec=pltpu.PrefetchScalarGridSpec(
            num_scalar_prefetch=1,
            grid=(tokens // tile,),
            in_specs=[
                rows,
                rows,
                pl.BlockSpec((tile, 3 * units), lambda i, c: (i, 0)),
                pl.BlockSpec((units, width), lambda i, c: (0, 0)),
            ],
            out_specs=[out, out],
            scratch_shapes=[pltpu.VMEM((width, 3 * units), F32)],
        ),
        out_shape=[
            jax.ShapeDtypeStruct((width // 2, 3 * units), F32),
            jax.ShapeDtypeStruct((width // 2, 3 * units), BF16),
        ],
        compiler_params=pltpu.CompilerParams(vmem_limit_bytes=VMEM_LIMIT),
        cost_estimate=pl.CostEstimate(
            flops=8 * tokens * width * units,
            bytes_accessed=4 * tokens * width,
            transcendentals=tokens * units,
        ),
    )(here, inner, grad, both, down)


def load_all(copies):
    for copy in copies:
        copy.start()


def in_time(rows):
    half = rows.shape[0] // 4
    return jnp.concatenate([rows[k * half : (k + 1) * half] for k in (0, 2, 1, 3)], axis=0)


def rows_out(acc_ref, core, mine_ref, other_ref):
    half = mine_ref.shape[0]
    mine_ref[...] = acc_ref[pl.ds(pl.multiple_of(core * half, half), half)]
    rest = acc_ref[pl.ds(pl.multiple_of((1 - core) * half, half), half)]
    other_ref[...] = rest.astype(BF16)


def weight_copies(whole_ref, out_ref, in_buf, out_buf, sems, start):
    size = in_buf.shape[2]
    copies = [
        pltpu.make_async_copy(
            whole_ref.at[:, pl.ds(start + k * size, size)], in_buf.at[k], sems.at[k]
        )
        for k in range(in_buf.shape[0])
    ]
    return copies, pltpu.make_async_copy(out_ref, out_buf, sems.at[len(copies)])


def conv_taps(mixed, kernel, masks):
    terms = [mixed]
    for lag in range(1, len(masks) + 1):
        terms.append(pltpu.roll(mixed, lag, 0) * masks[lag - 1])
    taps = kernel.shape[0]
    total = kernel[taps - 1 : taps] * terms[0]
    for lag in range(1, taps):
        total = total + kernel[taps - 1 - lag : taps - lag] * terms[lag]
    return terms, total


def conv_forward_kernel(
    core_ref, rows_ref, kernel_ref, masks_ref, whole_ref, out_ref,
    proj_ref, gated_ref, mine_ref, other_ref, in_buf, out_buf, acc_ref, sems,
):
    copies, last = weight_copies(whole_ref, out_ref, in_buf, out_buf, sems, 0)
    load_all([*copies, last])
    rows = rows_ref[...]
    parts = []
    for k, copy in enumerate(copies):
        copy.wait()
        part = product(rows, in_buf[k])
        proj_ref[k] = part.astype(BF16)
        parts.append(in_time(part))
    masks = [masks_ref[lag] for lag in range(masks_ref.shape[0])]
    gated = []
    for at in range(0, parts[0].shape[1], 128):
        before, after, signal = [part[:, at : at + 128] for part in parts]
        _, total = conv_taps(before * signal, kernel_ref[:, at : at + 128], masks)
        gated.append((after * total).astype(BF16))
    gated = in_time(jnp.concatenate(gated, axis=1))
    gated_ref[...] = gated
    last.wait()
    acc_ref[...] = product(gated, out_buf[...])
    rows_out(acc_ref, core_ref[0], mine_ref, other_ref)


def tiles_out(tiles_ref, mix_ref, grad_mix, columns):
    count = tiles_ref.shape[0]
    width = grad_mix.shape[1] // 2
    step = width // count
    for k in range(count):
        tiles_ref[k] = columns(k)
        mix_ref[k] = jnp.concatenate(
            [grad_mix[:, h * width + k * step : h * width + (k + 1) * step] for h in range(2)],
            axis=1,
        )


def conv_backward_kernel(
    core_ref, grad_ref, kernel_ref, masks_ref, proj_ref, whole_ref, out_ref,
    tiles_ref, mix_ref, taps_ref, mine_ref, other_ref, in_buf, out_buf, acc_ref, sems,
):
    copies, last = weight_copies(whole_ref, out_ref, in_buf, out_buf, sems, 0)
    load_all([last, *copies])
    last.wait()
    grad_gated = in_time(product_right(grad_ref[...], out_buf[...]))
    parts = [in_time(proj_ref[k].astype(F32)) for k in range(3)]
    masks = [masks_ref[lag] for lag in range(masks_ref.shape[0])]
    rows = grad_gated.shape[0]
    grads = [[], [], []]
    for at in range(0, grad_gated.shape[1], 128):
        before, after, signal = [part[:, at : at + 128] for part in parts]
        kernel = kernel_ref[:, at : at + 128]
        terms, total = conv_taps(before * signal, kernel, masks)
        grad = grad_gated[:, at : at + 128]
        grad_total = grad * after
        taps = kernel.shape[0]
        grad_mixed = kernel[taps - 1 : taps] * grad_total
        for lag in range(1, taps):
            sent = pltpu.roll(grad_total * masks[lag - 1], rows - lag, 0)
            grad_mixed = grad_mixed + kernel[taps - 1 - lag : taps - lag] * sent
        for lag in range(taps):
            taps_ref[taps - 1 - lag : taps - lag, at : at + 128] = jnp.sum(
                grad_total * terms[lag], axis=0, keepdims=True
            )
        for k, value in enumerate((grad_mixed * signal, grad * total, grad_mixed * before)):
            grads[k].append(value.astype(BF16))
    grads = [in_time(jnp.concatenate(g, axis=1)) for g in grads]
    step = grads[0].shape[1] // tiles_ref.shape[0]
    tiles_out(
        tiles_ref,
        mix_ref,
        grad_ref[...],
        lambda k: jnp.concatenate([g[:, k * step : (k + 1) * step] for g in grads], axis=1),
    )
    for k, copy in enumerate(copies):
        copy.wait()
        part = product_right(grads[k], in_buf[k])
        acc_ref[...] = part if k == 0 else acc_ref[...] + part
    rows_out(acc_ref, core_ref[0], mine_ref, other_ref)


def head_kind(head):
    return min(max(head % (GROUP + 2) - GROUP + 1, 0), 2)


def lane_facts(rows):
    lane = lax.broadcasted_iota(jnp.int32, (rows, 128), 1)
    return lane < HEAD_DIM, lax.rem(lane, HEAD_DIM) < HEAD_DIM // 2


def head_scales(block, low):
    squares = block * block
    first = jnp.sum(jnp.where(low, squares, 0.0), axis=1, keepdims=True)
    second = jnp.sum(jnp.where(low, 0.0, squares), axis=1, keepdims=True)
    return lax.rsqrt(jnp.where(low, first, second) * (1.0 / HEAD_DIM) + EPSILON)


def block_gains(gains_ref, at):
    heads = [head_kind(2 * at), head_kind(2 * at + 1)]
    return heads, gains_ref[3 * heads[0] + heads[1] : 3 * heads[0] + heads[1] + 1]


def attention_forward_kernel(
    core_ref, rows_ref, gains_ref, tables_ref, mask_ref, whole_ref, out_ref,
    qkv_ref, ready_ref, gated_ref, mine_ref, other_ref, in_buf, out_buf, acc_ref, sems,
):
    copies, last = weight_copies(
        whole_ref, out_ref, in_buf, out_buf, sems, whole_ref.shape[1] - in_buf.shape[2]
    )
    load_all([*copies, last])
    copies[0].wait()
    qkv_ref[...] = product(rows_ref[...], in_buf[0])
    rows, width = qkv_ref.shape
    low, front = lane_facts(rows)
    cosine, sine = tables_ref[0], tables_ref[1]
    for at in range(width // 128):
        block = qkv_ref[:, at * 128 : (at + 1) * 128]
        heads, gains = block_gains(gains_ref, at)
        normed = block * head_scales(block, low) * gains
        turned = jnp.where(front, -pltpu.roll(normed, 96, 1), pltpu.roll(normed, 32, 1))
        ready = normed * cosine + turned * sine
        if heads[0] == 2:
            ready = jnp.where(low, block, ready)
        if heads[1] == 2:
            ready = jnp.where(low, ready, block)
        ready_ref[:, at * 128 : (at + 1) * 128] = ready.astype(BF16)
    half = rows // 4
    span = (GROUP + 2) * HEAD_DIM
    for m in range(2):
        mask = mask_ref[m] > 0
        mask = jnp.concatenate([mask] * GROUP, axis=0)
        for g in range(width // span):
            queries, keys, values = head_rows(ready_ref, m, half, g * span)
            weights = softmax_weights(queries, keys, mask)
            attended = product(weights.astype(BF16), values).astype(BF16)
            for j in range(GROUP):
                at = (g * GROUP + j) * HEAD_DIM
                head = attended[j * 2 * half : (j + 1) * 2 * half]
                gated_ref[m * half : (m + 1) * half, at : at + HEAD_DIM] = head[:half]
                gated_ref[(m + 2) * half : (m + 3) * half, at : at + HEAD_DIM] = head[half:]
    last.wait()
    acc_ref[...] = product(gated_ref[...], out_buf[...])
    rows_out(acc_ref, core_ref[0], mine_ref, other_ref)


def sequence(ref, m, half, at):
    columns = slice(at, at + HEAD_DIM)
    return jnp.concatenate(
        [ref[m * half : (m + 1) * half, columns], ref[(m + 2) * half : (m + 3) * half, columns]],
        axis=0,
    )


def head_rows(ref, m, half, at):
    heads = [sequence(ref, m, half, at + j * HEAD_DIM) for j in range(GROUP + 2)]
    return jnp.concatenate(heads[:GROUP], axis=0), heads[GROUP], heads[GROUP + 1]


def softmax_weights(queries, keys, mask):
    scores = jnp.where(mask, product_right(queries, keys) * HEAD_DIM ** (-0.5), MASKED_SCORE)
    terms = jnp.exp(scores - jnp.max(scores, axis=1, keepdims=True))
    return terms / jnp.sum(terms, axis=1, keepdims=True)


def attention_backward_kernel(
    core_ref, grad_ref, gains_ref, tables_ref, mask_ref, qkv_ref, ready_ref, whole_ref, out_ref,
    tiles_ref, mix_ref, heads_ref, mine_ref, other_ref,
    in_buf, out_buf, acc_ref, attended_ref, ready_grad_ref, proj_ref, sems,
):
    copies, last = weight_copies(
        whole_ref, out_ref, in_buf, out_buf, sems, whole_ref.shape[1] - in_buf.shape[2]
    )
    load_all([last, *copies])
    last.wait()
    attended_ref[...] = product_right(grad_ref[...], out_buf[...]).astype(BF16)
    rows, width = qkv_ref.shape
    half = rows // 4
    span = (GROUP + 2) * HEAD_DIM
    scale = HEAD_DIM ** (-0.5)
    for m in range(2):
        mask = mask_ref[m] > 0
        mask = jnp.concatenate([mask] * GROUP, axis=0)
        for g in range(width // span):
            queries, keys, values = head_rows(ready_ref, m, half, g * span)
            weights = softmax_weights(queries, keys, mask)
            grad = jnp.concatenate(
                [
                    sequence(attended_ref, m, half, (g * GROUP + j) * HEAD_DIM)
                    for j in range(GROUP)
                ],
                axis=0,
            )
            grad_values = product_left(weights.astype(BF16), grad)
            grad_weights = product_right(grad, values)
            mean = jnp.sum(grad_weights * weights, axis=1, keepdims=True)
            grad_scores = (weights * (grad_weights - mean)).astype(BF16)
            grad_queries = product(grad_scores, keys) * scale
            grad_keys = product_left(grad_scores, queries) * scale
            outs = [grad_queries[j * 2 * half : (j + 1) * 2 * half] for j in range(GROUP)]
            for j, out in enumerate([*outs, grad_keys, grad_values]):
                at = g * span + j * HEAD_DIM
                ready_grad_ref[m * half : (m + 1) * half, at : at + HEAD_DIM] = out[:half]
                ready_grad_ref[(m + 2) * half : (m + 3) * half, at : at + HEAD_DIM] = out[half:]
    low, front = lane_facts(rows)
    cosine, sine = tables_ref[0], tables_ref[1]
    for at in range(width // 128):
        lanes = slice(at * 128, (at + 1) * 128)
        block, grad = qkv_ref[:, lanes], ready_grad_ref[:, lanes]
        heads, gains = block_gains(gains_ref, at)
        inverse = head_scales(block, low)
        normed = block * inverse
        turned = grad * sine
        grad_normed = grad * cosine + jnp.where(
            front, pltpu.roll(turned, 96, 1), -pltpu.roll(turned, 32, 1)
        )
        heads_ref[at : at + 1] = jnp.sum(grad_normed * normed, axis=0, keepdims=True)
        grad_normed = grad_normed * gains
        along = grad_normed * normed
        first = jnp.sum(jnp.where(low, along, 0.0), axis=1, keepdims=True)
        second = jnp.sum(jnp.where(low, 0.0, along), axis=1, keepdims=True)
        mean = jnp.where(low, first, second) * (1.0 / HEAD_DIM)
        raw = inverse * (grad_normed - normed * mean)
        if heads[0] == 2:
            raw = jnp.where(low, grad, raw)
        if heads[1] == 2:
            raw = jnp.where(low, raw, grad)
        proj_ref[:, lanes] = raw.astype(BF16)
    step = width // tiles_ref.shape[0]
    spare = jnp.zeros((rows, tiles_ref.shape[2] - step), BF16)
    tiles_out(
        tiles_ref,
        mix_ref,
        grad_ref[...],
        lambda k: jnp.concatenate([proj_ref[:, k * step : (k + 1) * step], spare], axis=1),
    )
    copies[0].wait()
    acc_ref[...] = product_right(proj_ref[...], in_buf[0])
    rows_out(acc_ref, core_ref[0], mine_ref, other_ref)


def mixer_call(kernel, core, operands, whole, weight_out, in_tiles, outs, scratch=(), flops=0):
    vmem, any_space = pl.BlockSpec(memory_space=pltpu.VMEM), pl.BlockSpec(memory_space=pl.ANY)
    rows, width = operands[0].shape
    channels = weight_out.shape[0]
    outs = [*outs, ((rows // 2, width), F32), ((rows // 2, width), BF16)]
    return pl.pallas_call(
        kernel,
        in_specs=[
            pl.BlockSpec(memory_space=pltpu.SMEM),
            *[vmem] * len(operands),
            any_space,
            any_space,
        ],
        out_specs=[vmem] * len(outs),
        out_shape=[jax.ShapeDtypeStruct(*out) for out in outs],
        scratch_shapes=[
            pltpu.VMEM((in_tiles[0], width, in_tiles[1]), BF16),
            pltpu.VMEM((channels, width), BF16),
            pltpu.VMEM((rows, width), F32),
            *scratch,
            pltpu.SemaphoreType.DMA((in_tiles[0] + 1,)),
        ],
        compiler_params=pltpu.CompilerParams(vmem_limit_bytes=VMEM_LIMIT),
        cost_estimate=pl.CostEstimate(
            flops=2 * rows * width * (channels + in_tiles[0] * in_tiles[1]),
            bytes_accessed=2 * width * (channels + in_tiles[0] * in_tiles[1]),
            transcendentals=rows * width,
        ),
    )(core, *operands, whole, weight_out)


def conv_forward_call(core, rows, kernel, masks, whole, weight_out):
    count, channels = rows.shape[0], kernel.shape[1]
    outs = [((3, count, channels), BF16), ((count, channels), BF16)]
    operands = (rows, kernel, masks)
    return mixer_call(
        conv_forward_kernel, core, operands, whole, weight_out, (3, channels), outs
    )


def conv_backward_call(core, grad, kernel, masks, projected, whole, weight_out):
    count, width = grad.shape
    taps, channels = kernel.shape
    outs = [
        ((4, count, 3 * channels // 4), BF16),
        ((4, count, width // 4), BF16),
        ((taps, channels), F32),
    ]
    operands = (grad, kernel, masks, projected)
    return mixer_call(
        conv_backward_kernel, core, operands, whole, weight_out, (3, channels), outs
    )


def attention_forward_call(core, rows, gains, tables, mask, whole, weight_out, qkv_width):
    count, channels = rows.shape[0], weight_out.shape[0]
    outs = [((count, qkv_width), F32), ((count, qkv_width), BF16), ((count, channels), BF16)]
    operands = (rows, gains, tables, mask)
    return mixer_call(
        attention_forward_kernel, core, operands, whole, weight_out, (1, qkv_width), outs
    )


def attention_backward_call(core, grad, gains, tables, mask, qkv, ready, whole, weight_out):
    count, width = grad.shape
    channels, qkv_width = weight_out.shape[0], qkv.shape[1]
    outs = [
        ((4, count, 3 * channels // 4), BF16),
        ((4, count, width // 4), BF16),
        ((qkv_width // 128, 128), F32),
    ]
    scratch = [
        pltpu.VMEM((count, channels), BF16),
        pltpu.VMEM((count, qkv_width), F32),
        pltpu.VMEM((count, qkv_width), BF16),
    ]
    operands = (grad, gains, tables, mask, qkv, ready)
    return mixer_call(
        attention_backward_kernel, core, operands, whole, weight_out, (1, qkv_width), outs, scratch
    )


def conv_masks(segments, taps):
    masks = []
    for lag in range(1, taps):
        same = (segments[:, lag:] == segments[:, :-lag]).astype(F32)
        same = jnp.pad(same, ((0, 0), (lag, 0))).reshape(-1, 1)
        masks.append(jnp.broadcast_to(same, (same.shape[0], 128)))
    return jnp.stack(masks)


def score_mask(segments):
    position = jnp.arange(segments.shape[1])
    allowed = position[:, None] >= position[None, :]
    return (allowed & (segments[:, :, None] == segments[:, None, :])).astype(F32)


def turn_tables(length):
    half = HEAD_DIM // 2
    exponent = jnp.arange(half, dtype=F32) * (2.0 / HEAD_DIM)
    frequency = jnp.exp(-exponent * jnp.log(ROPE_BASE))
    angles = jnp.arange(length, dtype=F32)[:, None] * frequency[None, :]
    tables = jnp.tile(jnp.stack([jnp.cos(angles), jnp.sin(angles)]), (1, 1, 4))
    tables = tables.reshape(2, 2, 1, length // 2, 128)
    return jnp.broadcast_to(tables, (2, 2, 2, length // 2, 128)).reshape(2, 2 * length, 128)


def gain_rows(head_gains):
    kinds = [head_gains[0], head_gains[1], jnp.ones_like(head_gains[0])]
    rows = [jnp.concatenate([a, b]) for a in kinds for b in kinds]
    return jnp.stack(rows)


def head_gain_sums(sums):
    heads = sums.reshape(-1, GROUP + 2, HEAD_DIM)
    return jnp.stack([heads[:, :GROUP].sum((0, 1)), heads[:, GROUP].sum(0)])


def local(
    inputs,
    out_cotangent,
    segments,
    norm_gains,
    conv_kernel,
    qk_gains,
    conv_in,
    attn_qkv,
    mixer_out,
    gate_up,
    down,
):
    section = lax.axis_index("xh")
    first = section == 0
    core = lax.axis_index("c")
    place = lax.axis_index("y") * 4 + lax.axis_index("z")
    xl = lax.axis_index("xl")
    plane = lax.axis_size("y") * lax.axis_size("z")

    shape = inputs.shape[1:]
    width = shape[-1]
    inputs, out_cotangent = inputs.reshape(-1, width), out_cotangent.reshape(-1, width)
    segments = segments[0]
    half = inputs.shape[0]
    rows = 2 * half
    channels = conv_in.shape[2]
    kernel = lax.dynamic_slice_in_dim(conv_kernel, core * channels, channels, 1).astype(F32)
    gains = lax.dynamic_index_in_dim(norm_gains, section, 0, keepdims=False).astype(F32)
    weight_out, weight_pair, weight_down = mixer_out[0], gate_up[0], down[0]
    hidden_units = weight_down.shape[0]
    part = hidden_units // plane
    in_width = 3 * channels
    qkv_width = attn_qkv.shape[1]
    core_scalar = core.astype(jnp.int32)[None]
    xl_scalar = xl.astype(jnp.int32)[None]

    def chosen(from_first, from_second):
        return jnp.where(first, from_first, from_second)

    def gathered(own, axes):
        return lax.all_gather(own, axes, tiled=True)

    both = jnp.concatenate([conv_in.reshape(-1, in_width), attn_qkv], axis=1)
    whole = gathered(both, ("xh", "xl", "y", "z"))

    lanes = -(-part // 256) * 256
    fill = lanes - part
    part_pair = jnp.concatenate(
        [
            jnp.pad(lax.dynamic_slice_in_dim(w, place * part, part, 1), ((0, 0), (0, fill)))
            for w in (weight_pair[0], weight_pair[1])
        ],
        axis=1,
    )
    part_down = lax.dynamic_slice_in_dim(weight_down, place * part, part, 0)
    part_down = jnp.pad(part_down, ((0, fill), (0, 0)))
    masks = conv_masks(segments, kernel.shape[0])
    mask = score_mask(segments)
    tables = turn_tables(segments.shape[1])
    head_gains = gain_rows(qk_gains.astype(F32))
    first_in = inputs.astype(F32)
    normed_own_0 = (normalize(first_in) * gains[0]).astype(BF16)
    normed_0 = spread(normed_own_0)
    cotangent_1 = spread(out_cotangent)
    whole, part_pair, part_down, masks, mask, tables, head_gains, normed_0, cotangent_1 = (
        lax.optimization_barrier(
            (whole, part_pair, part_down, masks, mask, tables, head_gains, normed_0, cotangent_1)
        )
    )

    def feed_forward(hidden):
        inner_own = (normalize(hidden) * gains[1]).astype(BF16)
        gate, up, mine, other = feed_forward_call(
            False, core_scalar, spread(inner_own), weight_pair, weight_down
        )
        return hidden + joined(mine, other), (inner_own, gate, up)

    def feed_forward_back(grad_full, grad, hidden, saved):
        mine, other = feed_forward_call(
            True, core_scalar, grad_full, weight_pair, weight_down, saved[1:]
        )
        back, grad_gain = norm_backward(joined(mine, other), gains[1], hidden)
        return grad + back, grad_gain

    def mixer_back(grad_hidden, mine, other, layer_in):
        back, grad_gain = norm_backward(joined(mine, other), gains[0], layer_in)
        return (grad_hidden + back).astype(BF16), grad_gain

    projected, gated_0, mine, other = conv_forward_call(
        core_scalar, normed_0, kernel, masks, whole, weight_out
    )
    hidden_0 = first_in + joined(mine, other)
    result_0, ffn_0 = feed_forward(hidden_0)
    result_0 = result_0.astype(BF16)

    second_in = lax.ppermute(result_0, "xh", [(0, 1)]).astype(F32)
    normed_own_1 = (normalize(second_in) * gains[0]).astype(BF16)
    normed_y = gathered(chosen(normed_own_0, normed_own_1), ("y", "c"))
    qkv, ready, gated_1, mine, other = attention_forward_call(
        core_scalar, spread(normed_own_1), head_gains, tables, mask, whole, weight_out, qkv_width
    )
    hidden_1 = second_in + joined(mine, other)
    result_1, ffn_1 = feed_forward(hidden_1)
    result_1 = result_1.astype(BF16)

    inner_all = gathered(chosen(ffn_0[0], ffn_1[0]), ("y", "z", "c"))
    part_kept = part_forward_call(inner_all, part_pair)

    grad_hidden_1, gain_inner_1 = feed_forward_back(
        cotangent_1, out_cotangent.astype(F32), hidden_1, ffn_1
    )
    proj_tiles_1, mix_tiles_1, head_sums, mine, other = attention_backward_call(
        core_scalar,
        spread(grad_hidden_1.astype(BF16)),
        head_gains,
        tables,
        mask,
        qkv,
        ready,
        whole,
        weight_out,
    )
    input_grad_1, gain_outer_1 = mixer_back(grad_hidden_1, mine, other, second_in)

    cotangent = lax.ppermute(input_grad_1, "xh", [(1, 0)])
    cotangent, part_kept = lax.optimization_barrier((cotangent, part_kept))
    grad_all = gathered(chosen(cotangent, out_cotangent), ("y", "z", "c"))
    grad_hidden_0, gain_inner_0 = feed_forward_back(
        spread(cotangent), cotangent.astype(F32), hidden_0, ffn_0
    )
    gated, grad_hidden_0 = lax.optimization_barrier((chosen(gated_0, gated_1), grad_hidden_0))
    gated_y = gathered(gated, "y")
    proj_tiles_0, mix_tiles_0, grad_kernel, mine, other = conv_backward_call(
        core_scalar, spread(grad_hidden_0.astype(BF16)), kernel, masks, projected, whole, weight_out
    )
    input_grad_0, gain_outer_0 = mixer_back(grad_hidden_0, mine, other, first_in)

    columns = exchanged(chosen(proj_tiles_0, proj_tiles_1), "y")
    columns = columns.reshape(4 * rows, -1)
    in_parts = product_left(normed_y, columns).reshape(2, 2, plane, -1, in_width // 4)
    mine = lax.dynamic_index_in_dim(in_parts, xl, 1, keepdims=False)
    other = lax.dynamic_index_in_dim(in_parts, 1 - xl, 1, keepdims=False)
    mine = (mine + swapped(other.astype(BF16), "xl").astype(F32)).astype(BF16)
    arrived = exchanged(jnp.moveaxis(mine, 1, 0), PLANE)
    lines = arrived.reshape(4, 4, *arrived.shape[1:]).astype(F32).sum(1)
    kept_lines = lax.dynamic_index_in_dim(lines, section, 1, keepdims=False)
    sent_lines = lax.dynamic_index_in_dim(lines, 1 - section, 1, keepdims=False)
    come = swapped(sent_lines.astype(BF16), "xh").astype(F32)
    lines = chosen(kept_lines, come).reshape(4, -1, 3, channels // 4)
    grad_conv_in = jnp.moveaxis(lines, 0, 2).reshape(conv_in.shape)
    lines = chosen(come, kept_lines)[:, :, : qkv_width // 4]
    grad_attn_qkv = jnp.moveaxis(lines, 0, 1).reshape(attn_qkv.shape)

    columns = exchanged(chosen(mix_tiles_0, mix_tiles_1), "y").reshape(4 * rows, -1)
    out_parts = product_left(columns, gated_y).astype(BF16).reshape(8, -1, channels)
    grad_mixer_out = exchanged(out_parts, ("xl", "z")).astype(F32).sum(0).T[None]

    mine, other = part_grads_call(xl_scalar, inner_all, grad_all, part_kept, part_down)
    mine = (mine + swapped(other, "xl").astype(F32)).astype(BF16)
    arrived = exchanged(mine.reshape(plane, -1, 3 * lanes), PLANE)
    lines = [
        jnp.moveaxis(arrived[:, :, k * lanes : k * lanes + part], 0, 1)
        .reshape(-1, hidden_units)
        .astype(F32)
        for k in range(3)
    ]
    grad_gate_up = jnp.stack(lines[:2])[None]
    grad_down = lines[2].T[None]

    full_kernel = lax.dynamic_update_slice(
        jnp.zeros(conv_kernel.shape, F32), grad_kernel, (0, core * channels)
    )
    small = jnp.concatenate(
        [
            chosen(gain_outer_0, gain_outer_1),
            chosen(gain_inner_0, gain_inner_1),
            full_kernel.reshape(-1),
            head_gain_sums(head_sums).reshape(-1),
        ]
    )
    count = small.shape[0]
    small = jnp.pad(small, (0, -count % 1024)).reshape(-1, 128)
    small = lax.all_gather(small, "c").sum(0)
    small = small + swapped(small, "xl")
    for axis in PLANE:
        copies = jnp.broadcast_to(small, (4, *small.shape))
        small = lax.all_to_all(copies, axis, 0, 0, tiled=True).sum(0)
    come = swapped(small, "xh")
    pair = [chosen(small, come).reshape(-1), chosen(come, small).reshape(-1)]
    grad_norm_gains = jnp.stack([a[: 2 * width].reshape(2, width) for a in pair])
    grad_conv_kernel = pair[0][2 * width : 5 * width].reshape(conv_kernel.shape)
    grad_qk_gains = pair[1][5 * width : count].reshape(qk_gains.shape)

    activations = chosen(result_0, result_1).reshape(1, 1, *shape)
    input_grads = chosen(input_grad_0, input_grad_1).reshape(1, 1, *shape)
    return (
        activations,
        input_grads,
        grad_norm_gains,
        grad_conv_kernel,
        grad_qk_gains,
        grad_conv_in,
        grad_attn_qkv,
        grad_mixer_out,
        grad_gate_up,
        grad_down,
    )


def solution(mesh):
    wide = Mesh(mesh.devices.reshape(2, 2, 4, 4, 2), AXES)
    dp = ("xl", "y", "z")
    everyone = ("xh", "xl", "y", "z")
    in_specs = (
        P(dp, None, "c", None),
        P(dp, None, "c", None),
        P(dp, None, None),
        P(),
        P(),
        P(),
        P(everyone, None, "c"),
        P(everyone, "c"),
        P("xh", "c", None),
        P("xh", None, None, "c"),
        P("xh", "c", None),
    )
    out_specs = (
        P("xh", dp, None, "c", None),
        P("xh", dp, None, "c", None),
        P(),
        P(),
        P(),
        P(everyone, None, "c"),
        P(everyone, "c"),
        P("xh", "c", dp),
        P("xh", None, dp, "c"),
        P("xh", "c", dp),
    )
    return jax.shard_map(local, mesh=wide, in_specs=in_specs, out_specs=out_specs, check_vma=False)
```

profile of v0, /device:TPU:0, one launch (start us, length us, event | category | flops | bytes accessed | tf_op | source)
XLA Modules:
  0.0 454.4 jit_solution(14683080512197941793)
XLA Ops:
  21.9 8.2 %fusion.44 = (bf16[1,1,1536,3456]{3,2,1,0:T(8,128)(2,1)S(1)}, bf16[1,1,1536,3456]{3,2,1,0:T(8,128)(2,1)S(1)}) fusion(bf16[1,2,1536,3456]{3,2,1,0:T(8,128)(2,1)} %param.20), kind=kLoop, calls=%fused_computation.137 | loop fusion | bytes 42467328 | tf_op jit(solution)/shard_map/slice | solution.py:790
  32.3 67.9 %all-gather.6.cloned.1.call-done.whole_ref = bf16[1536,3584]{1,0:T(8,128)(2,1)} async-done(((bf16[24,3584]{1,0:T(8,128)(2,1)}), bf16[1536,3584]{1,0:T(8,128)(2,1)}) %all-gather.6.cloned.1.call-update) | async-done | bytes 11010064 | tf_op jit(solution)/shard_map/all_gather | solution.py:780
  100.9 8.1 %shard_map.186 = (bf16[3,256,768]{2,1,0:T(8,128)(2,1)}, bf16[256,768]{1,0:T(8,128)(2,1)}, f32[128,1536]{1,0:T(8,128)}, bf16[128,1536]{1,0:T(8,128)(2,1)}) custom-call(s32[1]{0:T(128)} %bitcast.1.core_ref, bf16[256,1536]{1,0:T(8,128)(2,1)} %all_gather.43.rows_ref, f32[3,768]{1,0:T(4,128)} %dynamic-slice_convert_fusion.2.kernel_ref, ...), custom_call_target="tpu_custom_call" | custom-call | flops 2415919104 | bytes 9437184 | tf_op jit(solution)/shard_map/pallas_call | solution.py:626
  115.2 16.0 %shard_map.187 = (bf16[256,3456]{1,0:T(8,128)(2,1)}, bf16[256,3456]{1,0:T(8,128)(2,1)}, f32[128,1536]{1,0:T(8,128)}, bf16[128,1536]{1,0:T(8,128)(2,1)}) custom-call(s32[1]{0:T(128)} %bitcast.1.core_ref, bf16[256,1536]{1,0:T(8,128)(2,1)} %all_gather.45.rows_ref, bf16[2,1536,3456]{2,1,0:T(8,128)(2,1)} %bitcast.136, bf16[3456,1536]{1,0:T(8,128)(2,1)} %bitcast.140), custom_call_target="tpu_custom_call" | custom-call | flops 8153726976 | bytes 31850496 | tf_op jit(solution)/shard_map/pallas_call | solution.py:227
  134.5 4.9 %collective-permute-start.2 = (bf16[128,1536]{1,0:T(8,128)(2,1)S(1)}, bf16[128,1536]{1,0:T(8,128)(2,1)S(1)}, u32[]{:S(2)}, u32[]{:S(2)}) collective-permute-start(bf16[128,1536]{1,0:T(8,128)(2,1)S(1)} %add_convert_fusion.2), channel_id=1, source_target_pairs={{0,64},{1,65},{2,66},{3,67},{4,68},{5,69},{6,70},{7,71},{8,72},{9,... | collective-permute-start | bytes 1179656 | tf_op jit(solution)/shard_map/ppermute | solution.py:835
  139.4 8.6 %collective-permute-done.2 = bf16[128,1536]{1,0:T(8,128)(2,1)S(1)} collective-permute-done((bf16[128,1536]{1,0:T(8,128)(2,1)S(1)}, bf16[128,1536]{1,0:T(8,128)(2,1)S(1)}, u32[]{:S(2)}, u32[]{:S(2)}) %collective-permute-start.2) | collective-permute-done | bytes 393248 | tf_op jit(solution)/shard_map/ppermute | solution.py:835
  151.9 10.3 %shard_map.188 = (f32[256,1280]{1,0:T(8,128)}, bf16[256,1280]{1,0:T(8,128)(2,1)}, bf16[256,768]{1,0:T(8,128)(2,1)}, f32[128,1536]{1,0:T(8,128)}, bf16[128,1536]{1,0:T(8,128)(2,1)}) custom-call(s32[1]{0:T(128)} %bitcast.1.core_ref, bf16[256,1536]{1,0:T(8,128)(2,1)} %all_gather.46.rows_ref, f32[9,128]{1,0:T(8,128)} %stack.67.gains_ref, ...), custom_call_target="tpu_custom_call" | custom-call | flops 1610612736 | bytes 6291456 | tf_op jit(solution)/shard_map/pallas_call | solution.py:626
  170.2 16.5 %shard_map.189 = (bf16[256,3456]{1,0:T(8,128)(2,1)}, bf16[256,3456]{1,0:T(8,128)(2,1)}, f32[128,1536]{1,0:T(8,128)}, bf16[128,1536]{1,0:T(8,128)(2,1)}) custom-call(s32[1]{0:T(128)} %bitcast.1.core_ref, bf16[256,1536]{1,0:T(8,128)(2,1)} %all_gather.47.rows_ref, bf16[2,1536,3456]{2,1,0:T(8,128)(2,1)} %bitcast.137, bf16[3456,1536]{1,0:T(8,128)(2,1)} %bitcast.141), custom_call_target="tpu_custom_call" | custom-call | flops 8153726976 | bytes 31850496 | tf_op jit(solution)/shard_map/pallas_call | solution.py:227
  186.7 26.5 %shard_map.190 = (f32[128,1536]{1,0:T(8,128)}, bf16[128,1536]{1,0:T(8,128)(2,1)}) custom-call(s32[1]{0:T(128)} %bitcast.1.core_ref, bf16[256,1536]{1,0:T(8,128)(2,1)} %all_gather.44.rows_ref, bf16[256,3456]{1,0:T(8,128)(2,1)} %get-tuple-element.73.gate_ref, bf16[256,3456]{1,0:T(8,128)(2,1)} %get-tuple-element.74.up_ref, bf16[2,1536,3456]{2,1,0:T(8,128)(2,1)} %bitcast.138, ...), custom_call_target="tpu_custom_call" | custom-call | flops 8153726976 | bytes 31850496 | tf_op jit(solution)/shard_map/pallas_call | solution.py:227
  220.6 14.9 %shard_map.191 = (bf16[4,256,576]{2,1,0:T(8,128)(2,1)}, bf16[4,256,384]{2,1,0:T(8,128)(2,1)}, f32[10,128]{1,0:T(8,128)}, f32[128,1536]{1,0:T(8,128)}, bf16[128,1536]{1,0:T(8,128)(2,1)}) custom-call(s32[1]{0:T(128)} %bitcast.1.core_ref, bf16[256,1536]{1,0:T(8,128)(2,1)} %all_gather.48.grad_ref, f32[9,128]{1,0:T(8,128)} %stack.67.gains_ref, ...), custom_call_target="tpu_custom_call" | custom-call | flops 1610612736 | bytes 6291456 | tf_op jit(solution)/shard_map/pallas_call | solution.py:626
  242.0 11.9 %shard_map.192.kept_ref = bf16[4096,768]{1,0:T(8,128)(2,1)} custom-call(bf16[4096,1536]{1,0:T(8,128)(2,1)} %all-gather.8.cloned.1.call-done.rows_ref.inner_ref, bf16[1536,512]{1,0:T(8,128)(2,1)} %fusion.3.pair_ref), custom_call_target="tpu_custom_call" | custom-call | flops 6442450944 | bytes 18874368 | tf_op jit(solution)/shard_map/pallas_call | solution.py:257
  259.2 16.6 %shard_map.193 = (f32[128,1536]{1,0:T(8,128)}, bf16[128,1536]{1,0:T(8,128)(2,1)}) custom-call(s32[1]{0:T(128)} %bitcast.1.core_ref, bf16[256,1536]{1,0:T(8,128)(2,1)} %all_gather.50.rows_ref, bf16[256,3456]{1,0:T(8,128)(2,1)} %get-tuple-element.83.gate_ref, bf16[256,3456]{1,0:T(8,128)(2,1)} %get-tuple-element.84.up_ref, bf16[2,1536,3456]{2,1,0:T(8,128)(2,1)} %bitcast.139, ...), custom_call_target="tpu_custom_call" | custom-call | flops 8153726976 | bytes 31850496 | tf_op jit(solution)/shard_map/pallas_call | solution.py:227
  282.1 2.9 all_gather.51.grad_ref
  285.0 9.2 %shard_map.194 = (bf16[4,256,576]{2,1,0:T(8,128)(2,1)}, bf16[4,256,384]{2,1,0:T(8,128)(2,1)}, f32[3,768]{1,0:T(4,128)}, f32[128,1536]{1,0:T(8,128)}, bf16[128,1536]{1,0:T(8,128)(2,1)}) custom-call(s32[1]{0:T(128)} %bitcast.1.core_ref, bf16[256,1536]{1,0:T(8,128)(2,1)} %all_gather.51.grad_ref, f32[3,768]{1,0:T(4,128)} %dynamic-slice_convert_fusion.2.kernel_ref, ...), custom_call_target="tpu_custom_call" | custom-call | flops 2415919104 | bytes 9437184 | tf_op jit(solution)/shard_map/pallas_call | solution.py:626
  300.8 3.5 collective-permute-done.10
  304.9 4.1 all-to-all-start
  316.4 4.3 all-to-all-start.2
  322.7 4.8 %copy.79 = bf16[1536,1024]{1,0:T(8,128)(2,1)} copy(bf16[1536,1024]{0,1:T(8,128)(2,1)} %bitcast.149) | data formatting | bytes 6291456 | tf_op jit(solution)/shard_map/dot_general | solution.py:32
  328.6 8.0 %all-to-all-done.2 = bf16[4,256,576]{1,2,0:T(8,128)(2,1)} async-done(((bf16[4,256,576]{1,2,0:T(8,128)(2,1)}), bf16[4,256,576]{1,2,0:T(8,128)(2,1)}, u32[]{:S(2)}, u32[]{:S(2)}) %all-to-all-start.2) | async-done | bytes 1179680 | tf_op jit(solution)/shard_map/all_to_all | solution.py:72
  336.6 3.5 all-to-all-start.4
  344.0 5.0 %fusion.8 = f32[2,2,16,24,576]{4,3,2,1,0:T(8,128)S(1)} fusion(bf16[2,2,16,24,1024]{4,3,2,1,0:T(8,128)(2,1)} %bitcast.150, bf16[1024,576,1,1,1]{0,1,2,3,4:T(8,128)(2,1)} %reshape.313), kind=kOutput, calls=%fused_computation.19 | convolution fusion | flops 1811939328 | bytes 7864320 | tf_op jit(solution)/shard_map/dot_general | solution.py:32
  352.7 29.2 %shard_map.195 = (f32[768,768]{1,0:T(8,128)}, bf16[768,768]{1,0:T(8,128)(2,1)}) custom-call(s32[1]{0:T(128)} %bitcast.43.here_ref, bf16[4096,1536]{1,0:T(8,128)(2,1)} %all-gather.8.cloned.1.call-done.rows_ref.inner_ref, bf16[4096,1536]{1,0:T(8,128)(2,1)} %all-gather.14.cloned.1.call-done.grad_ref, bf16[4096,768]{1,0:T(8,128)(2,1)} %shard_map.192.kept_ref, ...), custom_call_target="tpu_custom_call" | custom-call | flops 12884901888 | bytes 25165824 | tf_op jit(solution)/shard_map/pallas_call | solution.py:314
  383.0 4.4 all-to-all-start.1
  393.4 5.5 %all-to-all-start.3 = ((bf16[16,2,24,576]{3,2,1,0:T(8,128)(2,1)}), bf16[16,2,24,576]{3,2,1,0:T(8,128)(2,1)S(1)}, u32[]{:S(2)}, u32[]{:S(2)}) async-start(bf16[16,2,24,576]{3,2,1,0:T(8,128)(2,1)} %copy.82), calls=%async_computation.3 | async-start | bytes 1966080 | tf_op jit(solution)/shard_map/all_to_all | solution.py:72
  401.4 3.0 collective-permute-start.11
  404.4 3.0 convolution_convert_fusion
  407.4 5.5 %all-to-all-done.3 = bf16[16,2,24,576]{3,2,1,0:T(8,128)(2,1)S(1)} async-done(((bf16[16,2,24,576]{3,2,1,0:T(8,128)(2,1)}), bf16[16,2,24,576]{3,2,1,0:T(8,128)(2,1)S(1)}, u32[]{:S(2)}, u32[]{:S(2)}) %all-to-all-start.3) | async-done | bytes 884768 | tf_op jit(solution)/shard_map/all_to_all | solution.py:72
  412.9 3.5 all-to-all-start.5
  416.5 3.2 add_convert_fusion
  419.7 5.1 %all-to-all-done.5 = bf16[8,48,768]{2,1,0:T(8,128)(2,1)S(1)} async-done(((bf16[8,48,768]{2,1,0:T(8,128)(2,1)}), bf16[8,48,768]{2,1,0:T(8,128)(2,1)S(1)}, u32[]{:S(2)}, u32[]{:S(2)}) %all-to-all-start.5) | async-done | bytes 589856 | tf_op jit(solution)/shard_map/all_to_all | solution.py:72
  424.9 3.8 all-to-all-start.6
  430.9 3.0 collective-permute-start.13
  (233 shorter events, 114.8 us)
Async XLA Ops:
  7.2 93.0 %all-gather.6.cloned.1.call-start = ((), (), s32[]{:S(2)}) async-start(), calls=%async_computation.7 | async-start | bytes 11182080 | tf_op jit(solution)/shard_map/all_gather | solution.py:780
  9.7 232.3 %all-gather.8.cloned.1.call-start = ((), (), s32[]{:S(2)}) async-start(), calls=%async_computation.8 | async-start | bytes 12976128 | tf_op jit(solution)/shard_map/all_gather | solution.py:780
  10.6 137.6 %copy-start.26 = (f32[128]{0:T(128)}, f32[128]{0:T(128)S(1)}, u32[]{:S(2)}) copy-start(f32[128]{0:T(128)S(1)} %rsqrt.40) | copy-start | bytes 1540
  109.0 2.0 collective-permute-start
  112.4 53.2 %copy-start.28 = (f32[128]{0:T(128)}, f32[128]{0:T(128)S(1)}, u32[]{:S(2)}) copy-start(f32[128]{0:T(128)S(1)} %add_rsqrt_fusion.3) | copy-start | bytes 1540
  131.2 2.0 collective-permute-start.1
  134.5 27.7 %copy-start.12 = (bf16[128,1536]{1,0:T(8,128)(2,1)}, bf16[128,1536]{1,0:T(8,128)(2,1)S(1)}, u32[]{:S(2)}) copy-start(bf16[128,1536]{1,0:T(8,128)(2,1)S(1)} %add_convert_fusion.2) | copy-start | bytes 1179652
  134.5 13.5 %collective-permute-start.2 = (bf16[128,1536]{1,0:T(8,128)(2,1)S(1)}, bf16[128,1536]{1,0:T(8,128)(2,1)S(1)}, u32[]{:S(2)}, u32[]{:S(2)}) collective-permute-start(bf16[128,1536]{1,0:T(8,128)(2,1)S(1)} %add_convert_fusion.2), channel_id=1, source_target_pairs={{0,64},{1,65},{2,66},{3,67},{4,68},{5,69},{6,70},{7,71},{8,72},{9,... | collective-permute-start | bytes 1179656 | tf_op jit(solution)/shard_map/ppermute | solution.py:835
  148.2 89.4 %copy-start.30 = (f32[128]{0:T(128)}, f32[128]{0:T(128)S(1)}, u32[]{:S(2)}) copy-start(f32[128]{0:T(128)S(1)} %add_rsqrt_fusion.2) | copy-start | bytes 1540
  162.2 2.0 collective-permute-start.3
  166.6 156.1 %all-gather.10.cloned.1.call-start = ((), (), s32[]{:S(2)}) async-start(), calls=%async_computation.9 | async-start | bytes 3538944 | tf_op jit(solution)/shard_map/all_gather | solution.py:780
  167.4 185.3 %all-gather.14.cloned.1.call-start = ((), (), s32[]{:S(2)}) async-start(), calls=%async_computation.11 | async-start | bytes 12976128 | tf_op jit(solution)/shard_map/all_gather | solution.py:780
  213.3 2.5 collective-permute-start.5
  235.6 2.0 collective-permute-start.6
  240.7 14.8 %collective-permute-start.7 = (bf16[128,1536]{1,0:T(8,128)(2,1)S(1)}, bf16[128,1536]{1,0:T(8,128)(2,1)S(1)}, u32[]{:S(2)}, u32[]{:S(2)}) collective-permute-start(bf16[128,1536]{1,0:T(8,128)(2,1)S(1)} %fusion.17), channel_id=1, source_target_pairs={{64,0},{65,1},{66,2},{67,3},{68,4},{69,5},{70,6},{71,7},{72,8},{73... | collective-permute-start | bytes 1179656 | tf_op jit(solution)/shard_map/ppermute | solution.py:864
  259.2 16.9 %copy-start.21 = (bf16[256,768]{1,0:T(8,128)(2,1)S(1)}, bf16[256,768]{1,0:T(8,128)(2,1)}, u32[]{:S(2)}) copy-start(bf16[256,768]{1,0:T(8,128)(2,1)} %get-tuple-element.71) | copy-start | bytes 1179652
  275.8 4.3 collective-permute-start.8
  276.9 43.9 %collective-permute-start.4 = (bf16[128,1536]{1,0:T(8,128)(2,1)}, bf16[128,1536]{1,0:T(8,128)(2,1)}, u32[]{:S(2)}, u32[]{:S(2)}) collective-permute-start(bf16[128,1536]{1,0:T(8,128)(2,1)} %get-tuple-element.69), channel_id=1, source_target_pairs={{0,1},{1,0},{2,3},{3,2},{4,5},{5,4},{6,7},{7,6},{8,9},{9,8},{10,11... | collective-permute-start | bytes 1179656 | tf_op jit(solution)/shard_map/ppermute | solution.py:40
  294.1 2.6 collective-permute-start.9
  300.3 4.0 collective-permute-start.10
  304.9 11.5 %all-to-all-start = ((f32[4,64,128]{2,1,0:T(8,128)}), f32[4,64,128]{2,1,0:T(8,128)S(1)}, u32[]{:S(2)}, u32[]{:S(2)}) async-start(f32[4,64,128]{2,1,0:T(8,128)} %broadcast_in_dim.59), calls=%async_computation | async-start | bytes 262144 | tf_op jit(solution)/shard_map/all_to_all | solution.py:926
  316.4 20.2 %all-to-all-start.2 = ((bf16[4,256,576]{1,2,0:T(8,128)(2,1)}), bf16[4,256,576]{1,2,0:T(8,128)(2,1)}, u32[]{:S(2)}, u32[]{:S(2)}) async-start(bf16[4,256,576]{1,2,0:T(8,128)(2,1)} %copy.80), calls=%async_computation.2 | async-start | bytes 2359296 | tf_op jit(solution)/shard_map/all_to_all | solution.py:72
  320.7 83.7 %all-gather.12.cloned.1.call-start = ((), (), s32[]{:S(2)}) async-start(), calls=%async_computation.10 | async-start | bytes 1966080 | tf_op jit(solution)/shard_map/all_gather | solution.py:780
  336.6 45.8 %all-to-all-start.4 = ((bf16[4,256,384]{2,1,0:T(8,128)(2,1)}), bf16[4,256,384]{2,1,0:T(8,128)(2,1)S(1)}, u32[]{:S(2)}, u32[]{:S(2)}) async-start(bf16[4,256,384]{2,1,0:T(8,128)(2,1)} %broadcast_select_fusion.1), calls=%async_computation.4 | async-start | bytes 1572864 | tf_op jit(solution)/shard_map/all_to_all | solution.py:72
  350.9 36.6 %collective-permute-start.12 = (bf16[2,16,24,576]{3,2,1,0:T(8,128)(2,1)S(1)}, bf16[2,16,24,576]{3,2,1,0:T(8,128)(2,1)}, u32[]{:S(2)}, u32[]{:S(2)}) collective-permute-start(bf16[2,16,24,576]{3,2,1,0:T(8,128)(2,1)S(1)} %fusion.10), channel_id=1, source_target_pairs={{0,32},{32,0},{1,33},{33,1},{2,34},{34,2},{3,35},{35,3},{4,36},{36... | collective-permute-start | bytes 2654216 | tf_op jit(solution)/shard_map/ppermute | solution.py:40
  381.8 34.7 %collective-permute-start.14 = (bf16[768,768]{1,0:T(8,128)(2,1)}, bf16[768,768]{1,0:T(8,128)(2,1)}, u32[]{:S(2)}, u32[]{:S(2)}) collective-permute-start(bf16[768,768]{1,0:T(8,128)(2,1)} %get-tuple-element.101), channel_id=1, source_target_pairs={{0,32},{32,0},{1,33},{33,1},{2,34},{34,2},{3,35},{35,3},{4,36},{36... | collective-permute-start | bytes 3538952 | tf_op jit(solution)/shard_map/ppermute | solution.py:40
  383.0 10.4 %all-to-all-start.1 = ((f32[4,64,128]{2,1,0:T(8,128)}), f32[4,64,128]{2,1,0:T(8,128)S(1)}, u32[]{:S(2)}, u32[]{:S(2)}) async-start(f32[4,64,128]{2,1,0:T(8,128)} %broadcast_in_dim.60), calls=%async_computation.1 | async-start | bytes 262144 | tf_op jit(solution)/shard_map/all_to_all | solution.py:926
  393.4 19.4 %all-to-all-start.3 = ((bf16[16,2,24,576]{3,2,1,0:T(8,128)(2,1)}), bf16[16,2,24,576]{3,2,1,0:T(8,128)(2,1)S(1)}, u32[]{:S(2)}, u32[]{:S(2)}) async-start(bf16[16,2,24,576]{3,2,1,0:T(8,128)(2,1)} %copy.82), calls=%async_computation.3 | async-start | bytes 1966080 | tf_op jit(solution)/shard_map/all_to_all | solution.py:72
  401.4 15.1 %collective-permute-start.11 = (f32[64,128]{1,0:T(8,128)S(1)}, f32[64,128]{1,0:T(8,128)S(1)}, u32[]{:S(2)}, u32[]{:S(2)}) collective-permute-start(f32[64,128]{1,0:T(8,128)S(1)} %reduce_sum.203), channel_id=1, source_target_pairs={{0,64},{64,0},{1,65},{65,1},{2,66},{66,2},{3,67},{67,3},{4,68},{68... | collective-permute-start | bytes 98312 | tf_op jit(solution)/shard_map/ppermute | solution.py:40
  412.9 12.0 %all-to-all-start.5 = ((bf16[8,48,768]{2,1,0:T(8,128)(2,1)}), bf16[8,48,768]{2,1,0:T(8,128)(2,1)S(1)}, u32[]{:S(2)}, u32[]{:S(2)}) async-start(bf16[8,48,768]{2,1,0:T(8,128)(2,1)} %bitcast.40), calls=%async_computation.5 | async-start | bytes 1179648 | tf_op jit(solution)/shard_map/all_to_all | solution.py:72
  424.9 18.5 %all-to-all-start.6 = ((bf16[16,48,768]{2,1,0:T(8,128)(2,1)}), bf16[16,48,768]{2,1,0:T(8,128)(2,1)S(1)}, u32[]{:S(2)}, u32[]{:S(2)}) async-start(bf16[16,48,768]{2,1,0:T(8,128)(2,1)} %bitcast.44), calls=%async_computation.6 | async-start | bytes 2359296 | tf_op jit(solution)/shard_map/all_to_all | solution.py:72
  430.9 6.5 %collective-permute-start.13 = (bf16[4,24,576]{2,1,0:T(8,128)(2,1)S(1)}, bf16[4,24,576]{2,1,0:T(8,128)(2,1)S(1)}, u32[]{:S(2)}, u32[]{:S(2)}) collective-permute-start(bf16[4,24,576]{2,1,0:T(8,128)(2,1)S(1)} %fusion.36), channel_id=1, source_target_pairs={{0,64},{64,0},{1,65},{65,1},{2,66},{66,2},{3,67},{67,3},{4,68},{68... | collective-permute-start | bytes 331784 | tf_op jit(solution)/shard_map/ppermute | solution.py:40
  (29 other events, 189.5 us)
Sparse Core Ops, SparseCore 0:
  11.4 88.7 all-gather.5
  166.8 63.5 all-gather.7
  232.0 27.2 all-gather.9
  261.4 64.4 all-gather.13
  327.7 35.3 all-gather.11
where the time goes:
time: 461 us; the launch traced here: 454 us
  Pallas kernels  159 us (34%)
  waiting for transfers between devices  122 us (26%)
  starting transfers between devices  46 us (10%)
  other arithmetic  41.4 us (9%)
  local copies, waits for them, and re-layouts  39.6 us (9%)
  blocking collectives  23.3 us (5%)
  between operations  14.7 us (3%)
  matrix products  7.99 us (2%)
    pallas_call x4, Pallas kernels, feed_forward_call(): pl.pallas_call(body, in_specs=in_specs, out_specs=out_specs, out_shape=ou...  75.6 us
    all_gather x5, waiting for transfers between devices, gathered(): return lax.all_gather(own, axes, tiled=True)  68 us
    pallas_call x4, Pallas kernels, mixer_call(): pl.pallas_call(kernel, in_specs=[pl.BlockSpec(memory_space=pltpu.SMEM), *...  42.4 us
    pallas_call x1, Pallas kernels, part_grads_call(): pl.pallas_call(part_grads_kernel, grid_spec=pltpu.PrefetchScalarGridSpec(...  29.2 us
    all_gather x8, blocking collectives, spread(): return lax.all_gather(own, 'c', tiled=True)  21.4 us
    all_to_all x5, waiting for transfers between devices, exchanged(): return lax.all_to_all(tiles, axes, 0, 0, tiled=True)  20.7 us
    all_to_all x5, starting transfers between devices, exchanged(): return lax.all_to_all(tiles, axes, 0, 0, tiled=True)  20.7 us
    ppermute x13, waiting for transfers between devices, swapped(): return lax.ppermute(shard, axis, [(0, 1), (1, 0)])  17.5 us
  transfers between devices with their start and end apart: 27, of which 17 were waited for; matrix products, arithmetic and copies ran while one was open for 16% of the time, Pallas kernels for 27%

commit v1 on v0

--- a/solution.py
+++ b/solution.py
@@ -272,70 +272,71 @@
     )(rows, pair)
 
 
-def part_grads_kernel(
-    here_ref, inner_ref, grad_ref, kept_ref, down_ref, mine_ref, other_ref, acc_ref
-):
+def accumulated(acc_ref, out_ref, part):
     step = pl.program_id(0)
-    inner, grad = inner_ref[...], grad_ref[...]
+
+    @pl.when(step == 0)
+    def _():
+        acc_ref[...] = part
+
+    @pl.when(step > 0)
+    def _():
+        acc_ref[...] += part
+
+    @pl.when(step == pl.num_programs(0) - 1)
+    def _():
+        out_ref[...] = acc_ref[...].astype(BF16)
+
+
+def part_down_kernel(grad_ref, kept_ref, down_ref, pair_ref, out_ref, acc_ref):
+    grad = grad_ref[...]
     units = down_ref.shape[0]
     grad_active = product_right(grad, down_ref[...])
-    grad_gate = (grad_active * kept_ref[:, :units].astype(F32)).astype(BF16)
-    grad_up = (grad_active * kept_ref[:, units : 2 * units].astype(F32)).astype(BF16)
-    parts = [
-        product_left(inner, jnp.concatenate([grad_gate, grad_up], axis=1)),
-        product_left(grad, kept_ref[:, 2 * units :]),
-    ]
-
-    @pl.when(step == 0)
-    def _():
-        acc_ref[:, : 2 * units] = parts[0]
-        acc_ref[:, 2 * units :] = parts[1]
-
-    @pl.when(step > 0)
-    def _():
-        acc_ref[:, : 2 * units] += parts[0]
-        acc_ref[:, 2 * units :] += parts[1]
-
-    @pl.when(step == pl.num_programs(0) - 1)
-    def _():
-        rows = mine_ref.shape[0]
-        here = here_ref[0]
-        mine_ref[...] = acc_ref[pl.ds(pl.multiple_of(here * rows, rows), rows)]
-        rest = acc_ref[pl.ds(pl.multiple_of((1 - here) * rows, rows), rows)]
-        other_ref[...] = rest.astype(BF16)
-
-
-def part_grads_call(here, inner, grad, both, down):
-    tokens, width = inner.shape
-    units = down.shape[0]
+    for k in range(2):
+        lanes = slice(k * units, (k + 1) * units)
+        pair_ref[:, lanes] = (grad_active * kept_ref[:, lanes].astype(F32)).astype(BF16)
+    accumulated(acc_ref, out_ref, product_left(grad, kept_ref[:, 2 * units :]))
+
+
+def part_pair_kernel(rows_ref, pair_ref, out_ref, acc_ref):
+    accumulated(acc_ref, out_ref, product_left(rows_ref[...], pair_ref[...]))
+
+
+def part_call(kernel, operands, fixed, outs, result, flops):
+    tokens = operands[0].shape[0]
     tile = 1024
-    rows = pl.BlockSpec((tile, width), lambda i, c: (i, 0))
-    out = pl.BlockSpec((width // 2, 3 * units), lambda i, c: (0, 0))
+    by_tokens = lambda width: pl.BlockSpec((tile, width), lambda i: (i, 0))
+    entire = lambda shape: pl.BlockSpec(shape, lambda i: (0, 0))
     return pl.pallas_call(
-        part_grads_kernel,
-        grid_spec=pltpu.PrefetchScalarGridSpec(
-            num_scalar_prefetch=1,
-            grid=(tokens // tile,),
-            in_specs=[
-                rows,
-                rows,
-                pl.BlockSpec((tile, 3 * units), lambda i, c: (i, 0)),
-                pl.BlockSpec((units, width), lambda i, c: (0, 0)),
-            ],
-            out_specs=[out, out],
-            scratch_shapes=[pltpu.VMEM((width, 3 * units), F32)],
-        ),
-        out_shape=[
-            jax.ShapeDtypeStruct((width // 2, 3 * units), F32),
-            jax.ShapeDtypeStruct((width // 2, 3 * units), BF16),
-        ],
+        kernel,
+        grid=(tokens // tile,),
+        in_specs=[by_tokens(a.shape[1]) for a in operands] + [entire(a.shape) for a in fixed],
+        out_specs=[by_tokens(width) for width in outs] + [entire(result)],
+        out_shape=[jax.ShapeDtypeStruct((tokens, width), BF16) for width in outs]
+        + [jax.ShapeDtypeStruct(result, BF16)],
+        scratch_shapes=[pltpu.VMEM(result, F32)],
         compiler_params=pltpu.CompilerParams(vmem_limit_bytes=VMEM_LIMIT),
         cost_estimate=pl.CostEstimate(
-            flops=8 * tokens * width * units,
-            bytes_accessed=4 * tokens * width,
-            transcendentals=tokens * units,
+            flops=flops,
+            bytes_accessed=2 * tokens * sum(a.shape[1] for a in operands),
+            transcendentals=0,
         ),
-    )(here, inner, grad, both, down)
+    )(*operands, *fixed)
+
+
+def part_down_call(grad, kept, down):
+    tokens, width = grad.shape
+    units = down.shape[0]
+    flops = 4 * tokens * width * units
+    return part_call(
+        part_down_kernel, (grad, kept), (down,), (2 * units,), (width, units), flops
+    )
+
+
+def part_pair_call(inner, pair):
+    (tokens, width), columns = inner.shape, pair.shape[1]
+    flops = 2 * tokens * width * columns
+    return part_call(part_pair_kernel, (inner, pair), (), (), (width, columns), flops)[0]
 
 
 def load_all(copies):
@@ -404,11 +405,11 @@
 
 
 def tiles_out(tiles_ref, mix_ref, grad_mix, columns):
-    count = tiles_ref.shape[0]
+    for k in range(tiles_ref.shape[0]):
+        tiles_ref[k] = columns(k)
     width = grad_mix.shape[1] // 2
-    step = width // count
-    for k in range(count):
-        tiles_ref[k] = columns(k)
+    step = width // mix_ref.shape[0]
+    for k in range(mix_ref.shape[0]):
         mix_ref[k] = jnp.concatenate(
             [grad_mix[:, h * width + k * step : h * width + (k + 1) * step] for h in range(2)],
             axis=1,
@@ -662,7 +663,7 @@
     count, width = grad.shape
     taps, channels = kernel.shape
     outs = [
-        ((4, count, 3 * channels // 4), BF16),
+        ((8, count, 3 * channels // 8), BF16),
         ((4, count, width // 4), BF16),
         ((taps, channels), F32),
     ]
@@ -685,7 +686,7 @@
     count, width = grad.shape
     channels, qkv_width = weight_out.shape[0], qkv.shape[1]
     outs = [
-        ((4, count, 3 * channels // 4), BF16),
+        ((8, count, 3 * channels // 8), BF16),
         ((4, count, width // 4), BF16),
         ((qkv_width // 128, 128), F32),
     ]
@@ -771,7 +772,6 @@
     in_width = 3 * channels
     qkv_width = attn_qkv.shape[1]
     core_scalar = core.astype(jnp.int32)[None]
-    xl_scalar = xl.astype(jnp.int32)[None]
 
     def chosen(from_first, from_second):
         return jnp.where(first, from_first, from_second)
@@ -779,8 +779,8 @@
     def gathered(own, axes):
         return lax.all_gather(own, axes, tiled=True)
 
-    both = jnp.concatenate([conv_in.reshape(-1, in_width), attn_qkv], axis=1)
-    whole = gathered(both, ("xh", "xl", "y", "z"))
+    everyone = ("xh", "xl", "y", "z")
+    whole = gathered(conv_in.reshape(-1, in_width), everyone)
 
     lanes = -(-part // 256) * 256
     fill = lanes - part
@@ -825,6 +825,9 @@
         back, grad_gain = norm_backward(joined(mine, other), gains[0], layer_in)
         return (grad_hidden + back).astype(BF16), grad_gain
 
+    attn_qkv, _ = lax.optimization_barrier((attn_qkv, whole[:8, :128]))
+    whole_qkv = gathered(attn_qkv, everyone)
+
     projected, gated_0, mine, other = conv_forward_call(
         core_scalar, normed_0, kernel, masks, whole, weight_out
     )
@@ -834,15 +837,21 @@
 
     second_in = lax.ppermute(result_0, "xh", [(0, 1)]).astype(F32)
     normed_own_1 = (normalize(second_in) * gains[0]).astype(BF16)
-    normed_y = gathered(chosen(normed_own_0, normed_own_1), ("y", "c"))
+    normed_own = chosen(normed_own_0, normed_own_1)
+    across = swapped(normed_own, "xl")
+    pair = [jnp.where(xl == 0, normed_own, across), jnp.where(xl == 0, across, normed_own)]
+    normed_near = gathered(jnp.concatenate(pair), ("y", "c"))
     qkv, ready, gated_1, mine, other = attention_forward_call(
-        core_scalar, spread(normed_own_1), head_gains, tables, mask, whole, weight_out, qkv_width
+        core_scalar, spread(normed_own_1), head_gains, tables, mask, whole_qkv, weight_out, qkv_width
     )
     hidden_1 = second_in + joined(mine, other)
     result_1, ffn_1 = feed_forward(hidden_1)
     result_1 = result_1.astype(BF16)
 
-    inner_all = gathered(chosen(ffn_0[0], ffn_1[0]), ("y", "z", "c"))
+    inner_own, normed_near = lax.optimization_barrier(
+        (chosen(ffn_0[0], ffn_1[0]), normed_near)
+    )
+    inner_all = gathered(inner_own, ("y", "z", "c"))
     part_kept = part_forward_call(inner_all, part_pair)
 
     grad_hidden_1, gain_inner_1 = feed_forward_back(
@@ -856,55 +865,53 @@
         mask,
         qkv,
         ready,
-        whole,
+        whole_qkv,
         weight_out,
     )
     input_grad_1, gain_outer_1 = mixer_back(grad_hidden_1, mine, other, second_in)
 
     cotangent = lax.ppermute(input_grad_1, "xh", [(1, 0)])
-    cotangent, part_kept = lax.optimization_barrier((cotangent, part_kept))
     grad_all = gathered(chosen(cotangent, out_cotangent), ("y", "z", "c"))
+    gated, _ = lax.optimization_barrier((chosen(gated_0, gated_1), input_grad_1))
+    gated_y = exchanged(jnp.broadcast_to(gated, (4, *gated.shape)), "y").reshape(4 * rows, -1)
     grad_hidden_0, gain_inner_0 = feed_forward_back(
         spread(cotangent), cotangent.astype(F32), hidden_0, ffn_0
     )
-    gated, grad_hidden_0 = lax.optimization_barrier((chosen(gated_0, gated_1), grad_hidden_0))
-    gated_y = gathered(gated, "y")
     proj_tiles_0, mix_tiles_0, grad_kernel, mine, other = conv_backward_call(
         core_scalar, spread(grad_hidden_0.astype(BF16)), kernel, masks, projected, whole, weight_out
     )
     input_grad_0, gain_outer_0 = mixer_back(grad_hidden_0, mine, other, first_in)
 
-    columns = exchanged(chosen(proj_tiles_0, proj_tiles_1), "y")
-    columns = columns.reshape(4 * rows, -1)
-    in_parts = product_left(normed_y, columns).reshape(2, 2, plane, -1, in_width // 4)
-    mine = lax.dynamic_index_in_dim(in_parts, xl, 1, keepdims=False)
-    other = lax.dynamic_index_in_dim(in_parts, 1 - xl, 1, keepdims=False)
-    mine = (mine + swapped(other.astype(BF16), "xl").astype(F32)).astype(BF16)
-    arrived = exchanged(jnp.moveaxis(mine, 1, 0), PLANE)
-    lines = arrived.reshape(4, 4, *arrived.shape[1:]).astype(F32).sum(1)
+    columns = exchanged(chosen(proj_tiles_0, proj_tiles_1), ("xl", "y"))
+    columns = columns.reshape(2, 4, 2, half, -1).transpose(1, 2, 0, 3, 4).reshape(8 * rows, -1)
+    in_parts = product_left(normed_near, columns).astype(BF16)
+    in_parts = jnp.moveaxis(in_parts.reshape(2, 2 * plane, -1, in_width // 8), 0, 1)
+    arrived = exchanged(in_parts, ("xl", "y", "z"))
+    lines = arrived.reshape(8, 4, *arrived.shape[1:]).astype(F32).sum(1)
     kept_lines = lax.dynamic_index_in_dim(lines, section, 1, keepdims=False)
     sent_lines = lax.dynamic_index_in_dim(lines, 1 - section, 1, keepdims=False)
     come = swapped(sent_lines.astype(BF16), "xh").astype(F32)
-    lines = chosen(kept_lines, come).reshape(4, -1, 3, channels // 4)
+    lines = chosen(kept_lines, come).reshape(8, -1, 3, channels // 8)
     grad_conv_in = jnp.moveaxis(lines, 0, 2).reshape(conv_in.shape)
-    lines = chosen(come, kept_lines)[:, :, : qkv_width // 4]
+    lines = chosen(come, kept_lines)[:, :, : qkv_width // 8]
     grad_attn_qkv = jnp.moveaxis(lines, 0, 1).reshape(attn_qkv.shape)
 
     columns = exchanged(chosen(mix_tiles_0, mix_tiles_1), "y").reshape(4 * rows, -1)
     out_parts = product_left(columns, gated_y).astype(BF16).reshape(8, -1, channels)
     grad_mixer_out = exchanged(out_parts, ("xl", "z")).astype(F32).sum(0).T[None]
 
-    mine, other = part_grads_call(xl_scalar, inner_all, grad_all, part_kept, part_down)
-    mine = (mine + swapped(other, "xl").astype(F32)).astype(BF16)
-    arrived = exchanged(mine.reshape(plane, -1, 3 * lanes), PLANE)
-    lines = [
-        jnp.moveaxis(arrived[:, :, k * lanes : k * lanes + part], 0, 1)
-        .reshape(-1, hidden_units)
-        .astype(F32)
-        for k in range(3)
-    ]
-    grad_gate_up = jnp.stack(lines[:2])[None]
-    grad_down = lines[2].T[None]
+    def finished(parts):
+        columns = parts.shape[1]
+        arrived = exchanged(parts.reshape(2 * plane, -1, columns), ("xl", "y", "z"))
+        total = arrived.reshape(2, plane, -1, columns).astype(F32).sum(0)
+        return [
+            jnp.moveaxis(total[:, :, at : at + part], 0, 1).reshape(-1, hidden_units)
+            for at in range(0, columns, lanes)
+        ]
+
+    pair_grads, down_parts = part_down_call(grad_all, part_kept, part_down)
+    grad_down = finished(down_parts)[0].T[None]
+    grad_gate_up = jnp.stack(finished(part_pair_call(inner_all, pair_grads)))[None]
 
     full_kernel = lax.dynamic_update_slice(
         jnp.zeros(conv_kernel.shape, F32), grad_kernel, (0, core * channels)
@@ -921,9 +928,7 @@
     small = jnp.pad(small, (0, -count % 1024)).reshape(-1, 128)
     small = lax.all_gather(small, "c").sum(0)
     small = small + swapped(small, "xl")
-    for axis in PLANE:
-        copies = jnp.broadcast_to(small, (4, *small.shape))
-        small = lax.all_to_all(copies, axis, 0, 0, tiled=True).sum(0)
+    small = exchanged(jnp.broadcast_to(small, (plane, *small.shape)), PLANE).sum(0)
     come = swapped(small, "xh")
     pair = [chosen(small, come).reshape(-1), chosen(come, small).reshape(-1)]
     grad_norm_gains = jnp.stack([a[: 2 * width].reshape(2, width) for a in pair])

time: 461 us -> 518 us (1.12)
  waiting for transfers between devices: 122 us -> 173 us
  Pallas kernels: 159 us -> 145 us
  starting transfers between devices: 46 us -> 55.2 us
  local copies, waits for them, and re-layouts: 39.6 us -> 47 us
    all_to_all x5 -> x8, starting transfers between devices: 20.7 us -> 44.8 us  [exchanged(): return lax.all_to_all(tiles, axes, 0, 0, tiled=True)]
    ppermute x13 -> x12, waiting for transfers between devices: 17.5 us -> 36.3 us  [swapped(): return lax.ppermute(shard, axis, [(0, 1), (1, 0)])]
    all_gather x5, waiting for transfers between devices: 68 us -> 83.3 us  [gathered(): return lax.all_gather(own, axes, tiled=True)]
    ppermute x1, waiting for transfers between devices: 1.55 us -> 13.3 us  [local(): cotangent = lax.ppermute(input_grad_1, 'xh', [(1, 0)])]
    pallas_call x4, Pallas kernels: 75.6 us -> 65.5 us  [feed_forward_call(): pl.pallas_call(body, in_specs=in_specs, out_specs=out_specs, out_shape=ou...]
    all_to_all x5 -> x8, waiting for transfers between devices: 20.7 us -> 30.3 us  [exchanged(): return lax.all_to_all(tiles, axes, 0, 0, tiled=True)]
    all_to_all x2 -> x0, starting transfers between devices: 8.51 us -> none  [local(): small = lax.all_to_all(copies, axis, 0, 0, tiled=True).sum(0)]
    slice x1, local copies, waits for them, and re-layouts: 8.19 us -> 15.8 us  [local(): weight_pair[0]]
  transfers between devices with their start and end apart: 27 -> 27, of which waited for: 17 -> 17; matrix products, arithmetic and copies ran while one was open for 16% -> 18% of each run, Pallas kernels for 27% -> 28%
where the time goes in v1:
time: 518 us; the launch traced here: 509 us
  waiting for transfers between devices  173 us (33%)
  Pallas kernels  145 us (28%)
  starting transfers between devices  55.2 us (11%)
  local copies, waits for them, and re-layouts  47 us (9%)
  other arithmetic  42.1 us (8%)
  blocking collectives  24 us (5%)
  between operations  14.8 us (3%)
  matrix products  7.32 us (1%)
    all_gather x5, waiting for transfers between devices, gathered(): return lax.all_gather(own, axes, tiled=True)  83.3 us
    pallas_call x4, Pallas kernels, feed_forward_call(): pl.pallas_call(body, in_specs=in_specs, out_specs=out_specs, out_shape=ou...  65.5 us
    all_to_all x8, starting transfers between devices, exchanged(): return lax.all_to_all(tiles, axes, 0, 0, tiled=True)  44.8 us
    pallas_call x4, Pallas kernels, mixer_call(): pl.pallas_call(kernel, in_specs=[pl.BlockSpec(memory_space=pltpu.SMEM), *...  42.8 us
    ppermute x12, waiting for transfers between devices, swapped(): return lax.ppermute(shard, axis, [(0, 1), (1, 0)])  36.3 us
    all_to_all x8, waiting for transfers between devices, exchanged(): return lax.all_to_all(tiles, axes, 0, 0, tiled=True)  30.3 us
    pallas_call x2, Pallas kernels, part_call(): pl.pallas_call(kernel, grid=(tokens // tile,), in_specs=[by_tokens(a.shap...  24.6 us
    all_gather x8, blocking collectives, spread(): return lax.all_gather(own, 'c', tiled=True)  22 us
  transfers between devices with their start and end apart: 27, of which 17 were waited for; matrix products, arithmetic and copies ran while one was open for 18% of the time, Pallas kernels for 28%

profile of v1, /device:TPU:0, one launch (start us, length us, event | category | flops | bytes accessed | tf_op | source)
XLA Modules:
  0.0 508.8 jit_solution(14983737310079529906)
XLA Ops:
  11.3 15.8 %fusion.40 = (bf16[1,1,1536,3456]{3,2,1,0:T(8,128)(2,1)}, bf16[1,1,1536,3456]{3,2,1,0:T(8,128)(2,1)}) fusion(bf16[1,2,1536,3456]{3,2,1,0:T(8,128)(2,1)} %param.20), kind=kLoop, calls=%fused_computation.136 | loop fusion | bytes 42467328 | tf_op jit(solution)/shard_map/slice | solution.py:790
  42.8 45.5 %all-gather.6.cloned.1.call-done.whole_ref = bf16[1536,2304]{1,0:T(8,128)(2,1)} async-done(((bf16[24,2304]{1,0:T(8,128)(2,1)}), bf16[1536,2304]{1,0:T(8,128)(2,1)}) %all-gather.6.cloned.1.call-update) | async-done | bytes 7077904 | tf_op jit(solution)/shard_map/all_gather | solution.py:780
  89.1 8.0 %shard_map.186 = (bf16[3,256,768]{2,1,0:T(8,128)(2,1)}, bf16[256,768]{1,0:T(8,128)(2,1)}, f32[128,1536]{1,0:T(8,128)}, bf16[128,1536]{1,0:T(8,128)(2,1)}) custom-call(s32[1]{0:T(128)} %bitcast.1.core_ref, bf16[256,1536]{1,0:T(8,128)(2,1)} %all_gather.43.rows_ref, f32[3,768]{1,0:T(4,128)} %dynamic-slice_convert_fusion.1.kernel_ref, ...), custom_call_target="tpu_custom_call" | custom-call | flops 2415919104 | bytes 9437184 | tf_op jit(solution)/shard_map/pallas_call | solution.py:627
  103.4 16.1 %shard_map.187 = (bf16[256,3456]{1,0:T(8,128)(2,1)}, bf16[256,3456]{1,0:T(8,128)(2,1)}, f32[128,1536]{1,0:T(8,128)}, bf16[128,1536]{1,0:T(8,128)(2,1)}) custom-call(s32[1]{0:T(128)} %bitcast.1.core_ref, bf16[256,1536]{1,0:T(8,128)(2,1)} %all_gather.45.rows_ref, bf16[2,1536,3456]{2,1,0:T(8,128)(2,1)} %bitcast.136, bf16[3456,1536]{1,0:T(8,128)(2,1)} %bitcast.140), custom_call_target="tpu_custom_call" | custom-call | flops 8153726976 | bytes 31850496 | tf_op jit(solution)/shard_map/pallas_call | solution.py:227
  122.8 4.9 collective-permute-start.2
  127.7 9.5 %collective-permute-done.2 = bf16[128,1536]{1,0:T(8,128)(2,1)S(1)} collective-permute-done((bf16[128,1536]{1,0:T(8,128)(2,1)S(1)}, bf16[128,1536]{1,0:T(8,128)(2,1)S(1)}, u32[]{:S(2)}, u32[]{:S(2)}) %collective-permute-start.2) | collective-permute-done | bytes 393248 | tf_op jit(solution)/shard_map/ppermute | solution.py:838
  138.7 9.5 %collective-permute-done.12 = bf16[128,1536]{1,0:T(8,128)(2,1)S(1)} collective-permute-done((bf16[128,1536]{1,0:T(8,128)(2,1)S(1)}, bf16[128,1536]{1,0:T(8,128)(2,1)S(1)}, u32[]{:S(2)}, u32[]{:S(2)}) %collective-permute-start.12) | collective-permute-done | bytes 393248 | tf_op jit(solution)/shard_map/ppermute | solution.py:40
  152.3 12.4 %all-gather.8.cloned.1.call-done.whole_ref = bf16[1536,1280]{1,0:T(8,128)(2,1)} async-done(((bf16[24,1280]{1,0:T(8,128)(2,1)}), bf16[1536,1280]{1,0:T(8,128)(2,1)}) %all-gather.8.cloned.1.call-update) | async-done | bytes 3932176 | tf_op jit(solution)/shard_map/all_gather | solution.py:780
  164.7 10.3 %shard_map.188 = (f32[256,1280]{1,0:T(8,128)}, bf16[256,1280]{1,0:T(8,128)(2,1)}, bf16[256,768]{1,0:T(8,128)(2,1)}, f32[128,1536]{1,0:T(8,128)}, bf16[128,1536]{1,0:T(8,128)(2,1)}) custom-call(s32[1]{0:T(128)} %bitcast.1.core_ref, bf16[256,1536]{1,0:T(8,128)(2,1)} %all_gather.46.rows_ref, f32[9,128]{1,0:T(8,128)} %stack.64.gains_ref, ...), custom_call_target="tpu_custom_call" | custom-call | flops 1610612736 | bytes 6291456 | tf_op jit(solution)/shard_map/pallas_call | solution.py:627
  179.3 25.3 %all-gather.10.cloned.1.call-done = bf16[2048,1536]{1,0:T(8,128)(2,1)} async-done(((bf16[256,1536]{1,0:T(8,128)(2,1)}), bf16[2048,1536]{1,0:T(8,128)(2,1)}) %all-gather.10.cloned.1.call-update) | async-done | bytes 6291472 | tf_op jit(solution)/shard_map/all_gather | solution.py:780
  207.2 16.3 %shard_map.189 = (bf16[256,3456]{1,0:T(8,128)(2,1)}, bf16[256,3456]{1,0:T(8,128)(2,1)}, f32[128,1536]{1,0:T(8,128)}, bf16[128,1536]{1,0:T(8,128)(2,1)}) custom-call(s32[1]{0:T(128)} %bitcast.1.core_ref, bf16[256,1536]{1,0:T(8,128)(2,1)} %all_gather.48.rows_ref, bf16[2,1536,3456]{2,1,0:T(8,128)(2,1)} %bitcast.137, bf16[3456,1536]{1,0:T(8,128)(2,1)} %bitcast.141), custom_call_target="tpu_custom_call" | custom-call | flops 8153726976 | bytes 31850496 | tf_op jit(solution)/shard_map/pallas_call | solution.py:227
  223.5 16.5 %shard_map.190 = (f32[128,1536]{1,0:T(8,128)}, bf16[128,1536]{1,0:T(8,128)(2,1)}) custom-call(s32[1]{0:T(128)} %bitcast.1.core_ref, bf16[256,1536]{1,0:T(8,128)(2,1)} %all_gather.44.rows_ref, bf16[256,3456]{1,0:T(8,128)(2,1)} %get-tuple-element.70.gate_ref, bf16[256,3456]{1,0:T(8,128)(2,1)} %get-tuple-element.71.up_ref, bf16[2,1536,3456]{2,1,0:T(8,128)(2,1)} %bitcast.138, ...), custom_call_target="tpu_custom_call" | custom-call | flops 8153726976 | bytes 31850496 | tf_op jit(solution)/shard_map/pallas_call | solution.py:227
  247.3 15.2 %shard_map.191 = (bf16[8,256,288]{2,1,0:T(8,128)(2,1)}, bf16[4,256,384]{2,1,0:T(8,128)(2,1)}, f32[10,128]{1,0:T(8,128)}, f32[128,1536]{1,0:T(8,128)}, bf16[128,1536]{1,0:T(8,128)(2,1)}) custom-call(s32[1]{0:T(128)} %bitcast.1.core_ref, bf16[256,1536]{1,0:T(8,128)(2,1)} %all_gather.49.grad_ref, f32[9,128]{1,0:T(8,128)} %stack.64.gains_ref, ...), custom_call_target="tpu_custom_call" | custom-call | flops 1610612736 | bytes 6291456 | tf_op jit(solution)/shard_map/pallas_call | solution.py:627
  268.2 13.3 %collective-permute-done.7 = bf16[128,1536]{1,0:T(8,128)(2,1)S(1)} collective-permute-done((bf16[128,1536]{1,0:T(8,128)(2,1)S(1)}, bf16[128,1536]{1,0:T(8,128)(2,1)S(1)}, u32[]{:S(2)}, u32[]{:S(2)}) %collective-permute-start.7) | collective-permute-done | bytes 393248 | tf_op jit(solution)/shard_map/ppermute | solution.py:873
  285.2 16.7 %shard_map.192 = (f32[128,1536]{1,0:T(8,128)}, bf16[128,1536]{1,0:T(8,128)(2,1)}) custom-call(s32[1]{0:T(128)} %bitcast.1.core_ref, bf16[256,1536]{1,0:T(8,128)(2,1)} %all_gather.50.rows_ref, bf16[256,3456]{1,0:T(8,128)(2,1)} %get-tuple-element.78.gate_ref, bf16[256,3456]{1,0:T(8,128)(2,1)} %get-tuple-element.79.up_ref, bf16[2,1536,3456]{2,1,0:T(8,128)(2,1)} %bitcast.139, ...), custom_call_target="tpu_custom_call" | custom-call | flops 8153726976 | bytes 31850496 | tf_op jit(solution)/shard_map/pallas_call | solution.py:227
  304.6 4.2 all-to-all-start.4
  316.2 9.3 %shard_map.193 = (bf16[8,256,288]{2,1,0:T(8,128)(2,1)}, bf16[4,256,384]{2,1,0:T(8,128)(2,1)}, f32[3,768]{1,0:T(4,128)}, f32[128,1536]{1,0:T(8,128)}, bf16[128,1536]{1,0:T(8,128)(2,1)}) custom-call(s32[1]{0:T(128)} %bitcast.1.core_ref, bf16[256,1536]{1,0:T(8,128)(2,1)} %all_gather.51.grad_ref, f32[3,768]{1,0:T(4,128)} %dynamic-slice_convert_fusion.1.kernel_ref, ...), custom_call_target="tpu_custom_call" | custom-call | flops 2415919104 | bytes 9437184 | tf_op jit(solution)/shard_map/pallas_call | solution.py:627
  328.6 14.4 %all-to-all-done.4 = bf16[4,256,768]{2,1,0:T(8,128)(2,1)S(1)} async-done(((bf16[4,256,768]{2,1,0:T(8,128)(2,1)}), bf16[4,256,768]{2,1,0:T(8,128)(2,1)S(1)}, u32[]{:S(2)}, u32[]{:S(2)}) %all-to-all-start.4) | async-done | bytes 1572896 | tf_op jit(solution)/shard_map/all_to_all | solution.py:72
  343.0 3.6 all-to-all-start.3
  365.2 5.0 all-to-all-start
  375.8 5.2 %all-to-all-done = f32[16,64,128]{2,1,0:T(8,128)} async-done(((f32[16,64,128]{2,1,0:T(8,128)}), f32[16,64,128]{2,1,0:T(8,128)}, u32[]{:S(2)}, u32[]{:S(2)}) %all-to-all-start) | async-done | bytes 524320 | tf_op jit(solution)/shard_map/all_to_all | solution.py:72
  381.0 3.6 all-to-all-start.1
  390.1 8.2 %all-to-all-done.1 = bf16[8,256,288]{1,2,0:T(8,128)(2,1)S(1)} async-done(((bf16[8,256,288]{1,2,0:T(8,128)(2,1)}), bf16[8,256,288]{1,2,0:T(8,128)(2,1)S(1)}, u32[]{:S(2)}, u32[]{:S(2)}) %all-to-all-start.1) | async-done | bytes 1179680 | tf_op jit(solution)/shard_map/all_to_all | solution.py:72
  398.3 4.2 all-to-all-start.5
  405.6 5.7 %convolution_convert_fusion = bf16[1536,288]{0,1:T(8,128)(2,1)} fusion(bf16[2048,288]{0,1:T(8,128)(2,1)S(1)} %reshape.285, bf16[2048,1536]{1,0:T(8,128)(2,1)} %all-gather.10.cloned.1.call-done), kind=kOutput, calls=%fused_computation.5 | convolution fusion | flops 1812381696 | bytes 8355840 | tf_op jit(solution)/shard_map/dot_general | solution.py:32
  414.1 7.6 %all-to-all-start.2 = ((bf16[32,2,24,288]{3,2,1,0:T(8,128)(2,1)}), bf16[32,2,24,288]{3,2,1,0:T(8,128)(2,1)S(1)}, u32[]{:S(2)}, u32[]{:S(2)}) async-start(bf16[32,2,24,288]{3,2,1,0:T(8,128)(2,1)} %copy.86), calls=%async_computation.2 | async-start | bytes 2359296 | tf_op jit(solution)/shard_map/all_to_all | solution.py:72
  421.7 11.9 %shard_map.194.kept_ref = bf16[4096,768]{1,0:T(8,128)(2,1)} custom-call(bf16[4096,1536]{1,0:T(8,128)(2,1)} %all-gather.12.cloned.1.call-done.rows_ref, bf16[1536,512]{1,0:T(8,128)(2,1)} %fusion.2.pair_ref), custom_call_target="tpu_custom_call" | custom-call | flops 6442450944 | bytes 18874368 | tf_op jit(solution)/shard_map/pallas_call | solution.py:257
  433.6 12.7 %shard_map.195 = (bf16[4096,512]{1,0:T(8,128)(2,1)}, bf16[1536,256]{1,0:T(8,128)(2,1)}) custom-call(bf16[4096,1536]{1,0:T(8,128)(2,1)} %all-gather.14.cloned.1.call-done.grad_ref, bf16[4096,768]{1,0:T(8,128)(2,1)} %shard_map.194.kept_ref, bf16[256,1536]{1,0:T(8,128)(2,1)} %pad.31.down_ref), custom_call_target="tpu_custom_call" | custom-call | flops 6442450944 | bytes 18874368 | tf_op jit(solution)/shard_map/pallas_call | solution.py:310
  446.3 8.3 %all-to-all-start.7 = ((bf16[32,48,256]{2,1,0:T(8,128)(2,1)}), bf16[32,48,256]{2,1,0:T(8,128)(2,1)S(1)}, u32[]{:S(2)}, u32[]{:S(2)}) async-start(bf16[32,48,256]{2,1,0:T(8,128)(2,1)} %bitcast.158), calls=%async_computation.7 | async-start | bytes 1572864 | tf_op jit(solution)/shard_map/all_to_all | solution.py:72
  456.0 12.0 %shard_map.196 = bf16[1536,512]{1,0:T(8,128)(2,1)} custom-call(bf16[4096,1536]{1,0:T(8,128)(2,1)} %all-gather.12.cloned.1.call-done.rows_ref, bf16[4096,512]{1,0:T(8,128)(2,1)} %get-tuple-element.98.pair_ref), custom_call_target="tpu_custom_call" | custom-call | flops 6442450944 | bytes 16777216 | tf_op jit(solution)/shard_map/pallas_call | solution.py:310
  468.8 8.3 %all-to-all-start.6 = ((bf16[32,48,512]{2,1,0:T(8,128)(2,1)}), bf16[32,48,512]{2,1,0:T(8,128)(2,1)S(1)}, u32[]{:S(2)}, u32[]{:S(2)}) async-start(bf16[32,48,512]{2,1,0:T(8,128)(2,1)} %bitcast.156), calls=%async_computation.6 | async-start | bytes 3145728 | tf_op jit(solution)/shard_map/all_to_all | solution.py:72
  479.9 14.5 %collective-permute-done.13 = bf16[8,24,288]{2,1,0:T(8,128)(2,1)S(1)} collective-permute-done((bf16[8,24,288]{2,1,0:T(8,128)(2,1)S(1)}, bf16[8,24,288]{2,1,0:T(8,128)(2,1)S(1)}, u32[]{:S(2)}, u32[]{:S(2)}) %collective-permute-start.13) | collective-permute-done | bytes 110624 | tf_op jit(solution)/shard_map/ppermute | solution.py:40
  (238 shorter events, 120.1 us)
Async XLA Ops:
  7.2 81.2 %all-gather.6.cloned.1.call-start = ((), (), s32[]{:S(2)}) async-start(), calls=%async_computation.8 | async-start | bytes 7188480 | tf_op jit(solution)/shard_map/all_gather | solution.py:780
  8.8 155.9 %all-gather.8.cloned.1.call-start = ((), (), s32[]{:S(2)}) async-start(), calls=%async_computation.9 | async-start | bytes 3993600 | tf_op jit(solution)/shard_map/all_gather | solution.py:780
  9.5 195.1 %all-gather.10.cloned.1.call-start = ((), (), s32[]{:S(2)}) async-start(), calls=%async_computation.10 | async-start | bytes 7077888 | tf_op jit(solution)/shard_map/all_gather | solution.py:780
  28.1 109.3 %copy-start.23 = (f32[128]{0:T(128)}, f32[128]{0:T(128)S(1)}, u32[]{:S(2)}) copy-start(f32[128]{0:T(128)S(1)} %rsqrt.40) | copy-start | bytes 1540
  97.1 2.0 collective-permute-start
  100.5 19.0 %copy-start.25 = (f32[128]{0:T(128)}, f32[128]{0:T(128)S(1)}, u32[]{:S(2)}) copy-start(f32[128]{0:T(128)S(1)} %add_rsqrt_fusion.3) | copy-start | bytes 1540
  119.5 2.0 collective-permute-start.1
  122.8 25.5 %copy-start.14 = (bf16[128,1536]{1,0:T(8,128)(2,1)}, bf16[128,1536]{1,0:T(8,128)(2,1)S(1)}, u32[]{:S(2)}) copy-start(bf16[128,1536]{1,0:T(8,128)(2,1)S(1)} %add_convert_fusion.1) | copy-start | bytes 1179652
  122.8 14.4 %collective-permute-start.2 = (bf16[128,1536]{1,0:T(8,128)(2,1)S(1)}, bf16[128,1536]{1,0:T(8,128)(2,1)S(1)}, u32[]{:S(2)}, u32[]{:S(2)}) collective-permute-start(bf16[128,1536]{1,0:T(8,128)(2,1)S(1)} %add_convert_fusion.1), channel_id=1, source_target_pairs={{0,64},{1,65},{2,66},{3,67},{4,68},{5,69},{6,70},{7,71},{8,72},{9,... | collective-permute-start | bytes 1179656 | tf_op jit(solution)/shard_map/ppermute | solution.py:838
  137.9 10.3 %collective-permute-start.12 = (bf16[128,1536]{1,0:T(8,128)(2,1)S(1)}, bf16[128,1536]{1,0:T(8,128)(2,1)S(1)}, u32[]{:S(2)}, u32[]{:S(2)}) collective-permute-start(bf16[128,1536]{1,0:T(8,128)(2,1)S(1)} %get-tuple-element.112), channel_id=1, source_target_pairs={{0,32},{32,0},{1,33},{33,1},{2,34},{34,2},{3,35},{35,3},{4,36},{36... | collective-permute-start | bytes 1179656 | tf_op jit(solution)/shard_map/ppermute | solution.py:40
  149.2 272.5 %all-gather.12.cloned.1.call-start = ((), (), s32[]{:S(2)}) async-start(), calls=%async_computation.11 | async-start | bytes 12976128 | tf_op jit(solution)/shard_map/all_gather | solution.py:780
  174.9 2.0 collective-permute-start.3
  204.7 228.9 %all-gather.14.cloned.1.call-start = ((), (), s32[]{:S(2)}) async-start(), calls=%async_computation.12 | async-start | bytes 12976128 | tf_op jit(solution)/shard_map/all_gather | solution.py:780
  240.0 2.2 collective-permute-start.5
  262.5 2.0 collective-permute-start.6
  266.9 14.6 %collective-permute-start.7 = (bf16[128,1536]{1,0:T(8,128)(2,1)S(1)}, bf16[128,1536]{1,0:T(8,128)(2,1)S(1)}, u32[]{:S(2)}, u32[]{:S(2)}) collective-permute-start(bf16[128,1536]{1,0:T(8,128)(2,1)S(1)} %fusion.13), channel_id=1, source_target_pairs={{64,0},{65,1},{66,2},{67,3},{68,4},{69,5},{70,6},{71,7},{72,8},{73... | collective-permute-start | bytes 1179656 | tf_op jit(solution)/shard_map/ppermute | solution.py:873
  281.5 20.3 %copy-start.2 = (bf16[128,1536]{1,0:T(8,128)(2,1)}, bf16[128,1536]{1,0:T(8,128)(2,1)S(1)}, u32[]{:S(2)}) copy-start(bf16[128,1536]{1,0:T(8,128)(2,1)S(1)} %collective-permute-done.7) | copy-start | bytes 1179652
  301.9 7.0 %collective-permute-start.8 = (bf16[128,1536]{1,0:T(8,128)(2,1)}, bf16[128,1536]{1,0:T(8,128)(2,1)}, u32[]{:S(2)}, u32[]{:S(2)}) collective-permute-start(bf16[128,1536]{1,0:T(8,128)(2,1)} %get-tuple-element.81), channel_id=1, source_target_pairs={{0,1},{1,0},{2,3},{3,2},{4,5},{5,4},{6,7},{7,6},{8,9},{9,8},{10,11... | collective-permute-start | bytes 1179656 | tf_op jit(solution)/shard_map/ppermute | solution.py:40
  302.2 68.0 %collective-permute-start.4 = (bf16[128,1536]{1,0:T(8,128)(2,1)}, bf16[128,1536]{1,0:T(8,128)(2,1)}, u32[]{:S(2)}, u32[]{:S(2)}) collective-permute-start(bf16[128,1536]{1,0:T(8,128)(2,1)} %get-tuple-element.68), channel_id=1, source_target_pairs={{0,1},{1,0},{2,3},{3,2},{4,5},{5,4},{6,7},{7,6},{8,9},{9,8},{10,11... | collective-permute-start | bytes 1179656 | tf_op jit(solution)/shard_map/ppermute | solution.py:40
  304.6 38.4 %all-to-all-start.4 = ((bf16[4,256,768]{2,1,0:T(8,128)(2,1)}), bf16[4,256,768]{2,1,0:T(8,128)(2,1)S(1)}, u32[]{:S(2)}, u32[]{:S(2)}) async-start(bf16[4,256,768]{2,1,0:T(8,128)(2,1)} %broadcast_in_dim.23), calls=%async_computation.4 | async-start | bytes 3145728 | tf_op jit(solution)/shard_map/all_to_all | solution.py:72
  325.5 24.3 %collective-permute-start.9 = (bf16[128,1536]{1,0:T(8,128)(2,1)}, bf16[128,1536]{1,0:T(8,128)(2,1)}, u32[]{:S(2)}, u32[]{:S(2)}) collective-permute-start(bf16[128,1536]{1,0:T(8,128)(2,1)} %get-tuple-element.84), channel_id=1, source_target_pairs={{0,1},{1,0},{2,3},{3,2},{4,5},{5,4},{6,7},{7,6},{8,9},{9,8},{10,11... | collective-permute-start | bytes 1179656 | tf_op jit(solution)/shard_map/ppermute | solution.py:40
  328.6 23.4 %copy-start.21 = (f32[1536]{0:T(1024)S(1)}, f32[1536]{0:T(1024)}, u32[]{:S(2)}) copy-start(f32[1536]{0:T(1024)} %get-tuple-element.104) | copy-start | bytes 18436
  343.0 20.6 %all-to-all-start.3 = ((bf16[4,256,384]{2,1,0:T(8,128)(2,1)}), bf16[4,256,384]{2,1,0:T(8,128)(2,1)S(1)}, u32[]{:S(2)}, u32[]{:S(2)}) async-start(bf16[4,256,384]{2,1,0:T(8,128)(2,1)} %broadcast_select_fusion.1), calls=%async_computation.3 | async-start | bytes 1572864 | tf_op jit(solution)/shard_map/all_to_all | solution.py:72
  355.4 4.2 collective-permute-start.10
  365.2 15.8 %all-to-all-start = ((f32[16,64,128]{2,1,0:T(8,128)}), f32[16,64,128]{2,1,0:T(8,128)}, u32[]{:S(2)}, u32[]{:S(2)}) async-start(f32[16,64,128]{2,1,0:T(8,128)} %broadcast_in_dim.22), calls=%async_computation | async-start | bytes 1048576 | tf_op jit(solution)/shard_map/all_to_all | solution.py:72
  381.0 17.3 %all-to-all-start.1 = ((bf16[8,256,288]{1,2,0:T(8,128)(2,1)}), bf16[8,256,288]{1,2,0:T(8,128)(2,1)S(1)}, u32[]{:S(2)}, u32[]{:S(2)}) async-start(bf16[8,256,288]{1,2,0:T(8,128)(2,1)} %copy.83), calls=%async_computation.1 | async-start | bytes 2359296 | tf_op jit(solution)/shard_map/all_to_all | solution.py:72
  390.0 64.6 %collective-permute-start.11 = (f32[64,128]{1,0:T(8,128)S(1)}, f32[64,128]{1,0:T(8,128)S(1)}, u32[]{:S(2)}, u32[]{:S(2)}) collective-permute-start(f32[64,128]{1,0:T(8,128)S(1)} %reduce_sum.211), channel_id=1, source_target_pairs={{0,64},{64,0},{1,65},{65,1},{2,66},{66,2},{3,67},{67,3},{4,68},{68... | collective-permute-start | bytes 98312 | tf_op jit(solution)/shard_map/ppermute | solution.py:40
  398.3 15.8 %all-to-all-start.5 = ((bf16[8,48,768]{2,1,0:T(8,128)(2,1)}), bf16[8,48,768]{2,1,0:T(8,128)(2,1)}, u32[]{:S(2)}, u32[]{:S(2)}) async-start(bf16[8,48,768]{2,1,0:T(8,128)(2,1)} %bitcast.155), calls=%async_computation.5 | async-start | bytes 1179648 | tf_op jit(solution)/shard_map/all_to_all | solution.py:72
  414.1 32.2 %all-to-all-start.2 = ((bf16[32,2,24,288]{3,2,1,0:T(8,128)(2,1)}), bf16[32,2,24,288]{3,2,1,0:T(8,128)(2,1)S(1)}, u32[]{:S(2)}, u32[]{:S(2)}) async-start(bf16[32,2,24,288]{3,2,1,0:T(8,128)(2,1)} %copy.86), calls=%async_computation.2 | async-start | bytes 2359296 | tf_op jit(solution)/shard_map/all_to_all | solution.py:72
  446.3 21.7 %all-to-all-start.7 = ((bf16[32,48,256]{2,1,0:T(8,128)(2,1)}), bf16[32,48,256]{2,1,0:T(8,128)(2,1)S(1)}, u32[]{:S(2)}, u32[]{:S(2)}) async-start(bf16[32,48,256]{2,1,0:T(8,128)(2,1)} %bitcast.158), calls=%async_computation.7 | async-start | bytes 1572864 | tf_op jit(solution)/shard_map/all_to_all | solution.py:72
  468.8 29.8 %all-to-all-start.6 = ((bf16[32,48,512]{2,1,0:T(8,128)(2,1)}), bf16[32,48,512]{2,1,0:T(8,128)(2,1)S(1)}, u32[]{:S(2)}, u32[]{:S(2)}) async-start(bf16[32,48,512]{2,1,0:T(8,128)(2,1)} %bitcast.156), calls=%async_computation.6 | async-start | bytes 3145728 | tf_op jit(solution)/shard_map/all_to_all | solution.py:72
  478.0 16.5 %collective-permute-start.13 = (bf16[8,24,288]{2,1,0:T(8,128)(2,1)S(1)}, bf16[8,24,288]{2,1,0:T(8,128)(2,1)S(1)}, u32[]{:S(2)}, u32[]{:S(2)}) collective-permute-start(bf16[8,24,288]{2,1,0:T(8,128)(2,1)S(1)} %fusion.31), channel_id=1, source_target_pairs={{0,64},{64,0},{1,65},{65,1},{2,66},{66,2},{3,67},{67,3},{4,68},{68... | collective-permute-start | bytes 331784 | tf_op jit(solution)/shard_map/ppermute | solution.py:40
  (31 other events, 232.1 us)
Sparse Core Ops, SparseCore 0:
  11.4 76.8 all-gather.5
  91.2 73.4 all-gather.7
  166.4 38.2 all-gather.9
  206.8 63.0 all-gather.11
  282.6 79.9 all-gather.13

commit v2 on v1

--- a/solution.py
+++ b/solution.py
@@ -80,6 +80,18 @@
 
 
 VMEM_LIMIT = 56 * 1024 * 1024
+SHORT = pl.CostEstimate(flops=1, bytes_accessed=1, transcendentals=0)
+
+
+def whole_lanes(columns):
+    return -(-columns // 128) * 128
+
+
+def ordered(kernel, count):
+    def body(scalar_ref, *refs):
+        kernel(scalar_ref, *refs[count:])
+
+    return body
 
 
 def unit_tiles(units, tile):
@@ -197,7 +209,7 @@
     rows_out(acc_ref, core_ref[0], mine_ref, other_ref)
 
 
-def feed_forward_call(backward, core, rows, pair, down, saved=()):
+def feed_forward_call(backward, core, rows, pair, down, saved=(), behind=()):
     count, width = rows.shape
     units = down.shape[0]
     tile = 768
@@ -224,19 +236,16 @@
         buffers += [pltpu.VMEM((count, units), BF16)] * 2
         scratch = [*buffers, acc]
         scratch += [pltpu.SemaphoreType.DMA((2, 3)), pltpu.SemaphoreType.DMA((len(tiles), 2))]
+    in_specs = [scalar, *[any_space] * len(behind), *in_specs[1:]]
     return pl.pallas_call(
-        body,
+        ordered(body, len(behind)),
         in_specs=in_specs,
         out_specs=out_specs,
         out_shape=out_shape,
         scratch_shapes=scratch,
         compiler_params=pltpu.CompilerParams(vmem_limit_bytes=VMEM_LIMIT),
-        cost_estimate=pl.CostEstimate(
-            flops=6 * count * width * units,
-            bytes_accessed=6 * width * units,
-            transcendentals=count * units,
-        ),
-    )(core, rows, *saved, pair, down)
+        cost_estimate=SHORT,
+    )(core, *behind, rows, *saved, pair, down)
 
 
 def part_forward_kernel(rows_ref, pair_ref, kept_ref):
@@ -264,15 +273,19 @@
         out_specs=pl.BlockSpec((tile, 3 * units), lambda i: (i, 0)),
         out_shape=jax.ShapeDtypeStruct((tokens, 3 * units), BF16),
         compiler_params=pltpu.CompilerParams(vmem_limit_bytes=VMEM_LIMIT),
-        cost_estimate=pl.CostEstimate(
-            flops=4 * tokens * width * units,
-            bytes_accessed=2 * tokens * (width + 3 * units),
-            transcendentals=tokens * units,
-        ),
+        cost_estimate=SHORT,
     )(rows, pair)
 
 
-def accumulated(acc_ref, out_ref, part):
+def pair_out(acc_ref, here, mine_ref, other_ref, runs):
+    span = mine_ref.shape[0] // runs
+    for k in range(runs):
+        for ref, half in ((mine_ref, here), (other_ref, 1 - here)):
+            start = pl.multiple_of((2 * k + half) * span, span)
+            ref[k * span : (k + 1) * span] = acc_ref[pl.ds(start, span)].astype(BF16)
+
+
+def accumulated(acc_ref, part, finish):
     step = pl.program_id(0)
 
     @pl.when(step == 0)
@@ -283,60 +296,121 @@
     def _():
         acc_ref[...] += part
 
-    @pl.when(step == pl.num_programs(0) - 1)
-    def _():
-        out_ref[...] = acc_ref[...].astype(BF16)
-
-
-def part_down_kernel(grad_ref, kept_ref, down_ref, pair_ref, out_ref, acc_ref):
+    pl.when(step == pl.num_programs(0) - 1)(finish)
+
+
+def part_down_kernel(here_ref, grad_ref, kept_ref, down_ref, pair_ref, mine_ref, other_ref, acc_ref):
     grad = grad_ref[...]
     units = down_ref.shape[0]
     grad_active = product_right(grad, down_ref[...])
     for k in range(2):
         lanes = slice(k * units, (k + 1) * units)
         pair_ref[:, lanes] = (grad_active * kept_ref[:, lanes].astype(F32)).astype(BF16)
-    accumulated(acc_ref, out_ref, product_left(grad, kept_ref[:, 2 * units :]))
-
-
-def part_pair_kernel(rows_ref, pair_ref, out_ref, acc_ref):
-    accumulated(acc_ref, out_ref, product_left(rows_ref[...], pair_ref[...]))
-
-
-def part_call(kernel, operands, fixed, outs, result, flops):
+    accumulated(
+        acc_ref,
+        product_left(grad, kept_ref[:, 2 * units :]),
+        lambda: pair_out(acc_ref, here_ref[0], mine_ref, other_ref, 1),
+    )
+
+
+def part_pair_kernel(here_ref, rows_ref, pair_ref, mine_ref, other_ref, acc_ref):
+    accumulated(
+        acc_ref,
+        product_left(rows_ref[...], pair_ref[...]),
+        lambda: pair_out(acc_ref, here_ref[0], mine_ref, other_ref, 1),
+    )
+
+
+def part_call(kernel, here, operands, fixed, outs, result, flops, behind=()):
     tokens = operands[0].shape[0]
     tile = 1024
-    by_tokens = lambda width: pl.BlockSpec((tile, width), lambda i: (i, 0))
-    entire = lambda shape: pl.BlockSpec(shape, lambda i: (0, 0))
+    by_tokens = lambda width: pl.BlockSpec((tile, width), lambda i, h: (i, 0))
+    entire = lambda shape: pl.BlockSpec(shape, lambda i, h: (0, 0))
+    half = (result[0] // 2, result[1])
     return pl.pallas_call(
-        kernel,
-        grid=(tokens // tile,),
-        in_specs=[by_tokens(a.shape[1]) for a in operands] + [entire(a.shape) for a in fixed],
-        out_specs=[by_tokens(width) for width in outs] + [entire(result)],
+        ordered(kernel, len(behind)),
+        grid_spec=pltpu.PrefetchScalarGridSpec(
+            num_scalar_prefetch=1,
+            grid=(tokens // tile,),
+            in_specs=[pl.BlockSpec(memory_space=pl.ANY)] * len(behind)
+            + [by_tokens(a.shape[1]) for a in operands]
+            + [entire(a.shape) for a in fixed],
+            out_specs=[by_tokens(width) for width in outs] + [entire(half)] * 2,
+            scratch_shapes=[pltpu.VMEM(result, F32)],
+        ),
         out_shape=[jax.ShapeDtypeStruct((tokens, width), BF16) for width in outs]
-        + [jax.ShapeDtypeStruct(result, BF16)],
-        scratch_shapes=[pltpu.VMEM(result, F32)],
+        + [jax.ShapeDtypeStruct(half, BF16)] * 2,
         compiler_params=pltpu.CompilerParams(vmem_limit_bytes=VMEM_LIMIT),
-        cost_estimate=pl.CostEstimate(
-            flops=flops,
-            bytes_accessed=2 * tokens * sum(a.shape[1] for a in operands),
-            transcendentals=0,
-        ),
-    )(*operands, *fixed)
-
-
-def part_down_call(grad, kept, down):
+        cost_estimate=SHORT,
+    )(here, *behind, *operands, *fixed)
+
+
+def part_down_call(here, grad, kept, down):
     tokens, width = grad.shape
     units = down.shape[0]
     flops = 4 * tokens * width * units
     return part_call(
-        part_down_kernel, (grad, kept), (down,), (2 * units,), (width, units), flops
-    )
-
-
-def part_pair_call(inner, pair):
+        part_down_kernel, here, (grad, kept), (down,), (2 * units,), (width, units), flops
+    )
+
+
+def part_pair_call(here, inner, pair, behind):
     (tokens, width), columns = inner.shape, pair.shape[1]
     flops = 2 * tokens * width * columns
-    return part_call(part_pair_kernel, (inner, pair), (), (), (width, columns), flops)[0]
+    return part_call(
+        part_pair_kernel, here, (inner, pair), (), (), (width, columns), flops, behind
+    )
+
+
+def section_sums_kernel(behind_ref, all_ref, sums_ref):
+    half = all_ref.shape[0] // 2
+    for k in range(2):
+        sums_ref[k] = jnp.sum(all_ref[k * half : (k + 1) * half], axis=0)
+
+
+def section_sums_call(small, behind):
+    vmem = pl.BlockSpec(memory_space=pltpu.VMEM)
+    return pl.pallas_call(
+        section_sums_kernel,
+        in_specs=[pl.BlockSpec(memory_space=pl.ANY), vmem],
+        out_specs=vmem,
+        out_shape=jax.ShapeDtypeStruct((2, *small.shape[1:]), F32),
+        compiler_params=pltpu.CompilerParams(vmem_limit_bytes=VMEM_LIMIT),
+        cost_estimate=SHORT,
+    )(*behind, small)
+
+
+def mixer_grads_kernel(
+    here_ref, columns_ref, normed_ref, gated_ref, out_ref, mine_ref, other_ref, acc_ref
+):
+    mix = out_ref.shape[0]
+    out_ref[...] = product_left(columns_ref[:, :mix], gated_ref[...]).astype(BF16)
+    acc_ref[...] = product_left(normed_ref[...], columns_ref[:, mix:])
+    pair_out(acc_ref, here_ref[0], mine_ref, other_ref, 2)
+
+
+def mixer_grads_call(here, columns, normed, gated, mix, behind):
+    vmem = pl.BlockSpec(memory_space=pltpu.VMEM)
+    tokens, width = normed.shape
+    size = columns.shape[1] - mix
+    channels = gated.shape[1]
+    return pl.pallas_call(
+        ordered(mixer_grads_kernel, len(behind)),
+        in_specs=[
+            pl.BlockSpec(memory_space=pltpu.SMEM),
+            *[pl.BlockSpec(memory_space=pl.ANY)] * len(behind),
+            *[vmem] * 3,
+        ],
+        out_specs=[vmem] * 3,
+        out_shape=[
+            jax.ShapeDtypeStruct((mix, channels), BF16),
+            jax.ShapeDtypeStruct((width // 2, size), BF16),
+            jax.ShapeDtypeStruct((width // 2, size), BF16),
+        ],
+        scratch_shapes=[pltpu.VMEM((width, size), F32)],
+        compiler_params=pltpu.CompilerParams(vmem_limit_bytes=VMEM_LIMIT),
+        cost_estimate=SHORT,
+    )(here, *behind, columns, normed, gated)
 
 
 def load_all(copies):
@@ -404,21 +478,22 @@
     rows_out(acc_ref, core_ref[0], mine_ref, other_ref)
 
 
-def tiles_out(tiles_ref, mix_ref, grad_mix, columns):
-    for k in range(tiles_ref.shape[0]):
-        tiles_ref[k] = columns(k)
+def tiles_out(tiles_ref, grad_mix, columns):
+    count, _, size = tiles_ref.shape
     width = grad_mix.shape[1] // 2
-    step = width // mix_ref.shape[0]
-    for k in range(mix_ref.shape[0]):
-        mix_ref[k] = jnp.concatenate(
-            [grad_mix[:, h * width + k * step : h * width + (k + 1) * step] for h in range(2)],
-            axis=1,
-        )
+    step = width // count
+    for k in range(count):
+        here = slice(k * step, (k + 1) * step)
+        parts = [grad_mix[:, :width][:, here], grad_mix[:, width:][:, here], columns(k)]
+        spare = size - sum(part.shape[1] for part in parts)
+        if spare:
+            parts.append(jnp.zeros((grad_mix.shape[0], spare), BF16))
+        tiles_ref[k] = jnp.concatenate(parts, axis=1)
 
 
 def conv_backward_kernel(
     core_ref, grad_ref, kernel_ref, masks_ref, proj_ref, whole_ref, out_ref,
-    tiles_ref, mix_ref, taps_ref, mine_ref, other_ref, in_buf, out_buf, acc_ref, sems,
+    tiles_ref, taps_ref, mine_ref, other_ref, in_buf, out_buf, acc_ref, sems,
 ):
     copies, last = weight_copies(whole_ref, out_ref, in_buf, out_buf, sems, 0)
     load_all([last, *copies])
@@ -449,7 +524,6 @@
     step = grads[0].shape[1] // tiles_ref.shape[0]
     tiles_out(
         tiles_ref,
-        mix_ref,
         grad_ref[...],
         lambda k: jnp.concatenate([g[:, k * step : (k + 1) * step] for g in grads], axis=1),
     )
@@ -545,7 +619,7 @@
 
 def attention_backward_kernel(
     core_ref, grad_ref, gains_ref, tables_ref, mask_ref, qkv_ref, ready_ref, whole_ref, out_ref,
-    tiles_ref, mix_ref, heads_ref, mine_ref, other_ref,
+    tiles_ref, heads_ref, mine_ref, other_ref,
     in_buf, out_buf, acc_ref, attended_ref, ready_grad_ref, proj_ref, sems,
 ):
     copies, last = weight_copies(
@@ -607,27 +681,22 @@
             raw = jnp.where(low, raw, grad)
         proj_ref[:, lanes] = raw.astype(BF16)
     step = width // tiles_ref.shape[0]
-    spare = jnp.zeros((rows, tiles_ref.shape[2] - step), BF16)
-    tiles_out(
-        tiles_ref,
-        mix_ref,
-        grad_ref[...],
-        lambda k: jnp.concatenate([proj_ref[:, k * step : (k + 1) * step], spare], axis=1),
-    )
+    tiles_out(tiles_ref, grad_ref[...], lambda k: proj_ref[:, k * step : (k + 1) * step])
     copies[0].wait()
     acc_ref[...] = product_right(proj_ref[...], in_buf[0])
     rows_out(acc_ref, core_ref[0], mine_ref, other_ref)
 
 
-def mixer_call(kernel, core, operands, whole, weight_out, in_tiles, outs, scratch=(), flops=0):
+def mixer_call(kernel, core, operands, whole, weight_out, in_tiles, outs, scratch=(), behind=()):
     vmem, any_space = pl.BlockSpec(memory_space=pltpu.VMEM), pl.BlockSpec(memory_space=pl.ANY)
     rows, width = operands[0].shape
     channels = weight_out.shape[0]
     outs = [*outs, ((rows // 2, width), F32), ((rows // 2, width), BF16)]
     return pl.pallas_call(
-        kernel,
+        ordered(kernel, len(behind)),
         in_specs=[
             pl.BlockSpec(memory_space=pltpu.SMEM),
+            *[any_space] * len(behind),
             *[vmem] * len(operands),
             any_space,
             any_space,
@@ -642,12 +711,8 @@
             pltpu.SemaphoreType.DMA((in_tiles[0] + 1,)),
         ],
         compiler_params=pltpu.CompilerParams(vmem_limit_bytes=VMEM_LIMIT),
-        cost_estimate=pl.CostEstimate(
-            flops=2 * rows * width * (channels + in_tiles[0] * in_tiles[1]),
-            bytes_accessed=2 * width * (channels + in_tiles[0] * in_tiles[1]),
-            transcendentals=rows * width,
-        ),
-    )(core, *operands, whole, weight_out)
+        cost_estimate=SHORT,
+    )(core, *behind, *operands, whole, weight_out)
 
 
 def conv_forward_call(core, rows, kernel, masks, whole, weight_out):
@@ -659,17 +724,16 @@
     )
 
 
-def conv_backward_call(core, grad, kernel, masks, projected, whole, weight_out):
+def conv_backward_call(core, grad, kernel, masks, projected, whole, weight_out, behind):
     count, width = grad.shape
     taps, channels = kernel.shape
     outs = [
-        ((8, count, 3 * channels // 8), BF16),
-        ((4, count, width // 4), BF16),
+        ((4, count, whole_lanes((width + 3 * channels) // 4)), BF16),
         ((taps, channels), F32),
     ]
     operands = (grad, kernel, masks, projected)
     return mixer_call(
-        conv_backward_kernel, core, operands, whole, weight_out, (3, channels), outs
+        conv_backward_kernel, core, operands, whole, weight_out, (3, channels), outs, (), behind
     )
 
 
@@ -686,8 +750,7 @@
     count, width = grad.shape
     channels, qkv_width = weight_out.shape[0], qkv.shape[1]
     outs = [
-        ((8, count, 3 * channels // 8), BF16),
-        ((4, count, width // 4), BF16),
+        ((4, count, whole_lanes((width + 3 * channels) // 4)), BF16),
         ((qkv_width // 128, 128), F32),
     ]
     scratch = [
@@ -772,6 +835,7 @@
     in_width = 3 * channels
     qkv_width = attn_qkv.shape[1]
     core_scalar = core.astype(jnp.int32)[None]
+    xl_scalar = xl.astype(jnp.int32)[None]
 
     def chosen(from_first, from_second):
         return jnp.where(first, from_first, from_second)
@@ -779,8 +843,9 @@
     def gathered(own, axes):
         return lax.all_gather(own, axes, tiled=True)
 
-    everyone = ("xh", "xl", "y", "z")
-    whole = gathered(conv_in.reshape(-1, in_width), everyone)
+
+    both = jnp.concatenate([conv_in.reshape(-1, in_width), attn_qkv], axis=1)
+    whole = gathered(both, ("xh", "xl", "y", "z"))
 
     lanes = -(-part // 256) * 256
     fill = lanes - part
@@ -807,10 +872,10 @@
         )
     )
 
-    def feed_forward(hidden):
+    def feed_forward(hidden, behind=()):
         inner_own = (normalize(hidden) * gains[1]).astype(BF16)
         gate, up, mine, other = feed_forward_call(
-            False, core_scalar, spread(inner_own), weight_pair, weight_down
+            False, core_scalar, spread(inner_own), weight_pair, weight_down, behind=behind
         )
         return hidden + joined(mine, other), (inner_own, gate, up)
 
@@ -825,8 +890,8 @@
         back, grad_gain = norm_backward(joined(mine, other), gains[0], layer_in)
         return (grad_hidden + back).astype(BF16), grad_gain
 
-    attn_qkv, _ = lax.optimization_barrier((attn_qkv, whole[:8, :128]))
-    whole_qkv = gathered(attn_qkv, everyone)
+    plane_axes = ("y", "z", "c")
+    early = gathered(chosen(normed_own_0, out_cotangent), plane_axes)
 
     projected, gated_0, mine, other = conv_forward_call(
         core_scalar, normed_0, kernel, masks, whole, weight_out
@@ -837,27 +902,19 @@
 
     second_in = lax.ppermute(result_0, "xh", [(0, 1)]).astype(F32)
     normed_own_1 = (normalize(second_in) * gains[0]).astype(BF16)
-    normed_own = chosen(normed_own_0, normed_own_1)
-    across = swapped(normed_own, "xl")
-    pair = [jnp.where(xl == 0, normed_own, across), jnp.where(xl == 0, across, normed_own)]
-    normed_near = gathered(jnp.concatenate(pair), ("y", "c"))
     qkv, ready, gated_1, mine, other = attention_forward_call(
-        core_scalar, spread(normed_own_1), head_gains, tables, mask, whole_qkv, weight_out, qkv_width
+        core_scalar, spread(normed_own_1), head_gains, tables, mask, whole, weight_out, qkv_width
     )
     hidden_1 = second_in + joined(mine, other)
-    result_1, ffn_1 = feed_forward(hidden_1)
+    result_1, ffn_1 = feed_forward(hidden_1, (early,))
     result_1 = result_1.astype(BF16)
 
-    inner_own, normed_near = lax.optimization_barrier(
-        (chosen(ffn_0[0], ffn_1[0]), normed_near)
-    )
-    inner_all = gathered(inner_own, ("y", "z", "c"))
-    part_kept = part_forward_call(inner_all, part_pair)
+    inner_all = gathered(chosen(ffn_0[0], ffn_1[0]), plane_axes)
 
     grad_hidden_1, gain_inner_1 = feed_forward_back(
         cotangent_1, out_cotangent.astype(F32), hidden_1, ffn_1
     )
-    proj_tiles_1, mix_tiles_1, head_sums, mine, other = attention_backward_call(
+    tiles_1, head_sums, mine, other = attention_backward_call(
         core_scalar,
         spread(grad_hidden_1.astype(BF16)),
         head_gains,
@@ -865,53 +922,78 @@
         mask,
         qkv,
         ready,
-        whole_qkv,
+        whole,
         weight_out,
     )
     input_grad_1, gain_outer_1 = mixer_back(grad_hidden_1, mine, other, second_in)
 
     cotangent = lax.ppermute(input_grad_1, "xh", [(1, 0)])
-    grad_all = gathered(chosen(cotangent, out_cotangent), ("y", "z", "c"))
-    gated, _ = lax.optimization_barrier((chosen(gated_0, gated_1), input_grad_1))
+    late = gathered(chosen(cotangent, normed_own_1), plane_axes)
+    gated = chosen(gated_0, gated_1)
     gated_y = exchanged(jnp.broadcast_to(gated, (4, *gated.shape)), "y").reshape(4 * rows, -1)
     grad_hidden_0, gain_inner_0 = feed_forward_back(
         spread(cotangent), cotangent.astype(F32), hidden_0, ffn_0
     )
-    proj_tiles_0, mix_tiles_0, grad_kernel, mine, other = conv_backward_call(
-        core_scalar, spread(grad_hidden_0.astype(BF16)), kernel, masks, projected, whole, weight_out
+    tiles_0, grad_kernel, mine, other = conv_backward_call(
+        core_scalar,
+        spread(grad_hidden_0.astype(BF16)),
+        kernel,
+        masks,
+        projected,
+        whole,
+        weight_out,
+        (gated_y,),
     )
     input_grad_0, gain_outer_0 = mixer_back(grad_hidden_0, mine, other, first_in)
 
-    columns = exchanged(chosen(proj_tiles_0, proj_tiles_1), ("xl", "y"))
-    columns = columns.reshape(2, 4, 2, half, -1).transpose(1, 2, 0, 3, 4).reshape(8 * rows, -1)
-    in_parts = product_left(normed_near, columns).astype(BF16)
-    in_parts = jnp.moveaxis(in_parts.reshape(2, 2 * plane, -1, in_width // 8), 0, 1)
-    arrived = exchanged(in_parts, ("xl", "y", "z"))
-    lines = arrived.reshape(8, 4, *arrived.shape[1:]).astype(F32).sum(1)
+    def summed_over_pair(mine, other):
+        return mine.astype(F32) + swapped(other, "xl").astype(F32)
+
+    columns = exchanged(chosen(tiles_0, tiles_1), "y").reshape(4 * rows, -1)
+    z = lax.axis_index("z")
+    along_y = [
+        lax.dynamic_index_in_dim(a.reshape(4, 4, rows, width), z, 1, keepdims=False)
+        for a in (early, late)
+    ]
+    normed_y = chosen(*along_y).reshape(4 * rows, width)
+
+    part_kept = part_forward_call(inner_all, part_pair)
+    pair_grads, down_mine, down_other = lax.cond(
+        first,
+        lambda: part_down_call(xl_scalar, late, part_kept, part_down),
+        lambda: part_down_call(xl_scalar, early, part_kept, part_down),
+    )
+    out_parts, in_mine, in_other = mixer_grads_call(
+        xl_scalar, columns, normed_y, gated_y, width // 4, (pair_grads,)
+    )
+    pair_mine, pair_other = part_pair_call(xl_scalar, inner_all, pair_grads, (in_mine,))
+
+    total = [summed_over_pair(pair_mine, pair_other), summed_over_pair(down_mine, down_other)]
+    total = jnp.concatenate(total, axis=1).astype(BF16)
+    arrived = exchanged(total.reshape(plane, -1, 3 * lanes), PLANE)
+    lines = [
+        jnp.moveaxis(arrived[:, :, k * lanes : k * lanes + part], 0, 1)
+        .reshape(-1, hidden_units)
+        .astype(F32)
+        for k in range(3)
+    ]
+    grad_gate_up = jnp.stack(lines[:2])[None]
+    grad_down = lines[2].T[None]
+
+    total = summed_over_pair(in_mine, in_other).astype(BF16)
+    total = total.reshape(2, plane, -1, total.shape[1])
+    come = exchanged(jnp.moveaxis(total, 1, 0), PLANE)
+    lines = come.reshape(4, 4, *come.shape[1:]).astype(F32).sum(1)
     kept_lines = lax.dynamic_index_in_dim(lines, section, 1, keepdims=False)
     sent_lines = lax.dynamic_index_in_dim(lines, 1 - section, 1, keepdims=False)
     come = swapped(sent_lines.astype(BF16), "xh").astype(F32)
-    lines = chosen(kept_lines, come).reshape(8, -1, 3, channels // 8)
+    lines = chosen(kept_lines, come)[:, :, : in_width // 4].reshape(4, -1, 3, channels // 4)
     grad_conv_in = jnp.moveaxis(lines, 0, 2).reshape(conv_in.shape)
-    lines = chosen(come, kept_lines)[:, :, : qkv_width // 8]
+    lines = chosen(come, kept_lines)[:, :, : qkv_width // 4]
     grad_attn_qkv = jnp.moveaxis(lines, 0, 1).reshape(attn_qkv.shape)
 
-    columns = exchanged(chosen(mix_tiles_0, mix_tiles_1), "y").reshape(4 * rows, -1)
-    out_parts = product_left(columns, gated_y).astype(BF16).reshape(8, -1, channels)
-    grad_mixer_out = exchanged(out_parts, ("xl", "z")).astype(F32).sum(0).T[None]
-
-    def finished(parts):
-        columns = parts.shape[1]
-        arrived = exchanged(parts.reshape(2 * plane, -1, columns), ("xl", "y", "z"))
-        total = arrived.reshape(2, plane, -1, columns).astype(F32).sum(0)
-        return [
-            jnp.moveaxis(total[:, :, at : at + part], 0, 1).reshape(-1, hidden_units)
-            for at in range(0, columns, lanes)
-        ]
-
-    pair_grads, down_parts = part_down_call(grad_all, part_kept, part_down)
-    grad_down = finished(down_parts)[0].T[None]
-    grad_gate_up = jnp.stack(finished(part_pair_call(inner_all, pair_grads)))[None]
+    out_parts = exchanged(out_parts.reshape(8, -1, channels), ("xl", "z"))
+    grad_mixer_out = out_parts.astype(F32).sum(0).T[None]
 
     full_kernel = lax.dynamic_update_slice(
         jnp.zeros(conv_kernel.shape, F32), grad_kernel, (0, core * channels)
@@ -926,11 +1008,8 @@
     )
     count = small.shape[0]
     small = jnp.pad(small, (0, -count % 1024)).reshape(-1, 128)
-    small = lax.all_gather(small, "c").sum(0)
-    small = small + swapped(small, "xl")
-    small = exchanged(jnp.broadcast_to(small, (plane, *small.shape)), PLANE).sum(0)
-    come = swapped(small, "xh")
-    pair = [chosen(small, come).reshape(-1), chosen(come, small).reshape(-1)]
+    sums = section_sums_call(lax.all_gather(small, AXES), (arrived,))
+    pair = [sums[0].reshape(-1), sums[1].reshape(-1)]
     grad_norm_gains = jnp.stack([a[: 2 * width].reshape(2, width) for a in pair])
     grad_conv_kernel = pair[0][2 * width : 5 * width].reshape(conv_kernel.shape)
     grad_qk_gains = pair[1][5 * width : count].reshape(qk_gains.shape)

time: 518 us -> 498 us (0.961)
  starting transfers between devices: 55.2 us -> 33.5 us
  local copies, waits for them, and re-layouts: 47 us -> 30.4 us
  Pallas kernels: 145 us -> 157 us
  other arithmetic: 42.1 us -> 52 us
  waiting for transfers between devices: 173 us -> 181 us
  matrix products: 7.32 us -> 0 us
    all_to_all x8 -> x5, waiting for transfers between devices: 30.3 us -> 67.9 us  [exchanged(): return lax.all_to_all(tiles, axes, 0, 0, tiled=True)]
    all_to_all x8 -> x5, starting transfers between devices: 44.8 us -> 21.8 us  [exchanged(): return lax.all_to_all(tiles, axes, 0, 0, tiled=True)]
    all_gather x5 -> x4, waiting for transfers between devices: 83.3 us -> 64.4 us  [gathered(): return lax.all_gather(own, axes, tiled=True)]
    pallas_call x10 -> x12, Pallas kernels: 133 us -> 145 us  [the longest x4 66.1 us: feed_forward_call(): pl.pallas_call(ordered(body, len(behind)), in_specs=in_specs, out_specs=o...]
    ppermute x12, waiting for transfers between devices: 36.3 us -> 27.1 us  [swapped(): return lax.ppermute(shard, axis, [(0, 1), (1, 0)])]
    slice x1, local copies, waits for them, and re-layouts: 15.8 us -> 8.06 us  [local(): weight_pair[0]]
    dot_general x2 -> x0, matrix products: 7.32 us -> none  [product_left(): lax.dot_general(left, right, (((0,), (0,)), ((), ())), preferred_element_...]
    select_n x12 -> x11, other arithmetic: 11.8 us -> 16.5 us  [chosen(): return jnp.where(first, from_first, from_second)]
  transfers between devices with their start and end apart: 27 -> 24, of which waited for: 17 -> 15; matrix products, arithmetic and copies ran while one was open for 18% -> 15% of each run, Pallas kernels for 28% -> 32%
where the time goes in v2:
time: 498 us; the launch traced here: 491 us
  waiting for transfers between devices  181 us (36%)
  Pallas kernels  157 us (32%)
  other arithmetic  52 us (10%)
  starting transfers between devices  33.5 us (7%)
  local copies, waits for them, and re-layouts  30.4 us (6%)
  blocking collectives  21.9 us (4%)
  between operations  14.7 us (3%)
    all_to_all x5, waiting for transfers between devices, exchanged(): return lax.all_to_all(tiles, axes, 0, 0, tiled=True)  67.9 us
    pallas_call x4, Pallas kernels, feed_forward_call(): pl.pallas_call(ordered(body, len(behind)), in_specs=in_specs, out_specs=o...  66.1 us
    all_gather x4, waiting for transfers between devices, gathered(): return lax.all_gather(own, axes, tiled=True)  64.4 us
    pallas_call x4, Pallas kernels, mixer_call(): pl.pallas_call(ordered(kernel, len(behind)), in_specs=[pl.BlockSpec(memor...  43.4 us
    ppermute x12, waiting for transfers between devices, swapped(): return lax.ppermute(shard, axis, [(0, 1), (1, 0)])  27.1 us
    pallas_call x2, Pallas kernels, part_call(): pl.pallas_call(ordered(kernel, len(behind)), grid_spec=pltpu.PrefetchScal...  24.6 us
    all_gather x8, blocking collectives, spread(): return lax.all_gather(own, 'c', tiled=True)  21.9 us
    all_to_all x5, starting transfers between devices, exchanged(): return lax.all_to_all(tiles, axes, 0, 0, tiled=True)  21.8 us
  transfers between devices with their start and end apart: 24, of which 15 were waited for; matrix products, arithmetic and copies ran while one was open for 15% of the time, Pallas kernels for 32%

profile of v2, /device:TPU:0, one launch (start us, length us, event | category | flops | bytes accessed | tf_op | source)
XLA Modules:
  0.0 490.6 jit_solution(5228837404241651148)
XLA Ops:
  25.5 8.1 %fusion.41 = (bf16[1,1,1536,3456]{3,2,1,0:T(8,128)(2,1)S(1)}, bf16[1,1,1536,3456]{3,2,1,0:T(8,128)(2,1)S(1)}) fusion(bf16[1,2,1536,3456]{3,2,1,0:T(8,128)(2,1)} %param.22), kind=kLoop, calls=%fused_computation.133 | loop fusion | bytes 42467328 | tf_op jit(solution)/shard_map/slice | solution.py:855
  35.8 64.4 %all-gather.6.cloned.1.call-done.refs_3_.refs_4_.refs_6_.refs_5_ = bf16[1536,3584]{1,0:T(8,128)(2,1)} async-done(((bf16[24,3584]{1,0:T(8,128)(2,1)}), bf16[1536,3584]{1,0:T(8,128)(2,1)}) %all-gather.6.cloned.1.call-update) | async-done | bytes 11010064 | tf_op jit(solution)/shard_map/all_gather | solution.py:844
  100.9 8.1 %shard_map.186 = (bf16[3,256,768]{2,1,0:T(8,128)(2,1)}, bf16[256,768]{1,0:T(8,128)(2,1)}, f32[128,1536]{1,0:T(8,128)}, bf16[128,1536]{1,0:T(8,128)(2,1)}) custom-call(s32[1]{0:T(128)} %bitcast.1.scalar_ref, bf16[256,1536]{1,0:T(8,128)(2,1)} %all_gather.40.refs_0_, f32[3,768]{1,0:T(4,128)} %dynamic-slice_convert_fusion.1.refs_1_.refs_2_, ...), custom_call_target="tpu_custom_call" | custom-call | flops 1 | bytes 1 | tf_op jit(solution)/shard_map/pallas_call | solution.py:695
  115.3 16.3 %shard_map.187 = (bf16[256,3456]{1,0:T(8,128)(2,1)}, bf16[256,3456]{1,0:T(8,128)(2,1)}, f32[128,1536]{1,0:T(8,128)}, bf16[128,1536]{1,0:T(8,128)(2,1)}) custom-call(s32[1]{0:T(128)} %bitcast.1.scalar_ref, bf16[256,1536]{1,0:T(8,128)(2,1)} %all_gather.42.refs_0_, bf16[2,1536,3456]{2,1,0:T(8,128)(2,1)} %bitcast.123, bf16[3456,1536]{1,0:T(8,128)(2,1)} %bitcast.127), custom_call_target="tpu_custom_call" | custom-call | flops 1 | bytes 1 | tf_op jit(solution)/shard_map/pallas_call | solution.py:240
  134.9 4.9 collective-permute-start.2
  139.8 8.7 %collective-permute-done.2 = bf16[128,1536]{1,0:T(8,128)(2,1)S(1)} collective-permute-done((bf16[128,1536]{1,0:T(8,128)(2,1)S(1)}, bf16[128,1536]{1,0:T(8,128)(2,1)S(1)}, u32[]{:S(2)}, u32[]{:S(2)}) %collective-permute-start.2) | collective-permute-done | bytes 393248 | tf_op jit(solution)/shard_map/ppermute | solution.py:903
  151.4 10.6 %shard_map.188 = (f32[256,1280]{1,0:T(8,128)}, bf16[256,1280]{1,0:T(8,128)(2,1)}, bf16[256,768]{1,0:T(8,128)(2,1)}, f32[128,1536]{1,0:T(8,128)}, bf16[128,1536]{1,0:T(8,128)(2,1)}) custom-call(s32[1]{0:T(128)} %bitcast.1.scalar_ref, bf16[256,1536]{1,0:T(8,128)(2,1)} %all_gather.43.refs_0_, f32[9,128]{1,0:T(8,128)} %stack.67.refs_1_, ...), custom_call_target="tpu_custom_call" | custom-call | flops 1 | bytes 1 | tf_op jit(solution)/shard_map/pallas_call | solution.py:695
  169.6 16.5 %shard_map.189 = (bf16[256,3456]{1,0:T(8,128)(2,1)}, bf16[256,3456]{1,0:T(8,128)(2,1)}, f32[128,1536]{1,0:T(8,128)}, bf16[128,1536]{1,0:T(8,128)(2,1)}) custom-call(s32[1]{0:T(128)} %bitcast.1.scalar_ref, bf16[4096,1536]{1,0:T(8,128)(2,1)} %all-gather.8.cloned.1.call-done.refs_0_, bf16[256,1536]{1,0:T(8,128)(2,1)} %all_gather.45.refs_1_, ...), custom_call_target="tpu_custom_call" | custom-call | flops 1 | bytes 1 | tf_op jit(solution)/shard_map/pallas_call | solution.py:240
  186.1 16.4 %shard_map.190 = (f32[128,1536]{1,0:T(8,128)}, bf16[128,1536]{1,0:T(8,128)(2,1)}) custom-call(s32[1]{0:T(128)} %bitcast.1.scalar_ref, bf16[256,1536]{1,0:T(8,128)(2,1)} %all_gather.41.refs_0_, bf16[256,3456]{1,0:T(8,128)(2,1)} %get-tuple-element.109.refs_1_, bf16[256,3456]{1,0:T(8,128)(2,1)} %get-tuple-element.110.refs_2_, bf16[2,1536,3456]{2,1,0:T(8,128)(2,1)} %bitcast.125, ...), custom_call_target="tpu_custom_call" | custom-call | flops 1 | bytes 1 | tf_op jit(solution)/shard_map/pallas_call | solution.py:240
  209.8 15.1 %shard_map.191 = (bf16[4,256,1024]{2,1,0:T(8,128)(2,1)}, f32[10,128]{1,0:T(8,128)}, f32[128,1536]{1,0:T(8,128)}, bf16[128,1536]{1,0:T(8,128)(2,1)}) custom-call(s32[1]{0:T(128)} %bitcast.1.scalar_ref, bf16[256,1536]{1,0:T(8,128)(2,1)} %all_gather.46.refs_0_, f32[9,128]{1,0:T(8,128)} %stack.67.refs_1_, f32[2,256,128]{2,1,0:T(8,128)} %bitcast.144, ...), custom_call_target="tpu_custom_call" | custom-call | flops 1 | bytes 1 | tf_op jit(solution)/shard_map/pallas_call | solution.py:695
  230.7 13.3 %collective-permute-done.7 = bf16[128,1536]{1,0:T(8,128)(2,1)S(1)} collective-permute-done((bf16[128,1536]{1,0:T(8,128)(2,1)S(1)}, bf16[128,1536]{1,0:T(8,128)(2,1)S(1)}, u32[]{:S(2)}, u32[]{:S(2)}) %collective-permute-start.7) | collective-permute-done | bytes 393248 | tf_op jit(solution)/shard_map/ppermute | solution.py:930
  247.7 16.8 %shard_map.192 = (f32[128,1536]{1,0:T(8,128)}, bf16[128,1536]{1,0:T(8,128)(2,1)}) custom-call(s32[1]{0:T(128)} %bitcast.1.scalar_ref, bf16[256,1536]{1,0:T(8,128)(2,1)} %all_gather.47.refs_0_, bf16[256,3456]{1,0:T(8,128)(2,1)} %get-tuple-element.117.refs_1_, bf16[256,3456]{1,0:T(8,128)(2,1)} %get-tuple-element.118.refs_2_, bf16[2,1536,3456]{2,1,0:T(8,128)(2,1)} %bitcast.126, ...), custom_call_target="tpu_custom_call" | custom-call | flops 1 | bytes 1 | tf_op jit(solution)/shard_map/pallas_call | solution.py:240
  266.1 4.3 all-to-all-start
  279.2 3.2 all_gather.48.refs_1_
  282.4 23.1 %all-to-all-done = bf16[4,256,768]{2,1,0:T(8,128)(2,1)S(1)} async-done(((bf16[4,256,768]{2,1,0:T(8,128)(2,1)}), bf16[4,256,768]{2,1,0:T(8,128)(2,1)S(1)}, u32[]{:S(2)}, u32[]{:S(2)}) %all-to-all-start) | async-done | bytes 1572896 | tf_op jit(solution)/shard_map/all_to_all | solution.py:72
  306.6 9.5 %shard_map.193 = (bf16[4,256,1024]{2,1,0:T(8,128)(2,1)}, f32[3,768]{1,0:T(4,128)}, f32[128,1536]{1,0:T(8,128)}, bf16[128,1536]{1,0:T(8,128)(2,1)}) custom-call(s32[1]{0:T(128)} %bitcast.1.scalar_ref, bf16[1024,768]{1,0:T(8,128)(2,1)} %bitcast.137, bf16[256,1536]{1,0:T(8,128)(2,1)} %all_gather.48.refs_1_, ...), custom_call_target="tpu_custom_call" | custom-call | flops 1 | bytes 1 | tf_op jit(solution)/shard_map/pallas_call | solution.py:695
  320.5 3.1 broadcast_select_fusion
  323.6 4.6 all-to-all-start.1
  328.5 11.9 %shard_map.194 = bf16[4096,768]{1,0:T(8,128)(2,1)} custom-call(bf16[4096,1536]{1,0:T(8,128)(2,1)} %all-gather.10.cloned.1.call-done.rows_ref.refs_1_, bf16[1536,512]{1,0:T(8,128)(2,1)} %fusion.2.pair_ref), custom_call_target="tpu_custom_call" | custom-call | flops 1 | bytes 1 | tf_op jit(solution)/shard_map/pallas_call | solution.py:266
  340.4 12.5 %conditional.1 = ((bf16[4096,512]{1,0:T(8,128)(2,1)}, bf16[768,256]{1,0:T(8,128)(2,1)}, bf16[768,256]{1,0:T(8,128)(2,1)})) conditional(s32[]{:T(128)} %convert_element_type.208, (s32[1]{0:T(128)}, bf16[4096,1536]{1,0:T(8,128)(2,1)}, bf16[4096,768]{1,0:T(8,128)(2,1)}, bf16[256,1536]{1,0:T(8,128)(2,1)S(1)}) %tuple.77, (s32[1]{0:T(128)}, ...), branch_computations={%region_8.9_spmd.clone, %region_9.10_spmd.clone} | conditional | flops 1 | bytes 9 | solution.py:961
  340.4 12.5 %branch_1_fun.2 = (bf16[4096,512]{1,0:T(8,128)(2,1)}, bf16[768,256]{1,0:T(8,128)(2,1)}, bf16[768,256]{1,0:T(8,128)(2,1)}) custom-call(s32[1]{0:T(128)} %get-tuple-element.157.scalar_ref, bf16[4096,1536]{1,0:T(8,128)(2,1)} %get-tuple-element.158.refs_0_, bf16[4096,768]{1,0:T(8,128)(2,1)} %get-tuple-element.159.refs_1_, ...), custom_call_target="tpu_custom_call" | custom-call | flops 1 | bytes 1 | tf_op jit(solution)/shard_map/cond/branch_1_fun/pallas_call | solution.py:330
  354.6 4.8 dynamic-slice_select_fusion
  359.3 7.6 %shard_map.195 = (bf16[384,768]{1,0:T(8,128)(2,1)}, bf16[768,640]{1,0:T(8,128)(2,1)}, bf16[768,640]{1,0:T(8,128)(2,1)}) custom-call(s32[1]{0:T(128)} %bitcast.26.scalar_ref, bf16[4096,512]{1,0:T(8,128)(2,1)} %get-tuple-element.151.refs_0_.refs_2_, bf16[1024,1024]{1,0:T(8,128)(2,1)} %bitcast.27.refs_1_, bf16[1024,1536]{1,0:T(8,128)(2,1)} %bitcast.139, ...), custom_call_target="tpu_custom_call" | custom-call | flops 1 | bytes 1 | tf_op jit(solution)/shard_map/pallas_call | solution.py:397
  367.0 12.1 %shard_map.196 = (bf16[768,512]{1,0:T(8,128)(2,1)}, bf16[768,512]{1,0:T(8,128)(2,1)}) custom-call(s32[1]{0:T(128)} %bitcast.26.scalar_ref, bf16[768,640]{1,0:T(8,128)(2,1)} %get-tuple-element.131.refs_0_, bf16[4096,1536]{1,0:T(8,128)(2,1)} %all-gather.10.cloned.1.call-done.rows_ref.refs_1_, bf16[4096,512]{1,0:T(8,128)(2,1)} %get-tuple-element.151.refs_0_.refs_2_), custom_call_target="tpu_custom_call" | custom-call | flops 1 | bytes 1 | tf_op jit(solution)/shard_map/pallas_call | solution.py:330
  383.9 3.5 all-to-all-start.4
  388.5 15.1 %collective-permute-done.10 = bf16[768,512]{1,0:T(8,128)(2,1)} collective-permute-done((bf16[768,512]{1,0:T(8,128)(2,1)}, bf16[768,512]{1,0:T(8,128)(2,1)}, u32[]{:S(2)}, u32[]{:S(2)}) %collective-permute-start.10) | collective-permute-done | bytes 786464 | tf_op jit(solution)/shard_map/ppermute | solution.py:40
  406.1 25.0 %all-to-all-done.4 = bf16[8,48,768]{2,1,0:T(8,128)(2,1)S(1)} async-done(((bf16[8,48,768]{2,1,0:T(8,128)(2,1)}), bf16[8,48,768]{2,1,0:T(8,128)(2,1)S(1)}, u32[]{:S(2)}, u32[]{:S(2)}) %all-to-all-start.4) | async-done | bytes 589856 | tf_op jit(solution)/shard_map/all_to_all | solution.py:72
  432.0 5.7 %all-to-all-start.2 = ((bf16[16,48,768]{2,1,0:T(8,128)(2,1)}), bf16[16,48,768]{2,1,0:T(8,128)(2,1)S(1)}, u32[]{:S(2)}, u32[]{:S(2)}) async-start(bf16[16,48,768]{2,1,0:T(8,128)(2,1)} %pad_maximum_fusion), calls=%async_computation.2 | async-start | bytes 2359296 | tf_op jit(solution)/shard_map/all_to_all | solution.py:72
  443.4 13.5 %all-to-all-done.2.behind_ref = bf16[16,48,768]{2,1,0:T(8,128)(2,1)S(1)} async-done(((bf16[16,48,768]{2,1,0:T(8,128)(2,1)}), bf16[16,48,768]{2,1,0:T(8,128)(2,1)S(1)}, u32[]{:S(2)}, u32[]{:S(2)}) %all-to-all-start.2) | async-done | bytes 1179680 | tf_op jit(solution)/shard_map/all_to_all | solution.py:72
  457.0 3.6 all-to-all-start.3
  460.6 3.0 shard_map.197
  468.9 6.2 %all-to-all-done.3 = bf16[16,2,24,640]{3,2,1,0:T(8,128)(2,1)S(1)} async-done(((bf16[16,2,24,640]{3,2,1,0:T(8,128)(2,1)}), bf16[16,2,24,640]{3,2,1,0:T(8,128)(2,1)S(1)}, u32[]{:S(2)}, u32[]{:S(2)}) %all-to-all-start.3) | async-done | bytes 983072 | tf_op jit(solution)/shard_map/all_to_all | solution.py:72
  (228 shorter events, 104.0 us)
Async XLA Ops:
  7.2 93.0 %all-gather.6.cloned.1.call-start = ((), (), s32[]{:S(2)}) async-start(), calls=%async_computation.5 | async-start | bytes 11182080 | tf_op jit(solution)/shard_map/all_gather | solution.py:844
  9.7 159.9 %all-gather.8.cloned.1.call-start = ((), (), s32[]{:S(2)}) async-start(), calls=%async_computation.6 | async-start | bytes 12976128 | tf_op jit(solution)/shard_map/all_gather | solution.py:844
  13.8 314.6 %all-gather.10.cloned.1.call-start = ((), (), s32[]{:S(2)}) async-start(), calls=%async_computation.7 | async-start | bytes 12976128 | tf_op jit(solution)/shard_map/all_gather | solution.py:844
  109.0 2.0 collective-permute-start
  112.5 53.1 %copy-start.27 = (f32[128]{0:T(128)}, f32[128]{0:T(128)S(1)}, u32[]{:S(2)}) copy-start(f32[128]{0:T(128)S(1)} %add_rsqrt_fusion.3) | copy-start | bytes 1540
  131.6 2.0 collective-permute-start.1
  134.9 27.2 %copy-start.16 = (bf16[128,1536]{1,0:T(8,128)(2,1)}, bf16[128,1536]{1,0:T(8,128)(2,1)S(1)}, u32[]{:S(2)}) copy-start(bf16[128,1536]{1,0:T(8,128)(2,1)S(1)} %add_convert_fusion.3) | copy-start | bytes 1179652
  134.9 13.6 %collective-permute-start.2 = (bf16[128,1536]{1,0:T(8,128)(2,1)S(1)}, bf16[128,1536]{1,0:T(8,128)(2,1)S(1)}, u32[]{:S(2)}, u32[]{:S(2)}) collective-permute-start(bf16[128,1536]{1,0:T(8,128)(2,1)S(1)} %add_convert_fusion.3), channel_id=1, source_target_pairs={{0,64},{1,65},{2,66},{3,67},{4,68},{5,69},{6,70},{7,71},{8,72},{9,... | collective-permute-start | bytes 1179656 | tf_op jit(solution)/shard_map/ppermute | solution.py:903
  162.1 2.1 collective-permute-start.3
  165.5 20.5 %copy-start.32 = (f32[128]{0:T(128)}, f32[128]{0:T(128)S(1)}, u32[]{:S(2)}) copy-start(f32[128]{0:T(128)S(1)} %add_rsqrt_fusion.1) | copy-start | bytes 1540
  166.6 173.8 %all-gather.12.cloned.1.call-start = ((), (), s32[]{:S(2)}) async-start(), calls=%async_computation.8 | async-start | bytes 12976128 | tf_op jit(solution)/shard_map/all_gather | solution.py:844
  186.1 18.5 %copy-start.33 = (f32[128]{0:T(128)S(1)}, f32[128]{0:T(128)}, u32[]{:S(2)}) copy-start(f32[128]{0:T(128)} %copy-done.32) | copy-start | bytes 1540
  202.5 2.0 collective-permute-start.5
  224.9 2.0 collective-permute-start.6
  229.4 35.2 %copy-start.14 = (bf16[128,1536]{1,0:T(8,128)(2,1)}, bf16[128,1536]{1,0:T(8,128)(2,1)S(1)}, u32[]{:S(2)}) copy-start(bf16[128,1536]{1,0:T(8,128)(2,1)S(1)} %fusion.12) | copy-start | bytes 1179652
  229.4 14.6 %collective-permute-start.7 = (bf16[128,1536]{1,0:T(8,128)(2,1)S(1)}, bf16[128,1536]{1,0:T(8,128)(2,1)S(1)}, u32[]{:S(2)}, u32[]{:S(2)}) collective-permute-start(bf16[128,1536]{1,0:T(8,128)(2,1)S(1)} %fusion.12), channel_id=1, source_target_pairs={{64,0},{65,1},{66,2},{67,3},{68,4},{69,5},{70,6},{71,7},{72,8},{73... | collective-permute-start | bytes 1179656 | tf_op jit(solution)/shard_map/ppermute | solution.py:930
  244.0 20.6 %copy-start.6 = (bf16[128,1536]{1,0:T(8,128)(2,1)}, bf16[128,1536]{1,0:T(8,128)(2,1)S(1)}, u32[]{:S(2)}) copy-start(bf16[128,1536]{1,0:T(8,128)(2,1)S(1)} %collective-permute-done.7) | copy-start | bytes 1179652
  264.6 9.9 %collective-permute-start.8 = (bf16[128,1536]{1,0:T(8,128)(2,1)}, bf16[128,1536]{1,0:T(8,128)(2,1)}, u32[]{:S(2)}, u32[]{:S(2)}) collective-permute-start(bf16[128,1536]{1,0:T(8,128)(2,1)} %get-tuple-element.120), channel_id=1, source_target_pairs={{0,1},{1,0},{2,3},{3,2},{4,5},{5,4},{6,7},{7,6},{8,9},{9,8},{10,11... | collective-permute-start | bytes 1179656 | tf_op jit(solution)/shard_map/ppermute | solution.py:40
  266.1 39.4 %all-to-all-start = ((bf16[4,256,768]{2,1,0:T(8,128)(2,1)}), bf16[4,256,768]{2,1,0:T(8,128)(2,1)S(1)}, u32[]{:S(2)}, u32[]{:S(2)}) async-start(bf16[4,256,768]{2,1,0:T(8,128)(2,1)} %broadcast_in_dim.27), calls=%async_computation | async-start | bytes 3145728 | tf_op jit(solution)/shard_map/all_to_all | solution.py:72
  270.4 190.2 %all-gather.14.cloned.1.call-start = ((), (), s32[]{:S(2)}) async-start(), calls=%async_computation.9 | async-start | bytes 4227072 | tf_op jit(solution)/shard_map/all_gather | solution.py:1011
  316.2 2.0 collective-permute-start.9
  323.6 35.7 %all-to-all-start.1 = ((bf16[4,256,1024]{2,1,0:T(8,128)(2,1)}), bf16[4,256,1024]{2,1,0:T(8,128)(2,1)}, u32[]{:S(2)}, u32[]{:S(2)}) async-start(bf16[4,256,1024]{2,1,0:T(8,128)(2,1)} %broadcast_select_fusion), calls=%async_computation.1 | async-start | bytes 4194304 | tf_op jit(solution)/shard_map/all_to_all | solution.py:72
  328.3 51.3 %collective-permute-start.4 = (bf16[128,1536]{1,0:T(8,128)(2,1)S(1)}, bf16[128,1536]{1,0:T(8,128)(2,1)S(1)}, u32[]{:S(2)}, u32[]{:S(2)}) collective-permute-start(bf16[128,1536]{1,0:T(8,128)(2,1)S(1)} %copy-done.37), channel_id=1, source_target_pairs={{0,1},{1,0},{2,3},{3,2},{4,5},{5,4},{6,7},{7,6},{8,9},{9,8},{10,11... | collective-permute-start | bytes 1179656 | tf_op jit(solution)/shard_map/ppermute | solution.py:40
  352.9 34.5 %collective-permute-start.11 = (bf16[768,256]{1,0:T(8,128)(2,1)}, bf16[768,256]{1,0:T(8,128)(2,1)S(1)}, u32[]{:S(2)}, u32[]{:S(2)}) collective-permute-start(bf16[768,256]{1,0:T(8,128)(2,1)} %get-tuple-element.150), channel_id=1, source_target_pairs={{0,32},{32,0},{1,33},{33,1},{2,34},{34,2},{3,35},{35,3},{4,36},{36... | collective-permute-start | bytes 1179656 | tf_op jit(solution)/shard_map/ppermute | solution.py:40
  379.1 24.6 %collective-permute-start.10 = (bf16[768,512]{1,0:T(8,128)(2,1)}, bf16[768,512]{1,0:T(8,128)(2,1)}, u32[]{:S(2)}, u32[]{:S(2)}) collective-permute-start(bf16[768,512]{1,0:T(8,128)(2,1)} %get-tuple-element.133), channel_id=1, source_target_pairs={{0,32},{32,0},{1,33},{33,1},{2,34},{34,2},{3,35},{35,3},{4,36},{36... | collective-permute-start | bytes 2359304 | tf_op jit(solution)/shard_map/ppermute | solution.py:40
  380.4 23.3 %copy-start.19 = (bf16[768,512]{1,0:T(8,128)(2,1)S(1)}, bf16[768,512]{1,0:T(8,128)(2,1)}, u32[]{:S(2)}) copy-start(bf16[768,512]{1,0:T(8,128)(2,1)} %get-tuple-element.132) | copy-start | bytes 2359300
  382.3 58.6 %collective-permute-start.12 = (bf16[768,640]{1,0:T(8,128)(2,1)}, bf16[768,640]{1,0:T(8,128)(2,1)}, u32[]{:S(2)}, u32[]{:S(2)}) collective-permute-start(bf16[768,640]{1,0:T(8,128)(2,1)} %get-tuple-element.138), channel_id=1, source_target_pairs={{0,32},{32,0},{1,33},{33,1},{2,34},{34,2},{3,35},{35,3},{4,36},{36... | collective-permute-start | bytes 2949128 | tf_op jit(solution)/shard_map/ppermute | solution.py:40
  383.9 47.3 %all-to-all-start.4 = ((bf16[8,48,768]{2,1,0:T(8,128)(2,1)}), bf16[8,48,768]{2,1,0:T(8,128)(2,1)S(1)}, u32[]{:S(2)}, u32[]{:S(2)}) async-start(bf16[8,48,768]{2,1,0:T(8,128)(2,1)} %bitcast.148), calls=%async_computation.4 | async-start | bytes 1179648 | tf_op jit(solution)/shard_map/all_to_all | solution.py:72
  405.0 32.7 %copy-start.8 = (f32[128,1536]{1,0:T(8,128)S(1)}, f32[128,1536]{1,0:T(8,128)}, u32[]{:S(2)}) copy-start(f32[128,1536]{1,0:T(8,128)} %get-tuple-element.124) | copy-start | bytes 2359300
  432.0 25.0 %all-to-all-start.2 = ((bf16[16,48,768]{2,1,0:T(8,128)(2,1)}), bf16[16,48,768]{2,1,0:T(8,128)(2,1)S(1)}, u32[]{:S(2)}, u32[]{:S(2)}) async-start(bf16[16,48,768]{2,1,0:T(8,128)(2,1)} %pad_maximum_fusion), calls=%async_computation.2 | async-start | bytes 2359296 | tf_op jit(solution)/shard_map/all_to_all | solution.py:72
  457.0 18.1 %all-to-all-start.3 = ((bf16[16,2,24,640]{3,2,1,0:T(8,128)(2,1)}), bf16[16,2,24,640]{3,2,1,0:T(8,128)(2,1)S(1)}, u32[]{:S(2)}, u32[]{:S(2)}) async-start(bf16[16,2,24,640]{3,2,1,0:T(8,128)(2,1)} %bitcast.122), calls=%async_computation.3 | async-start | bytes 1966080 | tf_op jit(solution)/shard_map/all_to_all | solution.py:72
  475.3 6.5 %collective-permute-start.13 = (bf16[4,24,640]{2,1,0:T(8,128)(2,1)S(1)}, bf16[4,24,640]{2,1,0:T(8,128)(2,1)S(1)}, u32[]{:S(2)}, u32[]{:S(2)}) collective-permute-start(bf16[4,24,640]{2,1,0:T(8,128)(2,1)S(1)} %fusion.32), channel_id=1, source_target_pairs={{0,64},{64,0},{1,65},{65,1},{2,66},{66,2},{3,67},{67,3},{4,68},{68... | collective-permute-start | bytes 368648 | tf_op jit(solution)/shard_map/ppermute | solution.py:40
  (31 other events, 246.2 us)
Sparse Core Ops, SparseCore 0:
  11.4 88.7 all-gather.5
  103.0 62.5 all-gather.7
  167.8 62.4 all-gather.9
  245.1 73.2 all-gather.11
  322.0 74.4 all-gather.13

commit v3 on v2

--- a/solution.py
+++ b/solution.py
@@ -60,14 +60,6 @@
     return values * inverse_rms(values)
 
 
-def norm_backward(grad, gain, values):
-    inverse = inverse_rms(values)
-    normed = values * inverse
-    scaled = grad * gain
-    grad_gain = jnp.sum(grad * normed, axis=0)
-    return inverse * (scaled - normed * mean_last(scaled * normed)), grad_gain
-
-
 def exchanged(tiles, axes):
     return lax.all_to_all(tiles, axes, 0, 0, tiled=True)
 
@@ -81,10 +73,6 @@
 
 VMEM_LIMIT = 56 * 1024 * 1024
 SHORT = pl.CostEstimate(flops=1, bytes_accessed=1, transcendentals=0)
-
-
-def whole_lanes(columns):
-    return -(-columns // 128) * 128
 
 
 def ordered(kernel, count):
@@ -248,7 +236,7 @@
     )(core, *behind, rows, *saved, pair, down)
 
 
-def part_forward_kernel(rows_ref, pair_ref, kept_ref):
+def part_forward_kernel(behind_ref, rows_ref, pair_ref, kept_ref):
     both = product(rows_ref[...], pair_ref[...])
     units = both.shape[1] // 2
     gate, up = both[:, :units], both[:, units:]
@@ -259,7 +247,7 @@
     kept_ref[:, 2 * units :] = (silu * up).astype(BF16)
 
 
-def part_forward_call(rows, pair):
+def part_forward_call(behind, rows, pair):
     tokens, width = rows.shape
     units = pair.shape[1] // 2
     tile = 1024
@@ -267,22 +255,23 @@
         part_forward_kernel,
         grid=(tokens // tile,),
         in_specs=[
+            pl.BlockSpec(memory_space=pl.ANY),
             pl.BlockSpec((tile, width), lambda i: (i, 0)),
             pl.BlockSpec((width, 2 * units), lambda i: (0, 0)),
         ],
         out_specs=pl.BlockSpec((tile, 3 * units), lambda i: (i, 0)),
         out_shape=jax.ShapeDtypeStruct((tokens, 3 * units), BF16),
         compiler_params=pltpu.CompilerParams(vmem_limit_bytes=VMEM_LIMIT),
-        cost_estimate=SHORT,
-    )(rows, pair)
-
-
-def pair_out(acc_ref, here, mine_ref, other_ref, runs):
-    span = mine_ref.shape[0] // runs
-    for k in range(runs):
-        for ref, half in ((mine_ref, here), (other_ref, 1 - here)):
-            start = pl.multiple_of((2 * k + half) * span, span)
-            ref[k * span : (k + 1) * span] = acc_ref[pl.ds(start, span)].astype(BF16)
+        cost_estimate=pl.CostEstimate(
+            flops=8 * tokens * width * units, bytes_accessed=2 * tokens * width, transcendentals=0
+        ),
+    )(behind, rows, pair)
+
+
+def pair_out(acc_ref, here, mine_ref, other_ref):
+    rows = mine_ref.shape[0]
+    for ref, half in ((mine_ref, here), (other_ref, 1 - here)):
+        ref[...] = acc_ref[pl.ds(pl.multiple_of(half * rows, rows), rows)].astype(BF16)
 
 
 def accumulated(acc_ref, part, finish):
@@ -309,7 +298,7 @@
     accumulated(
         acc_ref,
         product_left(grad, kept_ref[:, 2 * units :]),
-        lambda: pair_out(acc_ref, here_ref[0], mine_ref, other_ref, 1),
+        lambda: pair_out(acc_ref, here_ref[0], mine_ref, other_ref),
     )
 
 
@@ -317,7 +306,7 @@
     accumulated(
         acc_ref,
         product_left(rows_ref[...], pair_ref[...]),
-        lambda: pair_out(acc_ref, here_ref[0], mine_ref, other_ref, 1),
+        lambda: pair_out(acc_ref, here_ref[0], mine_ref, other_ref),
     )
 
 
@@ -345,12 +334,19 @@
     )(here, *behind, *operands, *fixed)
 
 
-def part_down_call(here, grad, kept, down):
+def part_down_call(here, grad, kept, down, behind):
     tokens, width = grad.shape
     units = down.shape[0]
     flops = 4 * tokens * width * units
     return part_call(
-        part_down_kernel, here, (grad, kept), (down,), (2 * units,), (width, units), flops
+        part_down_kernel,
+        here,
+        (grad, kept),
+        (down,),
+        (2 * units,),
+        (width, units),
+        flops,
+        behind,
     )
 
 
@@ -360,6 +356,38 @@
     return part_call(
         part_pair_kernel, here, (inner, pair), (), (), (width, columns), flops, behind
     )
+
+
+def back_join_kernel(
+    behind_ref, mine_ref, come_ref, values_ref, base_ref, gain_ref, wide_ref, low_ref, sums_ref
+):
+    grad = mine_ref[...] + come_ref[...].astype(F32)
+    values = values_ref[...]
+    inverse = inverse_rms(values)
+    normed = values * inverse
+    scaled = grad * gain_ref[...]
+    sums_ref[...] = jnp.sum(grad * normed, axis=0, keepdims=True)
+    total = base_ref[...] + inverse * (scaled - normed * mean_last(scaled * normed))
+    wide_ref[...] = total
+    low_ref[...] = total.astype(BF16)
+
+
+def back_join_call(behind, mine, come, values, base, gain):
+    vmem = pl.BlockSpec(memory_space=pltpu.VMEM)
+    shape = values.shape
+    wide, low, sums = pl.pallas_call(
+        back_join_kernel,
+        in_specs=[pl.BlockSpec(memory_space=pl.ANY), *[vmem] * 5],
+        out_specs=[vmem] * 3,
+        out_shape=[
+            jax.ShapeDtypeStruct(shape, F32),
+            jax.ShapeDtypeStruct(shape, BF16),
+            jax.ShapeDtypeStruct((1, shape[1]), F32),
+        ],
+        compiler_params=pltpu.CompilerParams(vmem_limit_bytes=VMEM_LIMIT),
+        cost_estimate=SHORT,
+    )(behind, mine, come, values, base, gain[None])
+    return wide, low, sums[0]
 
 
 def section_sums_kernel(behind_ref, all_ref, sums_ref):
@@ -381,36 +409,68 @@
 
 
 def mixer_grads_kernel(
-    here_ref, columns_ref, normed_ref, gated_ref, out_ref, mine_ref, other_ref, acc_ref
+    places_ref, columns_ref, mix_ref, early_ref, late_ref, mine_ref, other_ref,
+    normed_ref, in_ref, out_ref, sems,
 ):
-    mix = out_ref.shape[0]
-    out_ref[...] = product_left(columns_ref[:, :mix], gated_ref[...]).astype(BF16)
-    acc_ref[...] = product_left(normed_ref[...], columns_ref[:, mix:])
-    pair_out(acc_ref, here_ref[0], mine_ref, other_ref, 2)
-
-
-def mixer_grads_call(here, columns, normed, gated, mix, behind):
-    vmem = pl.BlockSpec(memory_space=pltpu.VMEM)
-    tokens, width = normed.shape
-    size = columns.shape[1] - mix
-    channels = gated.shape[1]
+    count, rows = sems.shape[0], normed_ref.shape[0] // sems.shape[0]
+    here, section, z = places_ref[0], places_ref[1], places_ref[2]
+
+    def copies(all_ref):
+        span = all_ref.shape[0] // count
+        return [
+            pltpu.make_async_copy(
+                all_ref.at[pl.ds(pl.multiple_of(k * span + z * rows, rows), rows)],
+                normed_ref.at[pl.ds(k * rows, rows)],
+                sems.at[k],
+            )
+            for k in range(count)
+        ]
+
+    @pl.when(section == 0)
+    def _():
+        load_all(copies(early_ref))
+
+    @pl.when(section > 0)
+    def _():
+        load_all(copies(late_ref))
+
+    out_columns = columns_ref.shape[1] // 4
+    split = columns_ref.shape[1] - out_columns
+    out_ref[...] = product_left(mix_ref[...], columns_ref[:, split:])
+    for copy in copies(early_ref):
+        copy.wait()
+    in_ref[...] = product_left(normed_ref[...], columns_ref[:, :split])
+    plane, block, _ = mine_ref.shape
+    short = block // 2
+    for ref, half in ((mine_ref, here), (other_ref, 1 - here)):
+        for k in range(plane):
+            for s in range(2):
+                start = pl.multiple_of(((2 * s + half) * plane + k) * short, short)
+                rows_in = in_ref[pl.ds(start, short)]
+                ref[k, s * short : (s + 1) * short, :split] = rows_in.astype(BF16)
+            start = pl.multiple_of((half * plane + k) * block, block)
+            ref[k, :, split:] = out_ref[pl.ds(start, block)].astype(BF16)
+
+
+def mixer_grads_call(places, columns, mix, early, late, plane):
+    vmem, any_space = pl.BlockSpec(memory_space=pltpu.VMEM), pl.BlockSpec(memory_space=pl.ANY)
+    tokens, width = mix.shape
+    size = columns.shape[1]
+    half = jax.ShapeDtypeStruct((plane, width // (2 * plane), size), BF16)
     return pl.pallas_call(
-        ordered(mixer_grads_kernel, len(behind)),
-        in_specs=[
-            pl.BlockSpec(memory_space=pltpu.SMEM),
-            *[pl.BlockSpec(memory_space=pl.ANY)] * len(behind),
-            *[vmem] * 3,
+        mixer_grads_kernel,
+        in_specs=[pl.BlockSpec(memory_space=pltpu.SMEM), vmem, vmem, any_space, any_space],
+        out_specs=[vmem] * 2,
+        out_shape=[half, half],
+        scratch_shapes=[
+            pltpu.VMEM((tokens, width), BF16),
+            pltpu.VMEM((width, size - size // 4), F32),
+            pltpu.VMEM((width, size // 4), F32),
+            pltpu.SemaphoreType.DMA((4,)),
         ],
-        out_specs=[vmem] * 3,
-        out_shape=[
-            jax.ShapeDtypeStruct((mix, channels), BF16),
-            jax.ShapeDtypeStruct((width // 2, size), BF16),
-            jax.ShapeDtypeStruct((width // 2, size), BF16),
-        ],
-        scratch_shapes=[pltpu.VMEM((width, size), F32)],
         compiler_params=pltpu.CompilerParams(vmem_limit_bytes=VMEM_LIMIT),
         cost_estimate=SHORT,
-    )(here, *behind, columns, normed, gated)
+    )(places, columns, mix, early, late)
 
 
 def load_all(copies):
@@ -478,22 +538,20 @@
     rows_out(acc_ref, core_ref[0], mine_ref, other_ref)
 
 
-def tiles_out(tiles_ref, grad_mix, columns):
-    count, _, size = tiles_ref.shape
-    width = grad_mix.shape[1] // 2
-    step = width // count
+def tiles_out(tiles_ref, gated_ref, columns):
+    count, rows, size = tiles_ref.shape
+    step = gated_ref.shape[1] // count
     for k in range(count):
-        here = slice(k * step, (k + 1) * step)
-        parts = [grad_mix[:, :width][:, here], grad_mix[:, width:][:, here], columns(k)]
-        spare = size - sum(part.shape[1] for part in parts)
+        parts = [columns(k)]
+        spare = size - parts[0].shape[1] - step
         if spare:
-            parts.append(jnp.zeros((grad_mix.shape[0], spare), BF16))
-        tiles_ref[k] = jnp.concatenate(parts, axis=1)
+            parts.append(jnp.zeros((rows, spare), BF16))
+        tiles_ref[k] = jnp.concatenate([*parts, gated_ref[:, k * step : (k + 1) * step]], axis=1)
 
 
 def conv_backward_kernel(
-    core_ref, grad_ref, kernel_ref, masks_ref, proj_ref, whole_ref, out_ref,
-    tiles_ref, taps_ref, mine_ref, other_ref, in_buf, out_buf, acc_ref, sems,
+    core_ref, grad_ref, kernel_ref, masks_ref, proj_ref, gated_ref, other_tiles_ref,
+    whole_ref, out_ref, tiles_ref, taps_ref, mine_ref, other_ref, in_buf, out_buf, acc_ref, sems,
 ):
     copies, last = weight_copies(whole_ref, out_ref, in_buf, out_buf, sems, 0)
     load_all([last, *copies])
@@ -522,11 +580,19 @@
             grads[k].append(value.astype(BF16))
     grads = [in_time(jnp.concatenate(g, axis=1)) for g in grads]
     step = grads[0].shape[1] // tiles_ref.shape[0]
-    tiles_out(
-        tiles_ref,
-        grad_ref[...],
-        lambda k: jnp.concatenate([g[:, k * step : (k + 1) * step] for g in grads], axis=1),
-    )
+
+    @pl.when(core_ref[1] == 0)
+    def _():
+        tiles_out(
+            tiles_ref,
+            gated_ref,
+            lambda k: jnp.concatenate([g[:, k * step : (k + 1) * step] for g in grads], axis=1),
+        )
+
+    @pl.when(core_ref[1] > 0)
+    def _():
+        tiles_ref[...] = other_tiles_ref[...]
+
     for k, copy in enumerate(copies):
         copy.wait()
         part = product_right(grads[k], in_buf[k])
@@ -618,8 +684,8 @@
 
 
 def attention_backward_kernel(
-    core_ref, grad_ref, gains_ref, tables_ref, mask_ref, qkv_ref, ready_ref, whole_ref, out_ref,
-    tiles_ref, heads_ref, mine_ref, other_ref,
+    core_ref, grad_ref, gains_ref, tables_ref, mask_ref, qkv_ref, ready_ref, gated_ref,
+    whole_ref, out_ref, tiles_ref, heads_ref, mine_ref, other_ref,
     in_buf, out_buf, acc_ref, attended_ref, ready_grad_ref, proj_ref, sems,
 ):
     copies, last = weight_copies(
@@ -681,22 +747,21 @@
             raw = jnp.where(low, raw, grad)
         proj_ref[:, lanes] = raw.astype(BF16)
     step = width // tiles_ref.shape[0]
-    tiles_out(tiles_ref, grad_ref[...], lambda k: proj_ref[:, k * step : (k + 1) * step])
+    tiles_out(tiles_ref, gated_ref, lambda k: proj_ref[:, k * step : (k + 1) * step])
     copies[0].wait()
     acc_ref[...] = product_right(proj_ref[...], in_buf[0])
     rows_out(acc_ref, core_ref[0], mine_ref, other_ref)
 
 
-def mixer_call(kernel, core, operands, whole, weight_out, in_tiles, outs, scratch=(), behind=()):
+def mixer_call(kernel, core, operands, whole, weight_out, in_tiles, outs, scratch=()):
     vmem, any_space = pl.BlockSpec(memory_space=pltpu.VMEM), pl.BlockSpec(memory_space=pl.ANY)
     rows, width = operands[0].shape
     channels = weight_out.shape[0]
     outs = [*outs, ((rows // 2, width), F32), ((rows // 2, width), BF16)]
     return pl.pallas_call(
-        ordered(kernel, len(behind)),
+        kernel,
         in_specs=[
             pl.BlockSpec(memory_space=pltpu.SMEM),
-            *[any_space] * len(behind),
             *[vmem] * len(operands),
             any_space,
             any_space,
@@ -712,7 +777,7 @@
         ],
         compiler_params=pltpu.CompilerParams(vmem_limit_bytes=VMEM_LIMIT),
         cost_estimate=SHORT,
-    )(core, *behind, *operands, whole, weight_out)
+    )(core, *operands, whole, weight_out)
 
 
 def conv_forward_call(core, rows, kernel, masks, whole, weight_out):
@@ -724,16 +789,16 @@
     )
 
 
-def conv_backward_call(core, grad, kernel, masks, projected, whole, weight_out, behind):
+def conv_backward_call(core, grad, kernel, masks, projected, gated, tiles, whole, weight_out):
     count, width = grad.shape
     taps, channels = kernel.shape
     outs = [
-        ((4, count, whole_lanes((width + 3 * channels) // 4)), BF16),
+        (tiles.shape, BF16),
         ((taps, channels), F32),
     ]
-    operands = (grad, kernel, masks, projected)
+    operands = (grad, kernel, masks, projected, gated, tiles)
     return mixer_call(
-        conv_backward_kernel, core, operands, whole, weight_out, (3, channels), outs, (), behind
+        conv_backward_kernel, core, operands, whole, weight_out, (3, channels), outs
     )
 
 
@@ -746,11 +811,13 @@
     )
 
 
-def attention_backward_call(core, grad, gains, tables, mask, qkv, ready, whole, weight_out):
+def attention_backward_call(
+    core, grad, gains, tables, mask, qkv, ready, gated, whole, weight_out
+):
     count, width = grad.shape
     channels, qkv_width = weight_out.shape[0], qkv.shape[1]
     outs = [
-        ((4, count, whole_lanes((width + 3 * channels) // 4)), BF16),
+        ((4, count, channels), BF16),
         ((qkv_width // 128, 128), F32),
     ]
     scratch = [
@@ -758,7 +825,7 @@
         pltpu.VMEM((count, qkv_width), F32),
         pltpu.VMEM((count, qkv_width), BF16),
     ]
-    operands = (grad, gains, tables, mask, qkv, ready)
+    operands = (grad, gains, tables, mask, qkv, ready, gated)
     return mixer_call(
         attention_backward_kernel, core, operands, whole, weight_out, (1, qkv_width), outs, scratch
     )
@@ -834,8 +901,9 @@
     part = hidden_units // plane
     in_width = 3 * channels
     qkv_width = attn_qkv.shape[1]
-    core_scalar = core.astype(jnp.int32)[None]
-    xl_scalar = xl.astype(jnp.int32)[None]
+    z = lax.axis_index("z")
+    core_scalar = jnp.stack([core, section]).astype(jnp.int32)
+    xl_scalar = jnp.stack([xl, section, z]).astype(jnp.int32)
 
     def chosen(from_first, from_second):
         return jnp.where(first, from_first, from_second)
@@ -879,16 +947,15 @@
         )
         return hidden + joined(mine, other), (inner_own, gate, up)
 
-    def feed_forward_back(grad_full, grad, hidden, saved):
+    def feed_forward_back(grad_full, grad, hidden, saved, behind=()):
         mine, other = feed_forward_call(
-            True, core_scalar, grad_full, weight_pair, weight_down, saved[1:]
+            True, core_scalar, grad_full, weight_pair, weight_down, saved[1:], behind
         )
-        back, grad_gain = norm_backward(joined(mine, other), gains[1], hidden)
-        return grad + back, grad_gain
-
-    def mixer_back(grad_hidden, mine, other, layer_in):
-        back, grad_gain = norm_backward(joined(mine, other), gains[0], layer_in)
-        return (grad_hidden + back).astype(BF16), grad_gain
+        return back_join_call(core_scalar, mine, swapped(other, "c"), hidden, grad, gains[1])
+
+    def mixer_back(grad_hidden, mine, other, layer_in, behind):
+        come = swapped(other, "c")
+        return back_join_call(behind, mine, come, layer_in, grad_hidden, gains[0])[1:]
 
     plane_axes = ("y", "z", "c")
     early = gathered(chosen(normed_own_0, out_cotangent), plane_axes)
@@ -911,62 +978,54 @@
 
     inner_all = gathered(chosen(ffn_0[0], ffn_1[0]), plane_axes)
 
-    grad_hidden_1, gain_inner_1 = feed_forward_back(
+    grad_hidden_1, grad_mix_1, gain_inner_1 = feed_forward_back(
         cotangent_1, out_cotangent.astype(F32), hidden_1, ffn_1
     )
     tiles_1, head_sums, mine, other = attention_backward_call(
         core_scalar,
-        spread(grad_hidden_1.astype(BF16)),
+        spread(grad_mix_1),
         head_gains,
         tables,
         mask,
         qkv,
         ready,
+        gated_1,
         whole,
         weight_out,
     )
-    input_grad_1, gain_outer_1 = mixer_back(grad_hidden_1, mine, other, second_in)
+    input_grad_1, gain_outer_1 = mixer_back(grad_hidden_1, mine, other, second_in, core_scalar)
 
     cotangent = lax.ppermute(input_grad_1, "xh", [(1, 0)])
     late = gathered(chosen(cotangent, normed_own_1), plane_axes)
-    gated = chosen(gated_0, gated_1)
-    gated_y = exchanged(jnp.broadcast_to(gated, (4, *gated.shape)), "y").reshape(4 * rows, -1)
-    grad_hidden_0, gain_inner_0 = feed_forward_back(
+    grad_hidden_0, grad_mix_0, gain_inner_0 = feed_forward_back(
         spread(cotangent), cotangent.astype(F32), hidden_0, ffn_0
     )
-    tiles_0, grad_kernel, mine, other = conv_backward_call(
+    mix_y = gathered(chosen(grad_mix_0, grad_mix_1), ("y", "c"))
+    tiles, grad_kernel, mine, other = conv_backward_call(
         core_scalar,
-        spread(grad_hidden_0.astype(BF16)),
+        spread(grad_mix_0),
         kernel,
         masks,
         projected,
+        gated_0,
+        tiles_1,
         whole,
         weight_out,
-        (gated_y,),
-    )
-    input_grad_0, gain_outer_0 = mixer_back(grad_hidden_0, mine, other, first_in)
+    )
+    columns = exchanged(tiles, "y").reshape(4 * rows, -1)
+    part_kept = part_forward_call(tiles, inner_all, part_pair)
 
     def summed_over_pair(mine, other):
         return mine.astype(F32) + swapped(other, "xl").astype(F32)
 
-    columns = exchanged(chosen(tiles_0, tiles_1), "y").reshape(4 * rows, -1)
-    z = lax.axis_index("z")
-    along_y = [
-        lax.dynamic_index_in_dim(a.reshape(4, 4, rows, width), z, 1, keepdims=False)
-        for a in (early, late)
-    ]
-    normed_y = chosen(*along_y).reshape(4 * rows, width)
-
-    part_kept = part_forward_call(inner_all, part_pair)
     pair_grads, down_mine, down_other = lax.cond(
         first,
-        lambda: part_down_call(xl_scalar, late, part_kept, part_down),
-        lambda: part_down_call(xl_scalar, early, part_kept, part_down),
-    )
-    out_parts, in_mine, in_other = mixer_grads_call(
-        xl_scalar, columns, normed_y, gated_y, width // 4, (pair_grads,)
-    )
-    pair_mine, pair_other = part_pair_call(xl_scalar, inner_all, pair_grads, (in_mine,))
+        lambda: part_down_call(xl_scalar, late, part_kept, part_down, (columns,)),
+        lambda: part_down_call(xl_scalar, early, part_kept, part_down, (columns,)),
+    )
+    input_grad_0, gain_outer_0 = mixer_back(grad_hidden_0, mine, other, first_in, pair_grads)
+    pair_mine, pair_other = part_pair_call(xl_scalar, inner_all, pair_grads, ())
+    mix_mine, mix_other = mixer_grads_call(xl_scalar, columns, mix_y, early, late, plane)
 
     total = [summed_over_pair(pair_mine, pair_other), summed_over_pair(down_mine, down_other)]
     total = jnp.concatenate(total, axis=1).astype(BF16)
@@ -980,20 +1039,19 @@
     grad_gate_up = jnp.stack(lines[:2])[None]
     grad_down = lines[2].T[None]
 
-    total = summed_over_pair(in_mine, in_other).astype(BF16)
-    total = total.reshape(2, plane, -1, total.shape[1])
-    come = exchanged(jnp.moveaxis(total, 1, 0), PLANE)
+    total = summed_over_pair(mix_mine, mix_other).astype(BF16)
+    come = exchanged(total, PLANE)
     lines = come.reshape(4, 4, *come.shape[1:]).astype(F32).sum(1)
+    split = in_width // 4
+    grad_mixer_out = lines[:, :, split:].transpose(0, 2, 1).reshape(1, channels, -1)
+    lines = lines[:, :, :split].reshape(4, 2, -1, split)
     kept_lines = lax.dynamic_index_in_dim(lines, section, 1, keepdims=False)
     sent_lines = lax.dynamic_index_in_dim(lines, 1 - section, 1, keepdims=False)
     come = swapped(sent_lines.astype(BF16), "xh").astype(F32)
-    lines = chosen(kept_lines, come)[:, :, : in_width // 4].reshape(4, -1, 3, channels // 4)
+    lines = chosen(kept_lines, come).reshape(4, -1, 3, channels // 4)
     grad_conv_in = jnp.moveaxis(lines, 0, 2).reshape(conv_in.shape)
     lines = chosen(come, kept_lines)[:, :, : qkv_width // 4]
     grad_attn_qkv = jnp.moveaxis(lines, 0, 1).reshape(attn_qkv.shape)
-
-    out_parts = exchanged(out_parts.reshape(8, -1, channels), ("xl", "z"))
-    grad_mixer_out = out_parts.astype(F32).sum(0).T[None]
 
     full_kernel = lax.dynamic_update_slice(
         jnp.zeros(conv_kernel.shape, F32), grad_kernel, (0, core * channels)

time: 498 us -> 470 us (0.944)
  waiting for transfers between devices: 181 us -> 159 us
  other arithmetic: 52 us -> 33.4 us
  Pallas kernels: 157 us -> 174 us
  starting transfers between devices: 33.5 us -> 27.5 us
    all_to_all x5 -> x3, waiting for transfers between devices: 67.9 us -> 25.1 us  [exchanged(): return lax.all_to_all(tiles, axes, 0, 0, tiled=True)]
    ppermute x12, waiting for transfers between devices: 27.1 us -> 48 us  [swapped(): return lax.ppermute(shard, axis, [(0, 1), (1, 0)])]
    pallas_call x5 -> x9, Pallas kernels: 51 us -> 67.1 us  [the longest x4 44.4 us: mixer_call(): pl.pallas_call(kernel, in_specs=[pl.BlockSpec(memory_space=pltpu.SMEM), *...]
    reduce_sum x5 -> x0, other arithmetic: 9.03 us -> none  [the longest x4 8.29 us: norm_backward(): grad_gain = jnp.sum(grad * normed, axis=0)]
    all_to_all x5 -> x3, starting transfers between devices: 21.8 us -> 14 us  [exchanged(): return lax.all_to_all(tiles, axes, 0, 0, tiled=True)]
    select_n x11 -> x9, other arithmetic: 16.5 us -> 10.1 us  [chosen(): return jnp.where(first, from_first, from_second)]
    all_gather x4 -> x5, waiting for transfers between devices: 64.4 us -> 64.1 us  [gathered(): return lax.all_gather(own, axes, tiled=True)]
  transfers between devices with their start and end apart: 24 -> 23, of which waited for: 15 -> 14; matrix products, arithmetic and copies ran while one was open for 15% -> 11% of each run, Pallas kernels for 32% -> 37%
where the time goes in v3:
time: 470 us; the launch traced here: 462 us
  Pallas kernels  174 us (37%)
  waiting for transfers between devices  159 us (34%)
  other arithmetic  33.4 us (7%)
  local copies, waits for them, and re-layouts  27.8 us (6%)
  starting transfers between devices  27.5 us (6%)
  blocking collectives  25.3 us (5%)
  between operations  15 us (3%)
    pallas_call x4, Pallas kernels, feed_forward_call(): pl.pallas_call(ordered(body, len(behind)), in_specs=in_specs, out_specs=o...  66.5 us
    all_gather x5, waiting for transfers between devices, gathered(): return lax.all_gather(own, axes, tiled=True)  64.1 us
    ppermute x12, waiting for transfers between devices, swapped(): return lax.ppermute(shard, axis, [(0, 1), (1, 0)])  48 us
    pallas_call x4, Pallas kernels, mixer_call(): pl.pallas_call(kernel, in_specs=[pl.BlockSpec(memory_space=pltpu.SMEM), *...  44.4 us
    pallas_call x2, Pallas kernels, part_call(): pl.pallas_call(ordered(kernel, len(behind)), grid_spec=pltpu.PrefetchScal...  25.3 us
    all_gather x8, blocking collectives, spread(): return lax.all_gather(own, 'c', tiled=True)  25.3 us
    all_to_all x3, waiting for transfers between devices, exchanged(): return lax.all_to_all(tiles, axes, 0, 0, tiled=True)  25.1 us
    all_to_all x3, starting transfers between devices, exchanged(): return lax.all_to_all(tiles, axes, 0, 0, tiled=True)  14 us
  transfers between devices with their start and end apart: 23, of which 14 were waited for; matrix products, arithmetic and copies ran while one was open for 11% of the time, Pallas kernels for 37%

profile of v3, /device:TPU:0, one launch (start us, length us, event | category | flops | bytes accessed | tf_op | source)
XLA Modules:
  0.0 462.5 jit_solution(8251393080478092995)
XLA Ops:
  25.8 8.1 %fusion.15 = (bf16[1,1,1536,3456]{3,2,1,0:T(8,128)(2,1)S(1)}, bf16[1,1,1536,3456]{3,2,1,0:T(8,128)(2,1)S(1)}) fusion(bf16[1,2,1536,3456]{3,2,1,0:T(8,128)(2,1)} %param.22), kind=kLoop, calls=%fused_computation.97 | loop fusion | bytes 42467328 | tf_op jit(solution)/shard_map/slice | solution.py:923
  36.1 64.1 %all-gather.7.cloned.1.call-done.whole_ref = bf16[1536,3584]{1,0:T(8,128)(2,1)} async-done(((bf16[24,3584]{1,0:T(8,128)(2,1)}), bf16[1536,3584]{1,0:T(8,128)(2,1)}) %all-gather.7.cloned.1.call-update) | async-done | bytes 11010064 | tf_op jit(solution)/shard_map/all_gather | solution.py:912
  100.9 8.1 %shard_map.186 = (bf16[3,256,768]{2,1,0:T(8,128)(2,1)}, bf16[256,768]{1,0:T(8,128)(2,1)}, f32[128,1536]{1,0:T(8,128)}, bf16[128,1536]{1,0:T(8,128)(2,1)}) custom-call(s32[2]{0:T(128)} %pad_add_fusion.core_ref.scalar_ref.behind_ref, bf16[256,1536]{1,0:T(8,128)(2,1)} %all_gather.43.rows_ref, f32[3,768]{1,0:T(4,128)} %dynamic-slice_convert_fusion.1.kernel_ref, ...), custom_call_target="tpu_custom_call" | custom-call | flops 1 | bytes 1 | tf_op jit(solution)/shard_map/pallas_call | solution.py:761
  115.3 16.3 %shard_map.187 = (bf16[256,3456]{1,0:T(8,128)(2,1)}, bf16[256,3456]{1,0:T(8,128)(2,1)}, f32[128,1536]{1,0:T(8,128)}, bf16[128,1536]{1,0:T(8,128)(2,1)}) custom-call(s32[2]{0:T(128)} %pad_add_fusion.core_ref.scalar_ref.behind_ref, bf16[256,1536]{1,0:T(8,128)(2,1)} %all_gather.45.refs_0_, bf16[2,1536,3456]{2,1,0:T(8,128)(2,1)} %bitcast.100, ...), custom_call_target="tpu_custom_call" | custom-call | flops 1 | bytes 1 | tf_op jit(solution)/shard_map/pallas_call | solution.py:228
  135.0 4.9 %collective-permute-start.2 = (bf16[128,1536]{1,0:T(8,128)(2,1)S(1)}, bf16[128,1536]{1,0:T(8,128)(2,1)S(1)}, u32[]{:S(2)}, u32[]{:S(2)}) collective-permute-start(bf16[128,1536]{1,0:T(8,128)(2,1)S(1)} %add_convert_fusion.3), channel_id=1, source_target_pairs={{0,64},{1,65},{2,66},{3,67},{4,68},{5,69},{6,70},{7,71},{8,72},{9,... | collective-permute-start | bytes 1179656 | tf_op jit(solution)/shard_map/ppermute | solution.py:970
  139.9 8.7 %collective-permute-done.2 = bf16[128,1536]{1,0:T(8,128)(2,1)S(1)} collective-permute-done((bf16[128,1536]{1,0:T(8,128)(2,1)S(1)}, bf16[128,1536]{1,0:T(8,128)(2,1)S(1)}, u32[]{:S(2)}, u32[]{:S(2)}) %collective-permute-start.2) | collective-permute-done | bytes 393248 | tf_op jit(solution)/shard_map/ppermute | solution.py:970
  151.4 10.6 %shard_map.188 = (f32[256,1280]{1,0:T(8,128)}, bf16[256,1280]{1,0:T(8,128)(2,1)}, bf16[256,768]{1,0:T(8,128)(2,1)}, f32[128,1536]{1,0:T(8,128)}, bf16[128,1536]{1,0:T(8,128)(2,1)}) custom-call(s32[2]{0:T(128)} %pad_add_fusion.core_ref.scalar_ref.behind_ref, bf16[256,1536]{1,0:T(8,128)(2,1)} %all_gather.46.rows_ref, f32[9,128]{1,0:T(8,128)} %stack.89.gains_ref, ...), custom_call_target="tpu_custom_call" | custom-call | flops 1 | bytes 1 | tf_op jit(solution)/shard_map/pallas_call | solution.py:761
  166.7 4.8 %all_gather.48.refs_1_ = bf16[256,1536]{1,0:T(8,128)(2,1)} all-gather(bf16[128,1536]{1,0:T(8,128)(2,1)} %get-tuple-element.193), channel_id=1, replica_groups=mesh['xh'=2,'xl'=2,'y'=4,'z'=4,'c'=2] {'c'}, dimensions={0}, use_global_device_ids=true | all-gather | bytes 1179648 | tf_op jit(solution)/shard_map/all_gather | solution.py:44
  171.5 16.4 %shard_map.189 = (bf16[256,3456]{1,0:T(8,128)(2,1)}, bf16[256,3456]{1,0:T(8,128)(2,1)}, f32[128,1536]{1,0:T(8,128)}, bf16[128,1536]{1,0:T(8,128)(2,1)}) custom-call(s32[2]{0:T(128)} %pad_add_fusion.core_ref.scalar_ref.behind_ref, bf16[4096,1536]{1,0:T(8,128)(2,1)} %all-gather.9.cloned.1.call-done.refs_0_.early_ref, bf16[256,1536]{1,0:T(8,128)(2,1)} %all_gather.48.refs_1_, ...), custom_call_target="tpu_custom_call" | custom-call | flops 1 | bytes 1 | tf_op jit(solution)/shard_map/pallas_call | solution.py:228
  187.9 17.0 %shard_map.190 = (f32[128,1536]{1,0:T(8,128)}, bf16[128,1536]{1,0:T(8,128)(2,1)}) custom-call(s32[2]{0:T(128)} %pad_add_fusion.core_ref.scalar_ref.behind_ref, bf16[256,1536]{1,0:T(8,128)(2,1)} %all_gather.44.refs_0_, bf16[256,3456]{1,0:T(8,128)(2,1)} %get-tuple-element.124.refs_1_, bf16[256,3456]{1,0:T(8,128)(2,1)} %get-tuple-element.125.refs_2_, ...), custom_call_target="tpu_custom_call" | custom-call | flops 1 | bytes 1 | tf_op jit(solution)/shard_map/pallas_call | solution.py:228
  208.1 3.3 shard_map.191
  211.4 4.5 all_gather.49.grad_ref
  215.9 15.1 %shard_map.192 = (bf16[4,256,768]{2,1,0:T(8,128)(2,1)}, f32[10,128]{1,0:T(8,128)}, f32[128,1536]{1,0:T(8,128)}, bf16[128,1536]{1,0:T(8,128)(2,1)}) custom-call(s32[2]{0:T(128)} %pad_add_fusion.core_ref.scalar_ref.behind_ref, bf16[256,1536]{1,0:T(8,128)(2,1)} %all_gather.49.grad_ref, f32[9,128]{1,0:T(8,128)} %stack.89.gains_ref, f32[2,256,128]{2,1,0:T(8,128)} %bitcast.118, ...), custom_call_target="tpu_custom_call" | custom-call | flops 1 | bytes 1 | tf_op jit(solution)/shard_map/pallas_call | solution.py:761
  233.8 3.2 shard_map.193
  238.3 13.5 %collective-permute-done.7 = bf16[128,1536]{1,0:T(8,128)(2,1)S(1)} collective-permute-done((bf16[128,1536]{1,0:T(8,128)(2,1)}, bf16[128,1536]{1,0:T(8,128)(2,1)S(1)}, u32[]{:S(2)}, u32[]{:S(2)}) %collective-permute-start.7) | collective-permute-done | bytes 393248 | tf_op jit(solution)/shard_map/ppermute | solution.py:998
  255.8 16.7 %shard_map.194 = (f32[128,1536]{1,0:T(8,128)}, bf16[128,1536]{1,0:T(8,128)(2,1)}) custom-call(s32[2]{0:T(128)} %pad_add_fusion.core_ref.scalar_ref.behind_ref, bf16[256,1536]{1,0:T(8,128)(2,1)} %all_gather.50.refs_0_, bf16[256,3456]{1,0:T(8,128)(2,1)} %get-tuple-element.136.refs_1_, bf16[256,3456]{1,0:T(8,128)(2,1)} %get-tuple-element.137.refs_2_, ...), custom_call_target="tpu_custom_call" | custom-call | flops 1 | bytes 1 | tf_op jit(solution)/shard_map/pallas_call | solution.py:228
  275.3 3.2 shard_map.195
  284.7 10.5 %shard_map.196 = (bf16[4,256,768]{2,1,0:T(8,128)(2,1)}, f32[3,768]{1,0:T(4,128)}, f32[128,1536]{1,0:T(8,128)}, bf16[128,1536]{1,0:T(8,128)(2,1)}) custom-call(s32[2]{0:T(128)} %pad_add_fusion.core_ref.scalar_ref.behind_ref, bf16[256,1536]{1,0:T(8,128)(2,1)} %all_gather.51.grad_ref, f32[3,768]{1,0:T(4,128)} %dynamic-slice_convert_fusion.1.kernel_ref, ...), custom_call_target="tpu_custom_call" | custom-call | flops 1 | bytes 1 | tf_op jit(solution)/shard_map/pallas_call | solution.py:761
  295.2 4.4 all-to-all-start
  299.8 12.1 %shard_map.197 = bf16[4096,768]{1,0:T(8,128)(2,1)} custom-call(bf16[4,256,768]{2,1,0:T(8,128)(2,1)} %get-tuple-element.144.behind_ref, bf16[4096,1536]{1,0:T(8,128)(2,1)} %all-gather.11.cloned.1.call-done.rows_ref.refs_0_, bf16[1536,512]{1,0:T(8,128)(2,1)} %fusion.2.pair_ref), custom_call_target="tpu_custom_call" | custom-call | flops 12884901888 | bytes 12582912 | tf_op jit(solution)/shard_map/pallas_call | solution.py:254
  312.0 15.4 %all-to-all-done = bf16[4,256,768]{2,1,0:T(8,128)(2,1)S(1)} async-done(((bf16[4,256,768]{2,1,0:T(8,128)(2,1)}), bf16[4,256,768]{2,1,0:T(8,128)(2,1)S(1)}, u32[]{:S(2)}, u32[]{:S(2)}) %all-to-all-start) | async-done | bytes 1572896 | tf_op jit(solution)/shard_map/all_to_all | solution.py:64
  327.4 12.6 %conditional.1 = ((bf16[4096,512]{1,0:T(8,128)(2,1)S(1)}, bf16[768,256]{1,0:T(8,128)(2,1)}, bf16[768,256]{1,0:T(8,128)(2,1)})) conditional(s32[]{:T(128)} %convert_element_type.169, (s32[3]{0:T(128)S(1)}, bf16[1024,768]{1,0:T(8,128)(2,1)S(1)}, bf16[4096,1536]{1,0:T(8,128)(2,1)}, bf16[4096,768]{1,0:T(8,128)(2,1)}, ...), branch_computations={%region_4.5_spmd.clone, %region_5.6_spmd.clone} | conditional | flops 1 | bytes 9 | solution.py:1021
  327.4 12.6 %branch_1_fun.2 = (bf16[4096,512]{1,0:T(8,128)(2,1)S(1)}, bf16[768,256]{1,0:T(8,128)(2,1)}, bf16[768,256]{1,0:T(8,128)(2,1)}) custom-call(s32[3]{0:T(128)S(1)} %get-tuple-element.182.scalar_ref, bf16[1024,768]{1,0:T(8,128)(2,1)S(1)} %get-tuple-element.183.refs_0_, bf16[4096,1536]{1,0:T(8,128)(2,1)} %get-tuple-element.184.refs_1_, ...), custom_call_target="tpu_custom_call" | custom-call | flops 1 | bytes 1 | tf_op jit(solution)/shard_map/cond/branch_1_fun/pallas_call | solution.py:319
  340.8 4.1 shard_map.198
  346.3 12.7 %shard_map.199 = (bf16[768,512]{1,0:T(8,128)(2,1)}, bf16[768,512]{1,0:T(8,128)(2,1)}) custom-call(s32[3]{0:T(128)S(1)} %pad_add_fusion.1.scalar_ref.places_ref, bf16[4096,1536]{1,0:T(8,128)(2,1)} %all-gather.11.cloned.1.call-done.rows_ref.refs_0_, bf16[4096,512]{1,0:T(8,128)(2,1)} %copy-done.1), custom_call_target="tpu_custom_call" | custom-call | flops 1 | bytes 1 | tf_op jit(solution)/shard_map/pallas_call | solution.py:319
  361.2 8.9 %shard_map.201 = (bf16[16,48,768]{2,1,0:T(8,128)(2,1)}, bf16[16,48,768]{2,1,0:T(8,128)(2,1)}) custom-call(s32[3]{0:T(128)S(1)} %pad_add_fusion.1.scalar_ref.places_ref, bf16[1024,768]{1,0:T(8,128)(2,1)S(1)} %bitcast.114, bf16[1024,1536]{1,0:T(8,128)(2,1)} %all-gather.17.cloned.1.call-done.mix_ref, ...), custom_call_target="tpu_custom_call" | custom-call | flops 1 | bytes 1 | tf_op jit(solution)/shard_map/pallas_call | solution.py:460
  371.6 16.8 %collective-permute-done.11 = bf16[768,256]{1,0:T(8,128)(2,1)S(1)} collective-permute-done((bf16[768,256]{1,0:T(8,128)(2,1)}, bf16[768,256]{1,0:T(8,128)(2,1)S(1)}, u32[]{:S(2)}, u32[]{:S(2)}) %collective-permute-start.11) | collective-permute-done | bytes 393248 | tf_op jit(solution)/shard_map/ppermute | solution.py:40
  389.9 4.9 %all-to-all-start.1 = ((bf16[16,48,768]{2,1,0:T(8,128)(2,1)}), bf16[16,48,768]{2,1,0:T(8,128)(2,1)S(1)}, u32[]{:S(2)}, u32[]{:S(2)}) async-start(bf16[16,48,768]{2,1,0:T(8,128)(2,1)} %pad_maximum_fusion), calls=%async_computation.1 | async-start | bytes 2359296 | tf_op jit(solution)/shard_map/all_to_all | solution.py:64
  397.0 18.6 %collective-permute-done.12 = bf16[16,48,768]{2,1,0:T(8,128)(2,1)} collective-permute-done((bf16[16,48,768]{2,1,0:T(8,128)(2,1)}, bf16[16,48,768]{2,1,0:T(8,128)(2,1)}, u32[]{:S(2)}, u32[]{:S(2)}) %collective-permute-start.12) | collective-permute-done | bytes 1179680 | tf_op jit(solution)/shard_map/ppermute | solution.py:40
  418.3 4.7 %all-to-all-start.2 = ((bf16[16,48,768]{2,1,0:T(8,128)(2,1)}), bf16[16,48,768]{2,1,0:T(8,128)(2,1)S(1)}, u32[]{:S(2)}, u32[]{:S(2)}) async-start(bf16[16,48,768]{2,1,0:T(8,128)(2,1)} %add_convert_fusion), calls=%async_computation.2 | async-start | bytes 2359296 | tf_op jit(solution)/shard_map/all_to_all | solution.py:64
  429.8 9.7 %all-to-all-done.2 = bf16[16,48,768]{2,1,0:T(8,128)(2,1)S(1)} async-done(((bf16[16,48,768]{2,1,0:T(8,128)(2,1)}), bf16[16,48,768]{2,1,0:T(8,128)(2,1)S(1)}, u32[]{:S(2)}, u32[]{:S(2)}) %all-to-all-start.2) | async-done | bytes 1179680 | tf_op jit(solution)/shard_map/all_to_all | solution.py:64
  442.8 3.3 collective-permute-done.13
  (209 shorter events, 90.2 us)
Async XLA Ops:
  7.2 93.0 %all-gather.7.cloned.1.call-start = ((), (), s32[]{:S(2)}) async-start(), calls=%async_computation.3 | async-start | bytes 11182080 | tf_op jit(solution)/shard_map/all_gather | solution.py:912
  9.7 161.8 %all-gather.9.cloned.1.call-start = ((), (), s32[]{:S(2)}) async-start(), calls=%async_computation.4 | async-start | bytes 12976128 | tf_op jit(solution)/shard_map/all_gather | solution.py:912
  14.4 285.4 %all-gather.11.cloned.1.call-start = ((), (), s32[]{:S(2)}) async-start(), calls=%async_computation.5 | async-start | bytes 12976128 | tf_op jit(solution)/shard_map/all_gather | solution.py:912
  16.2 6.4 %copy-start.6 = (bf16[1,2,64,1536]{3,2,1,0:T(8,128)(2,1)S(1)}, bf16[1,2,64,1536]{3,2,1,0:T(8,128)(2,1)}, u32[]{:S(2)}) copy-start(bf16[1,2,64,1536]{3,2,1,0:T(8,128)(2,1)} %param.14) | copy-start | bytes 1179652
  100.9 10.1 %copy-start.5 = (bf16[1,2,64,1536]{3,2,1,0:T(8,128)(2,1)S(1)}, bf16[1,2,64,1536]{3,2,1,0:T(8,128)(2,1)}, u32[]{:S(2)}) copy-start(bf16[1,2,64,1536]{3,2,1,0:T(8,128)(2,1)} %param.13) | copy-start | bytes 1179652
  109.0 2.0 collective-permute-start
  112.4 53.1 %copy-start = (f32[128,1536]{1,0:T(8,128)}, f32[128,1536]{1,0:T(8,128)S(1)}, u32[]{:S(2)}) copy-start(f32[128,1536]{1,0:T(8,128)S(1)} %get-tuple-element.199.values_ref) | copy-start | bytes 2359300
  131.7 2.0 collective-permute-start.1
  134.9 27.1 %copy-start.8 = (bf16[128,1536]{1,0:T(8,128)(2,1)}, bf16[128,1536]{1,0:T(8,128)(2,1)S(1)}, u32[]{:S(2)}) copy-start(bf16[128,1536]{1,0:T(8,128)(2,1)S(1)} %add_convert_fusion.3) | copy-start | bytes 1179652
  135.0 13.6 %collective-permute-start.2 = (bf16[128,1536]{1,0:T(8,128)(2,1)S(1)}, bf16[128,1536]{1,0:T(8,128)(2,1)S(1)}, u32[]{:S(2)}, u32[]{:S(2)}) collective-permute-start(bf16[128,1536]{1,0:T(8,128)(2,1)S(1)} %add_convert_fusion.3), channel_id=1, source_target_pairs={{0,64},{1,65},{2,66},{3,67},{4,68},{5,69},{6,70},{7,71},{8,72},{9,... | collective-permute-start | bytes 1179656 | tf_op jit(solution)/shard_map/ppermute | solution.py:970
  148.7 13.4 %copy-start.29 = (f32[128]{0:T(128)}, f32[128]{0:T(128)S(1)}, u32[]{:S(2)}) copy-start(f32[128]{0:T(128)S(1)} %add_rsqrt_fusion.2) | copy-start | bytes 1540
  162.1 2.1 collective-permute-start.3
  166.7 160.7 %all-gather.13.cloned.1.call-start = ((), (), s32[]{:S(2)}) async-start(), calls=%async_computation.6 | async-start | bytes 12976128 | tf_op jit(solution)/shard_map/all_gather | solution.py:912
  205.0 2.3 collective-permute-start.5
  231.0 20.8 %copy-start.30 = (f32[128]{0:T(128)S(1)}, f32[128]{0:T(128)}, u32[]{:S(2)}) copy-start(f32[128]{0:T(128)} %copy-done.29) | copy-start | bytes 1540
  231.0 2.0 collective-permute-start.6
  237.0 14.8 %collective-permute-start.7 = (bf16[128,1536]{1,0:T(8,128)(2,1)}, bf16[128,1536]{1,0:T(8,128)(2,1)S(1)}, u32[]{:S(2)}, u32[]{:S(2)}) collective-permute-start(bf16[128,1536]{1,0:T(8,128)(2,1)} %get-tuple-element.135), channel_id=1, source_target_pairs={{64,0},{65,1},{66,2},{67,3},{68,4},{69,5},{70,6},{71,7},{72,8},{73... | collective-permute-start | bytes 1179656 | tf_op jit(solution)/shard_map/ppermute | solution.py:998
  253.0 108.1 %all-gather.17.cloned.1.call-start = ((), (), s32[]{:S(2)}) async-start(), calls=%async_computation.8 | async-start | bytes 3538944 | tf_op jit(solution)/shard_map/all_gather | solution.py:912
  272.5 2.0 collective-permute-start.8
  295.2 32.2 %all-to-all-start = ((bf16[4,256,768]{2,1,0:T(8,128)(2,1)}), bf16[4,256,768]{2,1,0:T(8,128)(2,1)S(1)}, u32[]{:S(2)}, u32[]{:S(2)}) async-start(bf16[4,256,768]{2,1,0:T(8,128)(2,1)} %get-tuple-element.144.behind_ref), calls=%async_computation | async-start | bytes 3145728 | tf_op jit(solution)/shard_map/all_to_all | solution.py:64
  299.6 148.7 %all-gather.15.cloned.1.call-start = ((), (), s32[]{:S(2)}) async-start(), calls=%async_computation.7 | async-start | bytes 4227072 | tf_op jit(solution)/shard_map/all_gather | solution.py:1069
  299.6 40.4 %collective-permute-start.9 = (bf16[128,1536]{1,0:T(8,128)(2,1)}, bf16[128,1536]{1,0:T(8,128)(2,1)S(1)}, u32[]{:S(2)}, u32[]{:S(2)}) collective-permute-start(bf16[128,1536]{1,0:T(8,128)(2,1)} %get-tuple-element.149), channel_id=1, source_target_pairs={{0,1},{1,0},{2,3},{3,2},{4,5},{5,4},{6,7},{7,6},{8,9},{9,8},{10,11... | collective-permute-start | bytes 1179656 | tf_op jit(solution)/shard_map/ppermute | solution.py:40
  359.0 29.6 %collective-permute-start.10 = (bf16[768,512]{1,0:T(8,128)(2,1)}, bf16[768,512]{1,0:T(8,128)(2,1)S(1)}, u32[]{:S(2)}, u32[]{:S(2)}) collective-permute-start(bf16[768,512]{1,0:T(8,128)(2,1)} %get-tuple-element.153), channel_id=1, source_target_pairs={{0,32},{32,0},{1,33},{33,1},{2,34},{34,2},{3,35},{35,3},{4,36},{36... | collective-permute-start | bytes 2359304 | tf_op jit(solution)/shard_map/ppermute | solution.py:40
  360.4 28.1 %collective-permute-start.11 = (bf16[768,256]{1,0:T(8,128)(2,1)}, bf16[768,256]{1,0:T(8,128)(2,1)S(1)}, u32[]{:S(2)}, u32[]{:S(2)}) collective-permute-start(bf16[768,256]{1,0:T(8,128)(2,1)} %get-tuple-element.174), channel_id=1, source_target_pairs={{0,32},{32,0},{1,33},{33,1},{2,34},{34,2},{3,35},{35,3},{4,36},{36... | collective-permute-start | bytes 1179656 | tf_op jit(solution)/shard_map/ppermute | solution.py:40
  361.0 27.6 %copy-start.14 = (bf16[768,512]{1,0:T(8,128)(2,1)S(1)}, bf16[768,512]{1,0:T(8,128)(2,1)}, u32[]{:S(2)}) copy-start(bf16[768,512]{1,0:T(8,128)(2,1)} %get-tuple-element.152) | copy-start | bytes 2359300
  361.0 33.8 %collective-permute-start.4 = (bf16[128,1536]{1,0:T(8,128)(2,1)}, bf16[128,1536]{1,0:T(8,128)(2,1)}, u32[]{:S(2)}, u32[]{:S(2)}) collective-permute-start(bf16[128,1536]{1,0:T(8,128)(2,1)} %get-tuple-element.122), channel_id=1, source_target_pairs={{0,1},{1,0},{2,3},{3,2},{4,5},{5,4},{6,7},{7,6},{8,9},{9,8},{10,11... | collective-permute-start | bytes 1179656 | tf_op jit(solution)/shard_map/ppermute | solution.py:40
  361.2 27.2 %copy-start.18 = (bf16[768,256]{1,0:T(8,128)(2,1)S(1)}, bf16[768,256]{1,0:T(8,128)(2,1)}, u32[]{:S(2)}) copy-start(bf16[768,256]{1,0:T(8,128)(2,1)} %get-tuple-element.173) | copy-start | bytes 1179652
  370.1 45.5 %collective-permute-start.12 = (bf16[16,48,768]{2,1,0:T(8,128)(2,1)}, bf16[16,48,768]{2,1,0:T(8,128)(2,1)}, u32[]{:S(2)}, u32[]{:S(2)}) collective-permute-start(bf16[16,48,768]{2,1,0:T(8,128)(2,1)} %get-tuple-element.163), channel_id=1, source_target_pairs={{0,32},{32,0},{1,33},{33,1},{2,34},{34,2},{3,35},{35,3},{4,36},{36... | collective-permute-start | bytes 3538952 | tf_op jit(solution)/shard_map/ppermute | solution.py:40
  389.9 28.5 %all-to-all-start.1 = ((bf16[16,48,768]{2,1,0:T(8,128)(2,1)}), bf16[16,48,768]{2,1,0:T(8,128)(2,1)S(1)}, u32[]{:S(2)}, u32[]{:S(2)}) async-start(bf16[16,48,768]{2,1,0:T(8,128)(2,1)} %pad_maximum_fusion), calls=%async_computation.1 | async-start | bytes 2359296 | tf_op jit(solution)/shard_map/all_to_all | solution.py:64
  394.7 20.9 %copy-start.13 = (bf16[16,48,768]{2,1,0:T(8,128)(2,1)S(1)}, bf16[16,48,768]{2,1,0:T(8,128)(2,1)}, u32[]{:S(2)}) copy-start(bf16[16,48,768]{2,1,0:T(8,128)(2,1)} %get-tuple-element.162) | copy-start | bytes 3538948
  418.3 21.1 %all-to-all-start.2 = ((bf16[16,48,768]{2,1,0:T(8,128)(2,1)}), bf16[16,48,768]{2,1,0:T(8,128)(2,1)S(1)}, u32[]{:S(2)}, u32[]{:S(2)}) async-start(bf16[16,48,768]{2,1,0:T(8,128)(2,1)} %add_convert_fusion), calls=%async_computation.2 | async-start | bytes 2359296 | tf_op jit(solution)/shard_map/all_to_all | solution.py:64
  439.7 6.5 %collective-permute-start.13 = (bf16[4,24,576]{2,1,0:T(8,128)(2,1)S(1)}, bf16[4,24,576]{2,1,0:T(8,128)(2,1)S(1)}, u32[]{:S(2)}, u32[]{:S(2)}) collective-permute-start(bf16[4,24,576]{2,1,0:T(8,128)(2,1)S(1)} %fusion.7), channel_id=1, source_target_pairs={{0,64},{64,0},{1,65},{65,1},{2,66},{66,2},{3,67},{67,3},{4,68},{68... | collective-permute-start | bytes 331784 | tf_op jit(solution)/shard_map/ppermute | solution.py:40
  (23 other events, 85.0 us)
Sparse Core Ops, SparseCore 0:
  11.4 88.7 all-gather.6
  103.0 62.5 all-gather.8
  167.8 62.4 all-gather.10
  253.2 65.3 all-gather.12
  320.1 33.3 all-gather.16
  356.5 71.5 all-gather.14

commit v4 on v3

--- a/solution.py
+++ b/solution.py
@@ -73,6 +73,10 @@
 
 VMEM_LIMIT = 56 * 1024 * 1024
 SHORT = pl.CostEstimate(flops=1, bytes_accessed=1, transcendentals=0)
+
+
+def whole_lanes(columns):
+    return -(-columns // 128) * 128
 
 
 def ordered(kernel, count):
@@ -390,6 +394,30 @@
     return wide, low, sums[0]
 
 
+def pair_join_kernel(count, *refs):
+    *refs, out_ref = refs[count:]
+    at = 0
+    for mine_ref, come_ref in zip(refs[::2], refs[1::2]):
+        size = mine_ref.shape[-1]
+        total = mine_ref[...].astype(F32) + come_ref[...].astype(F32)
+        out_ref[..., at : at + size] = total.astype(BF16)
+        at += size
+
+
+def pair_join_call(behind, pairs):
+    vmem = pl.BlockSpec(memory_space=pltpu.VMEM)
+    operands = [a for pair in pairs for a in pair]
+    shape = (*operands[0].shape[:-1], sum(mine.shape[-1] for mine, _ in pairs))
+    return pl.pallas_call(
+        functools.partial(pair_join_kernel, len(behind)),
+        in_specs=[pl.BlockSpec(memory_space=pl.ANY)] * len(behind) + [vmem] * len(operands),
+        out_specs=vmem,
+        out_shape=jax.ShapeDtypeStruct(shape, BF16),
+        compiler_params=pltpu.CompilerParams(vmem_limit_bytes=VMEM_LIMIT),
+        cost_estimate=SHORT,
+    )(*behind, *operands)
+
+
 def section_sums_kernel(behind_ref, all_ref, sums_ref):
     half = all_ref.shape[0] // 2
     for k in range(2):
@@ -404,13 +432,13 @@
         out_specs=vmem,
         out_shape=jax.ShapeDtypeStruct((2, *small.shape[1:]), F32),
         compiler_params=pltpu.CompilerParams(vmem_limit_bytes=VMEM_LIMIT),
-        cost_estimate=SHORT,
+        cost_estimate=pl.CostEstimate(flops=0, bytes_accessed=8 * small.size, transcendentals=0),
     )(*behind, small)
 
 
 def mixer_grads_kernel(
-    places_ref, columns_ref, mix_ref, early_ref, late_ref, mine_ref, other_ref,
-    normed_ref, in_ref, out_ref, sems,
+    places_ref, behind_ref, columns_ref, gated_ref, early_ref, late_ref,
+    in_mine_ref, in_other_ref, out_mine_ref, out_other_ref, normed_ref, in_ref, out_ref, sems,
 ):
     count, rows = sems.shape[0], normed_ref.shape[0] // sems.shape[0]
     here, section, z = places_ref[0], places_ref[1], places_ref[2]
@@ -434,43 +462,51 @@
     def _():
         load_all(copies(late_ref))
 
-    out_columns = columns_ref.shape[1] // 4
-    split = columns_ref.shape[1] - out_columns
-    out_ref[...] = product_left(mix_ref[...], columns_ref[:, split:])
+    mix = out_ref.shape[0]
+    out_ref[...] = product_left(columns_ref[:, :mix], gated_ref[...])
+    pair_out(out_ref, here, out_mine_ref, out_other_ref)
     for copy in copies(early_ref):
         copy.wait()
-    in_ref[...] = product_left(normed_ref[...], columns_ref[:, :split])
-    plane, block, _ = mine_ref.shape
+    in_ref[...] = product_left(normed_ref[...], columns_ref[:, mix:])
+    plane, block, _ = in_mine_ref.shape
     short = block // 2
-    for ref, half in ((mine_ref, here), (other_ref, 1 - here)):
+    for ref, half in ((in_mine_ref, here), (in_other_ref, 1 - here)):
         for k in range(plane):
             for s in range(2):
                 start = pl.multiple_of(((2 * s + half) * plane + k) * short, short)
                 rows_in = in_ref[pl.ds(start, short)]
-                ref[k, s * short : (s + 1) * short, :split] = rows_in.astype(BF16)
-            start = pl.multiple_of((half * plane + k) * block, block)
-            ref[k, :, split:] = out_ref[pl.ds(start, block)].astype(BF16)
-
-
-def mixer_grads_call(places, columns, mix, early, late, plane):
+                ref[k, s * short : (s + 1) * short] = rows_in.astype(BF16)
+
+
+def mixer_grads_call(places, behind, columns, gated, early, late, plane):
     vmem, any_space = pl.BlockSpec(memory_space=pltpu.VMEM), pl.BlockSpec(memory_space=pl.ANY)
-    tokens, width = mix.shape
-    size = columns.shape[1]
-    half = jax.ShapeDtypeStruct((plane, width // (2 * plane), size), BF16)
+    tokens, channels = gated.shape
+    width = early.shape[1]
+    mix = width // 4
+    size = columns.shape[1] - mix
+    in_half = jax.ShapeDtypeStruct((plane, width // (2 * plane), size), BF16)
+    out_half = jax.ShapeDtypeStruct((mix // 2, channels), BF16)
     return pl.pallas_call(
         mixer_grads_kernel,
-        in_specs=[pl.BlockSpec(memory_space=pltpu.SMEM), vmem, vmem, any_space, any_space],
-        out_specs=[vmem] * 2,
-        out_shape=[half, half],
+        in_specs=[
+            pl.BlockSpec(memory_space=pltpu.SMEM),
+            any_space,
+            vmem,
+            vmem,
+            any_space,
+            any_space,
+        ],
+        out_specs=[vmem] * 4,
+        out_shape=[in_half, in_half, out_half, out_half],
         scratch_shapes=[
             pltpu.VMEM((tokens, width), BF16),
-            pltpu.VMEM((width, size - size // 4), F32),
-            pltpu.VMEM((width, size // 4), F32),
+            pltpu.VMEM((width, size), F32),
+            pltpu.VMEM((mix, channels), F32),
             pltpu.SemaphoreType.DMA((4,)),
         ],
         compiler_params=pltpu.CompilerParams(vmem_limit_bytes=VMEM_LIMIT),
         cost_estimate=SHORT,
-    )(places, columns, mix, early, late)
+    )(places, behind, columns, gated, early, late)
 
 
 def load_all(copies):
@@ -538,19 +574,19 @@
     rows_out(acc_ref, core_ref[0], mine_ref, other_ref)
 
 
-def tiles_out(tiles_ref, gated_ref, columns):
+def tiles_out(tiles_ref, grad_ref, columns):
     count, rows, size = tiles_ref.shape
-    step = gated_ref.shape[1] // count
+    width = grad_ref.shape[1] // 2
+    step = width // count
     for k in range(count):
-        parts = [columns(k)]
-        spare = size - parts[0].shape[1] - step
-        if spare:
-            parts.append(jnp.zeros((rows, spare), BF16))
-        tiles_ref[k] = jnp.concatenate([*parts, gated_ref[:, k * step : (k + 1) * step]], axis=1)
+        parts = [grad_ref[:, h * width + k * step : h * width + (k + 1) * step] for h in range(2)]
+        parts.append(columns(k))
+        spare = size - sum(part.shape[1] for part in parts)
+        tiles_ref[k] = jnp.concatenate([*parts, jnp.zeros((rows, spare), BF16)], axis=1)
 
 
 def conv_backward_kernel(
-    core_ref, grad_ref, kernel_ref, masks_ref, proj_ref, gated_ref, other_tiles_ref,
+    core_ref, grad_ref, kernel_ref, masks_ref, proj_ref, other_tiles_ref,
     whole_ref, out_ref, tiles_ref, taps_ref, mine_ref, other_ref, in_buf, out_buf, acc_ref, sems,
 ):
     copies, last = weight_copies(whole_ref, out_ref, in_buf, out_buf, sems, 0)
@@ -585,7 +621,7 @@
     def _():
         tiles_out(
             tiles_ref,
-            gated_ref,
+            grad_ref,
             lambda k: jnp.concatenate([g[:, k * step : (k + 1) * step] for g in grads], axis=1),
         )
 
@@ -684,7 +720,7 @@
 
 
 def attention_backward_kernel(
-    core_ref, grad_ref, gains_ref, tables_ref, mask_ref, qkv_ref, ready_ref, gated_ref,
+    core_ref, grad_ref, gains_ref, tables_ref, mask_ref, qkv_ref, ready_ref,
     whole_ref, out_ref, tiles_ref, heads_ref, mine_ref, other_ref,
     in_buf, out_buf, acc_ref, attended_ref, ready_grad_ref, proj_ref, sems,
 ):
@@ -747,7 +783,7 @@
             raw = jnp.where(low, raw, grad)
         proj_ref[:, lanes] = raw.astype(BF16)
     step = width // tiles_ref.shape[0]
-    tiles_out(tiles_ref, gated_ref, lambda k: proj_ref[:, k * step : (k + 1) * step])
+    tiles_out(tiles_ref, grad_ref, lambda k: proj_ref[:, k * step : (k + 1) * step])
     copies[0].wait()
     acc_ref[...] = product_right(proj_ref[...], in_buf[0])
     rows_out(acc_ref, core_ref[0], mine_ref, other_ref)
@@ -789,14 +825,14 @@
     )
 
 
-def conv_backward_call(core, grad, kernel, masks, projected, gated, tiles, whole, weight_out):
+def conv_backward_call(core, grad, kernel, masks, projected, tiles, whole, weight_out):
     count, width = grad.shape
     taps, channels = kernel.shape
     outs = [
         (tiles.shape, BF16),
         ((taps, channels), F32),
     ]
-    operands = (grad, kernel, masks, projected, gated, tiles)
+    operands = (grad, kernel, masks, projected, tiles)
     return mixer_call(
         conv_backward_kernel, core, operands, whole, weight_out, (3, channels), outs
     )
@@ -811,13 +847,11 @@
     )
 
 
-def attention_backward_call(
-    core, grad, gains, tables, mask, qkv, ready, gated, whole, weight_out
-):
+def attention_backward_call(core, grad, gains, tables, mask, qkv, ready, whole, weight_out):
     count, width = grad.shape
     channels, qkv_width = weight_out.shape[0], qkv.shape[1]
     outs = [
-        ((4, count, channels), BF16),
+        ((4, count, whole_lanes((width + 3 * channels) // 4)), BF16),
         ((qkv_width // 128, 128), F32),
     ]
     scratch = [
@@ -825,7 +859,7 @@
         pltpu.VMEM((count, qkv_width), F32),
         pltpu.VMEM((count, qkv_width), BF16),
     ]
-    operands = (grad, gains, tables, mask, qkv, ready, gated)
+    operands = (grad, gains, tables, mask, qkv, ready)
     return mixer_call(
         attention_backward_kernel, core, operands, whole, weight_out, (1, qkv_width), outs, scratch
     )
@@ -977,6 +1011,7 @@
     result_1 = result_1.astype(BF16)
 
     inner_all = gathered(chosen(ffn_0[0], ffn_1[0]), plane_axes)
+    gated_y = gathered(chosen(gated_0, gated_1), "y")
 
     grad_hidden_1, grad_mix_1, gain_inner_1 = feed_forward_back(
         cotangent_1, out_cotangent.astype(F32), hidden_1, ffn_1
@@ -989,7 +1024,6 @@
         mask,
         qkv,
         ready,
-        gated_1,
         whole,
         weight_out,
     )
@@ -998,20 +1032,20 @@
     cotangent = lax.ppermute(input_grad_1, "xh", [(1, 0)])
     late = gathered(chosen(cotangent, normed_own_1), plane_axes)
     grad_hidden_0, grad_mix_0, gain_inner_0 = feed_forward_back(
-        spread(cotangent), cotangent.astype(F32), hidden_0, ffn_0
-    )
-    mix_y = gathered(chosen(grad_mix_0, grad_mix_1), ("y", "c"))
+        spread(cotangent), cotangent.astype(F32), hidden_0, ffn_0, (gated_y, inner_all)
+    )
     tiles, grad_kernel, mine, other = conv_backward_call(
         core_scalar,
         spread(grad_mix_0),
         kernel,
         masks,
         projected,
-        gated_0,
         tiles_1,
         whole,
         weight_out,
     )
+    input_grad_0, gain_outer_0 = mixer_back(grad_hidden_0, mine, other, first_in, core_scalar)
+
     columns = exchanged(tiles, "y").reshape(4 * rows, -1)
     part_kept = part_forward_call(tiles, inner_all, part_pair)
 
@@ -1023,12 +1057,25 @@
         lambda: part_down_call(xl_scalar, late, part_kept, part_down, (columns,)),
         lambda: part_down_call(xl_scalar, early, part_kept, part_down, (columns,)),
     )
-    input_grad_0, gain_outer_0 = mixer_back(grad_hidden_0, mine, other, first_in, pair_grads)
-    pair_mine, pair_other = part_pair_call(xl_scalar, inner_all, pair_grads, ())
-    mix_mine, mix_other = mixer_grads_call(xl_scalar, columns, mix_y, early, late, plane)
-
-    total = [summed_over_pair(pair_mine, pair_other), summed_over_pair(down_mine, down_other)]
-    total = jnp.concatenate(total, axis=1).astype(BF16)
+    in_mine, in_other, out_mine, out_other = mixer_grads_call(
+        xl_scalar, part_kept, columns, gated_y, early, late, plane
+    )
+    pair_mine, pair_other = part_pair_call(xl_scalar, inner_all, pair_grads, (in_mine,))
+
+    down_total = pair_join_call((), [(down_mine, swapped(down_other, "xl"))])
+    in_total = pair_join_call((pair_other, down_total), [(in_mine, swapped(in_other, "xl"))])
+    come = exchanged(in_total, PLANE)
+    lines = come.reshape(4, 4, 2, -1, come.shape[2]).astype(F32).sum(1)[..., : in_width // 4]
+    kept_lines = lax.dynamic_index_in_dim(lines, section, 1, keepdims=False)
+    sent_lines = lax.dynamic_index_in_dim(lines, 1 - section, 1, keepdims=False)
+    come = swapped(sent_lines.astype(BF16), "xh").astype(F32)
+    lines = chosen(kept_lines, come).reshape(4, -1, 3, channels // 4)
+    grad_conv_in = jnp.moveaxis(lines, 0, 2).reshape(conv_in.shape)
+    lines = chosen(come, kept_lines)[:, :, : qkv_width // 4]
+    grad_attn_qkv = jnp.moveaxis(lines, 0, 1).reshape(attn_qkv.shape)
+
+    pair_total = pair_join_call((in_total,), [(pair_mine, swapped(pair_other, "xl"))])
+    total = jnp.concatenate([pair_total, down_total], axis=1)
     arrived = exchanged(total.reshape(plane, -1, 3 * lanes), PLANE)
     lines = [
         jnp.moveaxis(arrived[:, :, k * lanes : k * lanes + part], 0, 1)
@@ -1039,19 +1086,13 @@
     grad_gate_up = jnp.stack(lines[:2])[None]
     grad_down = lines[2].T[None]
 
-    total = summed_over_pair(mix_mine, mix_other).astype(BF16)
-    come = exchanged(total, PLANE)
-    lines = come.reshape(4, 4, *come.shape[1:]).astype(F32).sum(1)
-    split = in_width // 4
-    grad_mixer_out = lines[:, :, split:].transpose(0, 2, 1).reshape(1, channels, -1)
-    lines = lines[:, :, :split].reshape(4, 2, -1, split)
-    kept_lines = lax.dynamic_index_in_dim(lines, section, 1, keepdims=False)
-    sent_lines = lax.dynamic_index_in_dim(lines, 1 - section, 1, keepdims=False)
-    come = swapped(sent_lines.astype(BF16), "xh").astype(F32)
-    lines = chosen(kept_lines, come).reshape(4, -1, 3, channels // 4)
-    grad_conv_in = jnp.moveaxis(lines, 0, 2).reshape(conv_in.shape)
-    lines = chosen(come, kept_lines)[:, :, : qkv_width // 4]
-    grad_attn_qkv = jnp.moveaxis(lines, 0, 1).reshape(attn_qkv.shape)
+    total = summed_over_pair(out_mine, out_other).reshape(4, -1, channels)
+    sent = total.astype(BF16)
+    lines = lax.dynamic_index_in_dim(total, z, 0, keepdims=False)
+    for by in range(1, 4):
+        block = lax.dynamic_index_in_dim(sent, (z + by) % 4, 0, keepdims=False)
+        lines += lax.ppermute(block, "z", [(k, (k + by) % 4) for k in range(4)]).astype(F32)
+    grad_mixer_out = lines.T[None]
 
     full_kernel = lax.dynamic_update_slice(
         jnp.zeros(conv_kernel.shape, F32), grad_kernel, (0, core * channels)
@@ -1066,7 +1107,7 @@
     )
     count = small.shape[0]
     small = jnp.pad(small, (0, -count % 1024)).reshape(-1, 128)
-    sums = section_sums_call(lax.all_gather(small, AXES), (arrived,))
+    sums = section_sums_call(lax.all_gather(small, AXES), (pair_total,))
     pair = [sums[0].reshape(-1), sums[1].reshape(-1)]
     grad_norm_gains = jnp.stack([a[: 2 * width].reshape(2, width) for a in pair])
     grad_conv_kernel = pair[0][2 * width : 5 * width].reshape(conv_kernel.shape)

time: 470 us -> 467 us (level)
  waiting for transfers between devices: 159 us -> 147 us
  starting transfers between devices: 27.5 us -> 36.3 us
    ppermute x12 -> x13, waiting for transfers between devices: 48 us -> 21.9 us  [swapped(): return lax.ppermute(shard, axis, [(0, 1), (1, 0)])]
    ppermute x0 -> x3, waiting for transfers between devices: none -> 10.5 us  [local(): lax.ppermute(block, 'z', [(k, (k + by) % 4) for k in range(4)]).astype(F32)]
    pallas_call x0 -> x3, Pallas kernels: none -> 7.23 us  [pair_join_call(): pl.pallas_call(functools.partial(pair_join_kernel, len(behind)), in_specs...]
    ppermute x0 -> x3, starting transfers between devices: none -> 4.92 us  [local(): lax.ppermute(block, 'z', [(k, (k + by) % 4) for k in range(4)]).astype(F32)]
    ppermute x12 -> x13, starting transfers between devices: 7.12 us -> 10.4 us  [swapped(): return lax.ppermute(shard, axis, [(0, 1), (1, 0)])]
  transfers between devices with their start and end apart: 23 -> 27, of which waited for: 14 -> 17; matrix products, arithmetic and copies ran while one was open for 11% -> 10% of each run, Pallas kernels for 37% -> 38%
where the time goes in v4:
time: 467 us; the launch traced here: 460 us
  Pallas kernels  178 us (38%)
  waiting for transfers between devices  147 us (31%)
  starting transfers between devices  36.3 us (8%)
  other arithmetic  30 us (6%)
  local copies, waits for them, and re-layouts  28.4 us (6%)
  blocking collectives  24.7 us (5%)
  between operations  15 us (3%)
    all_gather x5, waiting for transfers between devices, gathered(): return lax.all_gather(own, axes, tiled=True)  67.9 us
    pallas_call x4, Pallas kernels, feed_forward_call(): pl.pallas_call(ordered(body, len(behind)), in_specs=in_specs, out_specs=o...  65.7 us
    pallas_call x4, Pallas kernels, mixer_call(): pl.pallas_call(kernel, in_specs=[pl.BlockSpec(memory_space=pltpu.SMEM), *...  43.9 us
    pallas_call x2, Pallas kernels, part_call(): pl.pallas_call(ordered(kernel, len(behind)), grid_spec=pltpu.PrefetchScal...  25.4 us
    all_gather x8, blocking collectives, spread(): return lax.all_gather(own, 'c', tiled=True)  24.7 us
    all_to_all x3, waiting for transfers between devices, exchanged(): return lax.all_to_all(tiles, axes, 0, 0, tiled=True)  24.4 us
    ppermute x13, waiting for transfers between devices, swapped(): return lax.ppermute(shard, axis, [(0, 1), (1, 0)])  21.9 us
    all_to_all x3, starting transfers between devices, exchanged(): return lax.all_to_all(tiles, axes, 0, 0, tiled=True)  14.6 us
  transfers between devices with their start and end apart: 27, of which 17 were waited for; matrix products, arithmetic and copies ran while one was open for 10% of the time, Pallas kernels for 38%

profile of v4, /device:TPU:0, one launch (start us, length us, event | category | flops | bytes accessed | tf_op | source)
XLA Modules:
  0.0 460.1 jit_solution(1385133672040811203)
XLA Ops:
  26.7 8.1 %fusion.17 = (bf16[1,1,1536,3456]{3,2,1,0:T(8,128)(2,1)S(1)}, bf16[1,1,1536,3456]{3,2,1,0:T(8,128)(2,1)S(1)}) fusion(bf16[1,2,1536,3456]{3,2,1,0:T(8,128)(2,1)} %param.22), kind=kLoop, calls=%fused_computation.100 | loop fusion | bytes 42467328 | tf_op jit(solution)/shard_map/slice | solution.py:957
  36.9 63.3 %all-gather.7.cloned.1.call-done.whole_ref = bf16[1536,3584]{1,0:T(8,128)(2,1)} async-done(((bf16[24,3584]{1,0:T(8,128)(2,1)}), bf16[1536,3584]{1,0:T(8,128)(2,1)}) %all-gather.7.cloned.1.call-update) | async-done | bytes 11010064 | tf_op jit(solution)/shard_map/all_gather | solution.py:946
  100.9 8.1 %shard_map.186 = (bf16[3,256,768]{2,1,0:T(8,128)(2,1)}, bf16[256,768]{1,0:T(8,128)(2,1)}, f32[128,1536]{1,0:T(8,128)}, bf16[128,1536]{1,0:T(8,128)(2,1)}) custom-call(s32[2]{0:T(128)} %pad_add_fusion.core_ref.scalar_ref.behind_ref, bf16[256,1536]{1,0:T(8,128)(2,1)} %all_gather.43.rows_ref, f32[3,768]{1,0:T(4,128)} %dynamic-slice_convert_fusion.1.kernel_ref, ...), custom_call_target="tpu_custom_call" | custom-call | flops 1 | bytes 1 | tf_op jit(solution)/shard_map/pallas_call | solution.py:797
  115.3 16.3 %shard_map.187 = (bf16[256,3456]{1,0:T(8,128)(2,1)}, bf16[256,3456]{1,0:T(8,128)(2,1)}, f32[128,1536]{1,0:T(8,128)}, bf16[128,1536]{1,0:T(8,128)(2,1)}) custom-call(s32[2]{0:T(128)} %pad_add_fusion.core_ref.scalar_ref.behind_ref, bf16[256,1536]{1,0:T(8,128)(2,1)} %all_gather.45.refs_0_, bf16[2,1536,3456]{2,1,0:T(8,128)(2,1)} %bitcast.113, ...), custom_call_target="tpu_custom_call" | custom-call | flops 1 | bytes 1 | tf_op jit(solution)/shard_map/pallas_call | solution.py:232
  134.9 4.9 %collective-permute-start.2 = (bf16[128,1536]{1,0:T(8,128)(2,1)S(1)}, bf16[128,1536]{1,0:T(8,128)(2,1)S(1)}, u32[]{:S(2)}, u32[]{:S(2)}) collective-permute-start(bf16[128,1536]{1,0:T(8,128)(2,1)S(1)} %add_convert_fusion.1), channel_id=1, source_target_pairs={{0,64},{1,65},{2,66},{3,67},{4,68},{5,69},{6,70},{7,71},{8,72},{9,... | collective-permute-start | bytes 1179656 | tf_op jit(solution)/shard_map/ppermute | solution.py:1004
  139.8 8.7 %collective-permute-done.2 = bf16[128,1536]{1,0:T(8,128)(2,1)S(1)} collective-permute-done((bf16[128,1536]{1,0:T(8,128)(2,1)S(1)}, bf16[128,1536]{1,0:T(8,128)(2,1)S(1)}, u32[]{:S(2)}, u32[]{:S(2)}) %collective-permute-start.2) | collective-permute-done | bytes 393248 | tf_op jit(solution)/shard_map/ppermute | solution.py:1004
  151.4 10.7 %shard_map.188 = (f32[256,1280]{1,0:T(8,128)}, bf16[256,1280]{1,0:T(8,128)(2,1)}, bf16[256,768]{1,0:T(8,128)(2,1)}, f32[128,1536]{1,0:T(8,128)}, bf16[128,1536]{1,0:T(8,128)(2,1)}) custom-call(s32[2]{0:T(128)} %pad_add_fusion.core_ref.scalar_ref.behind_ref, bf16[256,1536]{1,0:T(8,128)(2,1)} %all_gather.46.rows_ref, f32[9,128]{1,0:T(8,128)} %stack.89.gains_ref, ...), custom_call_target="tpu_custom_call" | custom-call | flops 1 | bytes 1 | tf_op jit(solution)/shard_map/pallas_call | solution.py:797
  170.4 16.5 %shard_map.189 = (bf16[256,3456]{1,0:T(8,128)(2,1)}, bf16[256,3456]{1,0:T(8,128)(2,1)}, f32[128,1536]{1,0:T(8,128)}, bf16[128,1536]{1,0:T(8,128)(2,1)}) custom-call(s32[2]{0:T(128)} %pad_add_fusion.core_ref.scalar_ref.behind_ref, bf16[4096,1536]{1,0:T(8,128)(2,1)} %all-gather.9.cloned.1.call-done.refs_0_.early_ref, bf16[256,1536]{1,0:T(8,128)(2,1)} %all_gather.48.refs_1_, ...), custom_call_target="tpu_custom_call" | custom-call | flops 1 | bytes 1 | tf_op jit(solution)/shard_map/pallas_call | solution.py:232
  186.9 16.4 %shard_map.190 = (f32[128,1536]{1,0:T(8,128)}, bf16[128,1536]{1,0:T(8,128)(2,1)}) custom-call(s32[2]{0:T(128)} %pad_add_fusion.core_ref.scalar_ref.behind_ref, bf16[256,1536]{1,0:T(8,128)(2,1)} %all_gather.44.refs_0_, bf16[256,3456]{1,0:T(8,128)(2,1)} %get-tuple-element.114.refs_1_, bf16[256,3456]{1,0:T(8,128)(2,1)} %get-tuple-element.115.refs_2_, ...), custom_call_target="tpu_custom_call" | custom-call | flops 1 | bytes 1 | tf_op jit(solution)/shard_map/pallas_call | solution.py:232
  206.0 3.4 shard_map.191
  209.4 4.2 all_gather.51.grad_ref
  213.6 14.6 %shard_map.192 = (bf16[4,256,1024]{2,1,0:T(8,128)(2,1)}, f32[10,128]{1,0:T(8,128)}, f32[128,1536]{1,0:T(8,128)}, bf16[128,1536]{1,0:T(8,128)(2,1)}) custom-call(s32[2]{0:T(128)} %pad_add_fusion.core_ref.scalar_ref.behind_ref, bf16[256,1536]{1,0:T(8,128)(2,1)} %all_gather.51.grad_ref, f32[9,128]{1,0:T(8,128)} %stack.89.gains_ref, f32[2,256,128]{2,1,0:T(8,128)} %bitcast.133, ...), custom_call_target="tpu_custom_call" | custom-call | flops 1 | bytes 1 | tf_op jit(solution)/shard_map/pallas_call | solution.py:797
  236.0 13.9 %collective-permute-done.7 = bf16[128,1536]{1,0:T(8,128)(2,1)S(1)} collective-permute-done((bf16[128,1536]{1,0:T(8,128)(2,1)}, bf16[128,1536]{1,0:T(8,128)(2,1)S(1)}, u32[]{:S(2)}, u32[]{:S(2)}) %collective-permute-start.7) | collective-permute-done | bytes 393248 | tf_op jit(solution)/shard_map/ppermute | solution.py:1032
  251.2 3.2 all_gather.52.refs_2_
  254.3 4.7 %all-gather.13.cloned.1.call-done.refs_1_.rows_ref = bf16[4096,1536]{1,0:T(8,128)(2,1)} async-done(((bf16[128,1536]{1,0:T(8,128)(2,1)}), bf16[4096,1536]{1,0:T(8,128)(2,1)}) %all-gather.13.cloned.1.call-update) | async-done | bytes 12582928 | tf_op jit(solution)/shard_map/all_gather | solution.py:946
  259.0 16.5 %shard_map.194 = (f32[128,1536]{1,0:T(8,128)}, bf16[128,1536]{1,0:T(8,128)(2,1)}) custom-call(s32[2]{0:T(128)} %pad_add_fusion.core_ref.scalar_ref.behind_ref, bf16[1024,768]{1,0:T(8,128)(2,1)} %all-gather.11.cloned.1.call-done.refs_0_.gated_ref, bf16[4096,1536]{1,0:T(8,128)(2,1)} %all-gather.13.cloned.1.call-done.refs_1_.rows_ref, ...), custom_call_target="tpu_custom_call" | custom-call | flops 1 | bytes 1 | tf_op jit(solution)/shard_map/pallas_call | solution.py:232
  281.5 4.2 all_gather.53.grad_ref
  285.7 10.4 %shard_map.196 = (bf16[4,256,1024]{2,1,0:T(8,128)(2,1)}, f32[3,768]{1,0:T(4,128)}, f32[128,1536]{1,0:T(8,128)}, bf16[128,1536]{1,0:T(8,128)(2,1)}) custom-call(s32[2]{0:T(128)} %pad_add_fusion.core_ref.scalar_ref.behind_ref, bf16[256,1536]{1,0:T(8,128)(2,1)} %all_gather.53.grad_ref, f32[3,768]{1,0:T(4,128)} %dynamic-slice_convert_fusion.1.kernel_ref, ...), custom_call_target="tpu_custom_call" | custom-call | flops 1 | bytes 1 | tf_op jit(solution)/shard_map/pallas_call | solution.py:797
  298.9 3.4 shard_map.197
  303.6 4.3 all-to-all-start
  308.0 12.2 %shard_map.198.behind_ref = bf16[4096,768]{1,0:T(8,128)(2,1)} custom-call(bf16[4,256,1024]{2,1,0:T(8,128)(2,1)} %get-tuple-element.136.behind_ref, bf16[4096,1536]{1,0:T(8,128)(2,1)} %all-gather.13.cloned.1.call-done.refs_1_.rows_ref, bf16[1536,512]{1,0:T(8,128)(2,1)} %fusion.2.pair_ref), custom_call_target="tpu_custom_call" | custom-call | flops 12884901888 | bytes 12582912 | tf_op jit(solution)/shard_map/pallas_call | solution.py:258
  320.2 24.4 %all-to-all-done = bf16[4,256,1024]{2,1,0:T(8,128)(2,1)S(1)} async-done(((bf16[4,256,1024]{2,1,0:T(8,128)(2,1)}), bf16[4,256,1024]{2,1,0:T(8,128)(2,1)S(1)}, u32[]{:S(2)}, u32[]{:S(2)}) %all-to-all-start) | async-done | bytes 2097184 | tf_op jit(solution)/shard_map/all_to_all | solution.py:64
  344.6 7.8 %shard_map.199 = (bf16[16,48,640]{2,1,0:T(8,128)(2,1)}, bf16[16,48,640]{2,1,0:T(8,128)(2,1)}, bf16[192,768]{1,0:T(8,128)(2,1)}, bf16[192,768]{1,0:T(8,128)(2,1)}) custom-call(s32[3]{0:T(128)S(1)} %pad_add_fusion.1.places_ref.scalar_ref, bf16[4096,768]{1,0:T(8,128)(2,1)} %shard_map.198.behind_ref, bf16[1024,1024]{1,0:T(8,128)(2,1)S(1)} %bitcast.125, ...), custom_call_target="tpu_custom_call" | custom-call | flops 1 | bytes 1 | tf_op jit(solution)/shard_map/pallas_call | solution.py:489
  354.0 12.9 %conditional.1 = ((bf16[4096,512]{1,0:T(8,128)(2,1)}, bf16[768,256]{1,0:T(8,128)(2,1)S(1)}, bf16[768,256]{1,0:T(8,128)(2,1)})) conditional(s32[]{:T(128)} %convert_element_type.163, (s32[3]{0:T(128)S(1)}, bf16[1024,1024]{1,0:T(8,128)(2,1)S(1)}, bf16[4096,1536]{1,0:T(8,128)(2,1)}, bf16[4096,768]{1,0:T(8,128)(2,1)}, ...), branch_computations={%region_4.5_spmd, %region_5.6_spmd} | conditional | flops 1 | bytes 9 | solution.py:1055
  354.0 12.9 %branch_1_fun.1 = (bf16[4096,512]{1,0:T(8,128)(2,1)}, bf16[768,256]{1,0:T(8,128)(2,1)S(1)}, bf16[768,256]{1,0:T(8,128)(2,1)}) custom-call(s32[3]{0:T(128)S(1)} %get-tuple-element.25.scalar_ref, bf16[1024,1024]{1,0:T(8,128)(2,1)S(1)} %get-tuple-element.26.refs_0_, bf16[4096,1536]{1,0:T(8,128)(2,1)} %get-tuple-element.27.refs_1_, ...), custom_call_target="tpu_custom_call" | custom-call | flops 1 | bytes 1 | tf_op jit(solution)/shard_map/cond/branch_1_fun/pallas_call | solution.py:323
  367.7 12.6 %shard_map.200 = (bf16[768,512]{1,0:T(8,128)(2,1)}, bf16[768,512]{1,0:T(8,128)(2,1)}) custom-call(s32[3]{0:T(128)S(1)} %pad_add_fusion.1.places_ref.scalar_ref, bf16[16,48,640]{2,1,0:T(8,128)(2,1)} %get-tuple-element.138.refs_0_.refs_2_, bf16[4096,1536]{1,0:T(8,128)(2,1)} %all-gather.13.cloned.1.call-done.refs_1_.rows_ref, ...), custom_call_target="tpu_custom_call" | custom-call | flops 1 | bytes 1 | tf_op jit(solution)/shard_map/pallas_call | solution.py:323
  381.7 5.5 %collective-permute-done.10.refs_1_ = bf16[768,256]{1,0:T(8,128)(2,1)S(1)} collective-permute-done((bf16[768,256]{1,0:T(8,128)(2,1)}, bf16[768,256]{1,0:T(8,128)(2,1)S(1)}, u32[]{:S(2)}, u32[]{:S(2)}) %collective-permute-start.10) | collective-permute-done | bytes 393248 | tf_op jit(solution)/shard_map/ppermute | solution.py:40
  392.8 5.1 %all-to-all-start.1 = ((bf16[16,48,640]{2,1,0:T(8,128)(2,1)}), bf16[16,48,640]{2,1,0:T(8,128)(2,1)S(1)}, u32[]{:S(2)}, u32[]{:S(2)}) async-start(bf16[16,48,640]{2,1,0:T(8,128)(2,1)} %shard_map.202.refs_0_), calls=%async_computation.1 | async-start | bytes 1966080 | tf_op jit(solution)/shard_map/all_to_all | solution.py:64
  402.3 7.8 %collective-permute-done.12.refs_2_ = bf16[768,512]{1,0:T(8,128)(2,1)} collective-permute-done((bf16[768,512]{1,0:T(8,128)(2,1)}, bf16[768,512]{1,0:T(8,128)(2,1)}, u32[]{:S(2)}, u32[]{:S(2)}) %collective-permute-start.12) | collective-permute-done | bytes 786464 | tf_op jit(solution)/shard_map/ppermute | solution.py:40
  414.7 5.1 %all-to-all-start.2 = ((bf16[16,48,768]{2,1,0:T(8,128)(2,1)}), bf16[16,48,768]{2,1,0:T(8,128)(2,1)S(1)}, u32[]{:S(2)}, u32[]{:S(2)}) async-start(bf16[16,48,768]{2,1,0:T(8,128)(2,1)} %bitcast.46), calls=%async_computation.2 | async-start | bytes 2359296 | tf_op jit(solution)/shard_map/all_to_all | solution.py:64
  420.0 3.2 collective-permute-start.17
  428.2 7.3 %collective-permute-done.17 = bf16[48,768]{1,0:T(8,128)(2,1)S(1)} collective-permute-done((bf16[48,768]{1,0:T(8,128)(2,1)S(1)}, bf16[48,768]{1,0:T(8,128)(2,1)S(1)}, u32[]{:S(2)}, u32[]{:S(2)}) %collective-permute-start.17) | collective-permute-done | bytes 73760 | tf_op jit(solution)/shard_map/ppermute | solution.py:1094
  (205 shorter events, 105.6 us)
Async XLA Ops:
  7.2 93.0 %all-gather.7.cloned.1.call-start = ((), (), s32[]{:S(2)}) async-start(), calls=%async_computation.3 | async-start | bytes 11182080 | tf_op jit(solution)/shard_map/all_gather | solution.py:946
  9.7 160.7 %all-gather.9.cloned.1.call-start = ((), (), s32[]{:S(2)}) async-start(), calls=%async_computation.4 | async-start | bytes 12976128 | tf_op jit(solution)/shard_map/all_gather | solution.py:946
  14.4 239.9 %all-gather.11.cloned.1.call-start = ((), (), s32[]{:S(2)}) async-start(), calls=%async_computation.5 | async-start | bytes 1966080 | tf_op jit(solution)/shard_map/all_gather | solution.py:946
  109.0 2.0 collective-permute-start
  112.5 54.0 %copy-start = (f32[128,1536]{1,0:T(8,128)}, f32[128,1536]{1,0:T(8,128)S(1)}, u32[]{:S(2)}) copy-start(f32[128,1536]{1,0:T(8,128)S(1)} %get-tuple-element.165.values_ref) | copy-start | bytes 2359300
  131.6 2.0 collective-permute-start.1
  134.9 13.6 %copy-start.7 = (bf16[128,1536]{1,0:T(8,128)(2,1)}, bf16[128,1536]{1,0:T(8,128)(2,1)S(1)}, u32[]{:S(2)}) copy-start(bf16[128,1536]{1,0:T(8,128)(2,1)S(1)} %add_convert_fusion.1) | copy-start | bytes 1179652
  134.9 13.6 %collective-permute-start.2 = (bf16[128,1536]{1,0:T(8,128)(2,1)S(1)}, bf16[128,1536]{1,0:T(8,128)(2,1)S(1)}, u32[]{:S(2)}, u32[]{:S(2)}) collective-permute-start(bf16[128,1536]{1,0:T(8,128)(2,1)S(1)} %add_convert_fusion.1), channel_id=1, source_target_pairs={{0,64},{1,65},{2,66},{3,67},{4,68},{5,69},{6,70},{7,71},{8,72},{9,... | collective-permute-start | bytes 1179656 | tf_op jit(solution)/shard_map/ppermute | solution.py:1004
  163.0 96.0 %all-gather.13.cloned.1.call-start = ((), (), s32[]{:S(2)}) async-start(), calls=%async_computation.6 | async-start | bytes 12976128 | tf_op jit(solution)/shard_map/all_gather | solution.py:946
  163.0 2.0 collective-permute-start.3
  166.4 20.5 %copy-start.1 = (f32[128,1536]{1,0:T(8,128)}, f32[128,1536]{1,0:T(8,128)S(1)}, u32[]{:S(2)}) copy-start(f32[128,1536]{1,0:T(8,128)S(1)} %get-tuple-element.161.values_ref) | copy-start | bytes 2359300
  167.5 177.2 %all-gather.15.cloned.1.call-start = ((), (), s32[]{:S(2)}) async-start(), calls=%async_computation.7 | async-start | bytes 12976128 | tf_op jit(solution)/shard_map/all_gather | solution.py:946
  203.3 2.0 collective-permute-start.5
  228.2 2.6 collective-permute-start.6
  234.7 15.2 %collective-permute-start.7 = (bf16[128,1536]{1,0:T(8,128)(2,1)}, bf16[128,1536]{1,0:T(8,128)(2,1)S(1)}, u32[]{:S(2)}, u32[]{:S(2)}) collective-permute-start(bf16[128,1536]{1,0:T(8,128)(2,1)} %get-tuple-element.124), channel_id=1, source_target_pairs={{64,0},{65,1},{66,2},{67,3},{68,4},{69,5},{70,6},{71,7},{72,8},{73... | collective-permute-start | bytes 1179656 | tf_op jit(solution)/shard_map/ppermute | solution.py:1032
  251.1 194.8 %all-gather.17.cloned.1.call-start = ((), (), s32[]{:S(2)}) async-start(), calls=%async_computation.8 | async-start | bytes 4227072 | tf_op jit(solution)/shard_map/all_gather | solution.py:1110
  259.0 17.9 %copy-start.20 = (f32[10,128]{1,0:T(8,128)S(1)}, f32[10,128]{1,0:T(8,128)}, u32[]{:S(2)}) copy-start(f32[10,128]{1,0:T(8,128)} %get-tuple-element.151) | copy-start | bytes 15364
  275.6 2.0 collective-permute-start.8
  296.1 2.0 collective-permute-start.9
  303.6 41.0 %all-to-all-start = ((bf16[4,256,1024]{2,1,0:T(8,128)(2,1)}), bf16[4,256,1024]{2,1,0:T(8,128)(2,1)S(1)}, u32[]{:S(2)}, u32[]{:S(2)}) async-start(bf16[4,256,1024]{2,1,0:T(8,128)(2,1)} %get-tuple-element.136.behind_ref), calls=%async_computation | async-start | bytes 4194304 | tf_op jit(solution)/shard_map/all_to_all | solution.py:64
  352.4 37.5 %collective-permute-start.11 = (bf16[16,48,640]{2,1,0:T(8,128)(2,1)}, bf16[16,48,640]{2,1,0:T(8,128)(2,1)}, u32[]{:S(2)}, u32[]{:S(2)}) collective-permute-start(bf16[16,48,640]{2,1,0:T(8,128)(2,1)} %get-tuple-element.144), channel_id=1, source_target_pairs={{0,32},{32,0},{1,33},{33,1},{2,34},{34,2},{3,35},{35,3},{4,36},{36... | collective-permute-start | bytes 2949128 | tf_op jit(solution)/shard_map/ppermute | solution.py:40
  366.8 20.4 %collective-permute-start.10 = (bf16[768,256]{1,0:T(8,128)(2,1)}, bf16[768,256]{1,0:T(8,128)(2,1)S(1)}, u32[]{:S(2)}, u32[]{:S(2)}) collective-permute-start(bf16[768,256]{1,0:T(8,128)(2,1)} %get-tuple-element.143), channel_id=1, source_target_pairs={{0,32},{32,0},{1,33},{33,1},{2,34},{34,2},{3,35},{35,3},{4,36},{36... | collective-permute-start | bytes 1179656 | tf_op jit(solution)/shard_map/ppermute | solution.py:40
  367.4 30.5 %collective-permute-start.4 = (bf16[128,1536]{1,0:T(8,128)(2,1)}, bf16[128,1536]{1,0:T(8,128)(2,1)}, u32[]{:S(2)}, u32[]{:S(2)}) collective-permute-start(bf16[128,1536]{1,0:T(8,128)(2,1)} %get-tuple-element.110), channel_id=1, source_target_pairs={{0,1},{1,0},{2,3},{3,2},{4,5},{5,4},{6,7},{7,6},{8,9},{9,8},{10,11... | collective-permute-start | bytes 1179656 | tf_op jit(solution)/shard_map/ppermute | solution.py:40
  380.2 29.8 %collective-permute-start.12 = (bf16[768,512]{1,0:T(8,128)(2,1)}, bf16[768,512]{1,0:T(8,128)(2,1)}, u32[]{:S(2)}, u32[]{:S(2)}) collective-permute-start(bf16[768,512]{1,0:T(8,128)(2,1)} %get-tuple-element.141.refs_0_), channel_id=1, source_target_pairs={{0,32},{32,0},{1,33},{33,1},{2,34},{34,2},{3,35},{35,3},{4,36},{36... | collective-permute-start | bytes 2359304 | tf_op jit(solution)/shard_map/ppermute | solution.py:40
  392.8 21.9 %all-to-all-start.1 = ((bf16[16,48,640]{2,1,0:T(8,128)(2,1)}), bf16[16,48,640]{2,1,0:T(8,128)(2,1)S(1)}, u32[]{:S(2)}, u32[]{:S(2)}) async-start(bf16[16,48,640]{2,1,0:T(8,128)(2,1)} %shard_map.202.refs_0_), calls=%async_computation.1 | async-start | bytes 1966080 | tf_op jit(solution)/shard_map/all_to_all | solution.py:64
  400.0 12.5 %copy-start.6 = (bf16[768,256]{1,0:T(8,128)(2,1)S(1)}, bf16[768,256]{1,0:T(8,128)(2,1)}, u32[]{:S(2)}) copy-start(bf16[768,256]{1,0:T(8,128)(2,1)} %shard_map.201.refs_1_) | copy-start | bytes 1179652
  400.0 19.9 %collective-permute-start.14 = (bf16[192,768]{1,0:T(8,128)(2,1)}, bf16[192,768]{1,0:T(8,128)(2,1)S(1)}, u32[]{:S(2)}, u32[]{:S(2)}) collective-permute-start(bf16[192,768]{1,0:T(8,128)(2,1)} %get-tuple-element.153), channel_id=1, source_target_pairs={{0,32},{32,0},{1,33},{33,1},{2,34},{34,2},{3,35},{35,3},{4,36},{36... | collective-permute-start | bytes 884744 | tf_op jit(solution)/shard_map/ppermute | solution.py:40
  414.7 26.9 %all-to-all-start.2 = ((bf16[16,48,768]{2,1,0:T(8,128)(2,1)}), bf16[16,48,768]{2,1,0:T(8,128)(2,1)S(1)}, u32[]{:S(2)}, u32[]{:S(2)}) async-start(bf16[16,48,768]{2,1,0:T(8,128)(2,1)} %bitcast.46), calls=%async_computation.2 | async-start | bytes 2359296 | tf_op jit(solution)/shard_map/all_to_all | solution.py:64
  420.0 15.5 %collective-permute-start.17 = (bf16[48,768]{1,0:T(8,128)(2,1)S(1)}, bf16[48,768]{1,0:T(8,128)(2,1)S(1)}, u32[]{:S(2)}, u32[]{:S(2)}) collective-permute-start(bf16[48,768]{1,0:T(8,128)(2,1)S(1)} %get-tuple-element.174), channel_id=1, source_target_pairs={{0,6},{2,0},{4,2},{6,4},{1,7},{3,1},{5,3},{7,5},{8,14},{10,8},{12,... | collective-permute-start | bytes 221192 | tf_op jit(solution)/shard_map/ppermute | solution.py:1094
  423.2 15.2 %collective-permute-start.16 = (bf16[48,768]{1,0:T(8,128)(2,1)S(1)}, bf16[48,768]{1,0:T(8,128)(2,1)S(1)}, u32[]{:S(2)}, u32[]{:S(2)}) collective-permute-start(bf16[48,768]{1,0:T(8,128)(2,1)S(1)} %get-tuple-element.175), channel_id=1, source_target_pairs={{0,4},{2,6},{4,0},{6,2},{1,5},{3,7},{5,1},{7,3},{8,12},{10,14},{12... | collective-permute-start | bytes 221192 | tf_op jit(solution)/shard_map/ppermute | solution.py:1094
  424.1 14.6 %collective-permute-start.15 = (bf16[48,768]{1,0:T(8,128)(2,1)S(1)}, bf16[48,768]{1,0:T(8,128)(2,1)S(1)}, u32[]{:S(2)}, u32[]{:S(2)}) collective-permute-start(bf16[48,768]{1,0:T(8,128)(2,1)S(1)} %get-tuple-element.173), channel_id=1, source_target_pairs={{0,2},{2,4},{4,6},{6,0},{1,3},{3,5},{5,7},{7,1},{8,10},{10,12},{12... | collective-permute-start | bytes 221192 | tf_op jit(solution)/shard_map/ppermute | solution.py:1094
  425.1 14.3 %collective-permute-start.13 = (bf16[4,24,576]{2,1,0:T(8,128)(2,1)S(1)}, bf16[4,24,576]{2,1,0:T(8,128)(2,1)S(1)}, u32[]{:S(2)}, u32[]{:S(2)}) collective-permute-start(bf16[4,24,576]{2,1,0:T(8,128)(2,1)S(1)} %fusion.9), channel_id=1, source_target_pairs={{0,64},{64,0},{1,65},{65,1},{2,66},{66,2},{3,67},{67,3},{4,68},{68... | collective-permute-start | bytes 331784 | tf_op jit(solution)/shard_map/ppermute | solution.py:40
  (21 other events, 133.0 us)
Sparse Core Ops, SparseCore 0:
  11.4 88.7 all-gather.6
  103.0 62.5 all-gather.8
  167.3 25.9 all-gather.10
  196.0 63.0 all-gather.12
  261.7 71.8 all-gather.14
  336.6 71.4 all-gather.16

commit v5 on v4

--- a/solution.py
+++ b/solution.py
@@ -58,6 +58,10 @@
 
 def normalize(values):
     return values * inverse_rms(values)
+
+
+def around(by):
+    return [(k, (k + by) % 4) for k in range(4)]
 
 
 def exchanged(tiles, axes):
@@ -199,6 +203,77 @@
 
     streamed(tiles, copies, work)
     rows_out(acc_ref, core_ref[0], mine_ref, other_ref)
+
+
+def ffn_both_kernel(
+    tiles, core_ref, rows_ref, grad_ref, pair_ref, down_ref,
+    mine_ref, other_ref, grad_mine_ref, grad_other_ref, pair_buf, down_buf, acc_ref, grad_acc_ref, sems,
+):
+    def copies(k, slot):
+        at, size = tiles[k]
+        columns, place = pl.ds(at, size), pl.ds(0, size)
+        return [
+            pltpu.make_async_copy(
+                pair_ref.at[0, :, columns], pair_buf.at[slot, :, place], sems.at[slot, 0]
+            ),
+            pltpu.make_async_copy(
+                pair_ref.at[1, :, columns],
+                pair_buf.at[slot, :, pl.ds(size, size)],
+                sems.at[slot, 1],
+            ),
+            pltpu.make_async_copy(
+                down_ref.at[columns], down_buf.at[slot, place], sems.at[slot, 2]
+            ),
+        ]
+
+    def work(k, slot):
+        _, size = tiles[k]
+        both = product(rows_ref[...], pair_buf[slot, :, : 2 * size])
+        grad_active = product_right(grad_ref[...], down_buf[slot, :size])
+        gate, up = both[:, :size], both[:, size:]
+        active = (gate * jax.nn.sigmoid(gate) * up).astype(BF16)
+        grads = jnp.concatenate(ffn_grads(grad_active, gate, up), axis=1)
+        part = product(active, down_buf[slot, :size])
+        grad_part = product_right(grads, pair_buf[slot, :, : 2 * size])
+        if k == 0:
+            acc_ref[...], grad_acc_ref[...] = part, grad_part
+        else:
+            acc_ref[...] += part
+            grad_acc_ref[...] += grad_part
+
+    streamed(tiles, copies, work)
+    rows_out(acc_ref, core_ref[0], mine_ref, other_ref)
+    rows_out(grad_acc_ref, core_ref[0], grad_mine_ref, grad_other_ref)
+
+
+def ffn_both_call(core, rows, grad, pair, down, behind):
+    count, width = rows.shape
+    units = down.shape[0]
+    tile = 768
+    vmem, any_space = pl.BlockSpec(memory_space=pltpu.VMEM), pl.BlockSpec(memory_space=pl.ANY)
+    half = (count // 2, width)
+    return pl.pallas_call(
+        ordered(functools.partial(ffn_both_kernel, unit_tiles(units, tile)), len(behind)),
+        in_specs=[
+            pl.BlockSpec(memory_space=pltpu.SMEM),
+            *[any_space] * len(behind),
+            vmem,
+            vmem,
+            any_space,
+            any_space,
+        ],
+        out_specs=[vmem] * 4,
+        out_shape=[jax.ShapeDtypeStruct(half, F32), jax.ShapeDtypeStruct(half, BF16)] * 2,
+        scratch_shapes=[
+            pltpu.VMEM((2, width, 2 * tile), BF16),
+            pltpu.VMEM((2, tile, width), BF16),
+            pltpu.VMEM((count, width), F32),
+            pltpu.VMEM((count, width), F32),
+            pltpu.SemaphoreType.DMA((2, 3)),
+        ],
+        compiler_params=pltpu.CompilerParams(vmem_limit_bytes=VMEM_LIMIT),
+        cost_estimate=SHORT,
+    )(core, *behind, rows, grad, pair, down)
 
 
 def feed_forward_call(backward, core, rows, pair, down, saved=(), behind=()):
@@ -418,55 +493,94 @@
     )(*behind, *operands)
 
 
-def section_sums_kernel(behind_ref, all_ref, sums_ref):
-    half = all_ref.shape[0] // 2
-    for k in range(2):
-        sums_ref[k] = jnp.sum(all_ref[k * half : (k + 1) * half], axis=0)
-
-
-def section_sums_call(small, behind):
+def widened_kernel(behind_ref, low_ref, wide_ref):
+    wide_ref[...] = low_ref[...].astype(F32)
+
+
+def widened_call(behind, low):
     vmem = pl.BlockSpec(memory_space=pltpu.VMEM)
     return pl.pallas_call(
-        section_sums_kernel,
+        widened_kernel,
         in_specs=[pl.BlockSpec(memory_space=pl.ANY), vmem],
         out_specs=vmem,
-        out_shape=jax.ShapeDtypeStruct((2, *small.shape[1:]), F32),
+        out_shape=jax.ShapeDtypeStruct(low.shape, F32),
         compiler_params=pltpu.CompilerParams(vmem_limit_bytes=VMEM_LIMIT),
-        cost_estimate=pl.CostEstimate(flops=0, bytes_accessed=8 * small.size, transcendentals=0),
-    )(*behind, small)
+        cost_estimate=SHORT,
+    )(behind, low)
+
+
+def finish_kernel(
+    places_ref, behind_ref, come_ref, small_ref, kept_ref, sent_ref, sums_ref, acc_ref
+):
+    section = places_ref[1]
+    count, short, _ = kept_ref.shape
+    for k in range(count):
+        tiles = [come_ref[m * count + k].astype(F32) for m in range(come_ref.shape[0] // count)]
+        acc_ref[...] = functools.reduce(jnp.add, tiles)
+        kept_ref[k] = acc_ref[pl.ds(pl.multiple_of(section * short, short), short)]
+        sent = acc_ref[pl.ds(pl.multiple_of((1 - section) * short, short), short)]
+        sent_ref[k] = sent.astype(BF16)
+    half = small_ref.shape[0] // 2
+    for k in range(2):
+        sums_ref[k] = jnp.sum(small_ref[k * half : (k + 1) * half], axis=0)
+
+
+def finish_call(places, behind, come, small):
+    vmem = pl.BlockSpec(memory_space=pltpu.VMEM)
+    plane, block, size = come.shape
+    lines = (4, block // 2, size)
+    return pl.pallas_call(
+        finish_kernel,
+        in_specs=[
+            pl.BlockSpec(memory_space=pltpu.SMEM),
+            pl.BlockSpec(memory_space=pl.ANY),
+            vmem,
+            vmem,
+        ],
+        out_specs=[vmem] * 3,
+        out_shape=[
+            jax.ShapeDtypeStruct(lines, F32),
+            jax.ShapeDtypeStruct(lines, BF16),
+            jax.ShapeDtypeStruct((2, *small.shape[1:]), F32),
+        ],
+        scratch_shapes=[pltpu.VMEM((block, size), F32)],
+        compiler_params=pltpu.CompilerParams(vmem_limit_bytes=VMEM_LIMIT),
+        cost_estimate=SHORT,
+    )(places, behind, come, small)
 
 
 def mixer_grads_kernel(
-    places_ref, behind_ref, columns_ref, gated_ref, early_ref, late_ref,
-    in_mine_ref, in_other_ref, out_mine_ref, out_other_ref, normed_ref, in_ref, out_ref, sems,
+    places_ref, behind_ref, columns_ref, gated_0_ref, gated_1_ref, gated_2_ref, gated_3_ref,
+    early_ref, late_ref, in_mine_ref, in_other_ref, out_mine_ref, out_other_ref,
+    normed_ref, in_ref, out_ref, sem,
 ):
-    count, rows = sems.shape[0], normed_ref.shape[0] // sems.shape[0]
-    here, section, z = places_ref[0], places_ref[1], places_ref[2]
-
-    def copies(all_ref):
-        span = all_ref.shape[0] // count
-        return [
-            pltpu.make_async_copy(
-                all_ref.at[pl.ds(pl.multiple_of(k * span + z * rows, rows), rows)],
-                normed_ref.at[pl.ds(k * rows, rows)],
-                sems.at[k],
-            )
-            for k in range(count)
-        ]
+    here, section, y = places_ref[0], places_ref[1], places_ref[2]
+
+    def copy(all_ref):
+        rows = normed_ref.shape[0]
+        start = pl.multiple_of(y * rows, rows)
+        return pltpu.make_async_copy(all_ref.at[pl.ds(start, rows)], normed_ref, sem)
 
     @pl.when(section == 0)
     def _():
-        load_all(copies(early_ref))
+        copy(early_ref).start()
 
     @pl.when(section > 0)
     def _():
-        load_all(copies(late_ref))
+        copy(late_ref).start()
 
     mix = out_ref.shape[0]
-    out_ref[...] = product_left(columns_ref[:, :mix], gated_ref[...])
+    blocks = (gated_0_ref, gated_1_ref, gated_2_ref, gated_3_ref)
+    span = gated_0_ref.shape[0]
+    total = None
+    for k, gated_ref in enumerate(blocks):
+        start = lax.rem(places_ref[3] - k + len(blocks), len(blocks)) * span
+        tiles = columns_ref[pl.ds(pl.multiple_of(start, span), span), :mix]
+        block = product_left(tiles, gated_ref[...])
+        total = block if total is None else total + block
+    out_ref[...] = total
     pair_out(out_ref, here, out_mine_ref, out_other_ref)
-    for copy in copies(early_ref):
-        copy.wait()
+    copy(early_ref).wait()
     in_ref[...] = product_left(normed_ref[...], columns_ref[:, mix:])
     plane, block, _ = in_mine_ref.shape
     short = block // 2
@@ -480,7 +594,7 @@
 
 def mixer_grads_call(places, behind, columns, gated, early, late, plane):
     vmem, any_space = pl.BlockSpec(memory_space=pltpu.VMEM), pl.BlockSpec(memory_space=pl.ANY)
-    tokens, channels = gated.shape
+    tokens, channels = columns.shape[0], gated[0].shape[1]
     width = early.shape[1]
     mix = width // 4
     size = columns.shape[1] - mix
@@ -492,7 +606,7 @@
             pl.BlockSpec(memory_space=pltpu.SMEM),
             any_space,
             vmem,
-            vmem,
+            *[vmem] * len(gated),
             any_space,
             any_space,
         ],
@@ -502,11 +616,11 @@
             pltpu.VMEM((tokens, width), BF16),
             pltpu.VMEM((width, size), F32),
             pltpu.VMEM((mix, channels), F32),
-            pltpu.SemaphoreType.DMA((4,)),
+            pltpu.SemaphoreType.DMA,
         ],
         compiler_params=pltpu.CompilerParams(vmem_limit_bytes=VMEM_LIMIT),
         cost_estimate=SHORT,
-    )(places, behind, columns, gated, early, late)
+    )(places, behind, columns, *gated, early, late)
 
 
 def load_all(copies):
@@ -576,10 +690,10 @@
 
 def tiles_out(tiles_ref, grad_ref, columns):
     count, rows, size = tiles_ref.shape
-    width = grad_ref.shape[1] // 2
-    step = width // count
+    step = grad_ref.shape[1] // (2 * count * count)
     for k in range(count):
-        parts = [grad_ref[:, h * width + k * step : h * width + (k + 1) * step] for h in range(2)]
+        starts = range(k * step, grad_ref.shape[1], count * step)
+        parts = [grad_ref[:, at : at + step] for at in starts]
         parts.append(columns(k))
         spare = size - sum(part.shape[1] for part in parts)
         tiles_ref[k] = jnp.concatenate([*parts, jnp.zeros((rows, spare), BF16)], axis=1)
@@ -789,15 +903,18 @@
     rows_out(acc_ref, core_ref[0], mine_ref, other_ref)
 
 
-def mixer_call(kernel, core, operands, whole, weight_out, in_tiles, outs, scratch=()):
+def mixer_call(
+    kernel, core, operands, whole, weight_out, in_tiles, outs, scratch=(), behind=()
+):
     vmem, any_space = pl.BlockSpec(memory_space=pltpu.VMEM), pl.BlockSpec(memory_space=pl.ANY)
     rows, width = operands[0].shape
     channels = weight_out.shape[0]
     outs = [*outs, ((rows // 2, width), F32), ((rows // 2, width), BF16)]
     return pl.pallas_call(
-        kernel,
+        ordered(kernel, len(behind)),
         in_specs=[
             pl.BlockSpec(memory_space=pltpu.SMEM),
+            *[any_space] * len(behind),
             *[vmem] * len(operands),
             any_space,
             any_space,
@@ -813,7 +930,7 @@
         ],
         compiler_params=pltpu.CompilerParams(vmem_limit_bytes=VMEM_LIMIT),
         cost_estimate=SHORT,
-    )(core, *operands, whole, weight_out)
+    )(core, *behind, *operands, whole, weight_out)
 
 
 def conv_forward_call(core, rows, kernel, masks, whole, weight_out):
@@ -825,7 +942,9 @@
     )
 
 
-def conv_backward_call(core, grad, kernel, masks, projected, tiles, whole, weight_out):
+def conv_backward_call(
+    core, grad, kernel, masks, projected, tiles, whole, weight_out, behind
+):
     count, width = grad.shape
     taps, channels = kernel.shape
     outs = [
@@ -834,7 +953,7 @@
     ]
     operands = (grad, kernel, masks, projected, tiles)
     return mixer_call(
-        conv_backward_kernel, core, operands, whole, weight_out, (3, channels), outs
+        conv_backward_kernel, core, operands, whole, weight_out, (3, channels), outs, (), behind
     )
 
 
@@ -935,9 +1054,9 @@
     part = hidden_units // plane
     in_width = 3 * channels
     qkv_width = attn_qkv.shape[1]
-    z = lax.axis_index("z")
+    y, z = lax.axis_index("y"), lax.axis_index("z")
     core_scalar = jnp.stack([core, section]).astype(jnp.int32)
-    xl_scalar = jnp.stack([xl, section, z]).astype(jnp.int32)
+    xl_scalar = jnp.stack([xl, section, y, z]).astype(jnp.int32)
 
     def chosen(from_first, from_second):
         return jnp.where(first, from_first, from_second)
@@ -974,17 +1093,10 @@
         )
     )
 
-    def feed_forward(hidden, behind=()):
-        inner_own = (normalize(hidden) * gains[1]).astype(BF16)
-        gate, up, mine, other = feed_forward_call(
-            False, core_scalar, spread(inner_own), weight_pair, weight_down, behind=behind
-        )
-        return hidden + joined(mine, other), (inner_own, gate, up)
-
-    def feed_forward_back(grad_full, grad, hidden, saved, behind=()):
-        mine, other = feed_forward_call(
-            True, core_scalar, grad_full, weight_pair, weight_down, saved[1:], behind
-        )
+    def inner_norm(hidden):
+        return (normalize(hidden) * gains[1]).astype(BF16)
+
+    def inner_back(mine, other, hidden, grad):
         return back_join_call(core_scalar, mine, swapped(other, "c"), hidden, grad, gains[1])
 
     def mixer_back(grad_hidden, mine, other, layer_in, behind):
@@ -998,8 +1110,11 @@
         core_scalar, normed_0, kernel, masks, whole, weight_out
     )
     hidden_0 = first_in + joined(mine, other)
-    result_0, ffn_0 = feed_forward(hidden_0)
-    result_0 = result_0.astype(BF16)
+    inner_0 = inner_norm(hidden_0)
+    gate, up, mine, other = feed_forward_call(
+        False, core_scalar, spread(inner_0), weight_pair, weight_down
+    )
+    result_0 = (hidden_0 + joined(mine, other)).astype(BF16)
 
     second_in = lax.ppermute(result_0, "xh", [(0, 1)]).astype(F32)
     normed_own_1 = (normalize(second_in) * gains[0]).astype(BF16)
@@ -1007,14 +1122,18 @@
         core_scalar, spread(normed_own_1), head_gains, tables, mask, whole, weight_out, qkv_width
     )
     hidden_1 = second_in + joined(mine, other)
-    result_1, ffn_1 = feed_forward(hidden_1, (early,))
-    result_1 = result_1.astype(BF16)
-
-    inner_all = gathered(chosen(ffn_0[0], ffn_1[0]), plane_axes)
-    gated_y = gathered(chosen(gated_0, gated_1), "y")
-
-    grad_hidden_1, grad_mix_1, gain_inner_1 = feed_forward_back(
-        cotangent_1, out_cotangent.astype(F32), hidden_1, ffn_1
+    inner_1 = inner_norm(hidden_1)
+    mine, other, grad_mine, grad_other = ffn_both_call(
+        core_scalar, spread(inner_1), cotangent_1, weight_pair, weight_down, (early,)
+    )
+    result_1 = (hidden_1 + joined(mine, other)).astype(BF16)
+
+    inner_all = gathered(chosen(inner_0, inner_1), plane_axes)
+    gated = chosen(gated_0, gated_1)
+    gated_z = [gated, *[lax.ppermute(gated, "z", around(by)) for by in range(1, 4)]]
+
+    grad_hidden_1, grad_mix_1, gain_inner_1 = inner_back(
+        grad_mine, grad_other, hidden_1, out_cotangent.astype(F32)
     )
     tiles_1, head_sums, mine, other = attention_backward_call(
         core_scalar,
@@ -1031,8 +1150,17 @@
 
     cotangent = lax.ppermute(input_grad_1, "xh", [(1, 0)])
     late = gathered(chosen(cotangent, normed_own_1), plane_axes)
-    grad_hidden_0, grad_mix_0, gain_inner_0 = feed_forward_back(
-        spread(cotangent), cotangent.astype(F32), hidden_0, ffn_0, (gated_y, inner_all)
+    mine, other = feed_forward_call(
+        True,
+        core_scalar,
+        spread(cotangent),
+        weight_pair,
+        weight_down,
+        (gate, up),
+        (inner_all,),
+    )
+    grad_hidden_0, grad_mix_0, gain_inner_0 = inner_back(
+        mine, other, hidden_0, cotangent.astype(F32)
     )
     tiles, grad_kernel, mine, other = conv_backward_call(
         core_scalar,
@@ -1043,10 +1171,9 @@
         tiles_1,
         whole,
         weight_out,
-    )
-    input_grad_0, gain_outer_0 = mixer_back(grad_hidden_0, mine, other, first_in, core_scalar)
-
-    columns = exchanged(tiles, "y").reshape(4 * rows, -1)
+        gated_z[1:],
+    )
+    columns = exchanged(tiles, "z").reshape(4 * rows, -1)
     part_kept = part_forward_call(tiles, inner_all, part_pair)
 
     def summed_over_pair(mine, other):
@@ -1057,42 +1184,11 @@
         lambda: part_down_call(xl_scalar, late, part_kept, part_down, (columns,)),
         lambda: part_down_call(xl_scalar, early, part_kept, part_down, (columns,)),
     )
+    input_grad_0, gain_outer_0 = mixer_back(grad_hidden_0, mine, other, first_in, pair_grads)
     in_mine, in_other, out_mine, out_other = mixer_grads_call(
-        xl_scalar, part_kept, columns, gated_y, early, late, plane
+        xl_scalar, pair_grads, columns, gated_z, early, late, plane
     )
     pair_mine, pair_other = part_pair_call(xl_scalar, inner_all, pair_grads, (in_mine,))
-
-    down_total = pair_join_call((), [(down_mine, swapped(down_other, "xl"))])
-    in_total = pair_join_call((pair_other, down_total), [(in_mine, swapped(in_other, "xl"))])
-    come = exchanged(in_total, PLANE)
-    lines = come.reshape(4, 4, 2, -1, come.shape[2]).astype(F32).sum(1)[..., : in_width // 4]
-    kept_lines = lax.dynamic_index_in_dim(lines, section, 1, keepdims=False)
-    sent_lines = lax.dynamic_index_in_dim(lines, 1 - section, 1, keepdims=False)
-    come = swapped(sent_lines.astype(BF16), "xh").astype(F32)
-    lines = chosen(kept_lines, come).reshape(4, -1, 3, channels // 4)
-    grad_conv_in = jnp.moveaxis(lines, 0, 2).reshape(conv_in.shape)
-    lines = chosen(come, kept_lines)[:, :, : qkv_width // 4]
-    grad_attn_qkv = jnp.moveaxis(lines, 0, 1).reshape(attn_qkv.shape)
-
-    pair_total = pair_join_call((in_total,), [(pair_mine, swapped(pair_other, "xl"))])
-    total = jnp.concatenate([pair_total, down_total], axis=1)
-    arrived = exchanged(total.reshape(plane, -1, 3 * lanes), PLANE)
-    lines = [
-        jnp.moveaxis(arrived[:, :, k * lanes : k * lanes + part], 0, 1)
-        .reshape(-1, hidden_units)
-        .astype(F32)
-        for k in range(3)
-    ]
-    grad_gate_up = jnp.stack(lines[:2])[None]
-    grad_down = lines[2].T[None]
-
-    total = summed_over_pair(out_mine, out_other).reshape(4, -1, channels)
-    sent = total.astype(BF16)
-    lines = lax.dynamic_index_in_dim(total, z, 0, keepdims=False)
-    for by in range(1, 4):
-        block = lax.dynamic_index_in_dim(sent, (z + by) % 4, 0, keepdims=False)
-        lines += lax.ppermute(block, "z", [(k, (k + by) % 4) for k in range(4)]).astype(F32)
-    grad_mixer_out = lines.T[None]
 
     full_kernel = lax.dynamic_update_slice(
         jnp.zeros(conv_kernel.shape, F32), grad_kernel, (0, core * channels)
@@ -1107,7 +1203,41 @@
     )
     count = small.shape[0]
     small = jnp.pad(small, (0, -count % 1024)).reshape(-1, 128)
-    sums = section_sums_call(lax.all_gather(small, AXES), (pair_total,))
+    small_all = lax.all_gather(small, AXES)
+
+    down_total = pair_join_call((), [(down_mine, swapped(down_other, "xl"))])
+    in_total = pair_join_call((pair_other, down_total), [(in_mine, swapped(in_other, "xl"))])
+    come = exchanged(in_total, PLANE)
+
+    pair_total = pair_join_call((come,), [(pair_mine, swapped(pair_other, "xl"))])
+    total = jnp.concatenate([pair_total, down_total], axis=1)
+    arrived = exchanged(total.reshape(plane, -1, 3 * lanes), PLANE)
+
+    kept_lines, sent_lines, sums = finish_call(xl_scalar, total, come, small_all)
+    across = swapped(sent_lines, "xh")
+    come = across.astype(F32)[:, :, : in_width // 4]
+    kept_lines = kept_lines[:, :, : in_width // 4]
+    lines = chosen(kept_lines, come).reshape(4, -1, 3, channels // 4)
+    grad_conv_in = jnp.moveaxis(lines, 0, 2).reshape(conv_in.shape)
+    lines = chosen(come, kept_lines)[:, :, : qkv_width // 4]
+    grad_attn_qkv = jnp.moveaxis(lines, 0, 1).reshape(attn_qkv.shape)
+
+    arrived = widened_call(across, arrived)
+    lines = [
+        jnp.moveaxis(arrived[:, :, k * lanes : k * lanes + part], 0, 1).reshape(-1, hidden_units)
+        for k in range(3)
+    ]
+    grad_gate_up = jnp.stack(lines[:2])[None]
+    grad_down = lines[2].T[None]
+
+    total = summed_over_pair(out_mine, out_other).reshape(4, -1, channels)
+    sent = total.astype(BF16)
+    lines = lax.dynamic_index_in_dim(total, y, 0, keepdims=False)
+    for by in range(1, 4):
+        block = lax.dynamic_index_in_dim(sent, (y + by) % 4, 0, keepdims=False)
+        lines += lax.ppermute(block, "y", around(by)).astype(F32)
+    grad_mixer_out = lines.T[None]
+
     pair = [sums[0].reshape(-1), sums[1].reshape(-1)]
     grad_norm_gains = jnp.stack([a[: 2 * width].reshape(2, width) for a in pair])
     grad_conv_kernel = pair[0][2 * width : 5 * width].reshape(conv_kernel.shape)

time: 467 us -> 475 us (1.017)
  local copies, waits for them, and re-layouts: 28.4 us -> 34.8 us
  Pallas kernels: 178 us -> 173 us
  waiting for transfers between devices: 147 us -> 152 us
    pallas_call x4 -> x2, Pallas kernels: 65.7 us -> 33.1 us  [feed_forward_call(): pl.pallas_call(ordered(body, len(behind)), in_specs=in_specs, out_specs=o...]
    pallas_call x5 -> x7, Pallas kernels: 46.9 us -> 75.1 us  [the longest x4 45.1 us: mixer_call(): pl.pallas_call(ordered(kernel, len(behind)), in_specs=[pl.BlockSpec(memor...]
    ppermute x3 -> x6, waiting for transfers between devices: 10.5 us -> 26.8 us  [the longest x3 19.4 us: local(): lax.ppermute(gated, 'z', around(by))]
    all_to_all x3, waiting for transfers between devices: 24.4 us -> 11.9 us  [exchanged(): return lax.all_to_all(tiles, axes, 0, 0, tiled=True)]
    ppermute x3 -> x6, starting transfers between devices: 4.92 us -> 9.92 us  [the longest x3 5 us: local(): lax.ppermute(gated, 'z', around(by))]
    all_gather x5 -> x4, waiting for transfers between devices: 67.9 us -> 63.2 us  [gathered(): return lax.all_gather(own, axes, tiled=True)]
  transfers between devices with their start and end apart: 27 -> 29, of which waited for: 17 -> 16; matrix products, arithmetic and copies ran while one was open for 10% -> 10% of each run, Pallas kernels for 38% -> 36%
where the time goes in v5:
time: 475 us; the launch traced here: 467 us
  Pallas kernels  173 us (36%)
  waiting for transfers between devices  152 us (32%)
  starting transfers between devices  37.5 us (8%)
  local copies, waits for them, and re-layouts  34.8 us (7%)
  other arithmetic  31 us (7%)
  blocking collectives  24.4 us (5%)
  between operations  14.7 us (3%)
    all_gather x4, waiting for transfers between devices, gathered(): return lax.all_gather(own, axes, tiled=True)  63.2 us
    pallas_call x4, Pallas kernels, mixer_call(): pl.pallas_call(ordered(kernel, len(behind)), in_specs=[pl.BlockSpec(memor...  45.1 us
    pallas_call x2, Pallas kernels, feed_forward_call(): pl.pallas_call(ordered(body, len(behind)), in_specs=in_specs, out_specs=o...  33.1 us
    ppermute x13, waiting for transfers between devices, swapped(): return lax.ppermute(shard, axis, [(0, 1), (1, 0)])  26.5 us
    pallas_call x2, Pallas kernels, part_call(): pl.pallas_call(ordered(kernel, len(behind)), grid_spec=pltpu.PrefetchScal...  25.6 us
    all_gather x8, blocking collectives, spread(): return lax.all_gather(own, 'c', tiled=True)  24.4 us
    pallas_call x1, Pallas kernels, ffn_both_call(): pl.pallas_call(ordered(functools.partial(ffn_both_kernel, unit_tiles(unit...  23.6 us
    ppermute x3, waiting for transfers between devices, local(): lax.ppermute(gated, 'z', around(by))  19.4 us
  transfers between devices with their start and end apart: 29, of which 16 were waited for; matrix products, arithmetic and copies ran while one was open for 10% of the time, Pallas kernels for 36%

profile of v5, /device:TPU:0, one launch (start us, length us, event | category | flops | bytes accessed | tf_op | source)
XLA Modules:
  0.0 467.4 jit_solution(11809688095437253954)
XLA Ops:
  26.7 8.1 %fusion.15 = (bf16[1,1,1536,3456]{3,2,1,0:T(8,128)(2,1)S(1)}, bf16[1,1,1536,3456]{3,2,1,0:T(8,128)(2,1)S(1)}) fusion(bf16[1,2,1536,3456]{3,2,1,0:T(8,128)(2,1)} %param.22), kind=kLoop, calls=%fused_computation.96 | loop fusion | bytes 42467328 | tf_op jit(solution)/shard_map/slice | solution.py:1076
  37.0 63.2 %all-gather.6.cloned.1.call-done.refs_3_.refs_4_.refs_6_.refs_8_ = bf16[1536,3584]{1,0:T(8,128)(2,1)} async-done(((bf16[24,3584]{1,0:T(8,128)(2,1)}), bf16[1536,3584]{1,0:T(8,128)(2,1)}) %all-gather.6.cloned.1.call-update) | async-done | bytes 11010064 | tf_op jit(solution)/shard_map/all_gather | solution.py:1065
  100.9 8.1 %shard_map.186 = (bf16[3,256,768]{2,1,0:T(8,128)(2,1)}, bf16[256,768]{1,0:T(8,128)(2,1)}, f32[128,1536]{1,0:T(8,128)}, bf16[128,1536]{1,0:T(8,128)(2,1)}) custom-call(s32[2]{0:T(128)} %pad_add_fusion.scalar_ref.behind_ref, bf16[256,1536]{1,0:T(8,128)(2,1)} %all_gather.40.refs_0_, f32[3,768]{1,0:T(4,128)} %dynamic-slice_convert_fusion.refs_1_.refs_4_, ...), custom_call_target="tpu_custom_call" | custom-call | flops 1 | bytes 1 | tf_op jit(solution)/shard_map/pallas_call | solution.py:913
  115.3 16.3 %shard_map.187 = (bf16[256,3456]{1,0:T(8,128)(2,1)}, bf16[256,3456]{1,0:T(8,128)(2,1)}, f32[128,1536]{1,0:T(8,128)}, bf16[128,1536]{1,0:T(8,128)(2,1)}) custom-call(s32[2]{0:T(128)} %pad_add_fusion.scalar_ref.behind_ref, bf16[256,1536]{1,0:T(8,128)(2,1)} %all_gather.42.refs_0_, bf16[2,1536,3456]{2,1,0:T(8,128)(2,1)} %bitcast.103, bf16[3456,1536]{1,0:T(8,128)(2,1)} %bitcast.106), custom_call_target="tpu_custom_call" | custom-call | flops 1 | bytes 1 | tf_op jit(solution)/shard_map/pallas_call | solution.py:307
  135.0 4.9 %collective-permute-start.2 = (bf16[128,1536]{1,0:T(8,128)(2,1)S(1)}, bf16[128,1536]{1,0:T(8,128)(2,1)S(1)}, u32[]{:S(2)}, u32[]{:S(2)}) collective-permute-start(bf16[128,1536]{1,0:T(8,128)(2,1)S(1)} %add_convert_fusion.1), channel_id=1, source_target_pairs={{0,64},{1,65},{2,66},{3,67},{4,68},{5,69},{6,70},{7,71},{8,72},{9,... | collective-permute-start | bytes 1179656 | tf_op jit(solution)/shard_map/ppermute | solution.py:1119
  139.9 8.7 %collective-permute-done.2 = bf16[128,1536]{1,0:T(8,128)(2,1)S(1)} collective-permute-done((bf16[128,1536]{1,0:T(8,128)(2,1)S(1)}, bf16[128,1536]{1,0:T(8,128)(2,1)S(1)}, u32[]{:S(2)}, u32[]{:S(2)}) %collective-permute-start.2) | collective-permute-done | bytes 393248 | tf_op jit(solution)/shard_map/ppermute | solution.py:1119
  151.4 10.7 %shard_map.188 = (f32[256,1280]{1,0:T(8,128)}, bf16[256,1280]{1,0:T(8,128)(2,1)}, bf16[256,768]{1,0:T(8,128)(2,1)}, f32[128,1536]{1,0:T(8,128)}, bf16[128,1536]{1,0:T(8,128)(2,1)}) custom-call(s32[2]{0:T(128)} %pad_add_fusion.scalar_ref.behind_ref, bf16[256,1536]{1,0:T(8,128)(2,1)} %all_gather.43.refs_0_, f32[9,128]{1,0:T(8,128)} %stack.89.refs_1_, ...), custom_call_target="tpu_custom_call" | custom-call | flops 1 | bytes 1 | tf_op jit(solution)/shard_map/pallas_call | solution.py:913
  169.6 23.6 %shard_map.189 = (f32[128,1536]{1,0:T(8,128)}, bf16[128,1536]{1,0:T(8,128)(2,1)}, f32[128,1536]{1,0:T(8,128)}, bf16[128,1536]{1,0:T(8,128)(2,1)}) custom-call(s32[2]{0:T(128)} %pad_add_fusion.scalar_ref.behind_ref, bf16[4096,1536]{1,0:T(8,128)(2,1)} %all-gather.8.cloned.1.call-done.refs_0_.early_ref, bf16[256,1536]{1,0:T(8,128)(2,1)} %all_gather.45.refs_1_, ...), custom_call_target="tpu_custom_call" | custom-call | flops 1 | bytes 1 | tf_op jit(solution)/shard_map/pallas_call | solution.py:255
  196.0 3.2 shard_map.190
  199.2 4.3 all_gather.47.refs_0_
  203.5 15.3 %shard_map.191 = (bf16[4,256,1024]{2,1,0:T(8,128)(2,1)}, f32[10,128]{1,0:T(8,128)}, f32[128,1536]{1,0:T(8,128)}, bf16[128,1536]{1,0:T(8,128)(2,1)}) custom-call(s32[2]{0:T(128)} %pad_add_fusion.scalar_ref.behind_ref, bf16[256,1536]{1,0:T(8,128)(2,1)} %all_gather.47.refs_0_, f32[9,128]{1,0:T(8,128)} %stack.89.refs_1_, f32[2,256,128]{2,1,0:T(8,128)} %bitcast.120, ...), custom_call_target="tpu_custom_call" | custom-call | flops 1 | bytes 1 | tf_op jit(solution)/shard_map/pallas_call | solution.py:913
  221.7 3.2 shard_map.192
  226.2 14.6 %collective-permute-done.10 = bf16[128,1536]{1,0:T(8,128)(2,1)S(1)} collective-permute-done((bf16[128,1536]{1,0:T(8,128)(2,1)}, bf16[128,1536]{1,0:T(8,128)(2,1)S(1)}, u32[]{:S(2)}, u32[]{:S(2)}) %collective-permute-start.10) | collective-permute-done | bytes 393248 | tf_op jit(solution)/shard_map/ppermute | solution.py:1151
  245.5 16.8 %shard_map.193 = (f32[128,1536]{1,0:T(8,128)}, bf16[128,1536]{1,0:T(8,128)(2,1)}) custom-call(s32[2]{0:T(128)} %pad_add_fusion.scalar_ref.behind_ref, bf16[4096,1536]{1,0:T(8,128)(2,1)} %all-gather.10.cloned.1.call-done.refs_0_.rows_ref.refs_1_, bf16[256,1536]{1,0:T(8,128)(2,1)} %all_gather.48.refs_1_, bf16[256,3456]{1,0:T(8,128)(2,1)} %get-tuple-element.124.refs_2_, ...), custom_call_target="tpu_custom_call" | custom-call | flops 1 | bytes 1 | tf_op jit(solution)/shard_map/pallas_call | solution.py:307
  271.6 4.5 all_gather.49.refs_3_
  276.1 17.1 %collective-permute-done.6.refs_1_.gated_2_ref = bf16[256,768]{1,0:T(8,128)(2,1)S(1)} collective-permute-done((bf16[256,768]{1,0:T(8,128)(2,1)S(1)}, bf16[256,768]{1,0:T(8,128)(2,1)S(1)}, u32[]{:S(2)}, u32[]{:S(2)}) %collective-permute-start.6) | collective-permute-done | bytes 393248 | tf_op jit(solution)/shard_map/ppermute | solution.py:1133
  296.3 11.1 %shard_map.195 = (bf16[4,256,1024]{2,1,0:T(8,128)(2,1)}, f32[3,768]{1,0:T(4,128)}, f32[128,1536]{1,0:T(8,128)}, bf16[128,1536]{1,0:T(8,128)(2,1)}) custom-call(s32[2]{0:T(128)} %pad_add_fusion.scalar_ref.behind_ref, bf16[256,768]{1,0:T(8,128)(2,1)} %copy-done.11, bf16[256,768]{1,0:T(8,128)(2,1)} %copy-done.12, bf16[256,768]{1,0:T(8,128)(2,1)} %copy-done.13, ...), custom_call_target="tpu_custom_call" | custom-call | flops 1 | bytes 1 | tf_op jit(solution)/shard_map/pallas_call | solution.py:913
  307.4 3.6 all-to-all-start
  311.4 11.9 %shard_map.196 = bf16[4096,768]{1,0:T(8,128)(2,1)} custom-call(bf16[4,256,1024]{2,1,0:T(8,128)(2,1)} %get-tuple-element.131.behind_ref, bf16[4096,1536]{1,0:T(8,128)(2,1)} %all-gather.10.cloned.1.call-done.refs_0_.rows_ref.refs_1_, bf16[1536,512]{1,0:T(8,128)(2,1)} %fusion.2.pair_ref), custom_call_target="tpu_custom_call" | custom-call | flops 12884901888 | bytes 12582912 | tf_op jit(solution)/shard_map/pallas_call | solution.py:333
  323.4 11.9 %all-to-all-done = bf16[4,256,1024]{2,1,0:T(8,128)(2,1)S(1)} async-done(((bf16[4,256,1024]{2,1,0:T(8,128)(2,1)}), bf16[4,256,1024]{2,1,0:T(8,128)(2,1)S(1)}, u32[]{:S(2)}, u32[]{:S(2)}) %all-to-all-start) | async-done | bytes 2097184 | tf_op jit(solution)/shard_map/all_to_all | solution.py:68
  335.3 13.2 %conditional.1 = ((bf16[4096,512]{1,0:T(8,128)(2,1)}, bf16[768,256]{1,0:T(8,128)(2,1)}, bf16[768,256]{1,0:T(8,128)(2,1)})) conditional(s32[]{:T(128)} %convert_element_type.112, (s32[4]{0:T(128)S(1)}, bf16[1024,1024]{1,0:T(8,128)(2,1)S(1)}, bf16[4096,1536]{1,0:T(8,128)(2,1)}, bf16[4096,768]{1,0:T(8,128)(2,1)}, ...), branch_computations={%region_4.5_spmd, %region_5.6_spmd} | conditional | flops 1 | bytes 9 | solution.py:1182
  335.3 13.1 %branch_1_fun.1 = (bf16[4096,512]{1,0:T(8,128)(2,1)}, bf16[768,256]{1,0:T(8,128)(2,1)}, bf16[768,256]{1,0:T(8,128)(2,1)}) custom-call(s32[4]{0:T(128)S(1)} %get-tuple-element.25.scalar_ref, bf16[1024,1024]{1,0:T(8,128)(2,1)S(1)} %get-tuple-element.26.refs_0_, bf16[4096,1536]{1,0:T(8,128)(2,1)} %get-tuple-element.27.refs_1_, ...), custom_call_target="tpu_custom_call" | custom-call | flops 1 | bytes 1 | tf_op jit(solution)/shard_map/cond/branch_1_fun/pallas_call | solution.py:398
  349.2 3.3 shard_map.197
  353.9 7.8 %shard_map.198 = (bf16[16,48,640]{2,1,0:T(8,128)(2,1)}, bf16[16,48,640]{2,1,0:T(8,128)(2,1)}, bf16[192,768]{1,0:T(8,128)(2,1)}, bf16[192,768]{1,0:T(8,128)(2,1)}) custom-call(s32[4]{0:T(128)S(1)} %pad_add_fusion.1.places_ref.scalar_ref, bf16[4096,512]{1,0:T(8,128)(2,1)} %get-tuple-element.134.behind_ref.refs_2_, bf16[1024,1024]{1,0:T(8,128)(2,1)S(1)} %bitcast.115, ...), custom_call_target="tpu_custom_call" | custom-call | flops 1 | bytes 1 | tf_op jit(solution)/shard_map/pallas_call | solution.py:603
  366.1 12.5 %shard_map.199 = (bf16[768,512]{1,0:T(8,128)(2,1)}, bf16[768,512]{1,0:T(8,128)(2,1)}) custom-call(s32[4]{0:T(128)S(1)} %pad_add_fusion.1.places_ref.scalar_ref, bf16[16,48,640]{2,1,0:T(8,128)(2,1)} %get-tuple-element.139.refs_0_.refs_2_, bf16[4096,1536]{1,0:T(8,128)(2,1)} %all-gather.10.cloned.1.call-done.refs_0_.rows_ref.refs_1_, ...), custom_call_target="tpu_custom_call" | custom-call | flops 1 | bytes 1 | tf_op jit(solution)/shard_map/pallas_call | solution.py:398
  380.4 16.2 %collective-permute-done.13.refs_1_ = bf16[768,256]{1,0:T(8,128)(2,1)S(1)} collective-permute-done((bf16[768,256]{1,0:T(8,128)(2,1)}, bf16[768,256]{1,0:T(8,128)(2,1)S(1)}, u32[]{:S(2)}, u32[]{:S(2)}) %collective-permute-start.13) | collective-permute-done | bytes 393248 | tf_op jit(solution)/shard_map/ppermute | solution.py:40
  402.9 3.9 all-to-all-start.1
  407.9 3.3 collective-permute-start.20
  413.6 5.2 %collective-permute-done.20 = bf16[48,768]{1,0:T(8,128)(2,1)S(1)} collective-permute-done((bf16[48,768]{1,0:T(8,128)(2,1)S(1)}, bf16[48,768]{1,0:T(8,128)(2,1)S(1)}, u32[]{:S(2)}, u32[]{:S(2)}) %collective-permute-start.20) | collective-permute-done | bytes 73760 | tf_op jit(solution)/shard_map/ppermute | solution.py:1238
  427.6 5.0 %all-to-all-start.2 = ((bf16[16,48,768]{2,1,0:T(8,128)(2,1)}), bf16[16,48,768]{2,1,0:T(8,128)(2,1)S(1)}, u32[]{:S(2)}, u32[]{:S(2)}) async-start(bf16[16,48,768]{2,1,0:T(8,128)(2,1)} %bitcast.44), calls=%async_computation.2 | async-start | bytes 2359296 | tf_op jit(solution)/shard_map/all_to_all | solution.py:68
  432.6 3.5 shard_map.203
  442.9 3.5 collective-permute-done.16.behind_ref
  (230 shorter events, 114.6 us)
Async XLA Ops:
  7.2 93.0 %all-gather.6.cloned.1.call-start = ((), (), s32[]{:S(2)}) async-start(), calls=%async_computation.3 | async-start | bytes 11182080 | tf_op jit(solution)/shard_map/all_gather | solution.py:1065
  9.7 159.9 %all-gather.8.cloned.1.call-start = ((), (), s32[]{:S(2)}) async-start(), calls=%async_computation.4 | async-start | bytes 12976128 | tf_op jit(solution)/shard_map/all_gather | solution.py:1065
  14.4 231.1 %all-gather.10.cloned.1.call-start = ((), (), s32[]{:S(2)}) async-start(), calls=%async_computation.5 | async-start | bytes 12976128 | tf_op jit(solution)/shard_map/all_gather | solution.py:1065
  109.1 2.0 collective-permute-start
  112.5 53.1 %copy-start = (f32[128,1536]{1,0:T(8,128)}, f32[128,1536]{1,0:T(8,128)S(1)}, u32[]{:S(2)}) copy-start(f32[128,1536]{1,0:T(8,128)S(1)} %get-tuple-element.165.values_ref) | copy-start | bytes 2359300
  131.7 2.0 collective-permute-start.1
  135.0 13.6 %collective-permute-start.2 = (bf16[128,1536]{1,0:T(8,128)(2,1)S(1)}, bf16[128,1536]{1,0:T(8,128)(2,1)S(1)}, u32[]{:S(2)}, u32[]{:S(2)}) collective-permute-start(bf16[128,1536]{1,0:T(8,128)(2,1)S(1)} %add_convert_fusion.1), channel_id=1, source_target_pairs={{0,64},{1,65},{2,66},{3,67},{4,68},{5,69},{6,70},{7,71},{8,72},{9,... | collective-permute-start | bytes 1179656 | tf_op jit(solution)/shard_map/ppermute | solution.py:1119
  162.1 2.1 collective-permute-start.3
  166.6 168.6 %all-gather.12.cloned.1.call-start = ((), (), s32[]{:S(2)}) async-start(), calls=%async_computation.6 | async-start | bytes 12976128 | tf_op jit(solution)/shard_map/all_gather | solution.py:1065
  193.2 2.0 collective-permute-start.8
  218.7 2.2 collective-permute-start.9
  224.9 15.9 %collective-permute-start.10 = (bf16[128,1536]{1,0:T(8,128)(2,1)}, bf16[128,1536]{1,0:T(8,128)(2,1)S(1)}, u32[]{:S(2)}, u32[]{:S(2)}) collective-permute-start(bf16[128,1536]{1,0:T(8,128)(2,1)} %get-tuple-element.123), channel_id=1, source_target_pairs={{64,0},{65,1},{66,2},{67,3},{68,4},{69,5},{70,6},{71,7},{72,8},{73... | collective-permute-start | bytes 1179656 | tf_op jit(solution)/shard_map/ppermute | solution.py:1151
  262.2 5.5 %collective-permute-start.11 = (bf16[128,1536]{1,0:T(8,128)(2,1)}, bf16[128,1536]{1,0:T(8,128)(2,1)S(1)}, u32[]{:S(2)}, u32[]{:S(2)}) collective-permute-start(bf16[128,1536]{1,0:T(8,128)(2,1)} %get-tuple-element.127), channel_id=1, source_target_pairs={{0,1},{1,0},{2,3},{3,2},{4,5},{5,4},{6,7},{7,6},{8,9},{9,8},{10,11... | collective-permute-start | bytes 1179656 | tf_op jit(solution)/shard_map/ppermute | solution.py:40
  262.5 44.9 %copy-start.10 = (bf16[256,768]{1,0:T(8,128)(2,1)}, bf16[256,768]{1,0:T(8,128)(2,1)S(1)}, u32[]{:S(2)}) copy-start(bf16[256,768]{1,0:T(8,128)(2,1)S(1)} %broadcast_select_fusion.gated_0_ref) | copy-start | bytes 1179652
  262.5 13.6 %collective-permute-start.5 = (bf16[256,768]{1,0:T(8,128)(2,1)S(1)}, bf16[256,768]{1,0:T(8,128)(2,1)S(1)}, u32[]{:S(2)}, u32[]{:S(2)}) collective-permute-start(bf16[256,768]{1,0:T(8,128)(2,1)S(1)} %broadcast_select_fusion.gated_0_ref), channel_id=1, source_target_pairs={{0,2},{2,4},{4,6},{6,0},{1,3},{3,5},{5,7},{7,1},{8,10},{10,12},{12... | collective-permute-start | bytes 1179656 | tf_op jit(solution)/shard_map/ppermute | solution.py:1133
  263.2 29.9 %collective-permute-start.6 = (bf16[256,768]{1,0:T(8,128)(2,1)S(1)}, bf16[256,768]{1,0:T(8,128)(2,1)S(1)}, u32[]{:S(2)}, u32[]{:S(2)}) collective-permute-start(bf16[256,768]{1,0:T(8,128)(2,1)S(1)} %broadcast_select_fusion.gated_0_ref), channel_id=1, source_target_pairs={{0,4},{2,6},{4,0},{6,2},{1,5},{3,7},{5,1},{7,3},{8,12},{10,14},{12... | collective-permute-start | bytes 1179656 | tf_op jit(solution)/shard_map/ppermute | solution.py:1133
  266.2 29.3 %collective-permute-start.7 = (bf16[256,768]{1,0:T(8,128)(2,1)S(1)}, bf16[256,768]{1,0:T(8,128)(2,1)S(1)}, u32[]{:S(2)}, u32[]{:S(2)}) collective-permute-start(bf16[256,768]{1,0:T(8,128)(2,1)S(1)} %broadcast_select_fusion.gated_0_ref), channel_id=1, source_target_pairs={{0,6},{2,0},{4,2},{6,4},{1,7},{3,1},{5,3},{7,5},{8,14},{10,8},{12,... | collective-permute-start | bytes 1179656 | tf_op jit(solution)/shard_map/ppermute | solution.py:1133
  307.4 27.8 %all-to-all-start = ((bf16[4,256,1024]{2,1,0:T(8,128)(2,1)}), bf16[4,256,1024]{2,1,0:T(8,128)(2,1)S(1)}, u32[]{:S(2)}, u32[]{:S(2)}) async-start(bf16[4,256,1024]{2,1,0:T(8,128)(2,1)} %get-tuple-element.131.behind_ref), calls=%async_computation | async-start | bytes 4194304 | tf_op jit(solution)/shard_map/all_to_all | solution.py:68
  311.1 121.5 %all-gather.14.cloned.1.call-start = ((), (), s32[]{:S(2)}) async-start(), calls=%async_computation.7 | async-start | bytes 4227072 | tf_op jit(solution)/shard_map/all_gather | solution.py:1206
  311.3 37.2 %collective-permute-start.12 = (bf16[128,1536]{1,0:T(8,128)(2,1)}, bf16[128,1536]{1,0:T(8,128)(2,1)S(1)}, u32[]{:S(2)}, u32[]{:S(2)}) collective-permute-start(bf16[128,1536]{1,0:T(8,128)(2,1)} %get-tuple-element.136), channel_id=1, source_target_pairs={{0,1},{1,0},{2,3},{3,2},{4,5},{5,4},{6,7},{7,6},{8,9},{9,8},{10,11... | collective-permute-start | bytes 1179656 | tf_op jit(solution)/shard_map/ppermute | solution.py:40
  361.7 37.6 %collective-permute-start.14 = (bf16[16,48,640]{2,1,0:T(8,128)(2,1)}, bf16[16,48,640]{2,1,0:T(8,128)(2,1)S(1)}, u32[]{:S(2)}, u32[]{:S(2)}) collective-permute-start(bf16[16,48,640]{2,1,0:T(8,128)(2,1)} %get-tuple-element.143), channel_id=1, source_target_pairs={{0,32},{32,0},{1,33},{33,1},{2,34},{34,2},{3,35},{35,3},{4,36},{36... | collective-permute-start | bytes 2949128 | tf_op jit(solution)/shard_map/ppermute | solution.py:40
  361.9 2.2 collective-permute-start.4
  361.9 34.7 %collective-permute-start.13 = (bf16[768,256]{1,0:T(8,128)(2,1)}, bf16[768,256]{1,0:T(8,128)(2,1)S(1)}, u32[]{:S(2)}, u32[]{:S(2)}) collective-permute-start(bf16[768,256]{1,0:T(8,128)(2,1)} %get-tuple-element.142), channel_id=1, source_target_pairs={{0,32},{32,0},{1,33},{33,1},{2,34},{34,2},{3,35},{35,3},{4,36},{36... | collective-permute-start | bytes 1179656 | tf_op jit(solution)/shard_map/ppermute | solution.py:40
  363.8 43.0 %collective-permute-start.17 = (bf16[192,768]{1,0:T(8,128)(2,1)}, bf16[192,768]{1,0:T(8,128)(2,1)}, u32[]{:S(2)}, u32[]{:S(2)}) collective-permute-start(bf16[192,768]{1,0:T(8,128)(2,1)} %get-tuple-element.155), channel_id=1, source_target_pairs={{0,32},{32,0},{1,33},{33,1},{2,34},{34,2},{3,35},{35,3},{4,36},{36... | collective-permute-start | bytes 884744 | tf_op jit(solution)/shard_map/ppermute | solution.py:40
  366.1 31.3 %copy-start.25 = (bf16[768,256]{1,0:T(8,128)(2,1)S(1)}, bf16[768,256]{1,0:T(8,128)(2,1)}, u32[]{:S(2)}) copy-start(bf16[768,256]{1,0:T(8,128)(2,1)} %get-tuple-element.141.refs_0_) | copy-start | bytes 1179652
  378.6 43.1 %collective-permute-start.15 = (bf16[768,512]{1,0:T(8,128)(2,1)}, bf16[768,512]{1,0:T(8,128)(2,1)S(1)}, u32[]{:S(2)}, u32[]{:S(2)}) collective-permute-start(bf16[768,512]{1,0:T(8,128)(2,1)} %get-tuple-element.140.refs_0_), channel_id=1, source_target_pairs={{0,32},{32,0},{1,33},{33,1},{2,34},{34,2},{3,35},{35,3},{4,36},{36... | collective-permute-start | bytes 2359304 | tf_op jit(solution)/shard_map/ppermute | solution.py:40
  402.9 18.8 %all-to-all-start.1 = ((bf16[16,48,640]{2,1,0:T(8,128)(2,1)}), bf16[16,48,640]{2,1,0:T(8,128)(2,1)S(1)}, u32[]{:S(2)}, u32[]{:S(2)}) async-start(bf16[16,48,640]{2,1,0:T(8,128)(2,1)} %shard_map.201), calls=%async_computation.1 | async-start | bytes 1966080 | tf_op jit(solution)/shard_map/all_to_all | solution.py:68
  407.9 10.9 %collective-permute-start.20 = (bf16[48,768]{1,0:T(8,128)(2,1)S(1)}, bf16[48,768]{1,0:T(8,128)(2,1)S(1)}, u32[]{:S(2)}, u32[]{:S(2)}) collective-permute-start(bf16[48,768]{1,0:T(8,128)(2,1)S(1)} %get-tuple-element.174), channel_id=1, source_target_pairs={{0,24},{8,0},{16,8},{24,16},{1,25},{9,1},{17,9},{25,17},{2,26},{10... | collective-permute-start | bytes 221192 | tf_op jit(solution)/shard_map/ppermute | solution.py:1238
  411.2 9.1 %collective-permute-start.19 = (bf16[48,768]{1,0:T(8,128)(2,1)S(1)}, bf16[48,768]{1,0:T(8,128)(2,1)S(1)}, u32[]{:S(2)}, u32[]{:S(2)}) collective-permute-start(bf16[48,768]{1,0:T(8,128)(2,1)S(1)} %get-tuple-element.175), channel_id=1, source_target_pairs={{0,16},{8,24},{16,0},{24,8},{1,17},{9,25},{17,1},{25,9},{2,18},{10... | collective-permute-start | bytes 221192 | tf_op jit(solution)/shard_map/ppermute | solution.py:1238
  412.0 9.0 %collective-permute-start.18 = (bf16[48,768]{1,0:T(8,128)(2,1)S(1)}, bf16[48,768]{1,0:T(8,128)(2,1)S(1)}, u32[]{:S(2)}, u32[]{:S(2)}) collective-permute-start(bf16[48,768]{1,0:T(8,128)(2,1)S(1)} %get-tuple-element.173), channel_id=1, source_target_pairs={{0,8},{8,16},{16,24},{24,0},{1,9},{9,17},{17,25},{25,1},{2,10},{10... | collective-permute-start | bytes 221192 | tf_op jit(solution)/shard_map/ppermute | solution.py:1238
  427.6 21.9 %all-to-all-start.2 = ((bf16[16,48,768]{2,1,0:T(8,128)(2,1)}), bf16[16,48,768]{2,1,0:T(8,128)(2,1)S(1)}, u32[]{:S(2)}, u32[]{:S(2)}) async-start(bf16[16,48,768]{2,1,0:T(8,128)(2,1)} %bitcast.44), calls=%async_computation.2 | async-start | bytes 2359296 | tf_op jit(solution)/shard_map/all_to_all | solution.py:68
  439.6 6.8 %collective-permute-start.16 = (bf16[4,24,640]{2,1,0:T(8,128)(2,1)}, bf16[4,24,640]{2,1,0:T(8,128)(2,1)S(1)}, u32[]{:S(2)}, u32[]{:S(2)}) collective-permute-start(bf16[4,24,640]{2,1,0:T(8,128)(2,1)} %get-tuple-element.153), channel_id=1, source_target_pairs={{0,64},{64,0},{1,65},{65,1},{2,66},{66,2},{3,67},{67,3},{4,68},{68... | collective-permute-start | bytes 368648 | tf_op jit(solution)/shard_map/ppermute | solution.py:40
  (35 other events, 292.6 us)
Sparse Core Ops, SparseCore 0:
  11.4 88.7 all-gather.5
  103.0 62.5 all-gather.7
  167.8 62.4 all-gather.9
  242.1 69.2 all-gather.11
  354.0 68.2 all-gather.13

commit v6 on v5

--- a/solution.py
+++ b/solution.py
@@ -303,6 +303,9 @@
         buffers += [pltpu.VMEM((count, units), BF16)] * 2
         scratch = [*buffers, acc]
         scratch += [pltpu.SemaphoreType.DMA((2, 3)), pltpu.SemaphoreType.DMA((len(tiles), 2))]
+    cost = pl.CostEstimate(
+        flops=12 * count * width * units, bytes_accessed=6 * width * units, transcendentals=0
+    )
     in_specs = [scalar, *[any_space] * len(behind), *in_specs[1:]]
     return pl.pallas_call(
         ordered(body, len(behind)),
@@ -311,11 +314,12 @@
         out_shape=out_shape,
         scratch_shapes=scratch,
         compiler_params=pltpu.CompilerParams(vmem_limit_bytes=VMEM_LIMIT),
-        cost_estimate=SHORT,
+        cost_estimate=cost if backward else SHORT,
     )(core, *behind, rows, *saved, pair, down)
 
 
-def part_forward_kernel(behind_ref, rows_ref, pair_ref, kept_ref):
+def part_forward_kernel(*refs):
+    rows_ref, pair_ref, kept_ref = refs[-3:]
     both = product(rows_ref[...], pair_ref[...])
     units = both.shape[1] // 2
     gate, up = both[:, :units], both[:, units:]
@@ -334,7 +338,7 @@
         part_forward_kernel,
         grid=(tokens // tile,),
         in_specs=[
-            pl.BlockSpec(memory_space=pl.ANY),
+            *[pl.BlockSpec(memory_space=pl.ANY)] * len(behind),
             pl.BlockSpec((tile, width), lambda i: (i, 0)),
             pl.BlockSpec((width, 2 * units), lambda i: (0, 0)),
         ],
@@ -344,7 +348,7 @@
         cost_estimate=pl.CostEstimate(
             flops=8 * tokens * width * units, bytes_accessed=2 * tokens * width, transcendentals=0
         ),
-    )(behind, rows, pair)
+    )(*behind, rows, pair)
 
 
 def pair_out(acc_ref, here, mine_ref, other_ref):
@@ -509,33 +513,56 @@
     )(behind, low)
 
 
-def finish_kernel(
-    places_ref, behind_ref, come_ref, small_ref, kept_ref, sent_ref, sums_ref, acc_ref
-):
-    section = places_ref[1]
-    count, short, _ = kept_ref.shape
+def line_sums_kernel(places_ref, come_ref, mine_ref, other_ref, acc_ref):
+    here = places_ref[0]
+    count, rows, _ = mine_ref.shape
     for k in range(count):
         tiles = [come_ref[m * count + k].astype(F32) for m in range(come_ref.shape[0] // count)]
         acc_ref[...] = functools.reduce(jnp.add, tiles)
-        kept_ref[k] = acc_ref[pl.ds(pl.multiple_of(section * short, short), short)]
-        sent = acc_ref[pl.ds(pl.multiple_of((1 - section) * short, short), short)]
-        sent_ref[k] = sent.astype(BF16)
+        mine_ref[k] = acc_ref[pl.ds(pl.multiple_of(here * rows, rows), rows)]
+        other = acc_ref[pl.ds(pl.multiple_of((1 - here) * rows, rows), rows)]
+        other_ref[k] = other.astype(BF16)
+
+
+def line_sums_call(places, come):
+    vmem = pl.BlockSpec(memory_space=pltpu.VMEM)
+    plane, block, size = come.shape
+    lines = (4, block // 2, size)
+    return pl.pallas_call(
+        line_sums_kernel,
+        in_specs=[pl.BlockSpec(memory_space=pltpu.SMEM), vmem],
+        out_specs=[vmem] * 2,
+        out_shape=[jax.ShapeDtypeStruct(lines, F32), jax.ShapeDtypeStruct(lines, BF16)],
+        scratch_shapes=[pltpu.VMEM((block, size), F32)],
+        compiler_params=pltpu.CompilerParams(vmem_limit_bytes=VMEM_LIMIT),
+        cost_estimate=SHORT,
+    )(places, come)
+
+
+def finish_kernel(
+    places_ref, behind_ref, mine_ref, come_ref, small_ref, kept_ref, sent_ref, sums_ref, acc_ref
+):
+    section = places_ref[1]
+    short = kept_ref.shape[1]
+    acc_ref[...] = mine_ref[...] + come_ref[...].astype(F32)
+    kept_ref[...] = acc_ref[:, pl.ds(pl.multiple_of(section * short, short), short)]
+    sent = acc_ref[:, pl.ds(pl.multiple_of((1 - section) * short, short), short)]
+    sent_ref[...] = sent.astype(BF16)
     half = small_ref.shape[0] // 2
     for k in range(2):
         sums_ref[k] = jnp.sum(small_ref[k * half : (k + 1) * half], axis=0)
 
 
-def finish_call(places, behind, come, small):
+def finish_call(places, behind, mine, come, small):
     vmem = pl.BlockSpec(memory_space=pltpu.VMEM)
-    plane, block, size = come.shape
-    lines = (4, block // 2, size)
+    count, rows, size = mine.shape
+    lines = (count, rows // 2, size)
     return pl.pallas_call(
         finish_kernel,
         in_specs=[
             pl.BlockSpec(memory_space=pltpu.SMEM),
             pl.BlockSpec(memory_space=pl.ANY),
-            vmem,
-            vmem,
+            *[vmem] * 3,
         ],
         out_specs=[vmem] * 3,
         out_shape=[
@@ -543,16 +570,16 @@
             jax.ShapeDtypeStruct(lines, BF16),
             jax.ShapeDtypeStruct((2, *small.shape[1:]), F32),
         ],
-        scratch_shapes=[pltpu.VMEM((block, size), F32)],
+        scratch_shapes=[pltpu.VMEM(mine.shape, F32)],
         compiler_params=pltpu.CompilerParams(vmem_limit_bytes=VMEM_LIMIT),
         cost_estimate=SHORT,
-    )(places, behind, come, small)
+    )(places, behind, mine, come, small)
 
 
 def mixer_grads_kernel(
     places_ref, behind_ref, columns_ref, gated_0_ref, gated_1_ref, gated_2_ref, gated_3_ref,
-    early_ref, late_ref, in_mine_ref, in_other_ref, out_mine_ref, out_other_ref,
-    normed_ref, in_ref, out_ref, sem,
+    early_ref, late_ref, parts_ref, out_mine_ref, out_other_ref, normed_ref,
+    in_ref, out_ref, sem,
 ):
     here, section, y = places_ref[0], places_ref[1], places_ref[2]
 
@@ -582,14 +609,15 @@
     pair_out(out_ref, here, out_mine_ref, out_other_ref)
     copy(early_ref).wait()
     in_ref[...] = product_left(normed_ref[...], columns_ref[:, mix:])
-    plane, block, _ = in_mine_ref.shape
-    short = block // 2
-    for ref, half in ((in_mine_ref, here), (in_other_ref, 1 - here)):
-        for k in range(plane):
+    plane, block, _ = parts_ref.shape
+    short = block // 4
+    for k in range(plane):
+        for half in range(2):
             for s in range(2):
-                start = pl.multiple_of(((2 * s + half) * plane + k) * short, short)
-                rows_in = in_ref[pl.ds(start, short)]
-                ref[k, s * short : (s + 1) * short] = rows_in.astype(BF16)
+                start = ((2 * s + half) * plane + k) * short
+                place = (2 * half + s) * short
+                rows_in = in_ref[start : start + short]
+                parts_ref[k, place : place + short] = rows_in.astype(BF16)
 
 
 def mixer_grads_call(places, behind, columns, gated, early, late, plane):
@@ -598,7 +626,7 @@
     width = early.shape[1]
     mix = width // 4
     size = columns.shape[1] - mix
-    in_half = jax.ShapeDtypeStruct((plane, width // (2 * plane), size), BF16)
+    in_parts = jax.ShapeDtypeStruct((plane, width // plane, size), BF16)
     out_half = jax.ShapeDtypeStruct((mix // 2, channels), BF16)
     return pl.pallas_call(
         mixer_grads_kernel,
@@ -610,8 +638,8 @@
             any_space,
             any_space,
         ],
-        out_specs=[vmem] * 4,
-        out_shape=[in_half, in_half, out_half, out_half],
+        out_specs=[vmem] * 3,
+        out_shape=[in_parts, out_half, out_half],
         scratch_shapes=[
             pltpu.VMEM((tokens, width), BF16),
             pltpu.VMEM((width, size), F32),
@@ -942,9 +970,7 @@
     )
 
 
-def conv_backward_call(
-    core, grad, kernel, masks, projected, tiles, whole, weight_out, behind
-):
+def conv_backward_call(core, grad, kernel, masks, projected, tiles, whole, weight_out):
     count, width = grad.shape
     taps, channels = kernel.shape
     outs = [
@@ -953,7 +979,7 @@
     ]
     operands = (grad, kernel, masks, projected, tiles)
     return mixer_call(
-        conv_backward_kernel, core, operands, whole, weight_out, (3, channels), outs, (), behind
+        conv_backward_kernel, core, operands, whole, weight_out, (3, channels), outs
     )
 
 
@@ -1171,10 +1197,9 @@
         tiles_1,
         whole,
         weight_out,
-        gated_z[1:],
     )
     columns = exchanged(tiles, "z").reshape(4 * rows, -1)
-    part_kept = part_forward_call(tiles, inner_all, part_pair)
+    part_kept = part_forward_call((tiles, *gated_z[1:]), inner_all, part_pair)
 
     def summed_over_pair(mine, other):
         return mine.astype(F32) + swapped(other, "xl").astype(F32)
@@ -1185,10 +1210,10 @@
         lambda: part_down_call(xl_scalar, early, part_kept, part_down, (columns,)),
     )
     input_grad_0, gain_outer_0 = mixer_back(grad_hidden_0, mine, other, first_in, pair_grads)
-    in_mine, in_other, out_mine, out_other = mixer_grads_call(
+    in_parts, out_mine, out_other = mixer_grads_call(
         xl_scalar, pair_grads, columns, gated_z, early, late, plane
     )
-    pair_mine, pair_other = part_pair_call(xl_scalar, inner_all, pair_grads, (in_mine,))
+    pair_mine, pair_other = part_pair_call(xl_scalar, inner_all, pair_grads, (in_parts,))
 
     full_kernel = lax.dynamic_update_slice(
         jnp.zeros(conv_kernel.shape, F32), grad_kernel, (0, core * channels)
@@ -1205,15 +1230,15 @@
     small = jnp.pad(small, (0, -count % 1024)).reshape(-1, 128)
     small_all = lax.all_gather(small, AXES)
 
-    down_total = pair_join_call((), [(down_mine, swapped(down_other, "xl"))])
-    in_total = pair_join_call((pair_other, down_total), [(in_mine, swapped(in_other, "xl"))])
-    come = exchanged(in_total, PLANE)
-
-    pair_total = pair_join_call((come,), [(pair_mine, swapped(pair_other, "xl"))])
-    total = jnp.concatenate([pair_total, down_total], axis=1)
+    come = exchanged(in_parts, PLANE)
+    line_mine, line_other = line_sums_call(xl_scalar, come)
+    line_come = swapped(line_other, "xl")
+
+    pairs = [(a, swapped(b, "xl")) for a, b in ((pair_mine, pair_other), (down_mine, down_other))]
+    total = pair_join_call((line_mine,), pairs)
     arrived = exchanged(total.reshape(plane, -1, 3 * lanes), PLANE)
 
-    kept_lines, sent_lines, sums = finish_call(xl_scalar, total, come, small_all)
+    kept_lines, sent_lines, sums = finish_call(xl_scalar, total, line_mine, line_come, small_all)
     across = swapped(sent_lines, "xh")
     come = across.astype(F32)[:, :, : in_width // 4]
     kept_lines = kept_lines[:, :, : in_width // 4]

time: 475 us -> 481 us (1.013)
  starting transfers between devices: 37.5 us -> 45 us
    all_to_all x3, waiting for transfers between devices: 11.9 us -> 31.9 us  [exchanged(): return lax.all_to_all(tiles, axes, 0, 0, tiled=True)]
    ppermute x3, waiting for transfers between devices: 19.4 us -> 0.01 us  [local(): lax.ppermute(gated, 'z', around(by))]
    all_gather x1, waiting for transfers between devices: 0.02 us -> 18.3 us  [local(): small_all = lax.all_gather(small, AXES)]
    ppermute x13, waiting for transfers between devices: 26.5 us -> 16.6 us  [swapped(): return lax.ppermute(shard, axis, [(0, 1), (1, 0)])]
    ppermute x3, waiting for transfers between devices: 7.36 us -> 0.01 us  [local(): lines += lax.ppermute(block, 'y', around(by)).astype(F32)]
    pallas_call x1 -> x2, Pallas kernels: 11.9 us -> 15.1 us  [the longest x1 12.2 us: part_forward_call(): pl.pallas_call(part_forward_kernel, grid=(tokens // tile,), in_specs=[*[p...]
  transfers between devices with their start and end apart: 29 -> 29, of which waited for: 16 -> 13; matrix products, arithmetic and copies ran while one was open for 10% -> 10% of each run, Pallas kernels for 36% -> 35%
where the time goes in v6:
time: 481 us; the launch traced here: 473 us
  Pallas kernels  172 us (36%)
  waiting for transfers between devices  152 us (32%)
  starting transfers between devices  45 us (9%)
  local copies, waits for them, and re-layouts  33.9 us (7%)
  other arithmetic  30.6 us (6%)
  blocking collectives  24.4 us (5%)
  between operations  14.6 us (3%)
    all_gather x4, waiting for transfers between devices, gathered(): return lax.all_gather(own, axes, tiled=True)  63.2 us
    pallas_call x4, Pallas kernels, mixer_call(): pl.pallas_call(ordered(kernel, len(behind)), in_specs=[pl.BlockSpec(memor...  45.5 us
    pallas_call x2, Pallas kernels, feed_forward_call(): pl.pallas_call(ordered(body, len(behind)), in_specs=in_specs, out_specs=o...  33.1 us
    all_to_all x3, waiting for transfers between devices, exchanged(): return lax.all_to_all(tiles, axes, 0, 0, tiled=True)  31.9 us
    pallas_call x2, Pallas kernels, part_call(): pl.pallas_call(ordered(kernel, len(behind)), grid_spec=pltpu.PrefetchScal...  25.7 us
    all_gather x8, blocking collectives, spread(): return lax.all_gather(own, 'c', tiled=True)  24.4 us
    pallas_call x1, Pallas kernels, ffn_both_call(): pl.pallas_call(ordered(functools.partial(ffn_both_kernel, unit_tiles(unit...  23.6 us
    all_gather x1, waiting for transfers between devices, local(): small_all = lax.all_gather(small, AXES)  18.3 us
  transfers between devices with their start and end apart: 29, of which 13 were waited for; matrix products, arithmetic and copies ran while one was open for 10% of the time, Pallas kernels for 35%

profile of v6, /device:TPU:0, one launch (start us, length us, event | category | flops | bytes accessed | tf_op | source)
XLA Modules:
  0.0 473.3 jit_solution(3786520633394102285)
XLA Ops:
  26.7 8.1 %fusion.15 = (bf16[1,1,1536,3456]{3,2,1,0:T(8,128)(2,1)S(1)}, bf16[1,1,1536,3456]{3,2,1,0:T(8,128)(2,1)S(1)}) fusion(bf16[1,2,1536,3456]{3,2,1,0:T(8,128)(2,1)} %param.22), kind=kLoop, calls=%fused_computation.95 | loop fusion | bytes 42467328 | tf_op jit(solution)/shard_map/slice | solution.py:1102
  37.0 63.2 %all-gather.6.cloned.1.call-done.refs_3_.refs_4_.refs_6_.refs_5_ = bf16[1536,3584]{1,0:T(8,128)(2,1)} async-done(((bf16[24,3584]{1,0:T(8,128)(2,1)}), bf16[1536,3584]{1,0:T(8,128)(2,1)}) %all-gather.6.cloned.1.call-update) | async-done | bytes 11010064 | tf_op jit(solution)/shard_map/all_gather | solution.py:1091
  100.9 8.1 %shard_map.186 = (bf16[3,256,768]{2,1,0:T(8,128)(2,1)}, bf16[256,768]{1,0:T(8,128)(2,1)}, f32[128,1536]{1,0:T(8,128)}, bf16[128,1536]{1,0:T(8,128)(2,1)}) custom-call(s32[2]{0:T(128)} %pad_add_fusion.scalar_ref.behind_ref, bf16[256,1536]{1,0:T(8,128)(2,1)} %all_gather.40.refs_0_, f32[3,768]{1,0:T(4,128)} %dynamic-slice_convert_fusion.refs_1_, ...), custom_call_target="tpu_custom_call" | custom-call | flops 1 | bytes 1 | tf_op jit(solution)/shard_map/pallas_call | solution.py:941
  115.3 16.3 %shard_map.187 = (bf16[256,3456]{1,0:T(8,128)(2,1)}, bf16[256,3456]{1,0:T(8,128)(2,1)}, f32[128,1536]{1,0:T(8,128)}, bf16[128,1536]{1,0:T(8,128)(2,1)}) custom-call(s32[2]{0:T(128)} %pad_add_fusion.scalar_ref.behind_ref, bf16[256,1536]{1,0:T(8,128)(2,1)} %all_gather.42.refs_0_, bf16[2,1536,3456]{2,1,0:T(8,128)(2,1)} %bitcast.103, bf16[3456,1536]{1,0:T(8,128)(2,1)} %bitcast.106), custom_call_target="tpu_custom_call" | custom-call | flops 1 | bytes 1 | tf_op jit(solution)/shard_map/pallas_call | solution.py:310
  134.9 4.9 %collective-permute-start.2 = (bf16[128,1536]{1,0:T(8,128)(2,1)S(1)}, bf16[128,1536]{1,0:T(8,128)(2,1)S(1)}, u32[]{:S(2)}, u32[]{:S(2)}) collective-permute-start(bf16[128,1536]{1,0:T(8,128)(2,1)S(1)} %add_convert_fusion.1), channel_id=1, source_target_pairs={{0,64},{1,65},{2,66},{3,67},{4,68},{5,69},{6,70},{7,71},{8,72},{9,... | collective-permute-start | bytes 1179656 | tf_op jit(solution)/shard_map/ppermute | solution.py:1145
  139.8 8.7 %collective-permute-done.2 = bf16[128,1536]{1,0:T(8,128)(2,1)S(1)} collective-permute-done((bf16[128,1536]{1,0:T(8,128)(2,1)S(1)}, bf16[128,1536]{1,0:T(8,128)(2,1)S(1)}, u32[]{:S(2)}, u32[]{:S(2)}) %collective-permute-start.2) | collective-permute-done | bytes 393248 | tf_op jit(solution)/shard_map/ppermute | solution.py:1145
  151.4 10.7 %shard_map.188 = (f32[256,1280]{1,0:T(8,128)}, bf16[256,1280]{1,0:T(8,128)(2,1)}, bf16[256,768]{1,0:T(8,128)(2,1)}, f32[128,1536]{1,0:T(8,128)}, bf16[128,1536]{1,0:T(8,128)(2,1)}) custom-call(s32[2]{0:T(128)} %pad_add_fusion.scalar_ref.behind_ref, bf16[256,1536]{1,0:T(8,128)(2,1)} %all_gather.43.refs_0_, f32[9,128]{1,0:T(8,128)} %stack.89.refs_1_, ...), custom_call_target="tpu_custom_call" | custom-call | flops 1 | bytes 1 | tf_op jit(solution)/shard_map/pallas_call | solution.py:941
  169.6 23.6 %shard_map.189 = (f32[128,1536]{1,0:T(8,128)}, bf16[128,1536]{1,0:T(8,128)(2,1)}, f32[128,1536]{1,0:T(8,128)}, bf16[128,1536]{1,0:T(8,128)(2,1)}) custom-call(s32[2]{0:T(128)} %pad_add_fusion.scalar_ref.behind_ref, bf16[4096,1536]{1,0:T(8,128)(2,1)} %all-gather.8.cloned.1.call-done.refs_0_.early_ref, bf16[256,1536]{1,0:T(8,128)(2,1)} %all_gather.45.refs_1_, ...), custom_call_target="tpu_custom_call" | custom-call | flops 1 | bytes 1 | tf_op jit(solution)/shard_map/pallas_call | solution.py:255
  196.0 3.2 shard_map.190
  199.2 4.3 all_gather.47.refs_0_
  203.5 15.3 %shard_map.191 = (bf16[4,256,1024]{2,1,0:T(8,128)(2,1)}, f32[10,128]{1,0:T(8,128)}, f32[128,1536]{1,0:T(8,128)}, bf16[128,1536]{1,0:T(8,128)(2,1)}) custom-call(s32[2]{0:T(128)} %pad_add_fusion.scalar_ref.behind_ref, bf16[256,1536]{1,0:T(8,128)(2,1)} %all_gather.47.refs_0_, f32[9,128]{1,0:T(8,128)} %stack.89.refs_1_, f32[2,256,128]{2,1,0:T(8,128)} %bitcast.121, ...), custom_call_target="tpu_custom_call" | custom-call | flops 1 | bytes 1 | tf_op jit(solution)/shard_map/pallas_call | solution.py:941
  221.7 3.2 shard_map.192
  226.2 13.7 %collective-permute-done.7 = bf16[128,1536]{1,0:T(8,128)(2,1)S(1)} collective-permute-done((bf16[128,1536]{1,0:T(8,128)(2,1)}, bf16[128,1536]{1,0:T(8,128)(2,1)S(1)}, u32[]{:S(2)}, u32[]{:S(2)}) %collective-permute-start.7) | collective-permute-done | bytes 393248 | tf_op jit(solution)/shard_map/ppermute | solution.py:1177
  244.6 16.8 %shard_map.193 = (f32[128,1536]{1,0:T(8,128)}, bf16[128,1536]{1,0:T(8,128)(2,1)}) custom-call(s32[2]{0:T(128)} %pad_add_fusion.scalar_ref.behind_ref, bf16[4096,1536]{1,0:T(8,128)(2,1)} %all-gather.10.cloned.1.call-done.refs_0_.refs_4_.refs_1_, bf16[256,1536]{1,0:T(8,128)(2,1)} %all_gather.48.refs_1_, bf16[256,3456]{1,0:T(8,128)(2,1)} %get-tuple-element.123.refs_2_, ...), custom_call_target="tpu_custom_call" | custom-call | flops 16307453952 | bytes 31850496 | tf_op jit(solution)/shard_map/pallas_call | solution.py:310
  271.7 4.4 all_gather.49.refs_0_
  276.1 11.4 %shard_map.195 = (bf16[4,256,1024]{2,1,0:T(8,128)(2,1)}, f32[3,768]{1,0:T(4,128)}, f32[128,1536]{1,0:T(8,128)}, bf16[128,1536]{1,0:T(8,128)(2,1)}) custom-call(s32[2]{0:T(128)} %pad_add_fusion.scalar_ref.behind_ref, bf16[256,1536]{1,0:T(8,128)(2,1)} %all_gather.49.refs_0_, f32[3,768]{1,0:T(4,128)} %dynamic-slice_convert_fusion.refs_1_, ...), custom_call_target="tpu_custom_call" | custom-call | flops 1 | bytes 1 | tf_op jit(solution)/shard_map/pallas_call | solution.py:941
  287.5 3.6 all-to-all-start
  291.6 12.2 %shard_map.196 = bf16[4096,768]{1,0:T(8,128)(2,1)} custom-call(bf16[4,256,1024]{2,1,0:T(8,128)(2,1)} %get-tuple-element.130.refs_0_, bf16[256,768]{1,0:T(8,128)(2,1)} %collective-permute-done.9.refs_1_.gated_1_ref, bf16[256,768]{1,0:T(8,128)(2,1)} %collective-permute-done.10.refs_2_.gated_2_ref, ...), custom_call_target="tpu_custom_call" | custom-call | flops 12884901888 | bytes 12582912 | tf_op jit(solution)/shard_map/pallas_call | solution.py:337
  303.9 27.9 %all-to-all-done = bf16[4,256,1024]{2,1,0:T(8,128)(2,1)S(1)} async-done(((bf16[4,256,1024]{2,1,0:T(8,128)(2,1)}), bf16[4,256,1024]{2,1,0:T(8,128)(2,1)S(1)}, u32[]{:S(2)}, u32[]{:S(2)}) %all-to-all-start) | async-done | bytes 2097184 | tf_op jit(solution)/shard_map/all_to_all | solution.py:68
  331.9 13.2 %conditional.1 = ((bf16[4096,512]{1,0:T(8,128)(2,1)}, bf16[768,256]{1,0:T(8,128)(2,1)}, bf16[768,256]{1,0:T(8,128)(2,1)})) conditional(s32[]{:T(128)} %convert_element_type.112, (s32[4]{0:T(128)S(1)}, bf16[1024,1024]{1,0:T(8,128)(2,1)S(1)}, bf16[4096,1536]{1,0:T(8,128)(2,1)}, bf16[4096,768]{1,0:T(8,128)(2,1)}, ...), branch_computations={%region_4.5_spmd, %region_5.6_spmd} | conditional | flops 1 | bytes 9 | solution.py:1207
  331.9 13.0 %branch_1_fun.1 = (bf16[4096,512]{1,0:T(8,128)(2,1)}, bf16[768,256]{1,0:T(8,128)(2,1)}, bf16[768,256]{1,0:T(8,128)(2,1)}) custom-call(s32[4]{0:T(128)S(1)} %get-tuple-element.25.scalar_ref, bf16[1024,1024]{1,0:T(8,128)(2,1)S(1)} %get-tuple-element.26.refs_0_, bf16[4096,1536]{1,0:T(8,128)(2,1)} %get-tuple-element.27.refs_1_, ...), custom_call_target="tpu_custom_call" | custom-call | flops 1 | bytes 1 | tf_op jit(solution)/shard_map/cond/branch_1_fun/pallas_call | solution.py:402
  345.1 3.3 shard_map.197
  349.7 7.5 %shard_map.198 = (bf16[16,96,640]{2,1,0:T(8,128)(2,1)}, bf16[192,768]{1,0:T(8,128)(2,1)}, bf16[192,768]{1,0:T(8,128)(2,1)}) custom-call(s32[4]{0:T(128)S(1)} %pad_add_fusion.1.places_ref.scalar_ref, bf16[4096,512]{1,0:T(8,128)(2,1)} %get-tuple-element.135.behind_ref.refs_2_, bf16[1024,1024]{1,0:T(8,128)(2,1)S(1)} %bitcast.115, bf16[256,768]{1,0:T(8,128)(2,1)} %copy-done.9, ...), custom_call_target="tpu_custom_call" | custom-call | flops 1 | bytes 1 | tf_op jit(solution)/shard_map/pallas_call | solution.py:631
  357.2 6.1 %all-to-all-start.1 = ((bf16[16,96,640]{2,1,0:T(8,128)(2,1)}), bf16[16,96,640]{2,1,0:T(8,128)(2,1)S(1)}, u32[]{:S(2)}, u32[]{:S(2)}) async-start(bf16[16,96,640]{2,1,0:T(8,128)(2,1)} %get-tuple-element.140.refs_0_), calls=%async_computation.1 | async-start | bytes 3932160 | tf_op jit(solution)/shard_map/all_to_all | solution.py:68
  364.6 12.6 %shard_map.200 = (bf16[768,512]{1,0:T(8,128)(2,1)}, bf16[768,512]{1,0:T(8,128)(2,1)}) custom-call(s32[4]{0:T(128)S(1)} %pad_add_fusion.1.places_ref.scalar_ref, bf16[16,96,640]{2,1,0:T(8,128)(2,1)} %get-tuple-element.140.refs_0_, bf16[4096,1536]{1,0:T(8,128)(2,1)} %all-gather.10.cloned.1.call-done.refs_0_.refs_4_.refs_1_, ...), custom_call_target="tpu_custom_call" | custom-call | flops 1 | bytes 1 | tf_op jit(solution)/shard_map/pallas_call | solution.py:402
  388.5 3.9 all-to-all-done.1.come_ref
  401.1 6.5 %collective-permute-done.14.refs_4_ = bf16[768,256]{1,0:T(8,128)(2,1)} collective-permute-done((bf16[768,256]{1,0:T(8,128)(2,1)}, bf16[768,256]{1,0:T(8,128)(2,1)}, u32[]{:S(2)}, u32[]{:S(2)}) %collective-permute-start.14) | collective-permute-done | bytes 393248 | tf_op jit(solution)/shard_map/ppermute | solution.py:40
  411.3 7.2 %all-to-all-start.2 = ((bf16[16,48,768]{2,1,0:T(8,128)(2,1)}), bf16[16,48,768]{2,1,0:T(8,128)(2,1)S(1)}, u32[]{:S(2)}, u32[]{:S(2)}) async-start(bf16[16,48,768]{2,1,0:T(8,128)(2,1)} %bitcast.116), calls=%async_computation.2 | async-start | bytes 2359296 | tf_op jit(solution)/shard_map/all_to_all | solution.py:68
  418.6 18.3 %all-gather.14.cloned.1.call-done.small_ref = f32[128,64,128]{2,1,0:T(8,128)} async-done(((f32[1,64,128]{2,1,0:T(8,128)}), f32[128,64,128]{2,1,0:T(8,128)}) %all-gather.14.cloned.1.call-update) | async-done | bytes 4194320 | tf_op jit(solution)/shard_map/all_gather | solution.py:1231
  436.9 3.4 shard_map.202
  443.7 4.5 collective-permute-start.16
  448.8 3.3 collective-permute-done.16.behind_ref
  (218 shorter events, 109.2 us)
Async XLA Ops:
  7.2 93.0 %all-gather.6.cloned.1.call-start = ((), (), s32[]{:S(2)}) async-start(), calls=%async_computation.3 | async-start | bytes 11182080 | tf_op jit(solution)/shard_map/all_gather | solution.py:1091
  9.7 159.9 %all-gather.8.cloned.1.call-start = ((), (), s32[]{:S(2)}) async-start(), calls=%async_computation.4 | async-start | bytes 12976128 | tf_op jit(solution)/shard_map/all_gather | solution.py:1091
  14.4 230.2 %all-gather.10.cloned.1.call-start = ((), (), s32[]{:S(2)}) async-start(), calls=%async_computation.5 | async-start | bytes 12976128 | tf_op jit(solution)/shard_map/all_gather | solution.py:1091
  109.0 2.0 collective-permute-start
  112.5 53.1 %copy-start = (f32[128,1536]{1,0:T(8,128)}, f32[128,1536]{1,0:T(8,128)S(1)}, u32[]{:S(2)}) copy-start(f32[128,1536]{1,0:T(8,128)S(1)} %get-tuple-element.167.values_ref) | copy-start | bytes 2359300
  131.6 2.0 collective-permute-start.1
  134.9 13.6 %collective-permute-start.2 = (bf16[128,1536]{1,0:T(8,128)(2,1)S(1)}, bf16[128,1536]{1,0:T(8,128)(2,1)S(1)}, u32[]{:S(2)}, u32[]{:S(2)}) collective-permute-start(bf16[128,1536]{1,0:T(8,128)(2,1)S(1)} %add_convert_fusion.1), channel_id=1, source_target_pairs={{0,64},{1,65},{2,66},{3,67},{4,68},{5,69},{6,70},{7,71},{8,72},{9,... | collective-permute-start | bytes 1179656 | tf_op jit(solution)/shard_map/ppermute | solution.py:1145
  162.1 2.1 collective-permute-start.3
  165.6 27.7 %copy-start.1 = (f32[128,1536]{1,0:T(8,128)}, f32[128,1536]{1,0:T(8,128)S(1)}, u32[]{:S(2)}) copy-start(f32[128,1536]{1,0:T(8,128)S(1)} %get-tuple-element.163.values_ref) | copy-start | bytes 2359300
  166.6 165.2 %all-gather.12.cloned.1.call-start = ((), (), s32[]{:S(2)}) async-start(), calls=%async_computation.6 | async-start | bytes 12976128 | tf_op jit(solution)/shard_map/all_gather | solution.py:1091
  193.2 2.0 collective-permute-start.5
  218.8 2.2 collective-permute-start.6
  224.9 15.0 %collective-permute-start.7 = (bf16[128,1536]{1,0:T(8,128)(2,1)}, bf16[128,1536]{1,0:T(8,128)(2,1)S(1)}, u32[]{:S(2)}, u32[]{:S(2)}) collective-permute-start(bf16[128,1536]{1,0:T(8,128)(2,1)} %get-tuple-element.122), channel_id=1, source_target_pairs={{64,0},{65,1},{66,2},{67,3},{68,4},{69,5},{70,6},{71,7},{72,8},{73... | collective-permute-start | bytes 1179656 | tf_op jit(solution)/shard_map/ppermute | solution.py:1177
  261.4 6.3 %collective-permute-start.8 = (bf16[128,1536]{1,0:T(8,128)(2,1)}, bf16[128,1536]{1,0:T(8,128)(2,1)S(1)}, u32[]{:S(2)}, u32[]{:S(2)}) collective-permute-start(bf16[128,1536]{1,0:T(8,128)(2,1)} %get-tuple-element.126), channel_id=1, source_target_pairs={{0,1},{1,0},{2,3},{3,2},{4,5},{5,4},{6,7},{7,6},{8,9},{9,8},{10,11... | collective-permute-start | bytes 1179656 | tf_op jit(solution)/shard_map/ppermute | solution.py:40
  261.8 29.9 %collective-permute-start.9 = (bf16[256,768]{1,0:T(8,128)(2,1)S(1)}, bf16[256,768]{1,0:T(8,128)(2,1)}, u32[]{:S(2)}, u32[]{:S(2)}) collective-permute-start(bf16[256,768]{1,0:T(8,128)(2,1)S(1)} %broadcast_select_fusion.gated_0_ref), channel_id=1, source_target_pairs={{0,2},{2,4},{4,6},{6,0},{1,3},{3,5},{5,7},{7,1},{8,10},{10,12},{12... | collective-permute-start | bytes 1179656 | tf_op jit(solution)/shard_map/ppermute | solution.py:1159
  263.3 28.3 %collective-permute-start.10 = (bf16[256,768]{1,0:T(8,128)(2,1)S(1)}, bf16[256,768]{1,0:T(8,128)(2,1)}, u32[]{:S(2)}, u32[]{:S(2)}) collective-permute-start(bf16[256,768]{1,0:T(8,128)(2,1)S(1)} %broadcast_select_fusion.gated_0_ref), channel_id=1, source_target_pairs={{0,4},{2,6},{4,0},{6,2},{1,5},{3,7},{5,1},{7,3},{8,12},{10,14},{12... | collective-permute-start | bytes 1179656 | tf_op jit(solution)/shard_map/ppermute | solution.py:1159
  266.3 25.3 %collective-permute-start.11 = (bf16[256,768]{1,0:T(8,128)(2,1)S(1)}, bf16[256,768]{1,0:T(8,128)(2,1)}, u32[]{:S(2)}, u32[]{:S(2)}) collective-permute-start(bf16[256,768]{1,0:T(8,128)(2,1)S(1)} %broadcast_select_fusion.gated_0_ref), channel_id=1, source_target_pairs={{0,6},{2,0},{4,2},{6,4},{1,7},{3,1},{5,3},{7,5},{8,14},{10,8},{12,... | collective-permute-start | bytes 1179656 | tf_op jit(solution)/shard_map/ppermute | solution.py:1159
  287.5 44.3 %all-to-all-start = ((bf16[4,256,1024]{2,1,0:T(8,128)(2,1)}), bf16[4,256,1024]{2,1,0:T(8,128)(2,1)S(1)}, u32[]{:S(2)}, u32[]{:S(2)}) async-start(bf16[4,256,1024]{2,1,0:T(8,128)(2,1)} %get-tuple-element.130.refs_0_), calls=%async_computation | async-start | bytes 4194304 | tf_op jit(solution)/shard_map/all_to_all | solution.py:68
  291.2 145.7 %all-gather.14.cloned.1.call-start = ((), (), s32[]{:S(2)}) async-start(), calls=%async_computation.7 | async-start | bytes 4227072 | tf_op jit(solution)/shard_map/all_gather | solution.py:1231
  291.4 40.5 %copy-start.4 = (bf16[256,1536]{1,0:T(8,128)(2,1)S(1)}, bf16[256,1536]{1,0:T(8,128)(2,1)}, u32[]{:S(2)}) copy-start(bf16[256,1536]{1,0:T(8,128)(2,1)} %pad.31) | copy-start | bytes 2359300
  291.4 53.7 %collective-permute-start.12 = (bf16[128,1536]{1,0:T(8,128)(2,1)}, bf16[128,1536]{1,0:T(8,128)(2,1)}, u32[]{:S(2)}, u32[]{:S(2)}) collective-permute-start(bf16[128,1536]{1,0:T(8,128)(2,1)} %get-tuple-element.137), channel_id=1, source_target_pairs={{0,1},{1,0},{2,3},{3,2},{4,5},{5,4},{6,7},{7,6},{8,9},{9,8},{10,11... | collective-permute-start | bytes 1179656 | tf_op jit(solution)/shard_map/ppermute | solution.py:40
  357.2 35.2 %all-to-all-start.1 = ((bf16[16,96,640]{2,1,0:T(8,128)(2,1)}), bf16[16,96,640]{2,1,0:T(8,128)(2,1)S(1)}, u32[]{:S(2)}, u32[]{:S(2)}) async-start(bf16[16,96,640]{2,1,0:T(8,128)(2,1)} %get-tuple-element.140.refs_0_), calls=%async_computation.1 | async-start | bytes 3932160 | tf_op jit(solution)/shard_map/all_to_all | solution.py:68
  363.3 14.8 %collective-permute-start.17 = (bf16[192,768]{1,0:T(8,128)(2,1)S(1)}, bf16[192,768]{1,0:T(8,128)(2,1)S(1)}, u32[]{:S(2)}, u32[]{:S(2)}) collective-permute-start(bf16[192,768]{1,0:T(8,128)(2,1)S(1)} %copy-done.31), channel_id=1, source_target_pairs={{0,32},{32,0},{1,33},{33,1},{2,34},{34,2},{3,35},{35,3},{4,36},{36... | collective-permute-start | bytes 884744 | tf_op jit(solution)/shard_map/ppermute | solution.py:40
  364.6 19.1 %collective-permute-start.4 = (bf16[128,1536]{1,0:T(8,128)(2,1)}, bf16[128,1536]{1,0:T(8,128)(2,1)}, u32[]{:S(2)}, u32[]{:S(2)}) collective-permute-start(bf16[128,1536]{1,0:T(8,128)(2,1)} %get-tuple-element.113), channel_id=1, source_target_pairs={{0,1},{1,0},{2,3},{3,2},{4,5},{5,4},{6,7},{7,6},{8,9},{9,8},{10,11... | collective-permute-start | bytes 1179656 | tf_op jit(solution)/shard_map/ppermute | solution.py:40
  377.2 30.4 %collective-permute-start.13 = (bf16[768,512]{1,0:T(8,128)(2,1)}, bf16[768,512]{1,0:T(8,128)(2,1)S(1)}, u32[]{:S(2)}, u32[]{:S(2)}) collective-permute-start(bf16[768,512]{1,0:T(8,128)(2,1)} %get-tuple-element.143), channel_id=1, source_target_pairs={{0,32},{32,0},{1,33},{33,1},{2,34},{34,2},{3,35},{35,3},{4,36},{36... | collective-permute-start | bytes 2359304 | tf_op jit(solution)/shard_map/ppermute | solution.py:40
  380.6 16.1 %collective-permute-start.20 = (bf16[48,768]{1,0:T(8,128)(2,1)}, bf16[48,768]{1,0:T(8,128)(2,1)S(1)}, u32[]{:S(2)}, u32[]{:S(2)}) collective-permute-start(bf16[48,768]{1,0:T(8,128)(2,1)} %get-tuple-element.176), channel_id=1, source_target_pairs={{0,24},{8,0},{16,8},{24,16},{1,25},{9,1},{17,9},{25,17},{2,26},{10... | collective-permute-start | bytes 221192 | tf_op jit(solution)/shard_map/ppermute | solution.py:1263
  385.6 22.0 %collective-permute-start.14 = (bf16[768,256]{1,0:T(8,128)(2,1)}, bf16[768,256]{1,0:T(8,128)(2,1)}, u32[]{:S(2)}, u32[]{:S(2)}) collective-permute-start(bf16[768,256]{1,0:T(8,128)(2,1)} %get-tuple-element.145), channel_id=1, source_target_pairs={{0,32},{32,0},{1,33},{33,1},{2,34},{34,2},{3,35},{35,3},{4,36},{36... | collective-permute-start | bytes 1179656 | tf_op jit(solution)/shard_map/ppermute | solution.py:40
  386.8 12.7 %collective-permute-start.19 = (bf16[48,768]{1,0:T(8,128)(2,1)}, bf16[48,768]{1,0:T(8,128)(2,1)S(1)}, u32[]{:S(2)}, u32[]{:S(2)}) collective-permute-start(bf16[48,768]{1,0:T(8,128)(2,1)} %get-tuple-element.177), channel_id=1, source_target_pairs={{0,16},{8,24},{16,0},{24,8},{1,17},{9,25},{17,1},{25,9},{2,18},{10... | collective-permute-start | bytes 221192 | tf_op jit(solution)/shard_map/ppermute | solution.py:1263
  387.7 11.9 %collective-permute-start.18 = (bf16[48,768]{1,0:T(8,128)(2,1)}, bf16[48,768]{1,0:T(8,128)(2,1)}, u32[]{:S(2)}, u32[]{:S(2)}) collective-permute-start(bf16[48,768]{1,0:T(8,128)(2,1)} %get-tuple-element.175), channel_id=1, source_target_pairs={{0,8},{8,16},{16,24},{24,0},{1,9},{9,17},{17,25},{25,1},{2,10},{10... | collective-permute-start | bytes 221192 | tf_op jit(solution)/shard_map/ppermute | solution.py:1263
  396.7 21.9 %collective-permute-start.15 = (bf16[4,48,640]{2,1,0:T(8,128)(2,1)}, bf16[4,48,640]{2,1,0:T(8,128)(2,1)S(1)}, u32[]{:S(2)}, u32[]{:S(2)}) collective-permute-start(bf16[4,48,640]{2,1,0:T(8,128)(2,1)} %get-tuple-element.146), channel_id=1, source_target_pairs={{0,32},{32,0},{1,33},{33,1},{2,34},{34,2},{3,35},{35,3},{4,36},{36... | collective-permute-start | bytes 737288 | tf_op jit(solution)/shard_map/ppermute | solution.py:40
  411.3 44.1 %all-to-all-start.2 = ((bf16[16,48,768]{2,1,0:T(8,128)(2,1)}), bf16[16,48,768]{2,1,0:T(8,128)(2,1)S(1)}, u32[]{:S(2)}, u32[]{:S(2)}) async-start(bf16[16,48,768]{2,1,0:T(8,128)(2,1)} %bitcast.116), calls=%async_computation.2 | async-start | bytes 2359296 | tf_op jit(solution)/shard_map/all_to_all | solution.py:68
  443.7 8.5 %collective-permute-start.16 = (bf16[4,24,640]{2,1,0:T(8,128)(2,1)}, bf16[4,24,640]{2,1,0:T(8,128)(2,1)S(1)}, u32[]{:S(2)}, u32[]{:S(2)}) collective-permute-start(bf16[4,24,640]{2,1,0:T(8,128)(2,1)} %get-tuple-element.155), channel_id=1, source_target_pairs={{0,64},{64,0},{1,65},{65,1},{2,66},{66,2},{3,67},{67,3},{4,68},{68... | collective-permute-start | bytes 368648 | tf_op jit(solution)/shard_map/ppermute | solution.py:40
  (30 other events, 305.5 us)
Sparse Core Ops, SparseCore 0:
  11.4 88.7 all-gather.5
  103.0 62.5 all-gather.7
  167.8 62.4 all-gather.9
  241.2 84.0 all-gather.11
  349.8 87.0 all-gather.13

commit v7 on v5

--- a/solution.py
+++ b/solution.py
@@ -550,9 +550,8 @@
 
 
 def mixer_grads_kernel(
-    places_ref, behind_ref, columns_ref, gated_0_ref, gated_1_ref, gated_2_ref, gated_3_ref,
-    early_ref, late_ref, in_mine_ref, in_other_ref, out_mine_ref, out_other_ref,
-    normed_ref, in_ref, out_ref, sem,
+    places_ref, behind_ref, columns_ref, gated_ref, early_ref, late_ref,
+    in_mine_ref, in_other_ref, out_mine_ref, out_other_ref, normed_ref, in_ref, out_ref, sem,
 ):
     here, section, y = places_ref[0], places_ref[1], places_ref[2]
 
@@ -570,15 +569,7 @@
         copy(late_ref).start()
 
     mix = out_ref.shape[0]
-    blocks = (gated_0_ref, gated_1_ref, gated_2_ref, gated_3_ref)
-    span = gated_0_ref.shape[0]
-    total = None
-    for k, gated_ref in enumerate(blocks):
-        start = lax.rem(places_ref[3] - k + len(blocks), len(blocks)) * span
-        tiles = columns_ref[pl.ds(pl.multiple_of(start, span), span), :mix]
-        block = product_left(tiles, gated_ref[...])
-        total = block if total is None else total + block
-    out_ref[...] = total
+    out_ref[...] = product_left(columns_ref[:, :mix], gated_ref[...])
     pair_out(out_ref, here, out_mine_ref, out_other_ref)
     copy(early_ref).wait()
     in_ref[...] = product_left(normed_ref[...], columns_ref[:, mix:])
@@ -594,7 +585,7 @@
 
 def mixer_grads_call(places, behind, columns, gated, early, late, plane):
     vmem, any_space = pl.BlockSpec(memory_space=pltpu.VMEM), pl.BlockSpec(memory_space=pl.ANY)
-    tokens, channels = columns.shape[0], gated[0].shape[1]
+    tokens, channels = gated.shape
     width = early.shape[1]
     mix = width // 4
     size = columns.shape[1] - mix
@@ -606,7 +597,7 @@
             pl.BlockSpec(memory_space=pltpu.SMEM),
             any_space,
             vmem,
-            *[vmem] * len(gated),
+            vmem,
             any_space,
             any_space,
         ],
@@ -620,7 +611,7 @@
         ],
         compiler_params=pltpu.CompilerParams(vmem_limit_bytes=VMEM_LIMIT),
         cost_estimate=SHORT,
-    )(places, behind, columns, *gated, early, late)
+    )(places, behind, columns, gated, early, late)
 
 
 def load_all(copies):
@@ -942,9 +933,7 @@
     )
 
 
-def conv_backward_call(
-    core, grad, kernel, masks, projected, tiles, whole, weight_out, behind
-):
+def conv_backward_call(core, grad, kernel, masks, projected, tiles, whole, weight_out):
     count, width = grad.shape
     taps, channels = kernel.shape
     outs = [
@@ -953,7 +942,7 @@
     ]
     operands = (grad, kernel, masks, projected, tiles)
     return mixer_call(
-        conv_backward_kernel, core, operands, whole, weight_out, (3, channels), outs, (), behind
+        conv_backward_kernel, core, operands, whole, weight_out, (3, channels), outs
     )
 
 
@@ -1054,9 +1043,9 @@
     part = hidden_units // plane
     in_width = 3 * channels
     qkv_width = attn_qkv.shape[1]
-    y, z = lax.axis_index("y"), lax.axis_index("z")
+    y = lax.axis_index("y")
     core_scalar = jnp.stack([core, section]).astype(jnp.int32)
-    xl_scalar = jnp.stack([xl, section, y, z]).astype(jnp.int32)
+    xl_scalar = jnp.stack([xl, section, y]).astype(jnp.int32)
 
     def chosen(from_first, from_second):
         return jnp.where(first, from_first, from_second)
@@ -1130,7 +1119,7 @@
 
     inner_all = gathered(chosen(inner_0, inner_1), plane_axes)
     gated = chosen(gated_0, gated_1)
-    gated_z = [gated, *[lax.ppermute(gated, "z", around(by)) for by in range(1, 4)]]
+    gated_z = gathered(gated, "z")
 
     grad_hidden_1, grad_mix_1, gain_inner_1 = inner_back(
         grad_mine, grad_other, hidden_1, out_cotangent.astype(F32)
@@ -1171,7 +1160,6 @@
         tiles_1,
         whole,
         weight_out,
-        gated_z[1:],
     )
     columns = exchanged(tiles, "z").reshape(4 * rows, -1)
     part_kept = part_forward_call(tiles, inner_all, part_pair)
@@ -1185,10 +1173,10 @@
         lambda: part_down_call(xl_scalar, early, part_kept, part_down, (columns,)),
     )
     input_grad_0, gain_outer_0 = mixer_back(grad_hidden_0, mine, other, first_in, pair_grads)
+    pair_mine, pair_other = part_pair_call(xl_scalar, inner_all, pair_grads, ())
     in_mine, in_other, out_mine, out_other = mixer_grads_call(
-        xl_scalar, pair_grads, columns, gated_z, early, late, plane
-    )
-    pair_mine, pair_other = part_pair_call(xl_scalar, inner_all, pair_grads, (in_mine,))
+        xl_scalar, pair_other, columns, gated_z, early, late, plane
+    )
 
     full_kernel = lax.dynamic_update_slice(
         jnp.zeros(conv_kernel.shape, F32), grad_kernel, (0, core * channels)
@@ -1205,30 +1193,26 @@
     small = jnp.pad(small, (0, -count % 1024)).reshape(-1, 128)
     small_all = lax.all_gather(small, AXES)
 
-    down_total = pair_join_call((), [(down_mine, swapped(down_other, "xl"))])
-    in_total = pair_join_call((pair_other, down_total), [(in_mine, swapped(in_other, "xl"))])
-    come = exchanged(in_total, PLANE)
-
-    pair_total = pair_join_call((come,), [(pair_mine, swapped(pair_other, "xl"))])
-    total = jnp.concatenate([pair_total, down_total], axis=1)
+    pairs = [(a, swapped(b, "xl")) for a, b in ((pair_mine, pair_other), (down_mine, down_other))]
+    total = pair_join_call((), pairs)
     arrived = exchanged(total.reshape(plane, -1, 3 * lanes), PLANE)
-
-    kept_lines, sent_lines, sums = finish_call(xl_scalar, total, come, small_all)
-    across = swapped(sent_lines, "xh")
-    come = across.astype(F32)[:, :, : in_width // 4]
-    kept_lines = kept_lines[:, :, : in_width // 4]
-    lines = chosen(kept_lines, come).reshape(4, -1, 3, channels // 4)
-    grad_conv_in = jnp.moveaxis(lines, 0, 2).reshape(conv_in.shape)
-    lines = chosen(come, kept_lines)[:, :, : qkv_width // 4]
-    grad_attn_qkv = jnp.moveaxis(lines, 0, 1).reshape(attn_qkv.shape)
-
-    arrived = widened_call(across, arrived)
+    arrived = widened_call(core_scalar, arrived)
     lines = [
         jnp.moveaxis(arrived[:, :, k * lanes : k * lanes + part], 0, 1).reshape(-1, hidden_units)
         for k in range(3)
     ]
     grad_gate_up = jnp.stack(lines[:2])[None]
     grad_down = lines[2].T[None]
+
+    in_total = pair_join_call((total,), [(in_mine, swapped(in_other, "xl"))])
+    come = exchanged(in_total, PLANE)
+    kept_lines, sent_lines, sums = finish_call(xl_scalar, arrived, come, small_all)
+    come = swapped(sent_lines, "xh").astype(F32)[:, :, : in_width // 4]
+    kept_lines = kept_lines[:, :, : in_width // 4]
+    lines = chosen(kept_lines, come).reshape(4, -1, 3, channels // 4)
+    grad_conv_in = jnp.moveaxis(lines, 0, 2).reshape(conv_in.shape)
+    lines = chosen(come, kept_lines)[:, :, : qkv_width // 4]
+    grad_attn_qkv = jnp.moveaxis(lines, 0, 1).reshape(attn_qkv.shape)
 
     total = summed_over_pair(out_mine, out_other).reshape(4, -1, channels)
     sent = total.astype(BF16)

time: 475 us -> 476 us (level)
    ppermute x3 -> x0, waiting for transfers between devices: 19.4 us -> none  [local(): lax.ppermute(gated, 'z', around(by))]
    ppermute x13, waiting for transfers between devices: 26.5 us -> 44.6 us  [swapped(): return lax.ppermute(shard, axis, [(0, 1), (1, 0)])]
    all_to_all x3, waiting for transfers between devices: 11.9 us -> 22.7 us  [exchanged(): return lax.all_to_all(tiles, axes, 0, 0, tiled=True)]
    ppermute x3, waiting for transfers between devices: 7.36 us -> 0.01 us  [local(): lines += lax.ppermute(block, 'y', around(by)).astype(F32)]
    ppermute x3 -> x0, starting transfers between devices: 5 us -> none  [local(): lax.ppermute(gated, 'z', around(by))]
    all_gather x4 -> x5, waiting for transfers between devices: 63.2 us -> 63.3 us  [gathered(): return lax.all_gather(own, axes, tiled=True)]
  transfers between devices with their start and end apart: 29 -> 27, of which waited for: 16 -> 13; matrix products, arithmetic and copies ran while one was open for 10% -> 12% of each run, Pallas kernels for 36% -> 36%
where the time goes in v7:
time: 476 us; the launch traced here: 468 us
  Pallas kernels  172 us (36%)
  waiting for transfers between devices  154 us (32%)
  local copies, waits for them, and re-layouts  37.5 us (8%)
  starting transfers between devices  34.5 us (7%)
  other arithmetic  31.1 us (7%)
  blocking collectives  24.2 us (5%)
  between operations  14.9 us (3%)
    all_gather x5, waiting for transfers between devices, gathered(): return lax.all_gather(own, axes, tiled=True)  63.3 us
    pallas_call x4, Pallas kernels, mixer_call(): pl.pallas_call(ordered(kernel, len(behind)), in_specs=[pl.BlockSpec(memor...  45.2 us
    ppermute x13, waiting for transfers between devices, swapped(): return lax.ppermute(shard, axis, [(0, 1), (1, 0)])  44.6 us
    pallas_call x2, Pallas kernels, feed_forward_call(): pl.pallas_call(ordered(body, len(behind)), in_specs=in_specs, out_specs=o...  33 us
    pallas_call x2, Pallas kernels, part_call(): pl.pallas_call(ordered(kernel, len(behind)), grid_spec=pltpu.PrefetchScal...  25.7 us
    all_gather x8, blocking collectives, spread(): return lax.all_gather(own, 'c', tiled=True)  24.2 us
    pallas_call x1, Pallas kernels, ffn_both_call(): pl.pallas_call(ordered(functools.partial(ffn_both_kernel, unit_tiles(unit...  23.6 us
    all_to_all x3, waiting for transfers between devices, exchanged(): return lax.all_to_all(tiles, axes, 0, 0, tiled=True)  22.7 us
  transfers between devices with their start and end apart: 27, of which 13 were waited for; matrix products, arithmetic and copies ran while one was open for 12% of the time, Pallas kernels for 36%

profile of v7, /device:TPU:0, one launch (start us, length us, event | category | flops | bytes accessed | tf_op | source)
XLA Modules:
  0.0 468.2 jit_solution(16643295573679802308)
XLA Ops:
  26.6 8.1 %fusion.15 = (bf16[1,1,1536,3456]{3,2,1,0:T(8,128)(2,1)S(1)}, bf16[1,1,1536,3456]{3,2,1,0:T(8,128)(2,1)S(1)}) fusion(bf16[1,2,1536,3456]{3,2,1,0:T(8,128)(2,1)} %param.22), kind=kLoop, calls=%fused_computation.95 | loop fusion | bytes 42467328 | tf_op jit(solution)/shard_map/slice | solution.py:1065
  36.9 63.3 %all-gather.7.cloned.1.call-done.refs_3_.refs_4_.refs_6_.refs_5_ = bf16[1536,3584]{1,0:T(8,128)(2,1)} async-done(((bf16[24,3584]{1,0:T(8,128)(2,1)}), bf16[1536,3584]{1,0:T(8,128)(2,1)}) %all-gather.7.cloned.1.call-update) | async-done | bytes 11010064 | tf_op jit(solution)/shard_map/all_gather | solution.py:1054
  100.9 8.1 %shard_map.186 = (bf16[3,256,768]{2,1,0:T(8,128)(2,1)}, bf16[256,768]{1,0:T(8,128)(2,1)}, f32[128,1536]{1,0:T(8,128)}, bf16[128,1536]{1,0:T(8,128)(2,1)}) custom-call(s32[2]{0:T(128)} %pad_add_fusion.scalar_ref.behind_ref, bf16[256,1536]{1,0:T(8,128)(2,1)} %all_gather.43.refs_0_, f32[3,768]{1,0:T(4,128)} %dynamic-slice_convert_fusion.refs_1_, ...), custom_call_target="tpu_custom_call" | custom-call | flops 1 | bytes 1 | tf_op jit(solution)/shard_map/pallas_call | solution.py:904
  115.3 16.3 %shard_map.187 = (bf16[256,3456]{1,0:T(8,128)(2,1)}, bf16[256,3456]{1,0:T(8,128)(2,1)}, f32[128,1536]{1,0:T(8,128)}, bf16[128,1536]{1,0:T(8,128)(2,1)}) custom-call(s32[2]{0:T(128)} %pad_add_fusion.scalar_ref.behind_ref, bf16[256,1536]{1,0:T(8,128)(2,1)} %all_gather.45.refs_0_, bf16[2,1536,3456]{2,1,0:T(8,128)(2,1)} %bitcast.102, bf16[3456,1536]{1,0:T(8,128)(2,1)} %bitcast.105), custom_call_target="tpu_custom_call" | custom-call | flops 1 | bytes 1 | tf_op jit(solution)/shard_map/pallas_call | solution.py:307
  134.9 4.9 %collective-permute-start.2 = (bf16[128,1536]{1,0:T(8,128)(2,1)S(1)}, bf16[128,1536]{1,0:T(8,128)(2,1)S(1)}, u32[]{:S(2)}, u32[]{:S(2)}) collective-permute-start(bf16[128,1536]{1,0:T(8,128)(2,1)S(1)} %add_convert_fusion.1), channel_id=1, source_target_pairs={{0,64},{1,65},{2,66},{3,67},{4,68},{5,69},{6,70},{7,71},{8,72},{9,... | collective-permute-start | bytes 1179656 | tf_op jit(solution)/shard_map/ppermute | solution.py:1108
  139.9 8.7 %collective-permute-done.2 = bf16[128,1536]{1,0:T(8,128)(2,1)S(1)} collective-permute-done((bf16[128,1536]{1,0:T(8,128)(2,1)S(1)}, bf16[128,1536]{1,0:T(8,128)(2,1)S(1)}, u32[]{:S(2)}, u32[]{:S(2)}) %collective-permute-start.2) | collective-permute-done | bytes 393248 | tf_op jit(solution)/shard_map/ppermute | solution.py:1108
  151.4 10.7 %shard_map.188 = (f32[256,1280]{1,0:T(8,128)}, bf16[256,1280]{1,0:T(8,128)(2,1)}, bf16[256,768]{1,0:T(8,128)(2,1)}, f32[128,1536]{1,0:T(8,128)}, bf16[128,1536]{1,0:T(8,128)(2,1)}) custom-call(s32[2]{0:T(128)} %pad_add_fusion.scalar_ref.behind_ref, bf16[256,1536]{1,0:T(8,128)(2,1)} %all_gather.46.refs_0_, f32[9,128]{1,0:T(8,128)} %stack.86.refs_1_, ...), custom_call_target="tpu_custom_call" | custom-call | flops 1 | bytes 1 | tf_op jit(solution)/shard_map/pallas_call | solution.py:904
  166.7 2.9 all_gather.48.refs_1_
  169.6 23.6 %shard_map.189 = (f32[128,1536]{1,0:T(8,128)}, bf16[128,1536]{1,0:T(8,128)(2,1)}, f32[128,1536]{1,0:T(8,128)}, bf16[128,1536]{1,0:T(8,128)(2,1)}) custom-call(s32[2]{0:T(128)} %pad_add_fusion.scalar_ref.behind_ref, bf16[4096,1536]{1,0:T(8,128)(2,1)} %all-gather.9.cloned.1.call-done.refs_0_.early_ref, bf16[256,1536]{1,0:T(8,128)(2,1)} %all_gather.48.refs_1_, ...), custom_call_target="tpu_custom_call" | custom-call | flops 1 | bytes 1 | tf_op jit(solution)/shard_map/pallas_call | solution.py:255
  196.0 3.2 shard_map.190
  199.2 4.3 all_gather.50.refs_0_
  203.5 15.3 %shard_map.191 = (bf16[4,256,1024]{2,1,0:T(8,128)(2,1)}, f32[10,128]{1,0:T(8,128)}, f32[128,1536]{1,0:T(8,128)}, bf16[128,1536]{1,0:T(8,128)(2,1)}) custom-call(s32[2]{0:T(128)} %pad_add_fusion.scalar_ref.behind_ref, bf16[256,1536]{1,0:T(8,128)(2,1)} %all_gather.50.refs_0_, f32[9,128]{1,0:T(8,128)} %stack.86.refs_1_, f32[2,256,128]{2,1,0:T(8,128)} %bitcast.120, ...), custom_call_target="tpu_custom_call" | custom-call | flops 1 | bytes 1 | tf_op jit(solution)/shard_map/pallas_call | solution.py:904
  221.8 3.2 shard_map.192
  226.2 14.5 %collective-permute-done.7 = bf16[128,1536]{1,0:T(8,128)(2,1)S(1)} collective-permute-done((bf16[128,1536]{1,0:T(8,128)(2,1)}, bf16[128,1536]{1,0:T(8,128)(2,1)S(1)}, u32[]{:S(2)}, u32[]{:S(2)}) %collective-permute-start.7) | collective-permute-done | bytes 393248 | tf_op jit(solution)/shard_map/ppermute | solution.py:1140
  245.4 16.7 %shard_map.193 = (f32[128,1536]{1,0:T(8,128)}, bf16[128,1536]{1,0:T(8,128)(2,1)}) custom-call(s32[2]{0:T(128)} %pad_add_fusion.scalar_ref.behind_ref, bf16[4096,1536]{1,0:T(8,128)(2,1)} %all-gather.11.cloned.1.call-done.refs_0_.rows_ref, bf16[256,1536]{1,0:T(8,128)(2,1)} %all_gather.51.refs_1_, bf16[256,3456]{1,0:T(8,128)(2,1)} %get-tuple-element.122.refs_2_, ...), custom_call_target="tpu_custom_call" | custom-call | flops 1 | bytes 1 | tf_op jit(solution)/shard_map/pallas_call | solution.py:307
  264.8 3.2 shard_map.194
  268.0 4.3 all_gather.52.refs_0_
  272.4 11.1 %shard_map.195 = (bf16[4,256,1024]{2,1,0:T(8,128)(2,1)}, f32[3,768]{1,0:T(4,128)}, f32[128,1536]{1,0:T(8,128)}, bf16[128,1536]{1,0:T(8,128)(2,1)}) custom-call(s32[2]{0:T(128)} %pad_add_fusion.scalar_ref.behind_ref, bf16[256,1536]{1,0:T(8,128)(2,1)} %all_gather.52.refs_0_, f32[3,768]{1,0:T(4,128)} %dynamic-slice_convert_fusion.refs_1_, ...), custom_call_target="tpu_custom_call" | custom-call | flops 1 | bytes 1 | tf_op jit(solution)/shard_map/pallas_call | solution.py:904
  283.5 3.9 all-to-all-start
  287.8 12.2 %shard_map.196 = bf16[4096,768]{1,0:T(8,128)(2,1)} custom-call(bf16[4,256,1024]{2,1,0:T(8,128)(2,1)} %get-tuple-element.129.behind_ref, bf16[4096,1536]{1,0:T(8,128)(2,1)} %all-gather.11.cloned.1.call-done.refs_0_.rows_ref, bf16[1536,512]{1,0:T(8,128)(2,1)} %fusion.2.pair_ref), custom_call_target="tpu_custom_call" | custom-call | flops 12884901888 | bytes 12582912 | tf_op jit(solution)/shard_map/pallas_call | solution.py:333
  300.0 22.7 %all-to-all-done = bf16[4,256,1024]{2,1,0:T(8,128)(2,1)S(1)} async-done(((bf16[4,256,1024]{2,1,0:T(8,128)(2,1)}), bf16[4,256,1024]{2,1,0:T(8,128)(2,1)S(1)}, u32[]{:S(2)}, u32[]{:S(2)}) %all-to-all-start) | async-done | bytes 2097184 | tf_op jit(solution)/shard_map/all_to_all | solution.py:68
  322.8 13.1 %conditional.1 = ((bf16[4096,512]{1,0:T(8,128)(2,1)}, bf16[768,256]{1,0:T(8,128)(2,1)}, bf16[768,256]{1,0:T(8,128)(2,1)})) conditional(s32[]{:T(128)} %convert_element_type.112, (s32[3]{0:T(128)S(1)}, bf16[1024,1024]{1,0:T(8,128)(2,1)S(1)}, bf16[4096,1536]{1,0:T(8,128)(2,1)}, bf16[4096,768]{1,0:T(8,128)(2,1)}, ...), branch_computations={%region_4.5_spmd, %region_5.6_spmd} | conditional | flops 1 | bytes 9 | solution.py:1170
  322.8 13.1 %branch_1_fun.1 = (bf16[4096,512]{1,0:T(8,128)(2,1)}, bf16[768,256]{1,0:T(8,128)(2,1)}, bf16[768,256]{1,0:T(8,128)(2,1)}) custom-call(s32[3]{0:T(128)S(1)} %get-tuple-element.25.scalar_ref, bf16[1024,1024]{1,0:T(8,128)(2,1)S(1)} %get-tuple-element.26.refs_0_, bf16[4096,1536]{1,0:T(8,128)(2,1)} %get-tuple-element.27.refs_1_, ...), custom_call_target="tpu_custom_call" | custom-call | flops 1 | bytes 1 | tf_op jit(solution)/shard_map/cond/branch_1_fun/pallas_call | solution.py:398
  336.6 3.2 shard_map.197
  341.1 12.6 %shard_map.198 = (bf16[768,512]{1,0:T(8,128)(2,1)}, bf16[768,512]{1,0:T(8,128)(2,1)}) custom-call(s32[3]{0:T(128)S(1)} %pad_add_fusion.1.scalar_ref.places_ref, bf16[4096,1536]{1,0:T(8,128)(2,1)} %all-gather.11.cloned.1.call-done.refs_0_.rows_ref, bf16[4096,512]{1,0:T(8,128)(2,1)} %get-tuple-element.132.behind_ref.refs_1_), custom_call_target="tpu_custom_call" | custom-call | flops 1 | bytes 1 | tf_op jit(solution)/shard_map/pallas_call | solution.py:398
  356.0 7.8 %shard_map.201 = (bf16[16,48,640]{2,1,0:T(8,128)(2,1)}, bf16[16,48,640]{2,1,0:T(8,128)(2,1)}, bf16[192,768]{1,0:T(8,128)(2,1)}, bf16[192,768]{1,0:T(8,128)(2,1)}) custom-call(s32[3]{0:T(128)S(1)} %pad_add_fusion.1.scalar_ref.places_ref, bf16[768,512]{1,0:T(8,128)(2,1)} %get-tuple-element.138.behind_ref, bf16[1024,1024]{1,0:T(8,128)(2,1)S(1)} %bitcast.114, ...), custom_call_target="tpu_custom_call" | custom-call | flops 1 | bytes 1 | tf_op jit(solution)/shard_map/pallas_call | solution.py:594
  365.9 17.4 %collective-permute-done.11.refs_3_ = bf16[768,256]{1,0:T(8,128)(2,1)} collective-permute-done((bf16[768,256]{1,0:T(8,128)(2,1)}, bf16[768,256]{1,0:T(8,128)(2,1)}, u32[]{:S(2)}, u32[]{:S(2)}) %collective-permute-start.11) | collective-permute-done | bytes 393248 | tf_op jit(solution)/shard_map/ppermute | solution.py:40
  386.0 5.0 %all-to-all-start.1 = ((bf16[16,48,768]{2,1,0:T(8,128)(2,1)}), bf16[16,48,768]{2,1,0:T(8,128)(2,1)S(1)}, u32[]{:S(2)}, u32[]{:S(2)}) async-start(bf16[16,48,768]{2,1,0:T(8,128)(2,1)} %bitcast.115), calls=%async_computation.1 | async-start | bytes 2359296 | tf_op jit(solution)/shard_map/all_to_all | solution.py:68
  393.3 17.5 %collective-permute-done.14 = bf16[192,768]{1,0:T(8,128)(2,1)} collective-permute-done((bf16[192,768]{1,0:T(8,128)(2,1)}, bf16[192,768]{1,0:T(8,128)(2,1)}, u32[]{:S(2)}, u32[]{:S(2)}) %collective-permute-start.14) | collective-permute-done | bytes 294944 | tf_op jit(solution)/shard_map/ppermute | solution.py:40
  421.6 4.5 all-to-all-start.2
  444.2 3.5 shard_map.203
  451.1 3.8 collective-permute-start.13
  (205 shorter events, 103.8 us)
Async XLA Ops:
  7.2 93.0 %all-gather.7.cloned.1.call-start = ((), (), s32[]{:S(2)}) async-start(), calls=%async_computation.3 | async-start | bytes 11182080 | tf_op jit(solution)/shard_map/all_gather | solution.py:1054
  9.7 159.9 %all-gather.9.cloned.1.call-start = ((), (), s32[]{:S(2)}) async-start(), calls=%async_computation.4 | async-start | bytes 12976128 | tf_op jit(solution)/shard_map/all_gather | solution.py:1054
  14.4 231.0 %all-gather.11.cloned.1.call-start = ((), (), s32[]{:S(2)}) async-start(), calls=%async_computation.5 | async-start | bytes 12976128 | tf_op jit(solution)/shard_map/all_gather | solution.py:1054
  109.1 2.0 collective-permute-start
  112.5 53.1 %copy-start = (f32[128,1536]{1,0:T(8,128)}, f32[128,1536]{1,0:T(8,128)S(1)}, u32[]{:S(2)}) copy-start(f32[128,1536]{1,0:T(8,128)S(1)} %get-tuple-element.165.values_ref) | copy-start | bytes 2359300
  131.7 2.0 collective-permute-start.1
  134.9 13.6 %collective-permute-start.2 = (bf16[128,1536]{1,0:T(8,128)(2,1)S(1)}, bf16[128,1536]{1,0:T(8,128)(2,1)S(1)}, u32[]{:S(2)}, u32[]{:S(2)}) collective-permute-start(bf16[128,1536]{1,0:T(8,128)(2,1)S(1)} %add_convert_fusion.1), channel_id=1, source_target_pairs={{0,64},{1,65},{2,66},{3,67},{4,68},{5,69},{6,70},{7,71},{8,72},{9,... | collective-permute-start | bytes 1179656 | tf_op jit(solution)/shard_map/ppermute | solution.py:1108
  162.1 2.1 collective-permute-start.3
  165.5 27.7 %copy-start.1 = (f32[128,1536]{1,0:T(8,128)}, f32[128,1536]{1,0:T(8,128)S(1)}, u32[]{:S(2)}) copy-start(f32[128,1536]{1,0:T(8,128)S(1)} %get-tuple-element.161.values_ref) | copy-start | bytes 2359300
  166.7 156.1 %all-gather.13.cloned.1.call-start = ((), (), s32[]{:S(2)}) async-start(), calls=%async_computation.6 | async-start | bytes 12976128 | tf_op jit(solution)/shard_map/all_gather | solution.py:1054
  193.2 2.0 collective-permute-start.5
  218.8 2.2 collective-permute-start.6
  225.0 15.8 %collective-permute-start.7 = (bf16[128,1536]{1,0:T(8,128)(2,1)}, bf16[128,1536]{1,0:T(8,128)(2,1)S(1)}, u32[]{:S(2)}, u32[]{:S(2)}) collective-permute-start(bf16[128,1536]{1,0:T(8,128)(2,1)} %get-tuple-element.121), channel_id=1, source_target_pairs={{64,0},{65,1},{66,2},{67,3},{68,4},{69,5},{70,6},{71,7},{72,8},{73... | collective-permute-start | bytes 1179656 | tf_op jit(solution)/shard_map/ppermute | solution.py:1140
  242.0 114.0 %all-gather.15.cloned.1.call-start = ((), (), s32[]{:S(2)}) async-start(), calls=%async_computation.7 | async-start | bytes 1966080 | tf_op jit(solution)/shard_map/all_gather | solution.py:1054
  262.1 2.0 collective-permute-start.8
  283.5 39.3 %all-to-all-start = ((bf16[4,256,1024]{2,1,0:T(8,128)(2,1)}), bf16[4,256,1024]{2,1,0:T(8,128)(2,1)S(1)}, u32[]{:S(2)}, u32[]{:S(2)}) async-start(bf16[4,256,1024]{2,1,0:T(8,128)(2,1)} %get-tuple-element.129.behind_ref), calls=%async_computation | async-start | bytes 4194304 | tf_op jit(solution)/shard_map/all_to_all | solution.py:68
  287.4 155.8 %all-gather.17.cloned.1.call-start = ((), (), s32[]{:S(2)}) async-start(), calls=%async_computation.8 | async-start | bytes 4227072 | tf_op jit(solution)/shard_map/all_gather | solution.py:1194
  287.5 35.2 %copy-start.3 = (bf16[256,1536]{1,0:T(8,128)(2,1)S(1)}, bf16[256,1536]{1,0:T(8,128)(2,1)}, u32[]{:S(2)}) copy-start(bf16[256,1536]{1,0:T(8,128)(2,1)} %pad.31) | copy-start | bytes 2359300
  287.5 48.3 %collective-permute-start.9 = (bf16[128,1536]{1,0:T(8,128)(2,1)}, bf16[128,1536]{1,0:T(8,128)(2,1)S(1)}, u32[]{:S(2)}, u32[]{:S(2)}) collective-permute-start(bf16[128,1536]{1,0:T(8,128)(2,1)} %get-tuple-element.134), channel_id=1, source_target_pairs={{0,1},{1,0},{2,3},{3,2},{4,5},{5,4},{6,7},{7,6},{8,9},{9,8},{10,11... | collective-permute-start | bytes 1179656 | tf_op jit(solution)/shard_map/ppermute | solution.py:40
  353.7 29.5 %collective-permute-start.10 = (bf16[768,512]{1,0:T(8,128)(2,1)}, bf16[768,512]{1,0:T(8,128)(2,1)}, u32[]{:S(2)}, u32[]{:S(2)}) collective-permute-start(bf16[768,512]{1,0:T(8,128)(2,1)} %get-tuple-element.138.behind_ref), channel_id=1, source_target_pairs={{0,32},{32,0},{1,33},{33,1},{2,34},{34,2},{3,35},{35,3},{4,36},{36... | collective-permute-start | bytes 2359304 | tf_op jit(solution)/shard_map/ppermute | solution.py:40
  355.2 28.1 %collective-permute-start.11 = (bf16[768,256]{1,0:T(8,128)(2,1)}, bf16[768,256]{1,0:T(8,128)(2,1)}, u32[]{:S(2)}, u32[]{:S(2)}) collective-permute-start(bf16[768,256]{1,0:T(8,128)(2,1)} %get-tuple-element.140), channel_id=1, source_target_pairs={{0,32},{32,0},{1,33},{33,1},{2,34},{34,2},{3,35},{35,3},{4,36},{36... | collective-permute-start | bytes 1179656 | tf_op jit(solution)/shard_map/ppermute | solution.py:40
  355.8 35.3 %collective-permute-start.4 = (bf16[128,1536]{1,0:T(8,128)(2,1)}, bf16[128,1536]{1,0:T(8,128)(2,1)}, u32[]{:S(2)}, u32[]{:S(2)}) collective-permute-start(bf16[128,1536]{1,0:T(8,128)(2,1)} %get-tuple-element.112), channel_id=1, source_target_pairs={{0,1},{1,0},{2,3},{3,2},{4,5},{5,4},{6,7},{7,6},{8,9},{9,8},{10,11... | collective-permute-start | bytes 1179656 | tf_op jit(solution)/shard_map/ppermute | solution.py:40
  363.8 27.3 %copy-start.2 = (f32[128,1536]{1,0:T(8,128)S(1)}, f32[128,1536]{1,0:T(8,128)}, u32[]{:S(2)}) copy-start(f32[128,1536]{1,0:T(8,128)} %copy-done.1) | copy-start | bytes 2359300
  363.8 27.3 %copy-start.9 = (bf16[128,1536]{1,0:T(8,128)(2,1)S(1)}, bf16[128,1536]{1,0:T(8,128)(2,1)}, u32[]{:S(2)}) copy-start(bf16[128,1536]{1,0:T(8,128)(2,1)} %copy-done.8) | copy-start | bytes 1179652
  363.8 54.1 %collective-permute-start.12 = (bf16[16,48,640]{2,1,0:T(8,128)(2,1)}, bf16[16,48,640]{2,1,0:T(8,128)(2,1)S(1)}, u32[]{:S(2)}, u32[]{:S(2)}) collective-permute-start(bf16[16,48,640]{2,1,0:T(8,128)(2,1)} %get-tuple-element.144), channel_id=1, source_target_pairs={{0,32},{32,0},{1,33},{33,1},{2,34},{34,2},{3,35},{35,3},{4,36},{36... | collective-permute-start | bytes 2949128 | tf_op jit(solution)/shard_map/ppermute | solution.py:40
  365.3 45.4 %collective-permute-start.14 = (bf16[192,768]{1,0:T(8,128)(2,1)}, bf16[192,768]{1,0:T(8,128)(2,1)}, u32[]{:S(2)}, u32[]{:S(2)}) collective-permute-start(bf16[192,768]{1,0:T(8,128)(2,1)} %get-tuple-element.155), channel_id=1, source_target_pairs={{0,32},{32,0},{1,33},{33,1},{2,34},{34,2},{3,35},{35,3},{4,36},{36... | collective-permute-start | bytes 884744 | tf_op jit(solution)/shard_map/ppermute | solution.py:40
  386.0 35.6 %all-to-all-start.1 = ((bf16[16,48,768]{2,1,0:T(8,128)(2,1)}), bf16[16,48,768]{2,1,0:T(8,128)(2,1)S(1)}, u32[]{:S(2)}, u32[]{:S(2)}) async-start(bf16[16,48,768]{2,1,0:T(8,128)(2,1)} %bitcast.115), calls=%async_computation.1 | async-start | bytes 2359296 | tf_op jit(solution)/shard_map/all_to_all | solution.py:68
  412.6 13.5 %collective-permute-start.17 = (bf16[48,768]{1,0:T(8,128)(2,1)}, bf16[48,768]{1,0:T(8,128)(2,1)S(1)}, u32[]{:S(2)}, u32[]{:S(2)}) collective-permute-start(bf16[48,768]{1,0:T(8,128)(2,1)} %get-tuple-element.174), channel_id=1, source_target_pairs={{0,24},{8,0},{16,8},{24,16},{1,25},{9,1},{17,9},{25,17},{2,26},{10... | collective-permute-start | bytes 221192 | tf_op jit(solution)/shard_map/ppermute | solution.py:1222
  415.4 10.8 %collective-permute-start.16 = (bf16[48,768]{1,0:T(8,128)(2,1)}, bf16[48,768]{1,0:T(8,128)(2,1)S(1)}, u32[]{:S(2)}, u32[]{:S(2)}) collective-permute-start(bf16[48,768]{1,0:T(8,128)(2,1)} %get-tuple-element.175), channel_id=1, source_target_pairs={{0,16},{8,24},{16,0},{24,8},{1,17},{9,25},{17,1},{25,9},{2,18},{10... | collective-permute-start | bytes 221192 | tf_op jit(solution)/shard_map/ppermute | solution.py:1222
  416.2 9.9 %collective-permute-start.15 = (bf16[48,768]{1,0:T(8,128)(2,1)S(1)}, bf16[48,768]{1,0:T(8,128)(2,1)S(1)}, u32[]{:S(2)}, u32[]{:S(2)}) collective-permute-start(bf16[48,768]{1,0:T(8,128)(2,1)S(1)} %get-tuple-element.173), channel_id=1, source_target_pairs={{0,8},{8,16},{16,24},{24,0},{1,9},{9,17},{17,25},{25,1},{2,10},{10... | collective-permute-start | bytes 221192 | tf_op jit(solution)/shard_map/ppermute | solution.py:1222
  421.6 21.6 %all-to-all-start.2 = ((bf16[16,48,640]{2,1,0:T(8,128)(2,1)}), bf16[16,48,640]{2,1,0:T(8,128)(2,1)S(1)}, u32[]{:S(2)}, u32[]{:S(2)}) async-start(bf16[16,48,640]{2,1,0:T(8,128)(2,1)} %shard_map.202), calls=%async_computation.2 | async-start | bytes 1966080 | tf_op jit(solution)/shard_map/all_to_all | solution.py:68
  451.1 6.9 %collective-permute-start.13 = (bf16[4,24,640]{2,1,0:T(8,128)(2,1)}, bf16[4,24,640]{2,1,0:T(8,128)(2,1)S(1)}, u32[]{:S(2)}, u32[]{:S(2)}) collective-permute-start(bf16[4,24,640]{2,1,0:T(8,128)(2,1)} %get-tuple-element.153), channel_id=1, source_target_pairs={{0,64},{64,0},{1,65},{65,1},{2,66},{66,2},{3,67},{67,3},{4,68},{68... | collective-permute-start | bytes 368648 | tf_op jit(solution)/shard_map/ppermute | solution.py:40
  (23 other events, 254.1 us)
Sparse Core Ops, SparseCore 0:
  11.4 88.7 all-gather.6
  103.0 62.5 all-gather.8
  167.8 62.4 all-gather.10
  242.1 68.5 all-gather.12
  312.2 39.4 all-gather.14
  355.2 75.6 all-gather.16

commit v8 on v6

--- a/solution.py
+++ b/solution.py
@@ -303,9 +303,6 @@
         buffers += [pltpu.VMEM((count, units), BF16)] * 2
         scratch = [*buffers, acc]
         scratch += [pltpu.SemaphoreType.DMA((2, 3)), pltpu.SemaphoreType.DMA((len(tiles), 2))]
-    cost = pl.CostEstimate(
-        flops=12 * count * width * units, bytes_accessed=6 * width * units, transcendentals=0
-    )
     in_specs = [scalar, *[any_space] * len(behind), *in_specs[1:]]
     return pl.pallas_call(
         ordered(body, len(behind)),
@@ -314,7 +311,7 @@
         out_shape=out_shape,
         scratch_shapes=scratch,
         compiler_params=pltpu.CompilerParams(vmem_limit_bytes=VMEM_LIMIT),
-        cost_estimate=cost if backward else SHORT,
+        cost_estimate=SHORT,
     )(core, *behind, rows, *saved, pair, down)
 
 
@@ -540,7 +537,7 @@
 
 
 def finish_kernel(
-    places_ref, behind_ref, mine_ref, come_ref, small_ref, kept_ref, sent_ref, sums_ref, acc_ref
+    places_ref, behind_ref, mine_ref, come_ref, kept_ref, sent_ref, acc_ref
 ):
     section = places_ref[1]
     short = kept_ref.shape[1]
@@ -548,12 +545,25 @@
     kept_ref[...] = acc_ref[:, pl.ds(pl.multiple_of(section * short, short), short)]
     sent = acc_ref[:, pl.ds(pl.multiple_of((1 - section) * short, short), short)]
     sent_ref[...] = sent.astype(BF16)
-    half = small_ref.shape[0] // 2
-    for k in range(2):
-        sums_ref[k] = jnp.sum(small_ref[k * half : (k + 1) * half], axis=0)
-
-
-def finish_call(places, behind, mine, come, small):
+
+
+def plane_sums_kernel(behind_ref, small_ref, sums_ref):
+    sums_ref[...] = jnp.sum(small_ref[...], axis=0)
+
+
+def plane_sums_call(behind, small):
+    vmem = pl.BlockSpec(memory_space=pltpu.VMEM)
+    return pl.pallas_call(
+        plane_sums_kernel,
+        in_specs=[pl.BlockSpec(memory_space=pl.ANY), vmem],
+        out_specs=vmem,
+        out_shape=jax.ShapeDtypeStruct(small.shape[1:], F32),
+        compiler_params=pltpu.CompilerParams(vmem_limit_bytes=VMEM_LIMIT),
+        cost_estimate=SHORT,
+    )(behind, small)
+
+
+def finish_call(places, behind, mine, come):
     vmem = pl.BlockSpec(memory_space=pltpu.VMEM)
     count, rows, size = mine.shape
     lines = (count, rows // 2, size)
@@ -562,24 +572,19 @@
         in_specs=[
             pl.BlockSpec(memory_space=pltpu.SMEM),
             pl.BlockSpec(memory_space=pl.ANY),
-            *[vmem] * 3,
+            *[vmem] * 2,
         ],
-        out_specs=[vmem] * 3,
-        out_shape=[
-            jax.ShapeDtypeStruct(lines, F32),
-            jax.ShapeDtypeStruct(lines, BF16),
-            jax.ShapeDtypeStruct((2, *small.shape[1:]), F32),
-        ],
+        out_specs=[vmem] * 2,
+        out_shape=[jax.ShapeDtypeStruct(lines, F32), jax.ShapeDtypeStruct(lines, BF16)],
         scratch_shapes=[pltpu.VMEM(mine.shape, F32)],
         compiler_params=pltpu.CompilerParams(vmem_limit_bytes=VMEM_LIMIT),
         cost_estimate=SHORT,
-    )(places, behind, mine, come, small)
+    )(places, behind, mine, come)
 
 
 def mixer_grads_kernel(
-    places_ref, behind_ref, columns_ref, gated_0_ref, gated_1_ref, gated_2_ref, gated_3_ref,
-    early_ref, late_ref, parts_ref, out_mine_ref, out_other_ref, normed_ref,
-    in_ref, out_ref, sem,
+    places_ref, behind_ref, columns_ref, gated_ref, early_ref, late_ref,
+    parts_ref, out_mine_ref, out_other_ref, normed_ref, in_ref, out_ref, sem,
 ):
     here, section, y = places_ref[0], places_ref[1], places_ref[2]
 
@@ -597,15 +602,7 @@
         copy(late_ref).start()
 
     mix = out_ref.shape[0]
-    blocks = (gated_0_ref, gated_1_ref, gated_2_ref, gated_3_ref)
-    span = gated_0_ref.shape[0]
-    total = None
-    for k, gated_ref in enumerate(blocks):
-        start = lax.rem(places_ref[3] - k + len(blocks), len(blocks)) * span
-        tiles = columns_ref[pl.ds(pl.multiple_of(start, span), span), :mix]
-        block = product_left(tiles, gated_ref[...])
-        total = block if total is None else total + block
-    out_ref[...] = total
+    out_ref[...] = product_left(columns_ref[:, :mix], gated_ref[...])
     pair_out(out_ref, here, out_mine_ref, out_other_ref)
     copy(early_ref).wait()
     in_ref[...] = product_left(normed_ref[...], columns_ref[:, mix:])
@@ -622,7 +619,7 @@
 
 def mixer_grads_call(places, behind, columns, gated, early, late, plane):
     vmem, any_space = pl.BlockSpec(memory_space=pltpu.VMEM), pl.BlockSpec(memory_space=pl.ANY)
-    tokens, channels = columns.shape[0], gated[0].shape[1]
+    tokens, channels = gated.shape
     width = early.shape[1]
     mix = width // 4
     size = columns.shape[1] - mix
@@ -634,7 +631,7 @@
             pl.BlockSpec(memory_space=pltpu.SMEM),
             any_space,
             vmem,
-            *[vmem] * len(gated),
+            vmem,
             any_space,
             any_space,
         ],
@@ -648,7 +645,7 @@
         ],
         compiler_params=pltpu.CompilerParams(vmem_limit_bytes=VMEM_LIMIT),
         cost_estimate=SHORT,
-    )(places, behind, columns, *gated, early, late)
+    )(places, behind, columns, gated, early, late)
 
 
 def load_all(copies):
@@ -1080,9 +1077,9 @@
     part = hidden_units // plane
     in_width = 3 * channels
     qkv_width = attn_qkv.shape[1]
-    y, z = lax.axis_index("y"), lax.axis_index("z")
+    y = lax.axis_index("y")
     core_scalar = jnp.stack([core, section]).astype(jnp.int32)
-    xl_scalar = jnp.stack([xl, section, y, z]).astype(jnp.int32)
+    xl_scalar = jnp.stack([xl, section, y]).astype(jnp.int32)
 
     def chosen(from_first, from_second):
         return jnp.where(first, from_first, from_second)
@@ -1155,8 +1152,7 @@
     result_1 = (hidden_1 + joined(mine, other)).astype(BF16)
 
     inner_all = gathered(chosen(inner_0, inner_1), plane_axes)
-    gated = chosen(gated_0, gated_1)
-    gated_z = [gated, *[lax.ppermute(gated, "z", around(by)) for by in range(1, 4)]]
+    gated_z = gathered(chosen(gated_0, gated_1), "z")
 
     grad_hidden_1, grad_mix_1, gain_inner_1 = inner_back(
         grad_mine, grad_other, hidden_1, out_cotangent.astype(F32)
@@ -1199,7 +1195,7 @@
         weight_out,
     )
     columns = exchanged(tiles, "z").reshape(4 * rows, -1)
-    part_kept = part_forward_call((tiles, *gated_z[1:]), inner_all, part_pair)
+    part_kept = part_forward_call((tiles,), inner_all, part_pair)
 
     def summed_over_pair(mine, other):
         return mine.astype(F32) + swapped(other, "xl").astype(F32)
@@ -1210,10 +1206,10 @@
         lambda: part_down_call(xl_scalar, early, part_kept, part_down, (columns,)),
     )
     input_grad_0, gain_outer_0 = mixer_back(grad_hidden_0, mine, other, first_in, pair_grads)
+    pair_mine, pair_other = part_pair_call(xl_scalar, inner_all, pair_grads, ())
     in_parts, out_mine, out_other = mixer_grads_call(
-        xl_scalar, pair_grads, columns, gated_z, early, late, plane
-    )
-    pair_mine, pair_other = part_pair_call(xl_scalar, inner_all, pair_grads, (in_parts,))
+        xl_scalar, pair_other, columns, gated_z, early, late, plane
+    )
 
     full_kernel = lax.dynamic_update_slice(
         jnp.zeros(conv_kernel.shape, F32), grad_kernel, (0, core * channels)
@@ -1228,17 +1224,21 @@
     )
     count = small.shape[0]
     small = jnp.pad(small, (0, -count % 1024)).reshape(-1, 128)
-    small_all = lax.all_gather(small, AXES)
+    small = lax.all_gather(small, "c").sum(0)
+    small = small + swapped(small, "xl")
+    across = swapped(small, "xh")
+    small = jnp.concatenate([chosen(small, across), chosen(across, small)])
+    small_all = lax.all_gather(small, PLANE)
 
     come = exchanged(in_parts, PLANE)
     line_mine, line_other = line_sums_call(xl_scalar, come)
     line_come = swapped(line_other, "xl")
 
     pairs = [(a, swapped(b, "xl")) for a, b in ((pair_mine, pair_other), (down_mine, down_other))]
-    total = pair_join_call((line_mine,), pairs)
+    total = pair_join_call((in_parts,), pairs)
     arrived = exchanged(total.reshape(plane, -1, 3 * lanes), PLANE)
 
-    kept_lines, sent_lines, sums = finish_call(xl_scalar, total, line_mine, line_come, small_all)
+    kept_lines, sent_lines = finish_call(xl_scalar, total, line_mine, line_come)
     across = swapped(sent_lines, "xh")
     come = across.astype(F32)[:, :, : in_width // 4]
     kept_lines = kept_lines[:, :, : in_width // 4]
@@ -1263,7 +1263,7 @@
         lines += lax.ppermute(block, "y", around(by)).astype(F32)
     grad_mixer_out = lines.T[None]
 
-    pair = [sums[0].reshape(-1), sums[1].reshape(-1)]
+    pair = plane_sums_call(arrived, small_all).reshape(2, -1)
     grad_norm_gains = jnp.stack([a[: 2 * width].reshape(2, width) for a in pair])
     grad_conv_kernel = pair[0][2 * width : 5 * width].reshape(conv_kernel.shape)
     grad_qk_gains = pair[1][5 * width : count].reshape(qk_gains.shape)

time: 481 us -> 476 us (0.990)
    ppermute x13 -> x15, waiting for transfers between devices: 16.6 us -> 38.5 us  [swapped(): return lax.ppermute(shard, axis, [(0, 1), (1, 0)])]
    all_gather x1, waiting for transfers between devices: 18.3 us -> 0.01 us  [local(): small_all = lax.all_gather(small, PLANE)]
    all_to_all x3, waiting for transfers between devices: 31.9 us -> 23.1 us  [exchanged(): return lax.all_to_all(tiles, axes, 0, 0, tiled=True)]
    ppermute x3 -> x0, starting transfers between devices: 5.87 us -> none  [local(): lax.ppermute(gated, 'z', around(by))]
    all_gather x4 -> x5, waiting for transfers between devices: 63.2 us -> 66.4 us  [gathered(): return lax.all_gather(own, axes, tiled=True)]
    ppermute x13 -> x15, starting transfers between devices: 10.9 us -> 12.4 us  [swapped(): return lax.ppermute(shard, axis, [(0, 1), (1, 0)])]
  transfers between devices with their start and end apart: 29 -> 29, of which waited for: 13 -> 17; matrix products, arithmetic and copies ran while one was open for 10% -> 8% of each run, Pallas kernels for 35% -> 35%
where the time goes in v8:
time: 476 us; the launch traced here: 470 us
  Pallas kernels  172 us (36%)
  waiting for transfers between devices  151 us (32%)
  starting transfers between devices  40.9 us (9%)
  local copies, waits for them, and re-layouts  35 us (7%)
  other arithmetic  28.7 us (6%)
  blocking collectives  26.1 us (5%)
  between operations  15 us (3%)
    all_gather x5, waiting for transfers between devices, gathered(): return lax.all_gather(own, axes, tiled=True)  66.4 us
    pallas_call x4, Pallas kernels, mixer_call(): pl.pallas_call(ordered(kernel, len(behind)), in_specs=[pl.BlockSpec(memor...  45.1 us
    ppermute x15, waiting for transfers between devices, swapped(): return lax.ppermute(shard, axis, [(0, 1), (1, 0)])  38.5 us
    pallas_call x2, Pallas kernels, feed_forward_call(): pl.pallas_call(ordered(body, len(behind)), in_specs=in_specs, out_specs=o...  33 us
    pallas_call x2, Pallas kernels, part_call(): pl.pallas_call(ordered(kernel, len(behind)), grid_spec=pltpu.PrefetchScal...  25.6 us
    all_gather x8, blocking collectives, spread(): return lax.all_gather(own, 'c', tiled=True)  24.3 us
    pallas_call x1, Pallas kernels, ffn_both_call(): pl.pallas_call(ordered(functools.partial(ffn_both_kernel, unit_tiles(unit...  23.6 us
    all_to_all x3, waiting for transfers between devices, exchanged(): return lax.all_to_all(tiles, axes, 0, 0, tiled=True)  23.1 us
  transfers between devices with their start and end apart: 29, of which 17 were waited for; matrix products, arithmetic and copies ran while one was open for 8% of the time, Pallas kernels for 35%

profile of v8, /device:TPU:0, one launch (start us, length us, event | category | flops | bytes accessed | tf_op | source)
XLA Modules:
  0.0 469.6 jit_solution(5472640718565566643)
XLA Ops:
  26.6 8.1 %fusion.15 = (bf16[1,1,1536,3456]{3,2,1,0:T(8,128)(2,1)S(1)}, bf16[1,1,1536,3456]{3,2,1,0:T(8,128)(2,1)S(1)}) fusion(bf16[1,2,1536,3456]{3,2,1,0:T(8,128)(2,1)} %param.22), kind=kLoop, calls=%fused_computation.98 | loop fusion | bytes 42467328 | tf_op jit(solution)/shard_map/slice | solution.py:1099
  36.9 63.3 %all-gather.8.cloned.1.call-done.refs_3_.refs_4_.refs_6_.refs_5_ = bf16[1536,3584]{1,0:T(8,128)(2,1)} async-done(((bf16[24,3584]{1,0:T(8,128)(2,1)}), bf16[1536,3584]{1,0:T(8,128)(2,1)}) %all-gather.8.cloned.1.call-update) | async-done | bytes 11010064 | tf_op jit(solution)/shard_map/all_gather | solution.py:1088
  100.9 8.1 %shard_map.186 = (bf16[3,256,768]{2,1,0:T(8,128)(2,1)}, bf16[256,768]{1,0:T(8,128)(2,1)}, f32[128,1536]{1,0:T(8,128)}, bf16[128,1536]{1,0:T(8,128)(2,1)}) custom-call(s32[2]{0:T(128)} %pad_add_fusion.scalar_ref.behind_ref, bf16[256,1536]{1,0:T(8,128)(2,1)} %all_gather.49.refs_0_, f32[3,768]{1,0:T(4,128)} %dynamic-slice_convert_fusion.refs_1_, ...), custom_call_target="tpu_custom_call" | custom-call | flops 1 | bytes 1 | tf_op jit(solution)/shard_map/pallas_call | solution.py:938
  115.3 16.3 %shard_map.187 = (bf16[256,3456]{1,0:T(8,128)(2,1)}, bf16[256,3456]{1,0:T(8,128)(2,1)}, f32[128,1536]{1,0:T(8,128)}, bf16[128,1536]{1,0:T(8,128)(2,1)}) custom-call(s32[2]{0:T(128)} %pad_add_fusion.scalar_ref.behind_ref, bf16[256,1536]{1,0:T(8,128)(2,1)} %all_gather.51.refs_0_, bf16[2,1536,3456]{2,1,0:T(8,128)(2,1)} %bitcast.103, bf16[3456,1536]{1,0:T(8,128)(2,1)} %bitcast.106), custom_call_target="tpu_custom_call" | custom-call | flops 1 | bytes 1 | tf_op jit(solution)/shard_map/pallas_call | solution.py:307
  134.9 4.9 %collective-permute-start.2 = (bf16[128,1536]{1,0:T(8,128)(2,1)S(1)}, bf16[128,1536]{1,0:T(8,128)(2,1)S(1)}, u32[]{:S(2)}, u32[]{:S(2)}) collective-permute-start(bf16[128,1536]{1,0:T(8,128)(2,1)S(1)} %add_convert_fusion.1), channel_id=1, source_target_pairs={{0,64},{1,65},{2,66},{3,67},{4,68},{5,69},{6,70},{7,71},{8,72},{9,... | collective-permute-start | bytes 1179656 | tf_op jit(solution)/shard_map/ppermute | solution.py:1142
  139.9 8.7 %collective-permute-done.2 = bf16[128,1536]{1,0:T(8,128)(2,1)S(1)} collective-permute-done((bf16[128,1536]{1,0:T(8,128)(2,1)S(1)}, bf16[128,1536]{1,0:T(8,128)(2,1)S(1)}, u32[]{:S(2)}, u32[]{:S(2)}) %collective-permute-start.2) | collective-permute-done | bytes 393248 | tf_op jit(solution)/shard_map/ppermute | solution.py:1142
  151.4 10.7 %shard_map.188 = (f32[256,1280]{1,0:T(8,128)}, bf16[256,1280]{1,0:T(8,128)(2,1)}, bf16[256,768]{1,0:T(8,128)(2,1)}, f32[128,1536]{1,0:T(8,128)}, bf16[128,1536]{1,0:T(8,128)(2,1)}) custom-call(s32[2]{0:T(128)} %pad_add_fusion.scalar_ref.behind_ref, bf16[256,1536]{1,0:T(8,128)(2,1)} %all_gather.52.refs_0_, f32[9,128]{1,0:T(8,128)} %stack.86.refs_1_, ...), custom_call_target="tpu_custom_call" | custom-call | flops 1 | bytes 1 | tf_op jit(solution)/shard_map/pallas_call | solution.py:938
  169.6 23.6 %shard_map.189 = (f32[128,1536]{1,0:T(8,128)}, bf16[128,1536]{1,0:T(8,128)(2,1)}, f32[128,1536]{1,0:T(8,128)}, bf16[128,1536]{1,0:T(8,128)(2,1)}) custom-call(s32[2]{0:T(128)} %pad_add_fusion.scalar_ref.behind_ref, bf16[4096,1536]{1,0:T(8,128)(2,1)} %all-gather.10.cloned.1.call-done.refs_0_.early_ref, bf16[256,1536]{1,0:T(8,128)(2,1)} %all_gather.54.refs_1_, ...), custom_call_target="tpu_custom_call" | custom-call | flops 1 | bytes 1 | tf_op jit(solution)/shard_map/pallas_call | solution.py:255
  196.0 3.2 shard_map.190
  199.1 4.3 all_gather.56.refs_0_
  203.4 15.2 %shard_map.191 = (bf16[4,256,1024]{2,1,0:T(8,128)(2,1)}, f32[10,128]{1,0:T(8,128)}, f32[128,1536]{1,0:T(8,128)}, bf16[128,1536]{1,0:T(8,128)(2,1)}) custom-call(s32[2]{0:T(128)} %pad_add_fusion.scalar_ref.behind_ref, bf16[256,1536]{1,0:T(8,128)(2,1)} %all_gather.56.refs_0_, f32[9,128]{1,0:T(8,128)} %stack.86.refs_1_, f32[2,256,128]{2,1,0:T(8,128)} %bitcast.121, ...), custom_call_target="tpu_custom_call" | custom-call | flops 1 | bytes 1 | tf_op jit(solution)/shard_map/pallas_call | solution.py:938
  221.6 3.2 shard_map.192
  226.2 14.6 %collective-permute-done.7 = bf16[128,1536]{1,0:T(8,128)(2,1)S(1)} collective-permute-done((bf16[128,1536]{1,0:T(8,128)(2,1)}, bf16[128,1536]{1,0:T(8,128)(2,1)S(1)}, u32[]{:S(2)}, u32[]{:S(2)}) %collective-permute-start.7) | collective-permute-done | bytes 393248 | tf_op jit(solution)/shard_map/ppermute | solution.py:1173
  245.4 16.7 %shard_map.193 = (f32[128,1536]{1,0:T(8,128)}, bf16[128,1536]{1,0:T(8,128)(2,1)}) custom-call(s32[2]{0:T(128)} %pad_add_fusion.scalar_ref.behind_ref, bf16[4096,1536]{1,0:T(8,128)(2,1)} %all-gather.12.cloned.1.call-done.refs_0_.refs_1_, bf16[256,1536]{1,0:T(8,128)(2,1)} %all_gather.57.refs_1_, bf16[256,3456]{1,0:T(8,128)(2,1)} %get-tuple-element.122.refs_2_, ...), custom_call_target="tpu_custom_call" | custom-call | flops 1 | bytes 1 | tf_op jit(solution)/shard_map/pallas_call | solution.py:307
  264.9 3.2 shard_map.194
  268.0 4.3 all_gather.58.refs_0_
  272.4 11.1 %shard_map.195 = (bf16[4,256,1024]{2,1,0:T(8,128)(2,1)}, f32[3,768]{1,0:T(4,128)}, f32[128,1536]{1,0:T(8,128)}, bf16[128,1536]{1,0:T(8,128)(2,1)}) custom-call(s32[2]{0:T(128)} %pad_add_fusion.scalar_ref.behind_ref, bf16[256,1536]{1,0:T(8,128)(2,1)} %all_gather.58.refs_0_, f32[3,768]{1,0:T(4,128)} %dynamic-slice_convert_fusion.refs_1_, ...), custom_call_target="tpu_custom_call" | custom-call | flops 1 | bytes 1 | tf_op jit(solution)/shard_map/pallas_call | solution.py:938
  283.5 3.9 all-to-all-start
  287.5 12.2 %shard_map.196 = bf16[4096,768]{1,0:T(8,128)(2,1)} custom-call(bf16[4,256,1024]{2,1,0:T(8,128)(2,1)} %get-tuple-element.129.refs_0_, bf16[4096,1536]{1,0:T(8,128)(2,1)} %all-gather.12.cloned.1.call-done.refs_0_.refs_1_, bf16[1536,512]{1,0:T(8,128)(2,1)} %fusion.2.refs_2_), custom_call_target="tpu_custom_call" | custom-call | flops 12884901888 | bytes 12582912 | tf_op jit(solution)/shard_map/pallas_call | solution.py:334
  299.7 23.1 %all-to-all-done = bf16[4,256,1024]{2,1,0:T(8,128)(2,1)S(1)} async-done(((bf16[4,256,1024]{2,1,0:T(8,128)(2,1)}), bf16[4,256,1024]{2,1,0:T(8,128)(2,1)S(1)}, u32[]{:S(2)}, u32[]{:S(2)}) %all-to-all-start) | async-done | bytes 2097184 | tf_op jit(solution)/shard_map/all_to_all | solution.py:68
  322.8 13.2 %conditional.1 = ((bf16[4096,512]{1,0:T(8,128)(2,1)}, bf16[768,256]{1,0:T(8,128)(2,1)}, bf16[768,256]{1,0:T(8,128)(2,1)})) conditional(s32[]{:T(128)} %convert_element_type.112, (s32[3]{0:T(128)S(1)}, bf16[1024,1024]{1,0:T(8,128)(2,1)S(1)}, bf16[4096,1536]{1,0:T(8,128)(2,1)}, bf16[4096,768]{1,0:T(8,128)(2,1)}, ...), branch_computations={%region_4.5_spmd, %region_5.6_spmd} | conditional | flops 1 | bytes 9 | solution.py:1203
  322.8 13.0 %branch_1_fun.1 = (bf16[4096,512]{1,0:T(8,128)(2,1)}, bf16[768,256]{1,0:T(8,128)(2,1)}, bf16[768,256]{1,0:T(8,128)(2,1)}) custom-call(s32[3]{0:T(128)S(1)} %get-tuple-element.25.scalar_ref, bf16[1024,1024]{1,0:T(8,128)(2,1)S(1)} %get-tuple-element.26.refs_0_, bf16[4096,1536]{1,0:T(8,128)(2,1)} %get-tuple-element.27.refs_1_, ...), custom_call_target="tpu_custom_call" | custom-call | flops 1 | bytes 1 | tf_op jit(solution)/shard_map/cond/branch_1_fun/pallas_call | solution.py:399
  336.0 12.6 %shard_map.198 = (bf16[768,512]{1,0:T(8,128)(2,1)}, bf16[768,512]{1,0:T(8,128)(2,1)}) custom-call(s32[3]{0:T(128)S(1)} %pad_add_fusion.1.scalar_ref.places_ref, bf16[4096,1536]{1,0:T(8,128)(2,1)} %all-gather.12.cloned.1.call-done.refs_0_.refs_1_, bf16[4096,512]{1,0:T(8,128)(2,1)} %get-tuple-element.132.behind_ref.refs_1_), custom_call_target="tpu_custom_call" | custom-call | flops 1 | bytes 1 | tf_op jit(solution)/shard_map/pallas_call | solution.py:399
  351.7 7.4 %shard_map.199 = (bf16[16,96,640]{2,1,0:T(8,128)(2,1)}, bf16[192,768]{1,0:T(8,128)(2,1)}, bf16[192,768]{1,0:T(8,128)(2,1)}) custom-call(s32[3]{0:T(128)S(1)} %pad_add_fusion.1.scalar_ref.places_ref, bf16[768,512]{1,0:T(8,128)(2,1)} %get-tuple-element.137.behind_ref, bf16[1024,1024]{1,0:T(8,128)(2,1)S(1)} %bitcast.115, ...), custom_call_target="tpu_custom_call" | custom-call | flops 1 | bytes 1 | tf_op jit(solution)/shard_map/pallas_call | solution.py:628
  359.2 5.8 %all-to-all-start.1 = ((bf16[16,96,640]{2,1,0:T(8,128)(2,1)}), bf16[16,96,640]{2,1,0:T(8,128)(2,1)S(1)}, u32[]{:S(2)}, u32[]{:S(2)}) async-start(bf16[16,96,640]{2,1,0:T(8,128)(2,1)} %get-tuple-element.140.refs_0_), calls=%async_computation.1 | async-start | bytes 3932160 | tf_op jit(solution)/shard_map/all_to_all | solution.py:68
  368.8 3.3 shard_map.197
  376.2 11.1 %collective-permute-done.14 = f32[64,128]{1,0:T(8,128)S(1)} collective-permute-done((f32[64,128]{1,0:T(8,128)S(1)}, f32[64,128]{1,0:T(8,128)S(1)}, u32[]{:S(2)}, u32[]{:S(2)}) %collective-permute-start.14) | collective-permute-done | bytes 32800 | tf_op jit(solution)/shard_map/ppermute | solution.py:40
  395.3 7.1 %collective-permute-done.11.refs_4_ = bf16[768,256]{1,0:T(8,128)(2,1)S(1)} collective-permute-done((bf16[768,256]{1,0:T(8,128)(2,1)}, bf16[768,256]{1,0:T(8,128)(2,1)S(1)}, u32[]{:S(2)}, u32[]{:S(2)}) %collective-permute-start.11) | collective-permute-done | bytes 393248 | tf_op jit(solution)/shard_map/ppermute | solution.py:40
  406.4 7.5 %all-to-all-start.2 = ((bf16[16,48,768]{2,1,0:T(8,128)(2,1)}), bf16[16,48,768]{2,1,0:T(8,128)(2,1)}, u32[]{:S(2)}, u32[]{:S(2)}) async-start(bf16[16,48,768]{2,1,0:T(8,128)(2,1)} %bitcast.116), calls=%async_computation.2 | async-start | bytes 2359296 | tf_op jit(solution)/shard_map/all_to_all | solution.py:68
  417.2 3.2 collective-permute-start.19
  426.3 5.1 %collective-permute-done.12.come_ref = bf16[4,48,640]{2,1,0:T(8,128)(2,1)S(1)} collective-permute-done((bf16[4,48,640]{2,1,0:T(8,128)(2,1)}, bf16[4,48,640]{2,1,0:T(8,128)(2,1)S(1)}, u32[]{:S(2)}, u32[]{:S(2)}) %collective-permute-start.12) | collective-permute-done | bytes 245792 | tf_op jit(solution)/shard_map/ppermute | solution.py:40
  436.1 4.7 %collective-permute-done.13.behind_ref = bf16[4,24,640]{2,1,0:T(8,128)(2,1)S(1)} collective-permute-done((bf16[4,24,640]{2,1,0:T(8,128)(2,1)}, bf16[4,24,640]{2,1,0:T(8,128)(2,1)S(1)}, u32[]{:S(2)}, u32[]{:S(2)}) %collective-permute-start.13) | collective-permute-done | bytes 122912 | tf_op jit(solution)/shard_map/ppermute | solution.py:40
  (236 shorter events, 114.9 us)
Async XLA Ops:
  7.2 93.0 %all-gather.8.cloned.1.call-start = ((), (), s32[]{:S(2)}) async-start(), calls=%async_computation.3 | async-start | bytes 11182080 | tf_op jit(solution)/shard_map/all_gather | solution.py:1088
  9.7 159.9 %all-gather.10.cloned.1.call-start = ((), (), s32[]{:S(2)}) async-start(), calls=%async_computation.4 | async-start | bytes 12976128 | tf_op jit(solution)/shard_map/all_gather | solution.py:1088
  14.4 231.0 %all-gather.12.cloned.1.call-start = ((), (), s32[]{:S(2)}) async-start(), calls=%async_computation.5 | async-start | bytes 12976128 | tf_op jit(solution)/shard_map/all_gather | solution.py:1088
  109.0 2.0 collective-permute-start
  112.5 53.1 %copy-start.1 = (f32[128,1536]{1,0:T(8,128)}, f32[128,1536]{1,0:T(8,128)S(1)}, u32[]{:S(2)}) copy-start(f32[128,1536]{1,0:T(8,128)S(1)} %get-tuple-element.165.values_ref) | copy-start | bytes 2359300
  131.7 2.0 collective-permute-start.1
  134.9 13.6 %collective-permute-start.2 = (bf16[128,1536]{1,0:T(8,128)(2,1)S(1)}, bf16[128,1536]{1,0:T(8,128)(2,1)S(1)}, u32[]{:S(2)}, u32[]{:S(2)}) collective-permute-start(bf16[128,1536]{1,0:T(8,128)(2,1)S(1)} %add_convert_fusion.1), channel_id=1, source_target_pairs={{0,64},{1,65},{2,66},{3,67},{4,68},{5,69},{6,70},{7,71},{8,72},{9,... | collective-permute-start | bytes 1179656 | tf_op jit(solution)/shard_map/ppermute | solution.py:1142
  162.1 2.1 collective-permute-start.3
  165.6 27.6 %copy-start.2 = (f32[128,1536]{1,0:T(8,128)}, f32[128,1536]{1,0:T(8,128)S(1)}, u32[]{:S(2)}) copy-start(f32[128,1536]{1,0:T(8,128)S(1)} %get-tuple-element.161.values_ref) | copy-start | bytes 2359300
  166.6 156.2 %all-gather.14.cloned.1.call-start = ((), (), s32[]{:S(2)}) async-start(), calls=%async_computation.6 | async-start | bytes 12976128 | tf_op jit(solution)/shard_map/all_gather | solution.py:1088
  193.2 2.0 collective-permute-start.5
  218.7 2.2 collective-permute-start.6
  224.9 15.9 %collective-permute-start.7 = (bf16[128,1536]{1,0:T(8,128)(2,1)}, bf16[128,1536]{1,0:T(8,128)(2,1)S(1)}, u32[]{:S(2)}, u32[]{:S(2)}) collective-permute-start(bf16[128,1536]{1,0:T(8,128)(2,1)} %get-tuple-element.121), channel_id=1, source_target_pairs={{64,0},{65,1},{66,2},{67,3},{68,4},{69,5},{70,6},{71,7},{72,8},{73... | collective-permute-start | bytes 1179656 | tf_op jit(solution)/shard_map/ppermute | solution.py:1173
  242.0 109.6 %all-gather.16.cloned.1.call-start = ((), (), s32[]{:S(2)}) async-start(), calls=%async_computation.7 | async-start | bytes 1966080 | tf_op jit(solution)/shard_map/all_gather | solution.py:1088
  262.1 2.0 collective-permute-start.8
  283.5 39.3 %all-to-all-start = ((bf16[4,256,1024]{2,1,0:T(8,128)(2,1)}), bf16[4,256,1024]{2,1,0:T(8,128)(2,1)S(1)}, u32[]{:S(2)}, u32[]{:S(2)}) async-start(bf16[4,256,1024]{2,1,0:T(8,128)(2,1)} %get-tuple-element.129.refs_0_), calls=%async_computation | async-start | bytes 4194304 | tf_op jit(solution)/shard_map/all_to_all | solution.py:68
  287.5 35.3 %copy-start.5 = (bf16[256,1536]{1,0:T(8,128)(2,1)S(1)}, bf16[256,1536]{1,0:T(8,128)(2,1)}, u32[]{:S(2)}) copy-start(bf16[256,1536]{1,0:T(8,128)(2,1)} %pad.31) | copy-start | bytes 2359300
  359.2 47.2 %all-to-all-start.1 = ((bf16[16,96,640]{2,1,0:T(8,128)(2,1)}), bf16[16,96,640]{2,1,0:T(8,128)(2,1)S(1)}, u32[]{:S(2)}, u32[]{:S(2)}) async-start(bf16[16,96,640]{2,1,0:T(8,128)(2,1)} %get-tuple-element.140.refs_0_), calls=%async_computation.1 | async-start | bytes 3932160 | tf_op jit(solution)/shard_map/all_to_all | solution.py:68
  365.0 79.3 %all-gather.18.cloned.1.call-start = ((), (), s32[]{:S(2)}) async-start(), calls=%async_computation.8 | async-start | bytes 1114112 | tf_op jit(solution)/shard_map/all_gather | solution.py:1231
  366.1 2.0 collective-permute-start.9
  366.4 36.0 %collective-permute-start.10 = (bf16[768,512]{1,0:T(8,128)(2,1)}, bf16[768,512]{1,0:T(8,128)(2,1)S(1)}, u32[]{:S(2)}, u32[]{:S(2)}) collective-permute-start(bf16[768,512]{1,0:T(8,128)(2,1)} %get-tuple-element.137.behind_ref), channel_id=1, source_target_pairs={{0,32},{32,0},{1,33},{33,1},{2,34},{34,2},{3,35},{35,3},{4,36},{36... | collective-permute-start | bytes 2359304 | tf_op jit(solution)/shard_map/ppermute | solution.py:40
  374.7 12.6 %collective-permute-start.14 = (f32[64,128]{1,0:T(8,128)S(1)}, f32[64,128]{1,0:T(8,128)S(1)}, u32[]{:S(2)}, u32[]{:S(2)}) collective-permute-start(f32[64,128]{1,0:T(8,128)S(1)} %reduce_sum.69), channel_id=1, source_target_pairs={{0,32},{32,0},{1,33},{33,1},{2,34},{34,2},{3,35},{35,3},{4,36},{36... | collective-permute-start | bytes 98312 | tf_op jit(solution)/shard_map/ppermute | solution.py:40
  387.3 5.4 %collective-permute-start.15 = (f32[64,128]{1,0:T(8,128)S(1)}, f32[64,128]{1,0:T(8,128)S(1)}, u32[]{:S(2)}, u32[]{:S(2)}) collective-permute-start(f32[64,128]{1,0:T(8,128)S(1)} %add.153), channel_id=1, source_target_pairs={{0,64},{64,0},{1,65},{65,1},{2,66},{66,2},{3,67},{67,3},{4,68},{68... | collective-permute-start | bytes 98312 | tf_op jit(solution)/shard_map/ppermute | solution.py:40
  390.3 23.6 %collective-permute-start.4 = (bf16[128,1536]{1,0:T(8,128)(2,1)}, bf16[128,1536]{1,0:T(8,128)(2,1)S(1)}, u32[]{:S(2)}, u32[]{:S(2)}) collective-permute-start(bf16[128,1536]{1,0:T(8,128)(2,1)} %get-tuple-element.112), channel_id=1, source_target_pairs={{0,1},{1,0},{2,3},{3,2},{4,5},{5,4},{6,7},{7,6},{8,9},{9,8},{10,11... | collective-permute-start | bytes 1179656 | tf_op jit(solution)/shard_map/ppermute | solution.py:40
  390.3 12.1 %collective-permute-start.11 = (bf16[768,256]{1,0:T(8,128)(2,1)}, bf16[768,256]{1,0:T(8,128)(2,1)S(1)}, u32[]{:S(2)}, u32[]{:S(2)}) collective-permute-start(bf16[768,256]{1,0:T(8,128)(2,1)} %get-tuple-element.143), channel_id=1, source_target_pairs={{0,32},{32,0},{1,33},{33,1},{2,34},{34,2},{3,35},{35,3},{4,36},{36... | collective-permute-start | bytes 1179656 | tf_op jit(solution)/shard_map/ppermute | solution.py:40
  393.5 22.6 %collective-permute-start.16 = (bf16[192,768]{1,0:T(8,128)(2,1)}, bf16[192,768]{1,0:T(8,128)(2,1)}, u32[]{:S(2)}, u32[]{:S(2)}) collective-permute-start(bf16[192,768]{1,0:T(8,128)(2,1)} %get-tuple-element.155), channel_id=1, source_target_pairs={{0,32},{32,0},{1,33},{33,1},{2,34},{34,2},{3,35},{35,3},{4,36},{36... | collective-permute-start | bytes 884744 | tf_op jit(solution)/shard_map/ppermute | solution.py:40
  406.4 29.7 %all-to-all-start.2 = ((bf16[16,48,768]{2,1,0:T(8,128)(2,1)}), bf16[16,48,768]{2,1,0:T(8,128)(2,1)}, u32[]{:S(2)}, u32[]{:S(2)}) async-start(bf16[16,48,768]{2,1,0:T(8,128)(2,1)} %bitcast.116), calls=%async_computation.2 | async-start | bytes 2359296 | tf_op jit(solution)/shard_map/all_to_all | solution.py:68
  417.2 18.1 %collective-permute-start.19 = (bf16[48,768]{1,0:T(8,128)(2,1)S(1)}, bf16[48,768]{1,0:T(8,128)(2,1)S(1)}, u32[]{:S(2)}, u32[]{:S(2)}) collective-permute-start(bf16[48,768]{1,0:T(8,128)(2,1)S(1)} %get-tuple-element.174), channel_id=1, source_target_pairs={{0,24},{8,0},{16,8},{24,16},{1,25},{9,1},{17,9},{25,17},{2,26},{10... | collective-permute-start | bytes 221192 | tf_op jit(solution)/shard_map/ppermute | solution.py:1263
  420.4 15.0 %collective-permute-start.18 = (bf16[48,768]{1,0:T(8,128)(2,1)S(1)}, bf16[48,768]{1,0:T(8,128)(2,1)S(1)}, u32[]{:S(2)}, u32[]{:S(2)}) collective-permute-start(bf16[48,768]{1,0:T(8,128)(2,1)S(1)} %get-tuple-element.175), channel_id=1, source_target_pairs={{0,16},{8,24},{16,0},{24,8},{1,17},{9,25},{17,1},{25,9},{2,18},{10... | collective-permute-start | bytes 221192 | tf_op jit(solution)/shard_map/ppermute | solution.py:1263
  421.3 14.1 %collective-permute-start.17 = (bf16[48,768]{1,0:T(8,128)(2,1)S(1)}, bf16[48,768]{1,0:T(8,128)(2,1)S(1)}, u32[]{:S(2)}, u32[]{:S(2)}) collective-permute-start(bf16[48,768]{1,0:T(8,128)(2,1)S(1)} %get-tuple-element.173), channel_id=1, source_target_pairs={{0,8},{8,16},{16,24},{24,0},{1,9},{9,17},{17,25},{25,1},{2,10},{10... | collective-permute-start | bytes 221192 | tf_op jit(solution)/shard_map/ppermute | solution.py:1263
  425.0 6.4 %collective-permute-start.12 = (bf16[4,48,640]{2,1,0:T(8,128)(2,1)}, bf16[4,48,640]{2,1,0:T(8,128)(2,1)S(1)}, u32[]{:S(2)}, u32[]{:S(2)}) collective-permute-start(bf16[4,48,640]{2,1,0:T(8,128)(2,1)} %get-tuple-element.145), channel_id=1, source_target_pairs={{0,32},{32,0},{1,33},{33,1},{2,34},{34,2},{3,35},{35,3},{4,36},{36... | collective-permute-start | bytes 737288 | tf_op jit(solution)/shard_map/ppermute | solution.py:40
  434.0 6.8 %collective-permute-start.13 = (bf16[4,24,640]{2,1,0:T(8,128)(2,1)}, bf16[4,24,640]{2,1,0:T(8,128)(2,1)S(1)}, u32[]{:S(2)}, u32[]{:S(2)}) collective-permute-start(bf16[4,24,640]{2,1,0:T(8,128)(2,1)} %get-tuple-element.146), channel_id=1, source_target_pairs={{0,64},{64,0},{1,65},{65,1},{2,66},{66,2},{3,67},{67,3},{4,68},{68... | collective-permute-start | bytes 368648 | tf_op jit(solution)/shard_map/ppermute | solution.py:40
  (36 other events, 223.5 us)
Sparse Core Ops, SparseCore 0:
  11.4 88.7 all-gather.7
  103.0 62.5 all-gather.9
  167.8 62.4 all-gather.11
  242.2 68.5 all-gather.13
  312.2 39.3 all-gather.15
  393.5 50.2 all-gather.17

commit v9 on v8

--- a/solution.py
+++ b/solution.py
@@ -494,20 +494,32 @@
     )(*behind, *operands)
 
 
-def widened_kernel(behind_ref, low_ref, wide_ref):
-    wide_ref[...] = low_ref[...].astype(F32)
-
-
-def widened_call(behind, low):
+def lines_kernel(behind_ref, arrived_ref, pair_ref, down_ref):
+    plane, _, lanes = arrived_ref.shape
+    lanes //= 3
+    part = down_ref.shape[1] // plane
+    for k in range(plane):
+        rows = arrived_ref[k].astype(F32)
+        at = slice(k * part, (k + 1) * part)
+        pair_ref[0, :, at] = rows[:, :part]
+        pair_ref[1, :, at] = rows[:, lanes : lanes + part]
+        down_ref[:, at] = rows[:, 2 * lanes : 2 * lanes + part]
+
+
+def lines_call(behind, arrived, units):
     vmem = pl.BlockSpec(memory_space=pltpu.VMEM)
+    rows = arrived.shape[1]
     return pl.pallas_call(
-        widened_kernel,
+        lines_kernel,
         in_specs=[pl.BlockSpec(memory_space=pl.ANY), vmem],
-        out_specs=vmem,
-        out_shape=jax.ShapeDtypeStruct(low.shape, F32),
+        out_specs=[vmem] * 2,
+        out_shape=[
+            jax.ShapeDtypeStruct((2, rows, units), F32),
+            jax.ShapeDtypeStruct((rows, units), F32),
+        ],
         compiler_params=pltpu.CompilerParams(vmem_limit_bytes=VMEM_LIMIT),
         cost_estimate=SHORT,
-    )(behind, low)
+    )(behind, arrived)
 
 
 def line_sums_kernel(places_ref, come_ref, mine_ref, other_ref, acc_ref):
@@ -582,11 +594,10 @@
     )(places, behind, mine, come)
 
 
-def mixer_grads_kernel(
-    places_ref, behind_ref, columns_ref, gated_ref, early_ref, late_ref,
-    parts_ref, out_mine_ref, out_other_ref, normed_ref, in_ref, out_ref, sem,
+def mixer_in_kernel(
+    places_ref, behind_ref, columns_ref, early_ref, late_ref, parts_ref, normed_ref, in_ref, sem
 ):
-    here, section, y = places_ref[0], places_ref[1], places_ref[2]
+    section, y = places_ref[1], places_ref[2]
 
     def copy(all_ref):
         rows = normed_ref.shape[0]
@@ -601,10 +612,8 @@
     def _():
         copy(late_ref).start()
 
-    mix = out_ref.shape[0]
-    out_ref[...] = product_left(columns_ref[:, :mix], gated_ref[...])
-    pair_out(out_ref, here, out_mine_ref, out_other_ref)
     copy(early_ref).wait()
+    mix = columns_ref.shape[1] - in_ref.shape[1]
     in_ref[...] = product_left(normed_ref[...], columns_ref[:, mix:])
     plane, block, _ = parts_ref.shape
     short = block // 4
@@ -617,35 +626,48 @@
                 parts_ref[k, place : place + short] = rows_in.astype(BF16)
 
 
-def mixer_grads_call(places, behind, columns, gated, early, late, plane):
+def mixer_in_call(places, behind, columns, early, late, plane):
     vmem, any_space = pl.BlockSpec(memory_space=pltpu.VMEM), pl.BlockSpec(memory_space=pl.ANY)
-    tokens, channels = gated.shape
-    width = early.shape[1]
-    mix = width // 4
-    size = columns.shape[1] - mix
-    in_parts = jax.ShapeDtypeStruct((plane, width // plane, size), BF16)
-    out_half = jax.ShapeDtypeStruct((mix // 2, channels), BF16)
+    tokens, width = columns.shape[0], early.shape[1]
+    size = columns.shape[1] - width // 4
     return pl.pallas_call(
-        mixer_grads_kernel,
-        in_specs=[
-            pl.BlockSpec(memory_space=pltpu.SMEM),
-            any_space,
-            vmem,
-            vmem,
-            any_space,
-            any_space,
-        ],
-        out_specs=[vmem] * 3,
-        out_shape=[in_parts, out_half, out_half],
+        mixer_in_kernel,
+        in_specs=[pl.BlockSpec(memory_space=pltpu.SMEM), any_space, vmem, any_space, any_space],
+        out_specs=vmem,
+        out_shape=jax.ShapeDtypeStruct((plane, width // plane, size), BF16),
         scratch_shapes=[
             pltpu.VMEM((tokens, width), BF16),
             pltpu.VMEM((width, size), F32),
-            pltpu.VMEM((mix, channels), F32),
             pltpu.SemaphoreType.DMA,
         ],
         compiler_params=pltpu.CompilerParams(vmem_limit_bytes=VMEM_LIMIT),
         cost_estimate=SHORT,
-    )(places, behind, columns, gated, early, late)
+    )(places, behind, columns, early, late)
+
+
+def mixer_out_kernel(places_ref, behind_ref, columns_ref, gated_ref, mine_ref, other_ref, out_ref):
+    out_ref[...] = product_left(columns_ref[:, : out_ref.shape[0]], gated_ref[...])
+    pair_out(out_ref, places_ref[0], mine_ref, other_ref)
+
+
+def mixer_out_call(places, behind, columns, gated, mix):
+    vmem = pl.BlockSpec(memory_space=pltpu.VMEM)
+    channels = gated.shape[1]
+    half = jax.ShapeDtypeStruct((mix // 2, channels), BF16)
+    return pl.pallas_call(
+        mixer_out_kernel,
+        in_specs=[
+            pl.BlockSpec(memory_space=pltpu.SMEM),
+            pl.BlockSpec(memory_space=pl.ANY),
+            vmem,
+            vmem,
+        ],
+        out_specs=[vmem] * 2,
+        out_shape=[half, half],
+        scratch_shapes=[pltpu.VMEM((mix, channels), F32)],
+        compiler_params=pltpu.CompilerParams(vmem_limit_bytes=VMEM_LIMIT),
+        cost_estimate=SHORT,
+    )(places, behind, columns, gated)
 
 
 def load_all(copies):
@@ -1206,10 +1228,9 @@
         lambda: part_down_call(xl_scalar, early, part_kept, part_down, (columns,)),
     )
     input_grad_0, gain_outer_0 = mixer_back(grad_hidden_0, mine, other, first_in, pair_grads)
-    pair_mine, pair_other = part_pair_call(xl_scalar, inner_all, pair_grads, ())
-    in_parts, out_mine, out_other = mixer_grads_call(
-        xl_scalar, pair_other, columns, gated_z, early, late, plane
-    )
+    in_parts = mixer_in_call(xl_scalar, pair_grads, columns, early, late, plane)
+    pair_mine, pair_other = part_pair_call(xl_scalar, inner_all, pair_grads, (in_parts,))
+    out_mine, out_other = mixer_out_call(xl_scalar, pair_other, columns, gated_z, width // 4)
 
     full_kernel = lax.dynamic_update_slice(
         jnp.zeros(conv_kernel.shape, F32), grad_kernel, (0, core * channels)
@@ -1247,13 +1268,8 @@
     lines = chosen(come, kept_lines)[:, :, : qkv_width // 4]
     grad_attn_qkv = jnp.moveaxis(lines, 0, 1).reshape(attn_qkv.shape)
 
-    arrived = widened_call(across, arrived)
-    lines = [
-        jnp.moveaxis(arrived[:, :, k * lanes : k * lanes + part], 0, 1).reshape(-1, hidden_units)
-        for k in range(3)
-    ]
-    grad_gate_up = jnp.stack(lines[:2])[None]
-    grad_down = lines[2].T[None]
+    grad_gate_up, grad_down = lines_call(across, arrived, hidden_units)
+    grad_gate_up, grad_down = grad_gate_up[None], grad_down.T[None]
 
     total = summed_over_pair(out_mine, out_other).reshape(4, -1, channels)
     sent = total.astype(BF16)
@@ -1263,7 +1279,7 @@
         lines += lax.ppermute(block, "y", around(by)).astype(F32)
     grad_mixer_out = lines.T[None]
 
-    pair = plane_sums_call(arrived, small_all).reshape(2, -1)
+    pair = plane_sums_call(grad_gate_up, small_all).reshape(2, -1)
     grad_norm_gains = jnp.stack([a[: 2 * width].reshape(2, width) for a in pair])
     grad_conv_kernel = pair[0][2 * width : 5 * width].reshape(conv_kernel.shape)
     grad_qk_gains = pair[1][5 * width : count].reshape(qk_gains.shape)

time: 476 us -> 463 us (0.973)
  local copies, waits for them, and re-layouts: 35 us -> 26.2 us
    pallas_call x2 -> x3, Pallas kernels: 10.2 us -> 12.4 us  [the longest x1 6.37 us: mixer_in_call(): pl.pallas_call(mixer_in_kernel, in_specs=[pl.BlockSpec(memory_space=pltpu...]
  transfers between devices with their start and end apart: 29 -> 29, of which waited for: 17 -> 16; matrix products, arithmetic and copies ran while one was open for 8% -> 8% of each run, Pallas kernels for 35% -> 38%
where the time goes in v9:
time: 463 us; the launch traced here: 456 us
  Pallas kernels  176 us (38%)
  waiting for transfers between devices  148 us (32%)
  starting transfers between devices  38.3 us (8%)
  other arithmetic  27.4 us (6%)
  local copies, waits for them, and re-layouts  26.2 us (6%)
  blocking collectives  25.9 us (6%)
  between operations  14.9 us (3%)
    all_gather x5, waiting for transfers between devices, gathered(): return lax.all_gather(own, axes, tiled=True)  63.2 us
    pallas_call x4, Pallas kernels, mixer_call(): pl.pallas_call(ordered(kernel, len(behind)), in_specs=[pl.BlockSpec(memor...  45.6 us
    ppermute x15, waiting for transfers between devices, swapped(): return lax.ppermute(shard, axis, [(0, 1), (1, 0)])  38.6 us
    pallas_call x2, Pallas kernels, feed_forward_call(): pl.pallas_call(ordered(body, len(behind)), in_specs=in_specs, out_specs=o...  33.1 us
    pallas_call x2, Pallas kernels, part_call(): pl.pallas_call(ordered(kernel, len(behind)), grid_spec=pltpu.PrefetchScal...  26.5 us
    all_gather x8, blocking collectives, spread(): return lax.all_gather(own, 'c', tiled=True)  24.1 us
    pallas_call x1, Pallas kernels, ffn_both_call(): pl.pallas_call(ordered(functools.partial(ffn_both_kernel, unit_tiles(unit...  23.6 us
    all_to_all x3, waiting for transfers between devices, exchanged(): return lax.all_to_all(tiles, axes, 0, 0, tiled=True)  22.6 us
  transfers between devices with their start and end apart: 29, of which 16 were waited for; matrix products, arithmetic and copies ran while one was open for 8% of the time, Pallas kernels for 38%

profile of v9, /device:TPU:0, one launch (start us, length us, event | category | flops | bytes accessed | tf_op | source)
XLA Modules:
  0.0 456.3 jit_solution(490999769805489598)
XLA Ops:
  26.8 8.1 %fusion.15 = (bf16[1,1,1536,3456]{3,2,1,0:T(8,128)(2,1)S(1)}, bf16[1,1,1536,3456]{3,2,1,0:T(8,128)(2,1)S(1)}) fusion(bf16[1,2,1536,3456]{3,2,1,0:T(8,128)(2,1)} %param.22), kind=kLoop, calls=%fused_computation.94 | loop fusion | bytes 42467328 | tf_op jit(solution)/shard_map/slice | solution.py:1121
  37.1 63.1 %all-gather.8.cloned.1.call-done.refs_3_.refs_4_.refs_6_.refs_5_ = bf16[1536,3584]{1,0:T(8,128)(2,1)} async-done(((bf16[24,3584]{1,0:T(8,128)(2,1)}), bf16[1536,3584]{1,0:T(8,128)(2,1)}) %all-gather.8.cloned.1.call-update) | async-done | bytes 11010064 | tf_op jit(solution)/shard_map/all_gather | solution.py:1110
  100.9 8.1 %shard_map.186 = (bf16[3,256,768]{2,1,0:T(8,128)(2,1)}, bf16[256,768]{1,0:T(8,128)(2,1)}, f32[128,1536]{1,0:T(8,128)}, bf16[128,1536]{1,0:T(8,128)(2,1)}) custom-call(s32[2]{0:T(128)} %pad_add_fusion.scalar_ref.behind_ref, bf16[256,1536]{1,0:T(8,128)(2,1)} %all_gather.49.refs_0_, f32[3,768]{1,0:T(4,128)} %dynamic-slice_convert_fusion.refs_1_, ...), custom_call_target="tpu_custom_call" | custom-call | flops 1 | bytes 1 | tf_op jit(solution)/shard_map/pallas_call | solution.py:960
  115.4 16.3 %shard_map.187 = (bf16[256,3456]{1,0:T(8,128)(2,1)}, bf16[256,3456]{1,0:T(8,128)(2,1)}, f32[128,1536]{1,0:T(8,128)}, bf16[128,1536]{1,0:T(8,128)(2,1)}) custom-call(s32[2]{0:T(128)} %pad_add_fusion.scalar_ref.behind_ref, bf16[256,1536]{1,0:T(8,128)(2,1)} %all_gather.51.refs_0_, bf16[2,1536,3456]{2,1,0:T(8,128)(2,1)} %bitcast.96, bf16[3456,1536]{1,0:T(8,128)(2,1)} %bitcast.99), custom_call_target="tpu_custom_call" | custom-call | flops 1 | bytes 1 | tf_op jit(solution)/shard_map/pallas_call | solution.py:307
  135.0 4.9 %collective-permute-start.2 = (bf16[128,1536]{1,0:T(8,128)(2,1)S(1)}, bf16[128,1536]{1,0:T(8,128)(2,1)S(1)}, u32[]{:S(2)}, u32[]{:S(2)}) collective-permute-start(bf16[128,1536]{1,0:T(8,128)(2,1)S(1)} %add_convert_fusion.1), channel_id=1, source_target_pairs={{0,64},{1,65},{2,66},{3,67},{4,68},{5,69},{6,70},{7,71},{8,72},{9,... | collective-permute-start | bytes 1179656 | tf_op jit(solution)/shard_map/ppermute | solution.py:1164
  139.9 8.7 %collective-permute-done.2 = bf16[128,1536]{1,0:T(8,128)(2,1)S(1)} collective-permute-done((bf16[128,1536]{1,0:T(8,128)(2,1)S(1)}, bf16[128,1536]{1,0:T(8,128)(2,1)S(1)}, u32[]{:S(2)}, u32[]{:S(2)}) %collective-permute-start.2) | collective-permute-done | bytes 393248 | tf_op jit(solution)/shard_map/ppermute | solution.py:1164
  151.4 10.6 %shard_map.188 = (f32[256,1280]{1,0:T(8,128)}, bf16[256,1280]{1,0:T(8,128)(2,1)}, bf16[256,768]{1,0:T(8,128)(2,1)}, f32[128,1536]{1,0:T(8,128)}, bf16[128,1536]{1,0:T(8,128)(2,1)}) custom-call(s32[2]{0:T(128)} %pad_add_fusion.scalar_ref.behind_ref, bf16[256,1536]{1,0:T(8,128)(2,1)} %all_gather.52.refs_0_, f32[9,128]{1,0:T(8,128)} %stack.83.refs_1_, ...), custom_call_target="tpu_custom_call" | custom-call | flops 1 | bytes 1 | tf_op jit(solution)/shard_map/pallas_call | solution.py:960
  169.7 23.6 %shard_map.189 = (f32[128,1536]{1,0:T(8,128)}, bf16[128,1536]{1,0:T(8,128)(2,1)}, f32[128,1536]{1,0:T(8,128)}, bf16[128,1536]{1,0:T(8,128)(2,1)}) custom-call(s32[2]{0:T(128)} %pad_add_fusion.scalar_ref.behind_ref, bf16[4096,1536]{1,0:T(8,128)(2,1)} %all-gather.10.cloned.1.call-done.refs_0_.early_ref, bf16[256,1536]{1,0:T(8,128)(2,1)} %all_gather.54.refs_1_, ...), custom_call_target="tpu_custom_call" | custom-call | flops 1 | bytes 1 | tf_op jit(solution)/shard_map/pallas_call | solution.py:255
  196.1 3.2 shard_map.190
  199.3 4.3 all_gather.56.refs_0_
  203.5 15.3 %shard_map.191 = (bf16[4,256,1024]{2,1,0:T(8,128)(2,1)}, f32[10,128]{1,0:T(8,128)}, f32[128,1536]{1,0:T(8,128)}, bf16[128,1536]{1,0:T(8,128)(2,1)}) custom-call(s32[2]{0:T(128)} %pad_add_fusion.scalar_ref.behind_ref, bf16[256,1536]{1,0:T(8,128)(2,1)} %all_gather.56.refs_0_, f32[9,128]{1,0:T(8,128)} %stack.83.refs_1_, f32[2,256,128]{2,1,0:T(8,128)} %bitcast.115, ...), custom_call_target="tpu_custom_call" | custom-call | flops 1 | bytes 1 | tf_op jit(solution)/shard_map/pallas_call | solution.py:960
  226.2 14.6 %collective-permute-done.7 = bf16[128,1536]{1,0:T(8,128)(2,1)S(1)} collective-permute-done((bf16[128,1536]{1,0:T(8,128)(2,1)}, bf16[128,1536]{1,0:T(8,128)(2,1)S(1)}, u32[]{:S(2)}, u32[]{:S(2)}) %collective-permute-start.7) | collective-permute-done | bytes 393248 | tf_op jit(solution)/shard_map/ppermute | solution.py:1195
  244.5 16.8 %shard_map.193 = (f32[128,1536]{1,0:T(8,128)}, bf16[128,1536]{1,0:T(8,128)(2,1)}) custom-call(s32[2]{0:T(128)} %pad_add_fusion.scalar_ref.behind_ref, bf16[4096,1536]{1,0:T(8,128)(2,1)} %all-gather.12.cloned.1.call-done.refs_0_.refs_1_, bf16[256,1536]{1,0:T(8,128)(2,1)} %all_gather.57.refs_1_, bf16[256,3456]{1,0:T(8,128)(2,1)} %get-tuple-element.123.refs_2_, ...), custom_call_target="tpu_custom_call" | custom-call | flops 1 | bytes 1 | tf_op jit(solution)/shard_map/pallas_call | solution.py:307
  264.0 3.2 shard_map.194
  267.3 4.0 all_gather.58.refs_0_
  271.3 11.6 %shard_map.195 = (bf16[4,256,1024]{2,1,0:T(8,128)(2,1)}, f32[3,768]{1,0:T(4,128)}, f32[128,1536]{1,0:T(8,128)}, bf16[128,1536]{1,0:T(8,128)(2,1)}) custom-call(s32[2]{0:T(128)} %pad_add_fusion.scalar_ref.behind_ref, bf16[256,1536]{1,0:T(8,128)(2,1)} %all_gather.58.refs_0_, f32[3,768]{1,0:T(4,128)} %dynamic-slice_convert_fusion.refs_1_, ...), custom_call_target="tpu_custom_call" | custom-call | flops 1 | bytes 1 | tf_op jit(solution)/shard_map/pallas_call | solution.py:960
  282.9 4.2 all-to-all-start
  288.0 12.2 %shard_map.196 = bf16[4096,768]{1,0:T(8,128)(2,1)} custom-call(bf16[4,256,1024]{2,1,0:T(8,128)(2,1)} %get-tuple-element.130.refs_0_, bf16[4096,1536]{1,0:T(8,128)(2,1)} %all-gather.12.cloned.1.call-done.refs_0_.refs_1_, bf16[1536,512]{1,0:T(8,128)(2,1)} %fusion.2.refs_2_), custom_call_target="tpu_custom_call" | custom-call | flops 12884901888 | bytes 12582912 | tf_op jit(solution)/shard_map/pallas_call | solution.py:334
  300.2 22.6 %all-to-all-done = bf16[4,256,1024]{2,1,0:T(8,128)(2,1)S(1)} async-done(((bf16[4,256,1024]{2,1,0:T(8,128)(2,1)}), bf16[4,256,1024]{2,1,0:T(8,128)(2,1)S(1)}, u32[]{:S(2)}, u32[]{:S(2)}) %all-to-all-start) | async-done | bytes 2097184 | tf_op jit(solution)/shard_map/all_to_all | solution.py:68
  322.8 13.0 %conditional.1 = ((bf16[4096,512]{1,0:T(8,128)(2,1)}, bf16[768,256]{1,0:T(8,128)(2,1)}, bf16[768,256]{1,0:T(8,128)(2,1)})) conditional(s32[]{:T(128)} %convert_element_type.112, (s32[3]{0:T(128)S(1)}, bf16[1024,1024]{1,0:T(8,128)(2,1)S(1)}, bf16[4096,1536]{1,0:T(8,128)(2,1)}, bf16[4096,768]{1,0:T(8,128)(2,1)}, ...), branch_computations={%region_4.5_spmd, %region_5.6_spmd} | conditional | flops 1 | bytes 9 | solution.py:1225
  322.8 13.0 %branch_1_fun.1 = (bf16[4096,512]{1,0:T(8,128)(2,1)}, bf16[768,256]{1,0:T(8,128)(2,1)}, bf16[768,256]{1,0:T(8,128)(2,1)}) custom-call(s32[3]{0:T(128)S(1)} %get-tuple-element.25.scalar_ref, bf16[1024,1024]{1,0:T(8,128)(2,1)S(1)} %get-tuple-element.26.refs_0_, bf16[4096,1536]{1,0:T(8,128)(2,1)} %get-tuple-element.27.refs_1_, ...), custom_call_target="tpu_custom_call" | custom-call | flops 1 | bytes 1 | tf_op jit(solution)/shard_map/cond/branch_1_fun/pallas_call | solution.py:399
  335.8 6.4 %shard_map.198.refs_0_ = bf16[16,96,640]{2,1,0:T(8,128)(2,1)} custom-call(s32[3]{0:T(128)S(1)} %pad_add_fusion.1.places_ref.scalar_ref, bf16[4096,512]{1,0:T(8,128)(2,1)} %get-tuple-element.133.behind_ref.refs_2_, bf16[1024,1024]{1,0:T(8,128)(2,1)S(1)} %bitcast.104, bf16[4096,1536]{1,0:T(8,128)(2,1)} %all-gather.10.cloned.1.call-done.refs_0_.early_ref, ...), custom_call_target="tpu_custom_call" | custom-call | flops 1 | bytes 1 | tf_op jit(solution)/shard_map/pallas_call | solution.py:633
  342.2 5.2 %all-to-all-start.1 = ((bf16[16,96,640]{2,1,0:T(8,128)(2,1)}), bf16[16,96,640]{2,1,0:T(8,128)(2,1)}, u32[]{:S(2)}, u32[]{:S(2)}) async-start(bf16[16,96,640]{2,1,0:T(8,128)(2,1)} %shard_map.198.refs_0_), calls=%async_computation.1 | async-start | bytes 3932160 | tf_op jit(solution)/shard_map/all_to_all | solution.py:68
  349.1 13.5 %shard_map.199 = (bf16[768,512]{1,0:T(8,128)(2,1)}, bf16[768,512]{1,0:T(8,128)(2,1)}) custom-call(s32[3]{0:T(128)S(1)} %pad_add_fusion.1.places_ref.scalar_ref, bf16[16,96,640]{2,1,0:T(8,128)(2,1)} %shard_map.198.refs_0_, bf16[4096,1536]{1,0:T(8,128)(2,1)} %all-gather.12.cloned.1.call-done.refs_0_.refs_1_, ...), custom_call_target="tpu_custom_call" | custom-call | flops 1 | bytes 1 | tf_op jit(solution)/shard_map/pallas_call | solution.py:399
  364.8 3.2 shard_map.197
  371.2 12.2 %collective-permute-done.14 = f32[64,128]{1,0:T(8,128)S(1)} collective-permute-done((f32[64,128]{1,0:T(8,128)S(1)}, f32[64,128]{1,0:T(8,128)S(1)}, u32[]{:S(2)}, u32[]{:S(2)}) %collective-permute-start.14) | collective-permute-done | bytes 32800 | tf_op jit(solution)/shard_map/ppermute | solution.py:40
  383.4 4.2 collective-permute-start.15
  394.2 5.7 %collective-permute-done.11.refs_4_ = bf16[768,256]{1,0:T(8,128)(2,1)} collective-permute-done((bf16[768,256]{1,0:T(8,128)(2,1)}, bf16[768,256]{1,0:T(8,128)(2,1)}, u32[]{:S(2)}, u32[]{:S(2)}) %collective-permute-start.11) | collective-permute-done | bytes 393248 | tf_op jit(solution)/shard_map/ppermute | solution.py:40
  403.7 7.2 %all-to-all-start.2 = ((bf16[16,48,768]{2,1,0:T(8,128)(2,1)}), bf16[16,48,768]{2,1,0:T(8,128)(2,1)S(1)}, u32[]{:S(2)}, u32[]{:S(2)}) async-start(bf16[16,48,768]{2,1,0:T(8,128)(2,1)} %bitcast.110), calls=%async_computation.2 | async-start | bytes 2359296 | tf_op jit(solution)/shard_map/all_to_all | solution.py:68
  413.1 3.2 collective-permute-start.19
  422.2 5.1 %collective-permute-done.12.come_ref = bf16[4,48,640]{2,1,0:T(8,128)(2,1)S(1)} collective-permute-done((bf16[4,48,640]{2,1,0:T(8,128)(2,1)}, bf16[4,48,640]{2,1,0:T(8,128)(2,1)S(1)}, u32[]{:S(2)}, u32[]{:S(2)}) %collective-permute-start.12) | collective-permute-done | bytes 245792 | tf_op jit(solution)/shard_map/ppermute | solution.py:40
  430.7 5.7 %collective-permute-done.13.behind_ref = bf16[4,24,640]{2,1,0:T(8,128)(2,1)S(1)} collective-permute-done((bf16[4,24,640]{2,1,0:T(8,128)(2,1)}, bf16[4,24,640]{2,1,0:T(8,128)(2,1)S(1)}, u32[]{:S(2)}, u32[]{:S(2)}) %collective-permute-start.13) | collective-permute-done | bytes 122912 | tf_op jit(solution)/shard_map/ppermute | solution.py:40
  (218 shorter events, 101.5 us)
Async XLA Ops:
  7.2 93.0 %all-gather.8.cloned.1.call-start = ((), (), s32[]{:S(2)}) async-start(), calls=%async_computation.3 | async-start | bytes 11182080 | tf_op jit(solution)/shard_map/all_gather | solution.py:1110
  9.7 160.0 %all-gather.10.cloned.1.call-start = ((), (), s32[]{:S(2)}) async-start(), calls=%async_computation.4 | async-start | bytes 12976128 | tf_op jit(solution)/shard_map/all_gather | solution.py:1110
  14.4 230.1 %all-gather.12.cloned.1.call-start = ((), (), s32[]{:S(2)}) async-start(), calls=%async_computation.5 | async-start | bytes 12976128 | tf_op jit(solution)/shard_map/all_gather | solution.py:1110
  109.0 2.0 collective-permute-start
  112.5 53.1 %copy-start.1 = (f32[128,1536]{1,0:T(8,128)}, f32[128,1536]{1,0:T(8,128)S(1)}, u32[]{:S(2)}) copy-start(f32[128,1536]{1,0:T(8,128)S(1)} %get-tuple-element.167.values_ref) | copy-start | bytes 2359300
  131.7 2.0 collective-permute-start.1
  135.0 13.6 %collective-permute-start.2 = (bf16[128,1536]{1,0:T(8,128)(2,1)S(1)}, bf16[128,1536]{1,0:T(8,128)(2,1)S(1)}, u32[]{:S(2)}, u32[]{:S(2)}) collective-permute-start(bf16[128,1536]{1,0:T(8,128)(2,1)S(1)} %add_convert_fusion.1), channel_id=1, source_target_pairs={{0,64},{1,65},{2,66},{3,67},{4,68},{5,69},{6,70},{7,71},{8,72},{9,... | collective-permute-start | bytes 1179656 | tf_op jit(solution)/shard_map/ppermute | solution.py:1164
  162.1 2.1 collective-permute-start.3
  165.6 27.7 %copy-start.2 = (f32[128,1536]{1,0:T(8,128)}, f32[128,1536]{1,0:T(8,128)S(1)}, u32[]{:S(2)}) copy-start(f32[128,1536]{1,0:T(8,128)S(1)} %get-tuple-element.163.values_ref) | copy-start | bytes 2359300
  166.6 156.1 %all-gather.14.cloned.1.call-start = ((), (), s32[]{:S(2)}) async-start(), calls=%async_computation.6 | async-start | bytes 12976128 | tf_op jit(solution)/shard_map/all_gather | solution.py:1110
  193.3 2.0 collective-permute-start.5
  218.8 2.2 collective-permute-start.6
  225.0 15.8 %collective-permute-start.7 = (bf16[128,1536]{1,0:T(8,128)(2,1)}, bf16[128,1536]{1,0:T(8,128)(2,1)S(1)}, u32[]{:S(2)}, u32[]{:S(2)}) collective-permute-start(bf16[128,1536]{1,0:T(8,128)(2,1)} %get-tuple-element.122), channel_id=1, source_target_pairs={{64,0},{65,1},{66,2},{67,3},{68,4},{69,5},{70,6},{71,7},{72,8},{73... | collective-permute-start | bytes 1179656 | tf_op jit(solution)/shard_map/ppermute | solution.py:1195
  261.3 2.0 collective-permute-start.8
  282.9 39.8 %all-to-all-start = ((bf16[4,256,1024]{2,1,0:T(8,128)(2,1)}), bf16[4,256,1024]{2,1,0:T(8,128)(2,1)S(1)}, u32[]{:S(2)}, u32[]{:S(2)}) async-start(bf16[4,256,1024]{2,1,0:T(8,128)(2,1)} %get-tuple-element.130.refs_0_), calls=%async_computation | async-start | bytes 4194304 | tf_op jit(solution)/shard_map/all_to_all | solution.py:68
  287.1 103.2 %all-gather.16.cloned.1.call-start = ((), (), s32[]{:S(2)}) async-start(), calls=%async_computation.7 | async-start | bytes 1966080 | tf_op jit(solution)/shard_map/all_gather | solution.py:1110
  288.0 34.8 %copy-start.4 = (bf16[256,1536]{1,0:T(8,128)(2,1)S(1)}, bf16[256,1536]{1,0:T(8,128)(2,1)}, u32[]{:S(2)}) copy-start(bf16[256,1536]{1,0:T(8,128)(2,1)} %pad.31) | copy-start | bytes 2359300
  342.2 61.5 %all-to-all-start.1 = ((bf16[16,96,640]{2,1,0:T(8,128)(2,1)}), bf16[16,96,640]{2,1,0:T(8,128)(2,1)}, u32[]{:S(2)}, u32[]{:S(2)}) async-start(bf16[16,96,640]{2,1,0:T(8,128)(2,1)} %shard_map.198.refs_0_), calls=%async_computation.1 | async-start | bytes 3932160 | tf_op jit(solution)/shard_map/all_to_all | solution.py:68
  347.5 92.7 %all-gather.18.cloned.1.call-start = ((), (), s32[]{:S(2)}) async-start(), calls=%async_computation.8 | async-start | bytes 1114112 | tf_op jit(solution)/shard_map/all_gather | solution.py:1252
  348.6 15.4 %collective-permute-start.9 = (bf16[128,1536]{1,0:T(8,128)(2,1)}, bf16[128,1536]{1,0:T(8,128)(2,1)S(1)}, u32[]{:S(2)}, u32[]{:S(2)}) collective-permute-start(bf16[128,1536]{1,0:T(8,128)(2,1)} %get-tuple-element.135), channel_id=1, source_target_pairs={{0,1},{1,0},{2,3},{3,2},{4,5},{5,4},{6,7},{7,6},{8,9},{9,8},{10,11... | collective-permute-start | bytes 1179656 | tf_op jit(solution)/shard_map/ppermute | solution.py:40
  362.6 37.3 %collective-permute-start.10 = (bf16[768,512]{1,0:T(8,128)(2,1)}, bf16[768,512]{1,0:T(8,128)(2,1)S(1)}, u32[]{:S(2)}, u32[]{:S(2)}) collective-permute-start(bf16[768,512]{1,0:T(8,128)(2,1)} %get-tuple-element.139.behind_ref), channel_id=1, source_target_pairs={{0,32},{32,0},{1,33},{33,1},{2,34},{34,2},{3,35},{35,3},{4,36},{36... | collective-permute-start | bytes 2359304 | tf_op jit(solution)/shard_map/ppermute | solution.py:40
  370.6 12.8 %collective-permute-start.14 = (f32[64,128]{1,0:T(8,128)S(1)}, f32[64,128]{1,0:T(8,128)S(1)}, u32[]{:S(2)}, u32[]{:S(2)}) collective-permute-start(f32[64,128]{1,0:T(8,128)S(1)} %reduce_sum.69), channel_id=1, source_target_pairs={{0,32},{32,0},{1,33},{33,1},{2,34},{34,2},{3,35},{35,3},{4,36},{36... | collective-permute-start | bytes 98312 | tf_op jit(solution)/shard_map/ppermute | solution.py:40
  383.4 6.1 %collective-permute-start.15 = (f32[64,128]{1,0:T(8,128)S(1)}, f32[64,128]{1,0:T(8,128)S(1)}, u32[]{:S(2)}, u32[]{:S(2)}) collective-permute-start(f32[64,128]{1,0:T(8,128)S(1)} %add.153), channel_id=1, source_target_pairs={{0,64},{64,0},{1,65},{65,1},{2,66},{66,2},{3,67},{67,3},{4,68},{68... | collective-permute-start | bytes 98312 | tf_op jit(solution)/shard_map/ppermute | solution.py:40
  387.7 23.3 %collective-permute-start.4 = (bf16[128,1536]{1,0:T(8,128)(2,1)}, bf16[128,1536]{1,0:T(8,128)(2,1)S(1)}, u32[]{:S(2)}, u32[]{:S(2)}) collective-permute-start(bf16[128,1536]{1,0:T(8,128)(2,1)} %get-tuple-element.113), channel_id=1, source_target_pairs={{0,1},{1,0},{2,3},{3,2},{4,5},{5,4},{6,7},{7,6},{8,9},{9,8},{10,11... | collective-permute-start | bytes 1179656 | tf_op jit(solution)/shard_map/ppermute | solution.py:40
  387.7 12.2 %collective-permute-start.11 = (bf16[768,256]{1,0:T(8,128)(2,1)}, bf16[768,256]{1,0:T(8,128)(2,1)}, u32[]{:S(2)}, u32[]{:S(2)}) collective-permute-start(bf16[768,256]{1,0:T(8,128)(2,1)} %get-tuple-element.141), channel_id=1, source_target_pairs={{0,32},{32,0},{1,33},{33,1},{2,34},{34,2},{3,35},{35,3},{4,36},{36... | collective-permute-start | bytes 1179656 | tf_op jit(solution)/shard_map/ppermute | solution.py:40
  393.4 18.5 %collective-permute-start.16 = (bf16[192,768]{1,0:T(8,128)(2,1)}, bf16[192,768]{1,0:T(8,128)(2,1)}, u32[]{:S(2)}, u32[]{:S(2)}) collective-permute-start(bf16[192,768]{1,0:T(8,128)(2,1)} %get-tuple-element.156), channel_id=1, source_target_pairs={{0,32},{32,0},{1,33},{33,1},{2,34},{34,2},{3,35},{35,3},{4,36},{36... | collective-permute-start | bytes 884744 | tf_op jit(solution)/shard_map/ppermute | solution.py:40
  403.7 27.0 %all-to-all-start.2 = ((bf16[16,48,768]{2,1,0:T(8,128)(2,1)}), bf16[16,48,768]{2,1,0:T(8,128)(2,1)S(1)}, u32[]{:S(2)}, u32[]{:S(2)}) async-start(bf16[16,48,768]{2,1,0:T(8,128)(2,1)} %bitcast.110), calls=%async_computation.2 | async-start | bytes 2359296 | tf_op jit(solution)/shard_map/all_to_all | solution.py:68
  413.1 16.9 %collective-permute-start.19 = (bf16[48,768]{1,0:T(8,128)(2,1)S(1)}, bf16[48,768]{1,0:T(8,128)(2,1)S(1)}, u32[]{:S(2)}, u32[]{:S(2)}) collective-permute-start(bf16[48,768]{1,0:T(8,128)(2,1)S(1)} %get-tuple-element.173), channel_id=1, source_target_pairs={{0,24},{8,0},{16,8},{24,16},{1,25},{9,1},{17,9},{25,17},{2,26},{10... | collective-permute-start | bytes 221192 | tf_op jit(solution)/shard_map/ppermute | solution.py:1279
  416.3 13.7 %collective-permute-start.18 = (bf16[48,768]{1,0:T(8,128)(2,1)S(1)}, bf16[48,768]{1,0:T(8,128)(2,1)S(1)}, u32[]{:S(2)}, u32[]{:S(2)}) collective-permute-start(bf16[48,768]{1,0:T(8,128)(2,1)S(1)} %get-tuple-element.174), channel_id=1, source_target_pairs={{0,16},{8,24},{16,0},{24,8},{1,17},{9,25},{17,1},{25,9},{2,18},{10... | collective-permute-start | bytes 221192 | tf_op jit(solution)/shard_map/ppermute | solution.py:1279
  417.1 12.9 %collective-permute-start.17 = (bf16[48,768]{1,0:T(8,128)(2,1)S(1)}, bf16[48,768]{1,0:T(8,128)(2,1)S(1)}, u32[]{:S(2)}, u32[]{:S(2)}) collective-permute-start(bf16[48,768]{1,0:T(8,128)(2,1)S(1)} %get-tuple-element.172), channel_id=1, source_target_pairs={{0,8},{8,16},{16,24},{24,0},{1,9},{9,17},{17,25},{25,1},{2,10},{10... | collective-permute-start | bytes 221192 | tf_op jit(solution)/shard_map/ppermute | solution.py:1279
  420.8 6.4 %collective-permute-start.12 = (bf16[4,48,640]{2,1,0:T(8,128)(2,1)}, bf16[4,48,640]{2,1,0:T(8,128)(2,1)S(1)}, u32[]{:S(2)}, u32[]{:S(2)}) collective-permute-start(bf16[4,48,640]{2,1,0:T(8,128)(2,1)} %get-tuple-element.143), channel_id=1, source_target_pairs={{0,32},{32,0},{1,33},{33,1},{2,34},{34,2},{3,35},{35,3},{4,36},{36... | collective-permute-start | bytes 737288 | tf_op jit(solution)/shard_map/ppermute | solution.py:40
  429.9 6.6 %collective-permute-start.13 = (bf16[4,24,640]{2,1,0:T(8,128)(2,1)}, bf16[4,24,640]{2,1,0:T(8,128)(2,1)S(1)}, u32[]{:S(2)}, u32[]{:S(2)}) collective-permute-start(bf16[4,24,640]{2,1,0:T(8,128)(2,1)} %get-tuple-element.144), channel_id=1, source_target_pairs={{0,64},{64,0},{1,65},{65,1},{2,66},{66,2},{3,67},{67,3},{4,68},{68... | collective-permute-start | bytes 368648 | tf_op jit(solution)/shard_map/ppermute | solution.py:40
  (30 other events, 223.6 us)
Sparse Core Ops, SparseCore 0:
  11.4 88.7 all-gather.7
  103.0 62.5 all-gather.9
  167.9 62.4 all-gather.11
  242.1 68.7 all-gather.13
  312.4 39.8 all-gather.15
  390.3 49.7 all-gather.17

commit v10 on v9

--- a/solution.py
+++ b/solution.py
@@ -559,17 +559,19 @@
     sent_ref[...] = sent.astype(BF16)
 
 
-def plane_sums_kernel(behind_ref, small_ref, sums_ref):
-    sums_ref[...] = jnp.sum(small_ref[...], axis=0)
-
-
-def plane_sums_call(behind, small):
+def section_sums_kernel(behind_ref, small_ref, sums_ref):
+    half = small_ref.shape[0] // 2
+    for k in range(2):
+        sums_ref[k] = jnp.sum(small_ref[k * half : (k + 1) * half], axis=0)
+
+
+def section_sums_call(behind, small):
     vmem = pl.BlockSpec(memory_space=pltpu.VMEM)
     return pl.pallas_call(
-        plane_sums_kernel,
+        section_sums_kernel,
         in_specs=[pl.BlockSpec(memory_space=pl.ANY), vmem],
         out_specs=vmem,
-        out_shape=jax.ShapeDtypeStruct(small.shape[1:], F32),
+        out_shape=jax.ShapeDtypeStruct((2, *small.shape[1:]), F32),
         compiler_params=pltpu.CompilerParams(vmem_limit_bytes=VMEM_LIMIT),
         cost_estimate=SHORT,
     )(behind, small)
@@ -1246,10 +1248,7 @@
     count = small.shape[0]
     small = jnp.pad(small, (0, -count % 1024)).reshape(-1, 128)
     small = lax.all_gather(small, "c").sum(0)
-    small = small + swapped(small, "xl")
-    across = swapped(small, "xh")
-    small = jnp.concatenate([chosen(small, across), chosen(across, small)])
-    small_all = lax.all_gather(small, PLANE)
+    small_all = lax.all_gather(small, ("xh", "xl", "y", "z"))
 
     come = exchanged(in_parts, PLANE)
     line_mine, line_other = line_sums_call(xl_scalar, come)
@@ -1279,7 +1278,7 @@
         lines += lax.ppermute(block, "y", around(by)).astype(F32)
     grad_mixer_out = lines.T[None]
 
-    pair = plane_sums_call(grad_gate_up, small_all).reshape(2, -1)
+    pair = section_sums_call(grad_gate_up, small_all).reshape(2, -1)
     grad_norm_gains = jnp.stack([a[: 2 * width].reshape(2, width) for a in pair])
     grad_conv_kernel = pair[0][2 * width : 5 * width].reshape(conv_kernel.shape)
     grad_qk_gains = pair[1][5 * width : count].reshape(qk_gains.shape)

time: 463 us -> 465 us (level)
    ppermute x15 -> x13, starting transfers between devices: 10.4 us -> 11.1 us  [swapped(): return lax.ppermute(shard, axis, [(0, 1), (1, 0)])]
    ppermute x15 -> x13, waiting for transfers between devices: 38.6 us -> 38.4 us  [swapped(): return lax.ppermute(shard, axis, [(0, 1), (1, 0)])]
  transfers between devices with their start and end apart: 29 -> 27, of which waited for: 16 -> 13; matrix products, arithmetic and copies ran while one was open for 8% -> 9% of each run, Pallas kernels for 38% -> 38%
where the time goes in v10:
time: 465 us; the launch traced here: 457 us
  Pallas kernels  175 us (38%)
  waiting for transfers between devices  148 us (32%)
  starting transfers between devices  38.7 us (8%)
  other arithmetic  28.3 us (6%)
  blocking collectives  26.3 us (6%)
  local copies, waits for them, and re-layouts  26.1 us (6%)
  between operations  14.9 us (3%)
    all_gather x5, waiting for transfers between devices, gathered(): return lax.all_gather(own, axes, tiled=True)  63.3 us
    pallas_call x4, Pallas kernels, mixer_call(): pl.pallas_call(ordered(kernel, len(behind)), in_specs=[pl.BlockSpec(memor...  45.2 us
    ppermute x13, waiting for transfers between devices, swapped(): return lax.ppermute(shard, axis, [(0, 1), (1, 0)])  38.4 us
    pallas_call x2, Pallas kernels, feed_forward_call(): pl.pallas_call(ordered(body, len(behind)), in_specs=in_specs, out_specs=o...  33 us
    pallas_call x2, Pallas kernels, part_call(): pl.pallas_call(ordered(kernel, len(behind)), grid_spec=pltpu.PrefetchScal...  25.5 us
    all_gather x8, blocking collectives, spread(): return lax.all_gather(own, 'c', tiled=True)  24.2 us
    pallas_call x1, Pallas kernels, ffn_both_call(): pl.pallas_call(ordered(functools.partial(ffn_both_kernel, unit_tiles(unit...  23.6 us
    all_to_all x3, waiting for transfers between devices, exchanged(): return lax.all_to_all(tiles, axes, 0, 0, tiled=True)  22.7 us
  transfers between devices with their start and end apart: 27, of which 13 were waited for; matrix products, arithmetic and copies ran while one was open for 9% of the time, Pallas kernels for 38%

profile of v10, /device:TPU:0, one launch (start us, length us, event | category | flops | bytes accessed | tf_op | source)
XLA Modules:
  0.0 456.7 jit_solution(1440637445873366927)
XLA Ops:
  26.6 8.1 %fusion.15 = (bf16[1,1,1536,3456]{3,2,1,0:T(8,128)(2,1)S(1)}, bf16[1,1,1536,3456]{3,2,1,0:T(8,128)(2,1)S(1)}) fusion(bf16[1,2,1536,3456]{3,2,1,0:T(8,128)(2,1)} %param.22), kind=kLoop, calls=%fused_computation.91 | loop fusion | bytes 42467328 | tf_op jit(solution)/shard_map/slice | solution.py:1123
  36.9 63.3 %all-gather.8.cloned.1.call-done.refs_3_.refs_4_.refs_6_.refs_5_ = bf16[1536,3584]{1,0:T(8,128)(2,1)} async-done(((bf16[24,3584]{1,0:T(8,128)(2,1)}), bf16[1536,3584]{1,0:T(8,128)(2,1)}) %all-gather.8.cloned.1.call-update) | async-done | bytes 11010064 | tf_op jit(solution)/shard_map/all_gather | solution.py:1112
  100.9 8.1 %shard_map.186 = (bf16[3,256,768]{2,1,0:T(8,128)(2,1)}, bf16[256,768]{1,0:T(8,128)(2,1)}, f32[128,1536]{1,0:T(8,128)}, bf16[128,1536]{1,0:T(8,128)(2,1)}) custom-call(s32[2]{0:T(128)} %pad_add_fusion.scalar_ref.behind_ref, bf16[256,1536]{1,0:T(8,128)(2,1)} %all_gather.49.refs_0_, f32[3,768]{1,0:T(4,128)} %dynamic-slice_convert_fusion.refs_1_, ...), custom_call_target="tpu_custom_call" | custom-call | flops 1 | bytes 1 | tf_op jit(solution)/shard_map/pallas_call | solution.py:962
  115.3 16.3 %shard_map.187 = (bf16[256,3456]{1,0:T(8,128)(2,1)}, bf16[256,3456]{1,0:T(8,128)(2,1)}, f32[128,1536]{1,0:T(8,128)}, bf16[128,1536]{1,0:T(8,128)(2,1)}) custom-call(s32[2]{0:T(128)} %pad_add_fusion.scalar_ref.behind_ref, bf16[256,1536]{1,0:T(8,128)(2,1)} %all_gather.51.refs_0_, bf16[2,1536,3456]{2,1,0:T(8,128)(2,1)} %bitcast.96, bf16[3456,1536]{1,0:T(8,128)(2,1)} %bitcast.99), custom_call_target="tpu_custom_call" | custom-call | flops 1 | bytes 1 | tf_op jit(solution)/shard_map/pallas_call | solution.py:307
  134.9 4.9 %collective-permute-start.2 = (bf16[128,1536]{1,0:T(8,128)(2,1)S(1)}, bf16[128,1536]{1,0:T(8,128)(2,1)S(1)}, u32[]{:S(2)}, u32[]{:S(2)}) collective-permute-start(bf16[128,1536]{1,0:T(8,128)(2,1)S(1)} %add_convert_fusion.1), channel_id=1, source_target_pairs={{0,64},{1,65},{2,66},{3,67},{4,68},{5,69},{6,70},{7,71},{8,72},{9,... | collective-permute-start | bytes 1179656 | tf_op jit(solution)/shard_map/ppermute | solution.py:1166
  139.9 8.7 %collective-permute-done.2 = bf16[128,1536]{1,0:T(8,128)(2,1)S(1)} collective-permute-done((bf16[128,1536]{1,0:T(8,128)(2,1)S(1)}, bf16[128,1536]{1,0:T(8,128)(2,1)S(1)}, u32[]{:S(2)}, u32[]{:S(2)}) %collective-permute-start.2) | collective-permute-done | bytes 393248 | tf_op jit(solution)/shard_map/ppermute | solution.py:1166
  151.4 10.7 %shard_map.188 = (f32[256,1280]{1,0:T(8,128)}, bf16[256,1280]{1,0:T(8,128)(2,1)}, bf16[256,768]{1,0:T(8,128)(2,1)}, f32[128,1536]{1,0:T(8,128)}, bf16[128,1536]{1,0:T(8,128)(2,1)}) custom-call(s32[2]{0:T(128)} %pad_add_fusion.scalar_ref.behind_ref, bf16[256,1536]{1,0:T(8,128)(2,1)} %all_gather.52.refs_0_, f32[9,128]{1,0:T(8,128)} %stack.83.refs_1_, ...), custom_call_target="tpu_custom_call" | custom-call | flops 1 | bytes 1 | tf_op jit(solution)/shard_map/pallas_call | solution.py:962
  169.6 23.6 %shard_map.189 = (f32[128,1536]{1,0:T(8,128)}, bf16[128,1536]{1,0:T(8,128)(2,1)}, f32[128,1536]{1,0:T(8,128)}, bf16[128,1536]{1,0:T(8,128)(2,1)}) custom-call(s32[2]{0:T(128)} %pad_add_fusion.scalar_ref.behind_ref, bf16[4096,1536]{1,0:T(8,128)(2,1)} %all-gather.10.cloned.1.call-done.refs_0_.early_ref, bf16[256,1536]{1,0:T(8,128)(2,1)} %all_gather.54.refs_1_, ...), custom_call_target="tpu_custom_call" | custom-call | flops 1 | bytes 1 | tf_op jit(solution)/shard_map/pallas_call | solution.py:255
  196.0 3.2 shard_map.190
  199.2 4.3 all_gather.56.refs_0_
  203.5 15.3 %shard_map.191 = (bf16[4,256,1024]{2,1,0:T(8,128)(2,1)}, f32[10,128]{1,0:T(8,128)}, f32[128,1536]{1,0:T(8,128)}, bf16[128,1536]{1,0:T(8,128)(2,1)}) custom-call(s32[2]{0:T(128)} %pad_add_fusion.scalar_ref.behind_ref, bf16[256,1536]{1,0:T(8,128)(2,1)} %all_gather.56.refs_0_, f32[9,128]{1,0:T(8,128)} %stack.83.refs_1_, f32[2,256,128]{2,1,0:T(8,128)} %bitcast.115, ...), custom_call_target="tpu_custom_call" | custom-call | flops 1 | bytes 1 | tf_op jit(solution)/shard_map/pallas_call | solution.py:962
  221.8 3.2 shard_map.192
  226.2 14.5 %collective-permute-done.7 = bf16[128,1536]{1,0:T(8,128)(2,1)S(1)} collective-permute-done((bf16[128,1536]{1,0:T(8,128)(2,1)}, bf16[128,1536]{1,0:T(8,128)(2,1)S(1)}, u32[]{:S(2)}, u32[]{:S(2)}) %collective-permute-start.7) | collective-permute-done | bytes 393248 | tf_op jit(solution)/shard_map/ppermute | solution.py:1197
  245.4 16.7 %shard_map.193 = (f32[128,1536]{1,0:T(8,128)}, bf16[128,1536]{1,0:T(8,128)(2,1)}) custom-call(s32[2]{0:T(128)} %pad_add_fusion.scalar_ref.behind_ref, bf16[4096,1536]{1,0:T(8,128)(2,1)} %all-gather.12.cloned.1.call-done.refs_0_.refs_1_, bf16[256,1536]{1,0:T(8,128)(2,1)} %all_gather.57.refs_1_, bf16[256,3456]{1,0:T(8,128)(2,1)} %get-tuple-element.123.refs_2_, ...), custom_call_target="tpu_custom_call" | custom-call | flops 1 | bytes 1 | tf_op jit(solution)/shard_map/pallas_call | solution.py:307
  264.8 3.2 shard_map.194
  268.0 4.3 all_gather.58.refs_0_
  272.4 11.1 %shard_map.195 = (bf16[4,256,1024]{2,1,0:T(8,128)(2,1)}, f32[3,768]{1,0:T(4,128)}, f32[128,1536]{1,0:T(8,128)}, bf16[128,1536]{1,0:T(8,128)(2,1)}) custom-call(s32[2]{0:T(128)} %pad_add_fusion.scalar_ref.behind_ref, bf16[256,1536]{1,0:T(8,128)(2,1)} %all_gather.58.refs_0_, f32[3,768]{1,0:T(4,128)} %dynamic-slice_convert_fusion.refs_1_, ...), custom_call_target="tpu_custom_call" | custom-call | flops 1 | bytes 1 | tf_op jit(solution)/shard_map/pallas_call | solution.py:962
  283.5 3.9 all-to-all-start
  287.7 12.2 %shard_map.196 = bf16[4096,768]{1,0:T(8,128)(2,1)} custom-call(bf16[4,256,1024]{2,1,0:T(8,128)(2,1)} %get-tuple-element.130.refs_0_, bf16[4096,1536]{1,0:T(8,128)(2,1)} %all-gather.12.cloned.1.call-done.refs_0_.refs_1_, bf16[1536,512]{1,0:T(8,128)(2,1)} %fusion.2.refs_2_), custom_call_target="tpu_custom_call" | custom-call | flops 12884901888 | bytes 12582912 | tf_op jit(solution)/shard_map/pallas_call | solution.py:334
  300.0 22.7 %all-to-all-done = bf16[4,256,1024]{2,1,0:T(8,128)(2,1)S(1)} async-done(((bf16[4,256,1024]{2,1,0:T(8,128)(2,1)}), bf16[4,256,1024]{2,1,0:T(8,128)(2,1)S(1)}, u32[]{:S(2)}, u32[]{:S(2)}) %all-to-all-start) | async-done | bytes 2097184 | tf_op jit(solution)/shard_map/all_to_all | solution.py:68
  322.8 13.0 %conditional.1 = ((bf16[4096,512]{1,0:T(8,128)(2,1)}, bf16[768,256]{1,0:T(8,128)(2,1)}, bf16[768,256]{1,0:T(8,128)(2,1)})) conditional(s32[]{:T(128)} %convert_element_type.112, (s32[3]{0:T(128)S(1)}, bf16[1024,1024]{1,0:T(8,128)(2,1)S(1)}, bf16[4096,1536]{1,0:T(8,128)(2,1)}, bf16[4096,768]{1,0:T(8,128)(2,1)}, ...), branch_computations={%region_4.5_spmd, %region_5.6_spmd} | conditional | flops 1 | bytes 9 | solution.py:1227
  322.8 13.0 %branch_1_fun.1 = (bf16[4096,512]{1,0:T(8,128)(2,1)}, bf16[768,256]{1,0:T(8,128)(2,1)}, bf16[768,256]{1,0:T(8,128)(2,1)}) custom-call(s32[3]{0:T(128)S(1)} %get-tuple-element.25.scalar_ref, bf16[1024,1024]{1,0:T(8,128)(2,1)S(1)} %get-tuple-element.26.refs_0_, bf16[4096,1536]{1,0:T(8,128)(2,1)} %get-tuple-element.27.refs_1_, ...), custom_call_target="tpu_custom_call" | custom-call | flops 1 | bytes 1 | tf_op jit(solution)/shard_map/cond/branch_1_fun/pallas_call | solution.py:399
  335.8 6.4 %shard_map.198.refs_0_ = bf16[16,96,640]{2,1,0:T(8,128)(2,1)} custom-call(s32[3]{0:T(128)S(1)} %pad_add_fusion.1.places_ref.scalar_ref, bf16[4096,512]{1,0:T(8,128)(2,1)} %get-tuple-element.133.behind_ref.refs_2_, bf16[1024,1024]{1,0:T(8,128)(2,1)S(1)} %bitcast.104, bf16[4096,1536]{1,0:T(8,128)(2,1)} %all-gather.10.cloned.1.call-done.refs_0_.early_ref, ...), custom_call_target="tpu_custom_call" | custom-call | flops 1 | bytes 1 | tf_op jit(solution)/shard_map/pallas_call | solution.py:635
  342.2 5.1 %all-to-all-start.1 = ((bf16[16,96,640]{2,1,0:T(8,128)(2,1)}), bf16[16,96,640]{2,1,0:T(8,128)(2,1)}, u32[]{:S(2)}, u32[]{:S(2)}) async-start(bf16[16,96,640]{2,1,0:T(8,128)(2,1)} %shard_map.198.refs_0_), calls=%async_computation.1 | async-start | bytes 3932160 | tf_op jit(solution)/shard_map/all_to_all | solution.py:68
  348.1 3.2 shard_map.197
  354.7 12.5 %shard_map.199 = (bf16[768,512]{1,0:T(8,128)(2,1)}, bf16[768,512]{1,0:T(8,128)(2,1)}) custom-call(s32[3]{0:T(128)S(1)} %pad_add_fusion.1.places_ref.scalar_ref, bf16[16,96,640]{2,1,0:T(8,128)(2,1)} %shard_map.198.refs_0_, bf16[4096,1536]{1,0:T(8,128)(2,1)} %all-gather.12.cloned.1.call-done.refs_0_.refs_1_, ...), custom_call_target="tpu_custom_call" | custom-call | flops 1 | bytes 1 | tf_op jit(solution)/shard_map/pallas_call | solution.py:399
  369.2 3.2 shard_map.205
  373.9 22.8 %collective-permute-done.11.refs_4_ = bf16[768,256]{1,0:T(8,128)(2,1)} collective-permute-done((bf16[768,256]{1,0:T(8,128)(2,1)}, bf16[768,256]{1,0:T(8,128)(2,1)}, u32[]{:S(2)}, u32[]{:S(2)}) %collective-permute-start.11) | collective-permute-done | bytes 393248 | tf_op jit(solution)/shard_map/ppermute | solution.py:40
  400.5 7.2 %all-to-all-start.2 = ((bf16[16,48,768]{2,1,0:T(8,128)(2,1)}), bf16[16,48,768]{2,1,0:T(8,128)(2,1)S(1)}, u32[]{:S(2)}, u32[]{:S(2)}) async-start(bf16[16,48,768]{2,1,0:T(8,128)(2,1)} %bitcast.110), calls=%async_computation.2 | async-start | bytes 2359296 | tf_op jit(solution)/shard_map/all_to_all | solution.py:68
  409.9 3.2 collective-permute-start.17
  419.9 5.4 %collective-permute-done.12.come_ref = bf16[4,48,640]{2,1,0:T(8,128)(2,1)S(1)} collective-permute-done((bf16[4,48,640]{2,1,0:T(8,128)(2,1)}, bf16[4,48,640]{2,1,0:T(8,128)(2,1)S(1)}, u32[]{:S(2)}, u32[]{:S(2)}) %collective-permute-start.12) | collective-permute-done | bytes 245792 | tf_op jit(solution)/shard_map/ppermute | solution.py:40
  427.9 4.2 collective-permute-start.13
  (205 shorter events, 97.4 us)
Async XLA Ops:
  7.2 93.0 %all-gather.8.cloned.1.call-start = ((), (), s32[]{:S(2)}) async-start(), calls=%async_computation.3 | async-start | bytes 11182080 | tf_op jit(solution)/shard_map/all_gather | solution.py:1112
  9.7 159.9 %all-gather.10.cloned.1.call-start = ((), (), s32[]{:S(2)}) async-start(), calls=%async_computation.4 | async-start | bytes 12976128 | tf_op jit(solution)/shard_map/all_gather | solution.py:1112
  14.4 231.0 %all-gather.12.cloned.1.call-start = ((), (), s32[]{:S(2)}) async-start(), calls=%async_computation.5 | async-start | bytes 12976128 | tf_op jit(solution)/shard_map/all_gather | solution.py:1112
  109.1 2.0 collective-permute-start
  112.5 53.1 %copy-start = (f32[128,1536]{1,0:T(8,128)}, f32[128,1536]{1,0:T(8,128)S(1)}, u32[]{:S(2)}) copy-start(f32[128,1536]{1,0:T(8,128)S(1)} %get-tuple-element.167.values_ref) | copy-start | bytes 2359300
  131.7 2.0 collective-permute-start.1
  134.9 13.6 %collective-permute-start.2 = (bf16[128,1536]{1,0:T(8,128)(2,1)S(1)}, bf16[128,1536]{1,0:T(8,128)(2,1)S(1)}, u32[]{:S(2)}, u32[]{:S(2)}) collective-permute-start(bf16[128,1536]{1,0:T(8,128)(2,1)S(1)} %add_convert_fusion.1), channel_id=1, source_target_pairs={{0,64},{1,65},{2,66},{3,67},{4,68},{5,69},{6,70},{7,71},{8,72},{9,... | collective-permute-start | bytes 1179656 | tf_op jit(solution)/shard_map/ppermute | solution.py:1166
  162.1 2.1 collective-permute-start.3
  165.5 27.7 %copy-start.1 = (f32[128,1536]{1,0:T(8,128)}, f32[128,1536]{1,0:T(8,128)S(1)}, u32[]{:S(2)}) copy-start(f32[128,1536]{1,0:T(8,128)S(1)} %get-tuple-element.163.values_ref) | copy-start | bytes 2359300
  166.7 156.1 %all-gather.14.cloned.1.call-start = ((), (), s32[]{:S(2)}) async-start(), calls=%async_computation.6 | async-start | bytes 12976128 | tf_op jit(solution)/shard_map/all_gather | solution.py:1112
  193.2 2.0 collective-permute-start.5
  218.8 23.3 %copy-start.15 = (bf16[256,768]{1,0:T(8,128)(2,1)S(1)}, bf16[256,768]{1,0:T(8,128)(2,1)}, u32[]{:S(2)}) copy-start(bf16[256,768]{1,0:T(8,128)(2,1)} %get-tuple-element.153) | copy-start | bytes 1179652
  218.8 2.2 collective-permute-start.6
  225.0 15.8 %collective-permute-start.7 = (bf16[128,1536]{1,0:T(8,128)(2,1)}, bf16[128,1536]{1,0:T(8,128)(2,1)S(1)}, u32[]{:S(2)}, u32[]{:S(2)}) collective-permute-start(bf16[128,1536]{1,0:T(8,128)(2,1)} %get-tuple-element.122), channel_id=1, source_target_pairs={{64,0},{65,1},{66,2},{67,3},{68,4},{69,5},{70,6},{71,7},{72,8},{73... | collective-permute-start | bytes 1179656 | tf_op jit(solution)/shard_map/ppermute | solution.py:1197
  242.0 127.2 %all-gather.16.cloned.1.call-start = ((), (), s32[]{:S(2)}) async-start(), calls=%async_computation.7 | async-start | bytes 1966080 | tf_op jit(solution)/shard_map/all_gather | solution.py:1112
  262.1 2.0 collective-permute-start.8
  283.5 39.3 %all-to-all-start = ((bf16[4,256,1024]{2,1,0:T(8,128)(2,1)}), bf16[4,256,1024]{2,1,0:T(8,128)(2,1)S(1)}, u32[]{:S(2)}, u32[]{:S(2)}) async-start(bf16[4,256,1024]{2,1,0:T(8,128)(2,1)} %get-tuple-element.130.refs_0_), calls=%async_computation | async-start | bytes 4194304 | tf_op jit(solution)/shard_map/all_to_all | solution.py:68
  287.5 35.2 %copy-start.3 = (bf16[256,1536]{1,0:T(8,128)(2,1)S(1)}, bf16[256,1536]{1,0:T(8,128)(2,1)}, u32[]{:S(2)}) copy-start(bf16[256,1536]{1,0:T(8,128)(2,1)} %pad.31) | copy-start | bytes 2359300
  287.5 59.8 %collective-permute-start.9 = (bf16[128,1536]{1,0:T(8,128)(2,1)}, bf16[128,1536]{1,0:T(8,128)(2,1)S(1)}, u32[]{:S(2)}, u32[]{:S(2)}) collective-permute-start(bf16[128,1536]{1,0:T(8,128)(2,1)} %get-tuple-element.135), channel_id=1, source_target_pairs={{0,1},{1,0},{2,3},{3,2},{4,5},{5,4},{6,7},{7,6},{8,9},{9,8},{10,11... | collective-permute-start | bytes 1179656 | tf_op jit(solution)/shard_map/ppermute | solution.py:40
  342.2 58.4 %all-to-all-start.1 = ((bf16[16,96,640]{2,1,0:T(8,128)(2,1)}), bf16[16,96,640]{2,1,0:T(8,128)(2,1)}, u32[]{:S(2)}, u32[]{:S(2)}) async-start(bf16[16,96,640]{2,1,0:T(8,128)(2,1)} %shard_map.198.refs_0_), calls=%async_computation.1 | async-start | bytes 3932160 | tf_op jit(solution)/shard_map/all_to_all | solution.py:68
  347.3 96.0 %all-gather.18.cloned.1.call-start = ((), (), s32[]{:S(2)}) async-start(), calls=%async_computation.8 | async-start | bytes 2129920 | tf_op jit(solution)/shard_map/all_gather | solution.py:1251
  367.2 29.5 %collective-permute-start.10 = (bf16[768,512]{1,0:T(8,128)(2,1)}, bf16[768,512]{1,0:T(8,128)(2,1)S(1)}, u32[]{:S(2)}, u32[]{:S(2)}) collective-permute-start(bf16[768,512]{1,0:T(8,128)(2,1)} %get-tuple-element.139.behind_ref), channel_id=1, source_target_pairs={{0,32},{32,0},{1,33},{33,1},{2,34},{34,2},{3,35},{35,3},{4,36},{36... | collective-permute-start | bytes 2359304 | tf_op jit(solution)/shard_map/ppermute | solution.py:40
  368.7 28.0 %collective-permute-start.11 = (bf16[768,256]{1,0:T(8,128)(2,1)}, bf16[768,256]{1,0:T(8,128)(2,1)}, u32[]{:S(2)}, u32[]{:S(2)}) collective-permute-start(bf16[768,256]{1,0:T(8,128)(2,1)} %get-tuple-element.141), channel_id=1, source_target_pairs={{0,32},{32,0},{1,33},{33,1},{2,34},{34,2},{3,35},{35,3},{4,36},{36... | collective-permute-start | bytes 1179656 | tf_op jit(solution)/shard_map/ppermute | solution.py:40
  369.2 38.5 %collective-permute-start.4 = (bf16[128,1536]{1,0:T(8,128)(2,1)}, bf16[128,1536]{1,0:T(8,128)(2,1)S(1)}, u32[]{:S(2)}, u32[]{:S(2)}) collective-permute-start(bf16[128,1536]{1,0:T(8,128)(2,1)} %get-tuple-element.113), channel_id=1, source_target_pairs={{0,1},{1,0},{2,3},{3,2},{4,5},{5,4},{6,7},{7,6},{8,9},{9,8},{10,11... | collective-permute-start | bytes 1179656 | tf_op jit(solution)/shard_map/ppermute | solution.py:40
  369.2 28.4 %copy-start.20 = (bf16[768,256]{1,0:T(8,128)(2,1)S(1)}, bf16[768,256]{1,0:T(8,128)(2,1)}, u32[]{:S(2)}) copy-start(bf16[768,256]{1,0:T(8,128)(2,1)} %get-tuple-element.140.refs_3_) | copy-start | bytes 1179652
  372.4 36.3 %collective-permute-start.14 = (bf16[192,768]{1,0:T(8,128)(2,1)}, bf16[192,768]{1,0:T(8,128)(2,1)}, u32[]{:S(2)}, u32[]{:S(2)}) collective-permute-start(bf16[192,768]{1,0:T(8,128)(2,1)} %get-tuple-element.156), channel_id=1, source_target_pairs={{0,32},{32,0},{1,33},{33,1},{2,34},{34,2},{3,35},{35,3},{4,36},{36... | collective-permute-start | bytes 884744 | tf_op jit(solution)/shard_map/ppermute | solution.py:40
  400.5 32.3 %all-to-all-start.2 = ((bf16[16,48,768]{2,1,0:T(8,128)(2,1)}), bf16[16,48,768]{2,1,0:T(8,128)(2,1)S(1)}, u32[]{:S(2)}, u32[]{:S(2)}) async-start(bf16[16,48,768]{2,1,0:T(8,128)(2,1)} %bitcast.110), calls=%async_computation.2 | async-start | bytes 2359296 | tf_op jit(solution)/shard_map/all_to_all | solution.py:68
  409.9 22.2 %collective-permute-start.17 = (bf16[48,768]{1,0:T(8,128)(2,1)S(1)}, bf16[48,768]{1,0:T(8,128)(2,1)S(1)}, u32[]{:S(2)}, u32[]{:S(2)}) collective-permute-start(bf16[48,768]{1,0:T(8,128)(2,1)S(1)} %get-tuple-element.173), channel_id=1, source_target_pairs={{0,24},{8,0},{16,8},{24,16},{1,25},{9,1},{17,9},{25,17},{2,26},{10... | collective-permute-start | bytes 221192 | tf_op jit(solution)/shard_map/ppermute | solution.py:1278
  413.1 19.0 %collective-permute-start.16 = (bf16[48,768]{1,0:T(8,128)(2,1)S(1)}, bf16[48,768]{1,0:T(8,128)(2,1)S(1)}, u32[]{:S(2)}, u32[]{:S(2)}) collective-permute-start(bf16[48,768]{1,0:T(8,128)(2,1)S(1)} %get-tuple-element.174), channel_id=1, source_target_pairs={{0,16},{8,24},{16,0},{24,8},{1,17},{9,25},{17,1},{25,9},{2,18},{10... | collective-permute-start | bytes 221192 | tf_op jit(solution)/shard_map/ppermute | solution.py:1278
  414.0 18.1 %collective-permute-start.15 = (bf16[48,768]{1,0:T(8,128)(2,1)S(1)}, bf16[48,768]{1,0:T(8,128)(2,1)S(1)}, u32[]{:S(2)}, u32[]{:S(2)}) collective-permute-start(bf16[48,768]{1,0:T(8,128)(2,1)S(1)} %get-tuple-element.172), channel_id=1, source_target_pairs={{0,8},{8,16},{16,24},{24,0},{1,9},{9,17},{17,25},{25,1},{2,10},{10... | collective-permute-start | bytes 221192 | tf_op jit(solution)/shard_map/ppermute | solution.py:1278
  417.6 7.6 %collective-permute-start.12 = (bf16[4,48,640]{2,1,0:T(8,128)(2,1)}, bf16[4,48,640]{2,1,0:T(8,128)(2,1)S(1)}, u32[]{:S(2)}, u32[]{:S(2)}) collective-permute-start(bf16[4,48,640]{2,1,0:T(8,128)(2,1)} %get-tuple-element.143), channel_id=1, source_target_pairs={{0,32},{32,0},{1,33},{33,1},{2,34},{34,2},{3,35},{35,3},{4,36},{36... | collective-permute-start | bytes 737288 | tf_op jit(solution)/shard_map/ppermute | solution.py:40
  427.9 7.7 %collective-permute-start.13 = (bf16[4,24,640]{2,1,0:T(8,128)(2,1)}, bf16[4,24,640]{2,1,0:T(8,128)(2,1)S(1)}, u32[]{:S(2)}, u32[]{:S(2)}) collective-permute-start(bf16[4,24,640]{2,1,0:T(8,128)(2,1)} %get-tuple-element.144), channel_id=1, source_target_pairs={{0,64},{64,0},{1,65},{65,1},{2,66},{66,2},{3,67},{67,3},{4,68},{68... | collective-permute-start | bytes 368648 | tf_op jit(solution)/shard_map/ppermute | solution.py:40
  (25 other events, 202.3 us)
Sparse Core Ops, SparseCore 0:
  11.4 88.7 all-gather.7
  103.0 62.5 all-gather.9
  167.8 62.4 all-gather.11
  242.1 68.5 all-gather.13
  312.2 41.6 all-gather.15
  356.7 81.3 all-gather.17
